TPU v7x, 256 devices: a whole 4x4x8 slice. The times are simulated.
256 devices in a mesh: section: 8 (over x, core), dp: 32 (over y, z).
Axes of the slice: x: 4, y: 4, z: 8, core: 2. Of those that a mesh axis runs over, the one named last changes fastest.
Arguments:
- stack_input: bfloat16 [4096, 12288], P('dp'), may hold values from -6 to 6
- out_cotangent: bfloat16 [4096, 12288], P('dp'), may hold values from -6 to 6
- norm_gain: float32 [8, 12288], P('section'), may hold values from 0.5 to 1.5
- master_in: float32 [8, 12288, 128], P('section', 'dp'), may hold values from -0.0546875 to 0.0546875
- master_out: float32 [8, 128, 12288], P('section', None, 'dp'), may hold values from -0.5 to 0.5
- first_in: float32 [8, 12288, 128], P('section', 'dp'), may hold values from -3 to 3
- first_out: float32 [8, 128, 12288], P('section', None, 'dp'), may hold values from -0.1 to 0.1
- second_in: float32 [8, 12288, 128], P('section', 'dp'), may hold values from 0.02 to 0.5
- second_out: float32 [8, 128, 12288], P('section', None, 'dp'), may hold values from 0.02 to 0.5
Outputs:
- section_outputs: bfloat16 [8, 4096, 12288], P('section', 'dp')
- new_master_in: float32 [8, 12288, 128], P('section', 'dp')
- new_master_out: float32 [8, 128, 12288], P('section', None, 'dp')
- new_first_in: float32 [8, 12288, 128], P('section', 'dp')
- new_first_out: float32 [8, 128, 12288], P('section', None, 'dp')
- new_second_in: float32 [8, 12288, 128], P('section', 'dp')
- new_second_out: float32 [8, 128, 12288], P('section', None, 'dp')
All inputs are finite; a program needn't handle non-finite values.
Results may differ from a plain program's by a relative error of at most 0.018.
Values may be sent and summed in bfloat16 or wider, within the bound.
No kernel may reach another device: no remote copies, remote signals or barrier semaphores. Data moves between devices by JAX's collectives and lax.ppermute only.
A program may use at most 128 MiB of HBM per device.

v0:
```python
import math

import jax
import jax.numpy as jnp
from jax import lax
from jax.sharding import PartitionSpec as P

MICRO = 4
STEP = 10


norm_eps = 1e-05
gelu_coef = 0.7978845608028654
beta_one = 0.9
beta_two = 0.95
adam_eps = 1e-08
learn_rate = 0.05
decay_rate = 0.1
clip_rms = 0.5


def passed_along(block, axis, distance):
    devices = range(lax.axis_size(axis))
    route = [(i - distance, i) for i in devices if i - distance in devices]
    return lax.ppermute(block, axis, route)


def gelu_pair(hidden_pre):
    inner_arg = gelu_coef * (hidden_pre + 0.044715 * hidden_pre * hidden_pre * hidden_pre)
    tangent = jnp.tanh(inner_arg)
    gelu_value = 0.5 * hidden_pre * (1.0 + tangent)
    gelu_slope = 0.5 * (1.0 + tangent) + 0.5 * hidden_pre * (
        1.0 - tangent * tangent
    ) * gelu_coef * (1.0 + 3.0 * 0.044715 * hidden_pre * hidden_pre)
    return (gelu_value, gelu_slope)


def contract_rows(left_arr, right_arr):
    return lax.dot_general(
        left_arr, right_arr, (((0,), (0,)), ((), ())), preferred_element_type=jnp.float32
    )


def contract_last(left_arr, right_arr):
    return lax.dot_general(
        left_arr, right_arr, (((1,), (1,)), ((), ())), preferred_element_type=jnp.float32
    )


def norm_parts(inputs, gain_row):
    wide_input = inputs.astype(jnp.float32)
    inv_rms = lax.rsqrt(jnp.mean(wide_input * wide_input, axis=-1, keepdims=True) + norm_eps)
    normed = (wide_input * inv_rms * gain_row).astype(jnp.bfloat16)
    return (wide_input, inv_rms, normed)


def layer_forward(inputs, gain_row, weight_in, weight_out):
    wide_input, inv_rms, normed = norm_parts(inputs, gain_row)
    hidden_pre = jnp.dot(normed, weight_in, preferred_element_type=jnp.float32)
    gelu_value, gelu_slope = gelu_pair(hidden_pre)
    act_low = gelu_value.astype(jnp.bfloat16)
    result = (wide_input + jnp.dot(act_low, weight_out, preferred_element_type=jnp.float32)).astype(
        jnp.bfloat16
    )
    return (result, hidden_pre)


def layer_backward(inputs, gain_row, weight_in, weight_out, hidden_pre, incoming):
    wide_input, inv_rms, normed = norm_parts(inputs, gain_row)
    gelu_value, gelu_slope = gelu_pair(hidden_pre)
    act_low = gelu_value.astype(jnp.bfloat16)
    d_act = contract_last(incoming, weight_out)
    d_pre = (d_act * gelu_slope).astype(jnp.bfloat16)
    scaled = contract_last(d_pre, weight_in) * gain_row
    d_inputs = (
        incoming.astype(jnp.float32)
        + inv_rms * scaled
        - wide_input * inv_rms**3 * jnp.mean(wide_input * scaled, axis=-1, keepdims=True)
    )
    return (d_inputs.astype(jnp.bfloat16), d_pre, act_low, normed)


def adam_update(master, first, second, grad):
    first_new = beta_one * first + (1.0 - beta_one) * grad
    second_new = beta_two * second + (1.0 - beta_two) * grad * grad
    first_hat = first_new / (1.0 - beta_one**STEP)
    second_hat = second_new / (1.0 - beta_two**STEP)
    master_new = master - learn_rate * (
        first_hat / (jnp.sqrt(second_hat) + adam_eps) + decay_rate * master
    )
    return (master_new, first_new, second_new)


def store_block(buffer, values, slot_pos, in_range):
    old_block = lax.dynamic_index_in_dim(buffer, slot_pos, 0, keepdims=False)
    return lax.dynamic_update_index_in_dim(
        buffer, jnp.where(in_range, values, old_block), slot_pos, 0
    )


def shards(
    stack_input,
    out_cotangent,
    norm_gain,
    master_in,
    master_out,
    first_in,
    first_out,
    second_in,
    second_out,
):
    num_sections = lax.axis_size("section")
    section_pos = lax.axis_index("section")
    gain_row = norm_gain[0]
    work_in, work_out = (
        lax.all_gather(master_in[0].astype(jnp.bfloat16), "dp", axis=0, tiled=True),
        lax.all_gather(master_out[0].astype(jnp.bfloat16), "dp", axis=1, tiled=True),
    )
    tok_rows = stack_input.shape[0]
    model_width = stack_input.shape[1]
    rank_width = work_in.shape[1]
    num_blocks = MICRO
    block_rows = tok_rows // num_blocks
    num_ticks = num_sections + num_blocks - 1
    input_blocks = stack_input.reshape(num_blocks, block_rows, model_width)
    cot_blocks = out_cotangent.reshape(num_blocks, block_rows, model_width)
    accumulate = False
    accumulate = True
    zero_rows = jnp.zeros((block_rows, model_width), jnp.bfloat16)
    zero_pre_rows = jnp.zeros((block_rows, rank_width), jnp.float32)

    def forward_tick(tick_num, loop_state):
        arriving, kept_inputs, kept_pre, produced = loop_state
        block_pos = tick_num - section_pos
        in_range = (block_pos >= 0) & (block_pos < num_blocks)
        slot_pos = jnp.clip(block_pos, 0, num_blocks - 1)
        first_rows = lax.dynamic_index_in_dim(input_blocks, slot_pos, 0, keepdims=False)
        current = jnp.where(section_pos == 0, first_rows, arriving)

        def forward_run_layer(operand):
            return layer_forward(operand, gain_row, work_in, work_out)

        def forward_skip_layer(operand):
            return (zero_rows, zero_pre_rows)

        result, hidden_pre = lax.cond(in_range, forward_run_layer, forward_skip_layer, current)
        kept_inputs = store_block(kept_inputs, current, slot_pos, in_range)
        kept_pre = store_block(kept_pre, hidden_pre, slot_pos, in_range)
        produced = store_block(produced, result, slot_pos, in_range)
        arriving = passed_along(result, "section", 1)
        return (arriving, kept_inputs, kept_pre, produced)

    zero_blocks = jnp.zeros((num_blocks, block_rows, model_width), jnp.bfloat16)
    zero_pre = jnp.zeros((num_blocks, block_rows, rank_width), jnp.float32)
    arriving, kept_inputs, kept_pre, produced = lax.fori_loop(
        0, num_ticks, forward_tick, (zero_rows, zero_blocks, zero_pre, zero_blocks)
    )
    zero_rank_rows = jnp.zeros((block_rows, rank_width), jnp.bfloat16)

    def backward_tick(tick_num, loop_state):
        arriving, acc_in, acc_out, kept_normed, kept_dpre, kept_act, kept_delta = loop_state
        block_pos = tick_num - (num_sections - 1 - section_pos)
        in_range = (block_pos >= 0) & (block_pos < num_blocks)
        slot_pos = jnp.clip(block_pos, 0, num_blocks - 1)
        last_rows = lax.dynamic_index_in_dim(cot_blocks, slot_pos, 0, keepdims=False)
        incoming = jnp.where(section_pos == num_sections - 1, last_rows, arriving)
        current = lax.dynamic_index_in_dim(kept_inputs, slot_pos, 0, keepdims=False)
        hidden_pre = lax.dynamic_index_in_dim(kept_pre, slot_pos, 0, keepdims=False)

        def backward_run_layer(operands):
            acc_first, acc_second = operands
            d_inputs, d_pre, act_low, normed = layer_backward(
                current, gain_row, work_in, work_out, hidden_pre, incoming
            )
            acc_first = acc_first + contract_rows(normed, d_pre)
            acc_second = acc_second + contract_rows(act_low, incoming)
            return (d_inputs, d_pre, act_low, normed, acc_first, acc_second)

        def backward_skip_layer(operands):
            acc_first, acc_second = operands
            return (zero_rows, zero_rank_rows, zero_rank_rows, zero_rows, acc_first, acc_second)

        d_inputs, d_pre, act_low, normed, acc_in, acc_out = lax.cond(
            in_range, backward_run_layer, backward_skip_layer, (acc_in, acc_out)
        )
        arriving = passed_along(d_inputs, "section", -1)
        return (arriving, acc_in, acc_out, kept_normed, kept_dpre, kept_act, kept_delta)

    acc_shape_in = (model_width, rank_width)
    acc_shape_out = (rank_width, model_width)
    keep_blocks = 1
    start_state = (
        zero_rows,
        jnp.zeros(acc_shape_in, jnp.float32),
        jnp.zeros(acc_shape_out, jnp.float32),
        jnp.zeros((keep_blocks, block_rows, model_width), jnp.bfloat16),
        jnp.zeros((keep_blocks, block_rows, rank_width), jnp.bfloat16),
        jnp.zeros((keep_blocks, block_rows, rank_width), jnp.bfloat16),
        jnp.zeros((keep_blocks, block_rows, model_width), jnp.bfloat16),
    )
    final_state = lax.fori_loop(0, num_ticks, backward_tick, start_state)
    acc_in, acc_out, kept_normed, kept_dpre, kept_act, kept_delta = final_state[1:]
    full_in, full_out = (acc_in, acc_out)
    shard_in, shard_out = (
        lax.psum_scatter(full_in, "dp", scatter_dimension=0, tiled=True),
        lax.psum_scatter(full_out, "dp", scatter_dimension=1, tiled=True),
    )
    local_sq = jnp.sum(shard_in * shard_in) + jnp.sum(shard_out * shard_out)
    total_sq = lax.psum(local_sq, ("section", "dp"))
    norm_limit = clip_rms * math.sqrt(2.0 * model_width * rank_width * num_sections)
    clip_factor = norm_limit / jnp.maximum(jnp.sqrt(total_sq), norm_limit)
    new_in, new_first_in, new_second_in = adam_update(
        master_in[0], first_in[0], second_in[0], clip_factor * shard_in
    )
    new_out, new_first_out, new_second_out = adam_update(
        master_out[0], first_out[0], second_out[0], clip_factor * shard_out
    )
    section_rows = produced.reshape(1, tok_rows, model_width)
    return (
        section_rows,
        new_in[None],
        new_out[None],
        new_first_in[None],
        new_first_out[None],
        new_second_in[None],
        new_second_out[None],
    )


def solution(mesh):
    in_specs = (
        P("dp", None),
        P("dp", None),
        P("section", None),
        P("section", "dp", None),
        P("section", None, "dp"),
        P("section", "dp", None),
        P("section", None, "dp"),
        P("section", "dp", None),
        P("section", None, "dp"),
    )
    out_specs = (
        P("section", "dp", None),
        P("section", "dp", None),
        P("section", None, "dp"),
        P("section", "dp", None),
        P("section", None, "dp"),
        P("section", "dp", None),
        P("section", None, "dp"),
    )
    return jax.shard_map(shards, mesh=mesh, in_specs=in_specs, out_specs=out_specs, check_vma=False)
```

profile of v0, /device:TPU:2, one launch (start us, length us, event | category | flops | bytes accessed | tf_op | source)
XLA Modules:
  0.0 1204.2 jit_solution(14347419688477722697)
XLA Ops:
  10.5 83.5 %all-gather.3.cloned.1.call-done = bf16[12288,128]{1,0:T(8,128)(2,1)} async-done(((bf16[384,128]{1,0:T(8,128)(2,1)}), bf16[12288,128]{1,0:T(8,128)(2,1)}) %all-gather.3.cloned.1.call-update) | async-done | bytes 3145744 | tf_op jit(solution)/shard_map/all_gather | solution.py:116
  94.0 78.3 %all-gather.5.cloned.1.call-done = bf16[128,12288]{1,0:T(8,128)(2,1)} async-done(((bf16[128,384]{1,0:T(8,128)(2,1)}), bf16[128,12288]{1,0:T(8,128)(2,1)}) %all-gather.5.cloned.1.call-update) | async-done | bytes 3145744 | tf_op jit(solution)/shard_map/all_gather | solution.py:117
  177.2 218.5 %while.39 = (s32[]{:T(128)}, bf16[32,12288]{1,0:T(8,128)(2,1)}, bf16[4,32,12288]{2,1,0:T(8,128)(2,1)}, f32[4,32,128]{2,1,0:T(8,128)S(1)}, bf16[4,32,12288]{2,1,0...) while((s32[]{:T(128)}, bf16[32,12288]{1,0:T(8,128)(2,1)}, ...), condition=%wide.region_4.5_spmd, body=%wide.region_0.4_spmd.sunk | while | flops 206479392 | bytes 34768216 | solution.py:155
  186.9 9.4 collective-permute-done
  206.0 9.4 collective-permute-done
  229.1 7.6 collective-permute-done
  250.3 7.6 collective-permute-done
  310.0 9.4 collective-permute-done
  329.1 9.4 collective-permute-done
  348.2 9.4 collective-permute-done
  367.2 9.4 collective-permute-done
  386.3 9.4 collective-permute-done
  402.8 262.1 %while.40 = (s32[]{:T(128)}, bf16[32,12288]{1,0:T(8,128)(2,1)}, f32[12288,128]{1,0:T(8,128)}, f32[128,12288]{1,0:T(8,128)}, s32[]{:T(128)}, /*index=5*/pred[]{:T...) while((s32[]{:T(128)}, bf16[32,12288]{1,0:T(8,128)(2,1)}, ...), condition=%wide.region_10.11_spmd, body=%wide.region_5.10_spmd.sunk | while | flops 413384800 | bytes 146434384 | solution.py:201
  405.7 9.8 collective-permute-done.1
  420.2 9.8 collective-permute-done.1
  434.8 9.8 collective-permute-done.1
  449.3 9.8 collective-permute-done.1
  463.9 45.8 %collective-permute-done.1 = bf16[32,12288]{1,0:T(8,128)(2,1)} collective-permute-done((bf16[32,12288]{1,0:T(8,128)(2,1)}, bf16[32,12288]{1,0:T(8,128)(2,1)}, u32[]{:S(2)}, u32[]{:S(2)}) %collective-permute-start.1) | collective-permute-done | bytes 786464 | tf_op jit(solution)/shard_map/while/body/eval_jaxpr/ppermute | solution.py:25
  509.7 14.9 %conditional.5 = (bf16[32,12288]{1,0:T(8,128)(2,1)}, f32[12288,128]{1,0:T(8,128)}, f32[128,12288]{1,0:T(8,128)}) conditional(s32[]{:T(128)} %convert_element_type.104, (f32[12288,128]{1,0:T(8,128)}, f32[128,12288]{1,0:T(8,128)}) %tuple.108, (pred[]{:T(512)}, s32[]{:T(128)}, bf16[4,32,12288]{2,1,0:T(8,128)(2,1)}, bf16[32,12288]{1,0:T(8,128)(2,1)}, ...), branch_computations={%region_6.6_spmd, %region_7.9_spmd} | conditional | flops 413384800 | bytes 143288320 | solution.py:183
  526.5 11.7 collective-permute-done.1
  538.2 14.9 %conditional.5 = (bf16[32,12288]{1,0:T(8,128)(2,1)}, f32[12288,128]{1,0:T(8,128)}, f32[128,12288]{1,0:T(8,128)}) conditional(s32[]{:T(128)} %convert_element_type.104, (f32[12288,128]{1,0:T(8,128)}, f32[128,12288]{1,0:T(8,128)}) %tuple.108, (pred[]{:T(512)}, s32[]{:T(128)}, bf16[4,32,12288]{2,1,0:T(8,128)(2,1)}, bf16[32,12288]{1,0:T(8,128)(2,1)}, ...), branch_computations={%region_6.6_spmd, %region_7.9_spmd} | conditional | flops 413384800 | bytes 143288320 | solution.py:183
  555.0 11.7 collective-permute-done.1
  566.7 14.9 %conditional.5 = (bf16[32,12288]{1,0:T(8,128)(2,1)}, f32[12288,128]{1,0:T(8,128)}, f32[128,12288]{1,0:T(8,128)}) conditional(s32[]{:T(128)} %convert_element_type.104, (f32[12288,128]{1,0:T(8,128)}, f32[128,12288]{1,0:T(8,128)}) %tuple.108, (pred[]{:T(512)}, s32[]{:T(128)}, bf16[4,32,12288]{2,1,0:T(8,128)(2,1)}, bf16[32,12288]{1,0:T(8,128)(2,1)}, ...), branch_computations={%region_6.6_spmd, %region_7.9_spmd} | conditional | flops 413384800 | bytes 143288320 | solution.py:183
  583.5 11.7 collective-permute-done.1
  595.2 14.9 %conditional.5 = (bf16[32,12288]{1,0:T(8,128)(2,1)}, f32[12288,128]{1,0:T(8,128)}, f32[128,12288]{1,0:T(8,128)}) conditional(s32[]{:T(128)} %convert_element_type.104, (f32[12288,128]{1,0:T(8,128)}, f32[128,12288]{1,0:T(8,128)}) %tuple.108, (pred[]{:T(512)}, s32[]{:T(128)}, bf16[4,32,12288]{2,1,0:T(8,128)(2,1)}, bf16[32,12288]{1,0:T(8,128)(2,1)}, ...), branch_computations={%region_6.6_spmd, %region_7.9_spmd} | conditional | flops 413384800 | bytes 143288320 | solution.py:183
  612.0 9.8 collective-permute-done.1
  622.8 17.8 %collective-permute-start.1 = (bf16[32,12288]{1,0:T(8,128)(2,1)}, bf16[32,12288]{1,0:T(8,128)(2,1)}, u32[]{:S(2)}, u32[]{:S(2)}) collective-permute-start(bf16[32,12288]{1,0:T(8,128)(2,1)} %get-tuple-element.854), channel_id=1, source_target_pairs={{32,0},{64,32},{96,64},{128,96},{160,128},{192,160},{224,192},{33,... | collective-permute-start | bytes 2359304 | tf_op jit(solution)/shard_map/while/body/eval_jaxpr/ppermute | solution.py:25
  640.5 9.8 collective-permute-done.1
  655.1 9.8 collective-permute-done.1
  665.5 224.0 %reduce-scatter.3.cloned.1.call-done = f32[384,128]{1,0:T(8,128)} async-done(((f32[12288,128]{1,0:T(8,128)}), f32[384,128]{1,0:T(8,128)}) %reduce-scatter.3.cloned.1.call-update) | async-done | bytes 196624 | tf_op jit(solution)/shard_map/reduce_scatter | solution.py:205
  891.1 225.8 %reduce-scatter.5.cloned.1.call-done = f32[128,384]{1,0:T(8,128)} async-done(((f32[128,12288]{1,0:T(8,128)}), f32[128,384]{1,0:T(8,128)}) %reduce-scatter.5.cloned.1.call-update) | async-done | bytes 196624 | tf_op jit(solution)/shard_map/reduce_scatter | solution.py:206
  1119.8 73.4 %psum.7 = f32[]{:T(128)} all-reduce(f32[]{:T(128)S(6)} %add.169), channel_id=1, replica_groups=mesh['section'=8,'dp'=32] {'section','dp'}, use_global_device_ids=true, to_apply=%region_15.16 | all-reduce | flops 1 | bytes 8 | tf_op jit(solution)/shard_map/psum | solution.py:209
  (295 shorter events, 286.4 us)
Async XLA Ops:
  7.2 86.9 %all-gather.3.cloned.1.call-start = ((), (), s32[]{:S(2)}) async-start(), calls=%async_computation.2 | async-start | bytes 3244032 | tf_op jit(solution)/shard_map/all_gather | solution.py:116
  8.8 163.5 %all-gather.5.cloned.1.call-start = ((), (), s32[]{:S(2)}) async-start(), calls=%async_computation.3 | async-start | bytes 3244032 | tf_op jit(solution)/shard_map/all_gather | solution.py:117
  10.5 879.0 %reduce-scatter.3.cloned.1.call-start = ((), (), s32[]{:S(2)}) async-start(), calls=%async_computation.4 | async-start | bytes 6488064 | tf_op jit(solution)/shard_map/reduce_scatter | solution.py:205
  182.7 13.6 %collective-permute-start = (bf16[32,12288]{1,0:T(8,128)(2,1)}, bf16[32,12288]{1,0:T(8,128)(2,1)}, u32[]{:S(2)}, u32[]{:S(2)}) collective-permute-start(bf16[32,12288]{1,0:T(8,128)(2,1)} %get-tuple-element.839), channel_id=1, source_target_pairs={{0,32},{32,64},{64,96},{96,128},{128,160},{160,192},{192,224},{1,3... | collective-permute-start | bytes 2359304 | tf_op jit(solution)/shard_map/while/body/eval_jaxpr/ppermute | solution.py:25
  201.8 13.6 %collective-permute-start = (bf16[32,12288]{1,0:T(8,128)(2,1)}, bf16[32,12288]{1,0:T(8,128)(2,1)}, u32[]{:S(2)}, u32[]{:S(2)}) collective-permute-start(bf16[32,12288]{1,0:T(8,128)(2,1)} %get-tuple-element.839), channel_id=1, source_target_pairs={{0,32},{32,64},{64,96},{96,128},{128,160},{160,192},{192,224},{1,3... | collective-permute-start | bytes 2359304 | tf_op jit(solution)/shard_map/while/body/eval_jaxpr/ppermute | solution.py:25
  223.0 13.6 %collective-permute-start = (bf16[32,12288]{1,0:T(8,128)(2,1)}, bf16[32,12288]{1,0:T(8,128)(2,1)}, u32[]{:S(2)}, u32[]{:S(2)}) collective-permute-start(bf16[32,12288]{1,0:T(8,128)(2,1)} %get-tuple-element.839), channel_id=1, source_target_pairs={{0,32},{32,64},{64,96},{96,128},{128,160},{160,192},{192,224},{1,3... | collective-permute-start | bytes 2359304 | tf_op jit(solution)/shard_map/while/body/eval_jaxpr/ppermute | solution.py:25
  244.3 13.6 %collective-permute-start = (bf16[32,12288]{1,0:T(8,128)(2,1)}, bf16[32,12288]{1,0:T(8,128)(2,1)}, u32[]{:S(2)}, u32[]{:S(2)}) collective-permute-start(bf16[32,12288]{1,0:T(8,128)(2,1)} %get-tuple-element.839), channel_id=1, source_target_pairs={{0,32},{32,64},{64,96},{96,128},{128,160},{160,192},{192,224},{1,3... | collective-permute-start | bytes 2359304 | tf_op jit(solution)/shard_map/while/body/eval_jaxpr/ppermute | solution.py:25
  265.5 13.6 %collective-permute-start = (bf16[32,12288]{1,0:T(8,128)(2,1)}, bf16[32,12288]{1,0:T(8,128)(2,1)}, u32[]{:S(2)}, u32[]{:S(2)}) collective-permute-start(bf16[32,12288]{1,0:T(8,128)(2,1)} %get-tuple-element.839), channel_id=1, source_target_pairs={{0,32},{32,64},{64,96},{96,128},{128,160},{160,192},{192,224},{1,3... | collective-permute-start | bytes 2359304 | tf_op jit(solution)/shard_map/while/body/eval_jaxpr/ppermute | solution.py:25
  286.7 13.6 %collective-permute-start = (bf16[32,12288]{1,0:T(8,128)(2,1)}, bf16[32,12288]{1,0:T(8,128)(2,1)}, u32[]{:S(2)}, u32[]{:S(2)}) collective-permute-start(bf16[32,12288]{1,0:T(8,128)(2,1)} %get-tuple-element.839), channel_id=1, source_target_pairs={{0,32},{32,64},{64,96},{96,128},{128,160},{160,192},{192,224},{1,3... | collective-permute-start | bytes 2359304 | tf_op jit(solution)/shard_map/while/body/eval_jaxpr/ppermute | solution.py:25
  305.8 13.6 %collective-permute-start = (bf16[32,12288]{1,0:T(8,128)(2,1)}, bf16[32,12288]{1,0:T(8,128)(2,1)}, u32[]{:S(2)}, u32[]{:S(2)}) collective-permute-start(bf16[32,12288]{1,0:T(8,128)(2,1)} %get-tuple-element.839), channel_id=1, source_target_pairs={{0,32},{32,64},{64,96},{96,128},{128,160},{160,192},{192,224},{1,3... | collective-permute-start | bytes 2359304 | tf_op jit(solution)/shard_map/while/body/eval_jaxpr/ppermute | solution.py:25
  324.9 13.6 %collective-permute-start = (bf16[32,12288]{1,0:T(8,128)(2,1)}, bf16[32,12288]{1,0:T(8,128)(2,1)}, u32[]{:S(2)}, u32[]{:S(2)}) collective-permute-start(bf16[32,12288]{1,0:T(8,128)(2,1)} %get-tuple-element.839), channel_id=1, source_target_pairs={{0,32},{32,64},{64,96},{96,128},{128,160},{160,192},{192,224},{1,3... | collective-permute-start | bytes 2359304 | tf_op jit(solution)/shard_map/while/body/eval_jaxpr/ppermute | solution.py:25
  344.0 13.6 %collective-permute-start = (bf16[32,12288]{1,0:T(8,128)(2,1)}, bf16[32,12288]{1,0:T(8,128)(2,1)}, u32[]{:S(2)}, u32[]{:S(2)}) collective-permute-start(bf16[32,12288]{1,0:T(8,128)(2,1)} %get-tuple-element.839), channel_id=1, source_target_pairs={{0,32},{32,64},{64,96},{96,128},{128,160},{160,192},{192,224},{1,3... | collective-permute-start | bytes 2359304 | tf_op jit(solution)/shard_map/while/body/eval_jaxpr/ppermute | solution.py:25
  363.1 13.6 %collective-permute-start = (bf16[32,12288]{1,0:T(8,128)(2,1)}, bf16[32,12288]{1,0:T(8,128)(2,1)}, u32[]{:S(2)}, u32[]{:S(2)}) collective-permute-start(bf16[32,12288]{1,0:T(8,128)(2,1)} %get-tuple-element.839), channel_id=1, source_target_pairs={{0,32},{32,64},{64,96},{96,128},{128,160},{160,192},{192,224},{1,3... | collective-permute-start | bytes 2359304 | tf_op jit(solution)/shard_map/while/body/eval_jaxpr/ppermute | solution.py:25
  382.1 13.6 %collective-permute-start = (bf16[32,12288]{1,0:T(8,128)(2,1)}, bf16[32,12288]{1,0:T(8,128)(2,1)}, u32[]{:S(2)}, u32[]{:S(2)}) collective-permute-start(bf16[32,12288]{1,0:T(8,128)(2,1)} %get-tuple-element.839), channel_id=1, source_target_pairs={{0,32},{32,64},{64,96},{96,128},{128,160},{160,192},{192,224},{1,3... | collective-permute-start | bytes 2359304 | tf_op jit(solution)/shard_map/while/body/eval_jaxpr/ppermute | solution.py:25
  403.7 11.7 collective-permute-start.1
  416.4 13.6 %collective-permute-start.1 = (bf16[32,12288]{1,0:T(8,128)(2,1)}, bf16[32,12288]{1,0:T(8,128)(2,1)}, u32[]{:S(2)}, u32[]{:S(2)}) collective-permute-start(bf16[32,12288]{1,0:T(8,128)(2,1)} %get-tuple-element.854), channel_id=1, source_target_pairs={{32,0},{64,32},{96,64},{128,96},{160,128},{192,160},{224,192},{33,... | collective-permute-start | bytes 2359304 | tf_op jit(solution)/shard_map/while/body/eval_jaxpr/ppermute | solution.py:25
  431.0 13.6 %collective-permute-start.1 = (bf16[32,12288]{1,0:T(8,128)(2,1)}, bf16[32,12288]{1,0:T(8,128)(2,1)}, u32[]{:S(2)}, u32[]{:S(2)}) collective-permute-start(bf16[32,12288]{1,0:T(8,128)(2,1)} %get-tuple-element.854), channel_id=1, source_target_pairs={{32,0},{64,32},{96,64},{128,96},{160,128},{192,160},{224,192},{33,... | collective-permute-start | bytes 2359304 | tf_op jit(solution)/shard_map/while/body/eval_jaxpr/ppermute | solution.py:25
  445.5 13.6 %collective-permute-start.1 = (bf16[32,12288]{1,0:T(8,128)(2,1)}, bf16[32,12288]{1,0:T(8,128)(2,1)}, u32[]{:S(2)}, u32[]{:S(2)}) collective-permute-start(bf16[32,12288]{1,0:T(8,128)(2,1)} %get-tuple-element.854), channel_id=1, source_target_pairs={{32,0},{64,32},{96,64},{128,96},{160,128},{192,160},{224,192},{33,... | collective-permute-start | bytes 2359304 | tf_op jit(solution)/shard_map/while/body/eval_jaxpr/ppermute | solution.py:25
  460.1 49.7 %collective-permute-start.1 = (bf16[32,12288]{1,0:T(8,128)(2,1)}, bf16[32,12288]{1,0:T(8,128)(2,1)}, u32[]{:S(2)}, u32[]{:S(2)}) collective-permute-start(bf16[32,12288]{1,0:T(8,128)(2,1)} %get-tuple-element.854), channel_id=1, source_target_pairs={{32,0},{64,32},{96,64},{128,96},{160,128},{192,160},{224,192},{33,... | collective-permute-start | bytes 2359304 | tf_op jit(solution)/shard_map/while/body/eval_jaxpr/ppermute | solution.py:25
  524.6 13.6 %collective-permute-start.1 = (bf16[32,12288]{1,0:T(8,128)(2,1)}, bf16[32,12288]{1,0:T(8,128)(2,1)}, u32[]{:S(2)}, u32[]{:S(2)}) collective-permute-start(bf16[32,12288]{1,0:T(8,128)(2,1)} %get-tuple-element.854), channel_id=1, source_target_pairs={{32,0},{64,32},{96,64},{128,96},{160,128},{192,160},{224,192},{33,... | collective-permute-start | bytes 2359304 | tf_op jit(solution)/shard_map/while/body/eval_jaxpr/ppermute | solution.py:25
  553.1 13.6 %collective-permute-start.1 = (bf16[32,12288]{1,0:T(8,128)(2,1)}, bf16[32,12288]{1,0:T(8,128)(2,1)}, u32[]{:S(2)}, u32[]{:S(2)}) collective-permute-start(bf16[32,12288]{1,0:T(8,128)(2,1)} %get-tuple-element.854), channel_id=1, source_target_pairs={{32,0},{64,32},{96,64},{128,96},{160,128},{192,160},{224,192},{33,... | collective-permute-start | bytes 2359304 | tf_op jit(solution)/shard_map/while/body/eval_jaxpr/ppermute | solution.py:25
  581.6 13.6 %collective-permute-start.1 = (bf16[32,12288]{1,0:T(8,128)(2,1)}, bf16[32,12288]{1,0:T(8,128)(2,1)}, u32[]{:S(2)}, u32[]{:S(2)}) collective-permute-start(bf16[32,12288]{1,0:T(8,128)(2,1)} %get-tuple-element.854), channel_id=1, source_target_pairs={{32,0},{64,32},{96,64},{128,96},{160,128},{192,160},{224,192},{33,... | collective-permute-start | bytes 2359304 | tf_op jit(solution)/shard_map/while/body/eval_jaxpr/ppermute | solution.py:25
  610.1 11.7 collective-permute-start.1
  622.8 27.6 %collective-permute-start.1 = (bf16[32,12288]{1,0:T(8,128)(2,1)}, bf16[32,12288]{1,0:T(8,128)(2,1)}, u32[]{:S(2)}, u32[]{:S(2)}) collective-permute-start(bf16[32,12288]{1,0:T(8,128)(2,1)} %get-tuple-element.854), channel_id=1, source_target_pairs={{32,0},{64,32},{96,64},{128,96},{160,128},{192,160},{224,192},{33,... | collective-permute-start | bytes 2359304 | tf_op jit(solution)/shard_map/while/body/eval_jaxpr/ppermute | solution.py:25
  651.3 13.6 %collective-permute-start.1 = (bf16[32,12288]{1,0:T(8,128)(2,1)}, bf16[32,12288]{1,0:T(8,128)(2,1)}, u32[]{:S(2)}, u32[]{:S(2)}) collective-permute-start(bf16[32,12288]{1,0:T(8,128)(2,1)} %get-tuple-element.854), channel_id=1, source_target_pairs={{32,0},{64,32},{96,64},{128,96},{160,128},{192,160},{224,192},{33,... | collective-permute-start | bytes 2359304 | tf_op jit(solution)/shard_map/while/body/eval_jaxpr/ppermute | solution.py:25
  664.9 452.0 %reduce-scatter.5.cloned.1.call-start = ((), (), s32[]{:S(2)}) async-start(), calls=%async_computation.5 | async-start | bytes 6488064 | tf_op jit(solution)/shard_map/reduce_scatter | solution.py:206
  664.9 529.0 %copy-start.6 = (f32[1,128,384]{2,1,0:T(8,128)S(1)}, f32[1,128,384]{2,1,0:T(8,128)}, u32[]{:S(2)}) copy-start(f32[1,128,384]{2,1,0:T(8,128)} %param.21) | copy-start | bytes 589828
  665.0 529.0 %copy-start.8 = (f32[1,128,384]{2,1,0:T(8,128)S(1)}, f32[1,128,384]{2,1,0:T(8,128)}, u32[]{:S(2)}) copy-start(f32[1,128,384]{2,1,0:T(8,128)} %param.25) | copy-start | bytes 589828
  665.0 528.9 %copy-start.9 = (f32[1,128,384]{2,1,0:T(8,128)S(1)}, f32[1,128,384]{2,1,0:T(8,128)}, u32[]{:S(2)}) copy-start(f32[1,128,384]{2,1,0:T(8,128)} %param.23) | copy-start | bytes 589828
  665.0 530.8 %copy-start.7 = (f32[1,384,128]{2,1,0:T(8,128)S(1)}, f32[1,384,128]{2,1,0:T(8,128)}, u32[]{:S(2)}) copy-start(f32[1,384,128]{2,1,0:T(8,128)} %param.20) | copy-start | bytes 589828
  665.0 530.8 %copy-start.10 = (f32[1,384,128]{2,1,0:T(8,128)S(1)}, f32[1,384,128]{2,1,0:T(8,128)}, u32[]{:S(2)}) copy-start(f32[1,384,128]{2,1,0:T(8,128)} %param.24) | copy-start | bytes 589828
  665.0 530.8 %copy-start.11 = (f32[1,384,128]{2,1,0:T(8,128)S(1)}, f32[1,384,128]{2,1,0:T(8,128)}, u32[]{:S(2)}) copy-start(f32[1,384,128]{2,1,0:T(8,128)} %param.22) | copy-start | bytes 589828
  (41 other events, 147.8 us)
Sparse Core Ops, SparseCore 0:
  11.2 82.8 all-gather.2
  97.1 75.1 all-gather.4
  665.0 224.4 reduce-scatter.2
  893.9 222.9 reduce-scatter.4
where the time goes:
time: 1210 us; the launch traced here: 1200 us
  waiting for transfers between devices  858 us (71%)
  blocking collectives  73.4 us (6%)
  local copies, waits for them, and re-layouts  72.4 us (6%)
  other arithmetic  70.6 us (6%)
  starting transfers between devices  67.5 us (6%)
  matrix products  45.9 us (4%)
  between operations  15.9 us (1%)
    ppermute x22, waiting for transfers between devices, passed_along(): return lax.ppermute(block, axis, route)  246 us
    reduce_scatter x1, waiting for transfers between devices, shards(): lax.psum_scatter(full_out, 'dp', scatter_dimension=1, tiled=True)  226 us
    reduce_scatter x1, waiting for transfers between devices, shards(): lax.psum_scatter(full_in, 'dp', scatter_dimension=0, tiled=True)  224 us
    all_gather x1, waiting for transfers between devices, shards(): lax.all_gather(master_in[0].astype(jnp.bfloat16), 'dp', axis=0, tiled=True)  83.5 us
    all_gather x1, waiting for transfers between devices, shards(): lax.all_gather(master_out[0].astype(jnp.bfloat16), 'dp', axis=1, tiled=True)  78.3 us
    psum x1, blocking collectives, shards(): total_sq = lax.psum(local_sq, ('section', 'dp'))  73.4 us
    ppermute x22, starting transfers between devices, passed_along(): return lax.ppermute(block, axis, route)  67.3 us
    dynamic_update_slice x33, other arithmetic, store_block(): lax.dynamic_update_index_in_dim(buffer, jnp.where(in_range, values, old_b...  47.6 us
  transfers between devices with their start and end apart: 26, of which 26 were waited for; matrix products, arithmetic and copies ran while one was open for 3% of the time, Pallas kernels for 0%

commit v1 on v0

v1 whole, which is shorter than its diff:
```python
import functools
import math

import jax
import jax.numpy as jnp
from jax import lax
from jax.experimental import pallas as pl
from jax.experimental.pallas import tpu as pltpu
from jax.sharding import Mesh, PartitionSpec as P

STEP = 10

norm_eps = 1e-05
gelu_coef = 0.7978845608028654
beta_one = 0.9
beta_two = 0.95
adam_eps = 1e-08
learn_rate = 0.05
decay_rate = 0.1
clip_rms = 0.5

LOW = jnp.bfloat16
WIDE = jnp.float32
PLANE = ("s", "y")
VMEM_BYTES = 48 * 1024 * 1024


def dot_nn(left, right):
    return lax.dot_general(left, right, (((1,), (0,)), ((), ())), preferred_element_type=WIDE)


def dot_nt(left, right):
    return lax.dot_general(left, right, (((1,), (1,)), ((), ())), preferred_element_type=WIDE)


def dot_tn(left, right):
    return lax.dot_general(left, right, (((0,), (0,)), ((), ())), preferred_element_type=WIDE)


def gelu_pair(hidden_pre):
    inner_arg = gelu_coef * (hidden_pre + 0.044715 * hidden_pre * hidden_pre * hidden_pre)
    tangent = jnp.tanh(inner_arg)
    gelu_value = 0.5 * hidden_pre * (1.0 + tangent)
    gelu_slope = 0.5 * (1.0 + tangent) + 0.5 * hidden_pre * (
        1.0 - tangent * tangent
    ) * gelu_coef * (1.0 + 3.0 * 0.044715 * hidden_pre * hidden_pre)
    return (gelu_value, gelu_slope)


def adam_update(master, first, second, grad):
    first_new = beta_one * first + (1.0 - beta_one) * grad
    second_new = beta_two * second + (1.0 - beta_two) * grad * grad
    first_hat = first_new / (1.0 - beta_one**STEP)
    second_hat = second_new / (1.0 - beta_two**STEP)
    master_new = master - learn_rate * (
        first_hat / (jnp.sqrt(second_hat) + adam_eps) + decay_rate * master
    )
    return (master_new, first_new, second_new)


def local_call(kernel, out_shape, operands, scratch=(), flops=0):
    specs = jax.tree.map(lambda _: pl.BlockSpec(memory_space=pltpu.VMEM), out_shape)
    moved = sum(a.size * a.dtype.itemsize for a in operands)
    moved += sum(a.size * a.dtype.itemsize for a in jax.tree.leaves(out_shape))
    return pl.pallas_call(
        kernel,
        out_shape=out_shape,
        in_specs=[pl.BlockSpec(memory_space=pltpu.VMEM)] * len(operands),
        out_specs=specs,
        scratch_shapes=list(scratch),
        compiler_params=pltpu.CompilerParams(vmem_limit_bytes=VMEM_BYTES),
        cost_estimate=pl.CostEstimate(flops=flops, bytes_accessed=moved, transcendentals=0),
    )(*operands)


def project_kernel(rank, rows_ref, weight_ref, out_ref):
    groups, both_rows, _ = rows_ref.shape
    layers = weight_ref.shape[0]
    half = both_rows // 2
    planes = out_ref.shape[0]
    piece = half // planes
    for group in range(groups):
        inputs = rows_ref[group, :half, :]
        cots = rows_ref[group, half:, :]
        for layer in range(layers):
            weight = weight_ref[layer]
            first = dot_nn(inputs, weight).astype(LOW)
            second = dot_nn(cots, weight[:, rank:]).astype(LOW)
            for plane in range(planes):
                sel = slice(plane * piece, (plane + 1) * piece)
                base = layer * 3 * rank
                out_ref[plane, group, :, base : base + 2 * rank] = first[sel]
                out_ref[plane, group, :, base + 2 * rank : base + 3 * rank] = second[sel]


def recursion_kernel(layers, rank, width, parts_ref, square_ref, cross_ref, out_ref, sums_ref):
    sources = parts_ref.shape[0]
    sums_ref[...] = parts_ref[0].astype(WIDE)

    def add_source(source, _):
        sums_ref[...] += parts_ref[source].astype(WIDE)
        return 0

    lax.fori_loop(1, sources, add_source, 0)
    rank3 = 3 * rank
    down = [sums_ref[:, k * rank3 : k * rank3 + rank] for k in range(layers)]
    up = [sums_ref[:, k * rank3 + rank : k * rank3 + 2 * rank] for k in range(layers)]
    back = [sums_ref[:, k * rank3 + 2 * rank : (k + 1) * rank3] for k in range(layers)]
    square = square_ref[:, 0:1]

    acts, pres, invs = [], [], []
    for s in range(layers):
        inv = lax.rsqrt(jnp.maximum(square, 0.0) / width + norm_eps)
        pre = inv * down[s]
        act, _ = gelu_pair(pre)
        act = act.astype(LOW)
        acts.append(act)
        pres.append(pre)
        invs.append(inv)
        out_ref[:, s * rank : (s + 1) * rank] = act
        low = s * rank
        forward = dot_nn(act, cross_ref[low : low + rank, low:])
        before = up[s]
        up[s] = before + forward[:, :rank]
        square = square + jnp.sum(act.astype(WIDE) * (before + up[s]), axis=-1, keepdims=True)
        if s + 1 < layers:
            mirrored = dot_nt(act, cross_ref[low + rank :, low : low + rank])
            for k in range(s + 1, layers):
                at = (k - s) * rank
                down[k] = down[k] + forward[:, at : at + rank]
                up[k] = up[k] + mirrored[:, at - rank : at]

    trailing = jnp.zeros_like(square)
    lane = lax.broadcasted_iota(jnp.int32, (square.shape[0], rank), 1)
    tail = jnp.zeros((square.shape[0], rank), WIDE)
    for s in reversed(range(layers)):
        _, slope = gelu_pair(pres[s])
        d_pre = (back[s] - trailing * up[s]) * slope
        coef = invs[s] * invs[s] * (1.0 / width) * jnp.sum(d_pre * pres[s], axis=-1, keepdims=True)
        moved = (invs[s] * d_pre).astype(LOW)
        out_ref[:, (layers + s) * rank : (layers + s + 1) * rank] = moved
        coef_high = coef.astype(LOW).astype(WIDE)
        tail = tail + jnp.where(lane == s, coef_high, 0.0)
        tail = tail + jnp.where(lane == s + layers, coef - coef_high, 0.0)
        if s > 0:
            low = s * rank
            gain_term = dot_nt(moved, cross_ref[:low, low : low + rank])
            scaled_act = (trailing * acts[s].astype(WIDE)).astype(LOW)
            norm_term = dot_nn(scaled_act, cross_ref[low : low + rank, :low])
            for k in range(s):
                sel = slice(k * rank, (k + 1) * rank)
                back[k] = back[k] + gain_term[:, sel] - norm_term[:, sel]
        trailing = trailing + coef
    out_ref[:, 2 * layers * rank :] = tail.astype(LOW)


def expand_kernel(
    layers, rank, rows_ref, weight_ref, coded_ref, out_ref, grad_ref, wide_ref, act_ref, moved_ref, coef_ref
):
    groups, both_rows, features = rows_ref.shape
    half = both_rows // 2
    planes = coded_ref.shape[0]
    piece = coded_ref.shape[2]
    span = layers * rank
    for group in range(groups):
        base = group * half
        wide_ref[base : base + half, :] = rows_ref[group, :half, :].astype(WIDE)
        for plane in range(planes):
            at = base + plane * piece
            act_ref[at : at + piece, :] = coded_ref[plane, group, :, :span]
            moved_ref[at : at + piece, :] = coded_ref[plane, group, :, span : 2 * span]
            coef_ref[at : at + piece, :] = coded_ref[plane, group, :, 2 * span :].astype(WIDE)

    for layer in range(layers):
        up_weight = weight_ref[layer, :, rank:]
        act = act_ref[:, layer * rank : (layer + 1) * rank]
        total = wide_ref[...] + dot_nt(act, up_weight)
        wide_ref[...] = total
        lowered = total.astype(LOW)
        for group in range(groups):
            out_ref[layer, group] = lowered[group * half : (group + 1) * half]

    for group in range(groups):
        base = group * half
        wide_ref[base : base + half, :] = rows_ref[group, half:, :].astype(WIDE)
    for layer in reversed(range(layers)):
        delta = wide_ref[...].astype(LOW)
        act = act_ref[:, layer * rank : (layer + 1) * rank]
        moved = moved_ref[:, layer * rank : (layer + 1) * rank]
        if layer > 0:
            current = out_ref[layer - 1].reshape(groups * half, features)
        else:
            current = rows_ref[:, :half, :].reshape(groups * half, features)
        grad_ref[layer, :, features:] = dot_tn(act, delta).astype(LOW)
        grad_ref[layer, :, :features] = dot_tn(moved, current).astype(LOW)
        if layer > 0:
            coef = coef_ref[:, layer : layer + 1] + coef_ref[:, layers + layer : layers + layer + 1]
            wide_ref[...] += dot_nt(moved, weight_ref[layer, :, :rank]) - coef * current.astype(WIDE)


def shards(
    stack_input,
    out_cotangent,
    norm_gain,
    master_in,
    master_out,
    first_in,
    first_out,
    second_in,
    second_out,
):
    layers, count_y, count_z = (lax.axis_size(a) for a in ("s", "y", "z"))
    pos_s, pos_y, pos_z = (lax.axis_index(a) for a in ("s", "y", "z"))
    sources = layers * count_y
    tok_rows, model_width = stack_input.shape
    features, rank = master_in.shape[1:]
    piece = tok_rows // layers
    swap = [(a * count_z + b, b * count_z + a) for a in range(layers) for b in range(count_z)]

    gain_own = lax.dynamic_slice_in_dim(norm_gain[0], (pos_y * count_z + pos_z) * features, features, 0)
    work_in = master_in[0].astype(LOW).astype(WIDE)
    gained_in = (work_in * gain_own[:, None]).astype(LOW)
    turned_out = master_out[0].astype(LOW).T
    packed = jnp.concatenate([gained_in, turned_out], axis=1)
    swapped = lax.ppermute(packed, ("s", "z"), swap)
    gain_swapped = lax.ppermute(gain_own, ("s", "z"), swap)
    weights = lax.all_gather(swapped, "z", axis=0)

    def blocks_of(rows):
        return jnp.stack(
            [
                lax.dynamic_slice_in_dim(rows, (g * count_z + pos_s) * features, features, 1)
                for g in range(count_y)
            ]
        )

    rows = jnp.concatenate([blocks_of(stack_input), blocks_of(out_cotangent)], axis=1)
    rows = lax.all_to_all(rows, "y", 0, 0, tiled=True)
    own_rows = lax.dynamic_slice_in_dim(stack_input, pos_s * piece, piece, 0).astype(WIDE)
    square = jnp.sum(own_rows * own_rows, axis=-1, keepdims=True)
    square = jnp.broadcast_to(square, (piece, 128))

    cross = lax.dot_general(
        swapped[:, rank:], weights, (((0,), (1,)), ((), ())), preferred_element_type=WIDE
    )
    later = (jnp.arange(layers) > pos_z)[None, :, None]
    cross = jnp.where(later, cross[..., :rank], cross[..., rank:]).astype(LOW)
    cut_r, cut_c = rank // layers, layers * rank // count_y
    cross = cross.reshape(layers, cut_r, count_y, cut_c).transpose(0, 2, 1, 3)
    cross = cross.reshape(sources, cut_r, cut_c)
    cross = lax.all_to_all(cross, PLANE, 0, 0, tiled=True)
    cross = jnp.sum(cross.astype(WIDE), axis=0, keepdims=True).astype(LOW)
    cross = jnp.broadcast_to(cross, (sources, cut_r, cut_c))
    cross = lax.all_to_all(cross, PLANE, 0, 0, tiled=True)
    cross = cross.reshape(layers, count_y, cut_r, cut_c).transpose(0, 2, 1, 3)
    cross = cross.reshape(rank, layers * rank)
    cross, rows, weights = lax.optimization_barrier((cross, rows, weights))
    cross = lax.all_gather(cross, "z", axis=0, tiled=True)

    parts = local_call(
        functools.partial(project_kernel, rank),
        jax.ShapeDtypeStruct((layers, count_y, piece, layers * 3 * rank), LOW),
        (rows, weights),
        flops=2 * rows.shape[0] * tok_rows * features * layers * rank * 3,
    )
    parts = parts.reshape(sources, piece, layers * 3 * rank)
    parts = lax.all_to_all(parts, PLANE, 0, 0, tiled=True)
    coded_width = 2 * layers * rank + rank
    coded = local_call(
        functools.partial(recursion_kernel, layers, rank, float(model_width)),
        jax.ShapeDtypeStruct((piece, coded_width), LOW),
        (parts, square, cross),
        scratch=[pltpu.VMEM((piece, layers * 3 * rank), WIDE)],
    )
    coded = jnp.broadcast_to(coded[None], (sources, piece, coded_width))
    coded = lax.all_to_all(coded, PLANE, 0, 0, tiled=True)
    coded = coded.reshape(layers, count_y, piece, coded_width)

    group_tokens = count_y * tok_rows
    outputs, grads = local_call(
        functools.partial(expand_kernel, layers, rank),
        (
            jax.ShapeDtypeStruct((layers, count_y, tok_rows, features), LOW),
            jax.ShapeDtypeStruct((layers, rank, 2 * features), LOW),
        ),
        (rows, weights, coded),
        scratch=[
            pltpu.VMEM((group_tokens, features), WIDE),
            pltpu.VMEM((group_tokens, layers * rank), LOW),
            pltpu.VMEM((group_tokens, layers * rank), LOW),
            pltpu.VMEM((group_tokens, rank), WIDE),
        ],
        flops=8 * group_tokens * features * layers * rank,
    )
    grads = lax.psum_scatter(grads, "z", scatter_dimension=0, tiled=True)[0]
    outputs = outputs.reshape(sources, tok_rows, features)
    outputs = lax.all_to_all(outputs, PLANE, 0, 0, tiled=True)
    outputs = outputs.reshape(layers, count_y, tok_rows, features).transpose(2, 1, 0, 3)
    section_rows = outputs.reshape(1, tok_rows, model_width)

    wide_grads = grads.astype(WIDE)
    swapped_in = wide_grads[:, :features] * gain_swapped[None, :]
    swapped_out = wide_grads[:, features:]
    local_sq = jnp.sum(swapped_in * swapped_in) + jnp.sum(swapped_out * swapped_out)
    everyone = ("s", "y", "z")
    total = jnp.broadcast_to(local_sq, (sources * count_z, 1, 128))
    total_sq = jnp.sum(lax.all_to_all(total, everyone, 0, 0, tiled=True)[:, 0, 0])
    norm_limit = clip_rms * math.sqrt(2.0 * model_width * rank * layers)
    clip_factor = norm_limit / jnp.maximum(jnp.sqrt(total_sq), norm_limit)

    own_grads = lax.ppermute(grads, ("s", "z"), swap).astype(WIDE)
    shard_in = (own_grads[:, :features] * gain_own[None, :]).T
    shard_out = own_grads[:, features:]
    new_in, new_first_in, new_second_in = adam_update(
        master_in[0], first_in[0], second_in[0], clip_factor * shard_in
    )
    new_out, new_first_out, new_second_out = adam_update(
        master_out[0], first_out[0], second_out[0], clip_factor * shard_out
    )
    return (
        section_rows,
        new_in[None],
        new_out[None],
        new_first_in[None],
        new_first_out[None],
        new_second_in[None],
        new_second_out[None],
    )


def solution(mesh):
    layers, groups = mesh.shape["section"], mesh.shape["dp"]
    fine = Mesh(mesh.devices.reshape(layers, groups // layers, layers), ("s", "y", "z"))
    split = ("y", "z")
    by_rows = P("s", split, None)
    by_cols = P("s", None, split)
    in_specs = (
        P(split, None),
        P(split, None),
        P("s", None),
        by_rows,
        by_cols,
        by_rows,
        by_cols,
        by_rows,
        by_cols,
    )
    out_specs = (by_rows, by_rows, by_cols, by_rows, by_cols, by_rows, by_cols)
    return jax.shard_map(shards, mesh=fine, in_specs=in_specs, out_specs=out_specs, check_vma=False)
```

time: 1210 us -> 309 us (0.26)
  waiting for transfers between devices: 858 us -> 155 us
  other arithmetic: 70.6 us -> 7.88 us
  matrix products: 45.9 us -> 0.44 us
  local copies, waits for them, and re-layouts: 72.4 us -> 28 us
  blocking collectives: 73.4 us -> 35.9 us
  starting transfers between devices: 67.5 us -> 49.4 us
  Pallas kernels: 0 us -> 13.6 us
    reduce_scatter x2 -> x1, waiting for transfers between devices: 450 us -> 28.3 us  [shards(): grads = lax.psum_scatter(grads, 'z', scatter_dimension=0, tiled=True)[0]]
    ppermute x22 -> x3, waiting for transfers between devices: 246 us -> 17.4 us  [the longest x1 14.6 us: shards(): swapped = lax.ppermute(packed, ('s', 'z'), swap)]
    all_gather x2, waiting for transfers between devices: 162 us -> 42 us  [the longest x1 42 us: shards(): weights = lax.all_gather(swapped, 'z', axis=0)]
    psum x1 -> x0, blocking collectives: 73.4 us -> none  [shards(): total_sq = lax.psum(local_sq, ('section', 'dp'))]
    all_to_all x0 -> x6, waiting for transfers between devices: none -> 67.5 us  [the longest x1 37.4 us: shards(): parts = lax.all_to_all(parts, PLANE, 0, 0, tiled=True)]
    ppermute x22 -> x3, starting transfers between devices: 67.3 us -> 12.3 us  [the longest x1 5.15 us: shards(): swapped = lax.ppermute(packed, ('s', 'z'), swap)]
    dynamic_update_slice x33 -> x0, other arithmetic: 47.6 us -> none  [store_block(): lax.dynamic_update_index_in_dim(buffer, jnp.where(in_range, values, old_b...]
    dot_general x24 -> x1, matrix products: 45.9 us -> 0.44 us  [shards(): lax.dot_general(swapped[:, rank:], weights, (((0,), (1,)), ((), ())), pre...]
  transfers between devices with their start and end apart: 26 -> 12, of which waited for: 26 -> 9; matrix products, arithmetic and copies ran while one was open for 3% -> 6% of each run, Pallas kernels for 0% -> 1%
where the time goes in v1:
time: 309 us; the launch traced here: 307 us
  waiting for transfers between devices  155 us (50%)
  starting transfers between devices  49.4 us (16%)
  blocking collectives  35.9 us (12%)
  local copies, waits for them, and re-layouts  28 us (9%)
  between operations  16.1 us (5%)
  Pallas kernels  13.6 us (4%)
  other arithmetic  7.88 us (3%)
    all_gather x1, waiting for transfers between devices, shards(): weights = lax.all_gather(swapped, 'z', axis=0)  42 us
    all_to_all x1, waiting for transfers between devices, shards(): parts = lax.all_to_all(parts, PLANE, 0, 0, tiled=True)  37.4 us
    all_to_all x1, blocking collectives, shards(): coded = lax.all_to_all(coded, PLANE, 0, 0, tiled=True)  35.9 us
    reduce_scatter x1, waiting for transfers between devices, shards(): grads = lax.psum_scatter(grads, 'z', scatter_dimension=0, tiled=True)[0]  28.3 us
    ppermute x1, waiting for transfers between devices, shards(): swapped = lax.ppermute(packed, ('s', 'z'), swap)  14.6 us
    pallas_call x3, Pallas kernels, local_call(): pl.pallas_call(kernel, out_shape=out_shape, in_specs=[pl.BlockSpec(memory...  13.6 us
    all_to_all x2, waiting for transfers between devices, shards(): cross = lax.all_to_all(cross, PLANE, 0, 0, tiled=True)  13.5 us
    unnamed x29, local copies, waits for them, and re-layouts  12.9 us
  transfers between devices with their start and end apart: 12, of which 9 were waited for; matrix products, arithmetic and copies ran while one was open for 6% of the time, Pallas kernels for 1%

profile of v1, /device:TPU:2, one launch (start us, length us, event | category | flops | bytes accessed | tf_op | source)
XLA Modules:
  0.0 306.7 jit_solution(18258303062125682545)
XLA Ops:
  9.3 5.2 %collective-permute-start = (bf16[384,256]{0,1:T(8,128)(2,1)S(1)}, bf16[384,256]{0,1:T(8,128)(2,1)S(1)}, u32[]{:S(2)}, u32[]{:S(2)}) collective-permute-start(bf16[384,256]{0,1:T(8,128)(2,1)S(1)} %pad_maximum_fusion), channel_id=1, source_target_pairs={{0,0},{1,32},{2,64},{3,96},{4,128},{5,160},{6,192},{7,224},{32,1},... | collective-permute-start | bytes 589832 | tf_op jit(solution)/shard_map/ppermute | solution.py:225
  14.5 14.6 %collective-permute-done = bf16[384,256]{0,1:T(8,128)(2,1)S(1)} collective-permute-done((bf16[384,256]{0,1:T(8,128)(2,1)S(1)}, bf16[384,256]{0,1:T(8,128)(2,1)S(1)}, u32[]{:S(2)}, u32[]{:S(2)}) %collective-permute-start) | collective-permute-done | bytes 196640 | tf_op jit(solution)/shard_map/ppermute | solution.py:225
  29.8 42.0 %all-gather.6.cloned.1.call-done = bf16[3072,256]{0,1:T(8,128)(2,1)} async-done(((bf16[384,256]{0,1:T(8,128)(2,1)}), bf16[3072,256]{0,1:T(8,128)(2,1)}) %all-gather.6.cloned.1.call-update) | async-done | bytes 1572880 | tf_op jit(solution)/shard_map/all_gather | solution.py:227
  71.8 1.7 copy.47
  75.2 7.4 %all-to-all-start = ((bf16[32,16,256]{2,1,0:T(8,128)(2,1)}), bf16[32,16,256]{2,1,0:T(8,128)(2,1)S(1)}, u32[]{:S(2)}, u32[]{:S(2)}) async-start(bf16[32,16,256]{2,1,0:T(8,128)(2,1)} %bitcast.6), calls=%async_computation | async-start | bytes 524288 | tf_op jit(solution)/shard_map/all_to_all | solution.py:251
  82.6 7.9 %all-to-all-done = bf16[32,16,256]{2,1,0:T(8,128)(2,1)S(1)} async-done(((bf16[32,16,256]{2,1,0:T(8,128)(2,1)}), bf16[32,16,256]{2,1,0:T(8,128)(2,1)S(1)}, u32[]{:S(2)}, u32[]{:S(2)}) %all-to-all-start) | async-done | bytes 262176 | tf_op jit(solution)/shard_map/all_to_all | solution.py:251
  91.3 5.1 %all-to-all-start.1 = ((bf16[32,16,256]{2,1,0:T(8,128)(2,1)}), bf16[32,16,256]{2,1,0:T(8,128)(2,1)S(1)}, u32[]{:S(2)}, u32[]{:S(2)}) async-start(bf16[32,16,256]{2,1,0:T(8,128)(2,1)} %broadcast_in_dim.52), calls=%async_computation.1 | async-start | bytes 524288 | tf_op jit(solution)/shard_map/all_to_all | solution.py:254
  96.4 1.3 dynamic-slice_bitcast_fusion.3
  98.6 5.7 %all-to-all-done.1 = bf16[32,16,256]{2,1,0:T(8,128)(2,1)S(1)} async-done(((bf16[32,16,256]{2,1,0:T(8,128)(2,1)}), bf16[32,16,256]{2,1,0:T(8,128)(2,1)S(1)}, u32[]{:S(2)}, u32[]{:S(2)}) %all-to-all-start.1) | async-done | bytes 262176 | tf_op jit(solution)/shard_map/all_to_all | solution.py:254
  104.3 3.5 %all-to-all-start.2 = ((bf16[4,256,384]{2,1,0:T(8,128)(2,1)}), bf16[4,256,384]{2,1,0:T(8,128)(2,1)S(1)}, u32[]{:S(2)}, u32[]{:S(2)}) async-start(bf16[4,256,384]{2,1,0:T(8,128)(2,1)} %maximum_maximum_fusion), calls=%async_computation.2 | async-start | bytes 1572864 | tf_op jit(solution)/shard_map/all_to_all | solution.py:238
  108.8 11.8 %all-to-all-done.2.rows_ref = bf16[4,256,384]{2,1,0:T(8,128)(2,1)S(1)} async-done(((bf16[4,256,384]{2,1,0:T(8,128)(2,1)}), bf16[4,256,384]{2,1,0:T(8,128)(2,1)S(1)}, u32[]{:S(2)}, u32[]{:S(2)}) %all-to-all-start.2) | async-done | bytes 786464 | tf_op jit(solution)/shard_map/all_to_all | solution.py:238
  120.6 2.3 shard_map.144
  122.9 1.7 copy-done.1
  124.6 5.8 %all-to-all-start.3 = ((bf16[32,16,3072]{2,1,0:T(8,128)(2,1)}), bf16[32,16,3072]{2,1,0:T(8,128)(2,1)}, u32[]{:S(2)}, u32[]{:S(2)}) async-start(bf16[32,16,3072]{2,1,0:T(8,128)(2,1)} %bitcast.123), calls=%async_computation.3 | async-start | bytes 6291456 | tf_op jit(solution)/shard_map/all_to_all | solution.py:267
  130.4 1.2 multiply_reduce_fusion
  131.6 37.4 %all-to-all-done.3.parts_ref = bf16[32,16,3072]{2,1,0:T(8,128)(2,1)} async-done(((bf16[32,16,3072]{2,1,0:T(8,128)(2,1)}), bf16[32,16,3072]{2,1,0:T(8,128)(2,1)}, u32[]{:S(2)}, u32[]{:S(2)}) %all-to-all-start.3) | async-done | bytes 3145760 | tf_op jit(solution)/shard_map/all_to_all | solution.py:267
  169.1 1.6 copy-done.2
  170.7 6.0 %shard_map.145 = bf16[16,2176]{1,0:T(8,128)(2,1)S(1)} custom-call(bf16[32,16,3072]{2,1,0:T(8,128)(2,1)} %all-to-all-done.3.parts_ref, f32[16,128]{1,0:T(8,128)S(1)} %broadcast_in_dim.53.square_ref, bf16[1024,1024]{1,0:T(8,128)(2,1)S(1)} %copy-done.2), custom_call_target="tpu_custom_call" | custom-call | bytes 5320704 | tf_op jit(solution)/shard_map/pallas_call | solution.py:65
  176.8 35.9 %all_to_all.35 = bf16[32,16,2176]{2,1,0:T(8,128)(2,1)S(1)} all-to-all(bf16[32,16,2176]{2,1,0:T(8,128)(2,1)S(1)} %broadcast_in_dim.54), channel_id=1, replica_groups=mesh['s'=8,'y'=4,'z'=8] {'s','y'}, dimensions={0} | all-to-all | bytes 4456448 | tf_op jit(solution)/shard_map/all_to_all | solution.py:276
  212.7 5.4 %shard_map.146 = (bf16[8,4,128,384]{3,2,1,0:T(8,128)(2,1)}, bf16[8,128,768]{2,1,0:T(8,128)(2,1)S(1)}) custom-call(bf16[4,256,384]{2,1,0:T(8,128)(2,1)S(1)} %all-to-all-done.2.rows_ref, bf16[8,384,256]{2,1,0:T(8,128)(2,1)S(1)} %bitcast.122, bf16[8,4,16,2176]{3,2,1,0:T(8,128)(2,1)S(1)} %bitcast.124), custom_call_target="tpu_custom_call" | custom-call | flops 1610612736 | bytes 9306112 | tf_op jit(solution)/shard_map/pallas_call | solution.py:65
  218.1 1.2 copy-done.3
  219.3 5.6 %all-to-all-start.5 = ((bf16[32,128,384]{2,1,0:T(8,128)(2,1)}), bf16[32,128,384]{2,1,0:T(8,128)(2,1)S(1)}, u32[]{:S(2)}, u32[]{:S(2)}) async-start(bf16[32,128,384]{2,1,0:T(8,128)(2,1)} %bitcast.127), calls=%async_computation.5 | async-start | bytes 6291456 | tf_op jit(solution)/shard_map/all_to_all | solution.py:297
  224.9 2.5 collective-permute-start.1
  227.4 28.3 %reduce-scatter.2.cloned.1.call-done = bf16[1,128,768]{2,1,0:T(8,128)(2,1)} async-done(((bf16[8,128,768]{2,1,0:T(8,128)(2,1)}), bf16[1,128,768]{2,1,0:T(8,128)(2,1)}) %reduce-scatter.2.cloned.1.call-update) | async-done | bytes 196624 | tf_op jit(solution)/shard_map/reduce_scatter | solution.py:295
  258.7 4.8 %all-to-all-done.5 = bf16[32,128,384]{2,1,0:T(8,128)(2,1)S(1)} async-done(((bf16[32,128,384]{2,1,0:T(8,128)(2,1)}), bf16[32,128,384]{2,1,0:T(8,128)(2,1)S(1)}, u32[]{:S(2)}, u32[]{:S(2)}) %all-to-all-start.5) | async-done | bytes 3145760 | tf_op jit(solution)/shard_map/all_to_all | solution.py:297
  264.2 9.7 %all-to-all-start.6 = ((f32[256,1,128]{2,1,0:T(1,128)}), f32[256,1,128]{2,1,0:T(1,128)S(1)}, u32[]{:S(2)}, u32[]{:S(2)}) async-start(f32[256,1,128]{2,1,0:T(1,128)} %broadcast_in_dim.55), calls=%async_computation.7 | async-start | bytes 262144 | tf_op jit(solution)/shard_map/all_to_all | solution.py:307
  273.8 4.7 %collective-permute-start.2 = (bf16[128,768]{1,0:T(8,128)(2,1)}, bf16[128,768]{1,0:T(8,128)(2,1)}, u32[]{:S(2)}, u32[]{:S(2)}) collective-permute-start(bf16[128,768]{1,0:T(8,128)(2,1)} %bitcast.132), channel_id=1, source_target_pairs={{0,0},{1,32},{2,64},{3,96},{4,128},{5,160},{6,192},{7,224},{32,1},... | collective-permute-start | bytes 589832 | tf_op jit(solution)/shard_map/ppermute | solution.py:311
  278.5 1.7 copy.52
  280.2 1.7 copy.54
  282.0 3.5 %copy.61 = bf16[8,4,128,384]{3,0,1,2:T(8,128)(2,1)} copy(bf16[8,4,128,384]{3,2,1,0:T(8,128)(2,1)S(1)} %bitcast.125) | data formatting | bytes 6291456 | tf_op jit(solution)/shard_map/reshape | solution.py:298
  285.5 5.7 %reshape.72 = bf16[1,128,12288]{2,1,0:T(8,128)(2,1)} reshape(bf16[128,4,8,384]{3,2,1,0:T(8,128)(2,1)} %bitcast.126) | data formatting | bytes 6291456 | tf_op jit(solution)/shard_map/reshape | solution.py:299
  291.2 2.8 collective-permute-done.2
  (56 shorter events, 15.2 us)
Async XLA Ops:
  7.2 2.1 copy-start
  7.2 64.7 %all-gather.6.cloned.1.call-start = ((), (), s32[]{:S(2)}) async-start(), calls=%async_computation.10 | async-start | bytes 1769472 | tf_op jit(solution)/shard_map/all_gather | solution.py:227
  9.3 19.8 %collective-permute-start = (bf16[384,256]{0,1:T(8,128)(2,1)S(1)}, bf16[384,256]{0,1:T(8,128)(2,1)S(1)}, u32[]{:S(2)}, u32[]{:S(2)}) collective-permute-start(bf16[384,256]{0,1:T(8,128)(2,1)S(1)} %pad_maximum_fusion), channel_id=1, source_target_pairs={{0,0},{1,32},{2,64},{3,96},{4,128},{5,160},{6,192},{7,224},{32,1},... | collective-permute-start | bytes 589832 | tf_op jit(solution)/shard_map/ppermute | solution.py:225
  29.1 0.7 copy-start.7
  29.8 43.7 %copy-start.8 = (bf16[384,256]{0,1:T(8,128)(2,1)S(1)}, bf16[384,256]{0,1:T(8,128)(2,1)}, u32[]{:S(2)}) copy-start(bf16[384,256]{0,1:T(8,128)(2,1)} %copy-done.7) | copy-start | bytes 589828
  75.2 15.3 %all-to-all-start = ((bf16[32,16,256]{2,1,0:T(8,128)(2,1)}), bf16[32,16,256]{2,1,0:T(8,128)(2,1)S(1)}, u32[]{:S(2)}, u32[]{:S(2)}) async-start(bf16[32,16,256]{2,1,0:T(8,128)(2,1)} %bitcast.6), calls=%async_computation | async-start | bytes 524288 | tf_op jit(solution)/shard_map/all_to_all | solution.py:251
  91.3 13.0 %all-to-all-start.1 = ((bf16[32,16,256]{2,1,0:T(8,128)(2,1)}), bf16[32,16,256]{2,1,0:T(8,128)(2,1)S(1)}, u32[]{:S(2)}, u32[]{:S(2)}) async-start(bf16[32,16,256]{2,1,0:T(8,128)(2,1)} %broadcast_in_dim.52), calls=%async_computation.1 | async-start | bytes 524288 | tf_op jit(solution)/shard_map/all_to_all | solution.py:254
  104.3 16.3 %all-to-all-start.2 = ((bf16[4,256,384]{2,1,0:T(8,128)(2,1)}), bf16[4,256,384]{2,1,0:T(8,128)(2,1)S(1)}, u32[]{:S(2)}, u32[]{:S(2)}) async-start(bf16[4,256,384]{2,1,0:T(8,128)(2,1)} %maximum_maximum_fusion), calls=%async_computation.2 | async-start | bytes 1572864 | tf_op jit(solution)/shard_map/all_to_all | solution.py:238
  107.8 61.2 %all-gather.4.cloned.1.call-start = ((), (), s32[]{:S(2)}) async-start(), calls=%async_computation.8 | async-start | bytes 2359296 | tf_op jit(solution)/shard_map/all_gather | solution.py:258
  122.9 1.7 copy-start.1
  124.6 44.4 %all-to-all-start.3 = ((bf16[32,16,3072]{2,1,0:T(8,128)(2,1)}), bf16[32,16,3072]{2,1,0:T(8,128)(2,1)}, u32[]{:S(2)}, u32[]{:S(2)}) async-start(bf16[32,16,3072]{2,1,0:T(8,128)(2,1)} %bitcast.123), calls=%async_computation.3 | async-start | bytes 6291456 | tf_op jit(solution)/shard_map/all_to_all | solution.py:267
  130.4 125.4 %reduce-scatter.2.cloned.1.call-start = ((), (), s32[]{:S(2)}) async-start(), calls=%async_computation.9 | async-start | bytes 1769472 | tf_op jit(solution)/shard_map/reduce_scatter | solution.py:295
  169.1 1.6 copy-start.2
  218.1 1.2 copy-start.3
  219.3 44.1 %all-to-all-start.5 = ((bf16[32,128,384]{2,1,0:T(8,128)(2,1)}), bf16[32,128,384]{2,1,0:T(8,128)(2,1)S(1)}, u32[]{:S(2)}, u32[]{:S(2)}) async-start(bf16[32,128,384]{2,1,0:T(8,128)(2,1)} %bitcast.127), calls=%async_computation.5 | async-start | bytes 6291456 | tf_op jit(solution)/shard_map/all_to_all | solution.py:297
  224.9 31.8 %collective-permute-start.1 = (f32[384]{0:T(512)S(1)}, f32[384]{0:T(512)S(1)}, u32[]{:S(2)}, u32[]{:S(2)}) collective-permute-start(f32[384]{0:T(512)S(1)} %fusion.20), channel_id=1, source_target_pairs={{0,0},{1,32},{2,64},{3,96},{4,128},{5,160},{6,192},{7,224},{32,1},... | collective-permute-start | bytes 4616 | tf_op jit(solution)/shard_map/ppermute | solution.py:226
  264.2 30.8 %all-to-all-start.6 = ((f32[256,1,128]{2,1,0:T(1,128)}), f32[256,1,128]{2,1,0:T(1,128)S(1)}, u32[]{:S(2)}, u32[]{:S(2)}) async-start(f32[256,1,128]{2,1,0:T(1,128)} %broadcast_in_dim.55), calls=%async_computation.7 | async-start | bytes 262144 | tf_op jit(solution)/shard_map/all_to_all | solution.py:307
  273.8 20.1 %collective-permute-start.2 = (bf16[128,768]{1,0:T(8,128)(2,1)}, bf16[128,768]{1,0:T(8,128)(2,1)}, u32[]{:S(2)}, u32[]{:S(2)}) collective-permute-start(bf16[128,768]{1,0:T(8,128)(2,1)} %bitcast.132), channel_id=1, source_target_pairs={{0,0},{1,32},{2,64},{3,96},{4,128},{5,160},{6,192},{7,224},{32,1},... | collective-permute-start | bytes 589832 | tf_op jit(solution)/shard_map/ppermute | solution.py:311
  285.5 11.1 %copy-start.5 = (f32[1,384,128]{1,2,0:T(8,128)S(1)}, f32[1,384,128]{1,2,0:T(8,128)}, u32[]{:S(2)}) copy-start(f32[1,384,128]{1,2,0:T(8,128)} %copy.52) | copy-start | bytes 589828
  285.5 11.1 %copy-start.6 = (f32[1,384,128]{1,2,0:T(8,128)S(1)}, f32[1,384,128]{1,2,0:T(8,128)}, u32[]{:S(2)}) copy-start(f32[1,384,128]{1,2,0:T(8,128)} %copy.54) | copy-start | bytes 589828
  291.2 8.0 %copy-start.4 = (f32[1,128,384]{2,1,0:T(8,128)S(1)}, f32[1,128,384]{2,1,0:T(8,128)}, u32[]{:S(2)}) copy-start(f32[1,128,384]{2,1,0:T(8,128)} %param.13) | copy-start | bytes 589828
  291.2 8.0 %copy-start.9 = (f32[1,128,384]{2,1,0:T(8,128)S(1)}, f32[1,128,384]{2,1,0:T(8,128)}, u32[]{:S(2)}) copy-start(f32[1,128,384]{2,1,0:T(8,128)} %param.17) | copy-start | bytes 589828
  291.2 8.0 %copy-start.10 = (f32[1,128,384]{2,1,0:T(8,128)S(1)}, f32[1,128,384]{2,1,0:T(8,128)}, u32[]{:S(2)}) copy-start(f32[1,128,384]{2,1,0:T(8,128)} %param.15) | copy-start | bytes 589828
Sparse Core Ops, SparseCore 0:
  29.9 41.8 all-gather.5
  120.8 36.8 all-gather.3
  219.4 36.2 reduce-scatter.1

commit v2 on v1

v2 whole, which is shorter than its diff:
```python
import functools
import math

import jax
import jax.numpy as jnp
from jax import lax
from jax.experimental import pallas as pl
from jax.experimental.pallas import tpu as pltpu
from jax.sharding import Mesh, PartitionSpec as P

STEP = 10

norm_eps = 1e-05
gelu_coef = 0.7978845608028654
beta_one = 0.9
beta_two = 0.95
adam_eps = 1e-08
learn_rate = 0.05
decay_rate = 0.1
clip_rms = 0.5

LOW = jnp.bfloat16
WIDE = jnp.float32
SECTION = ("x", "c")
PLANE = ("x", "c", "y")
EVERYONE = ("x", "c", "y", "z")
SHIFTS = (0, 1, -1, 2)
VMEM_BYTES = 48 * 1024 * 1024


def dot_nn(left, right):
    return lax.dot_general(left, right, (((1,), (0,)), ((), ())), preferred_element_type=WIDE)


def dot_nt(left, right):
    return lax.dot_general(left, right, (((1,), (1,)), ((), ())), preferred_element_type=WIDE)


def dot_tn(left, right):
    return lax.dot_general(left, right, (((0,), (0,)), ((), ())), preferred_element_type=WIDE)


def gelu_pair(hidden_pre):
    inner_arg = gelu_coef * (hidden_pre + 0.044715 * hidden_pre * hidden_pre * hidden_pre)
    tangent = jnp.tanh(inner_arg)
    gelu_value = 0.5 * hidden_pre * (1.0 + tangent)
    gelu_slope = 0.5 * (1.0 + tangent) + 0.5 * hidden_pre * (
        1.0 - tangent * tangent
    ) * gelu_coef * (1.0 + 3.0 * 0.044715 * hidden_pre * hidden_pre)
    return (gelu_value, gelu_slope)


def adam_update(master, first, second, grad):
    first_new = beta_one * first + (1.0 - beta_one) * grad
    second_new = beta_two * second + (1.0 - beta_two) * grad * grad
    first_hat = first_new / (1.0 - beta_one**STEP)
    second_hat = second_new / (1.0 - beta_two**STEP)
    master_new = master - learn_rate * (
        first_hat / (jnp.sqrt(second_hat) + adam_eps) + decay_rate * master
    )
    return (master_new, first_new, second_new)


def local_call(kernel, out_shape, operands, scalars=None, scratch=(), flops=0):
    specs = jax.tree.map(lambda _: pl.BlockSpec(memory_space=pltpu.VMEM), out_shape)
    moved = sum(a.size * a.dtype.itemsize for a in operands)
    moved += sum(a.size * a.dtype.itemsize for a in jax.tree.leaves(out_shape))
    in_specs = [pl.BlockSpec(memory_space=pltpu.VMEM)] * len(operands)
    if scalars is not None:
        operands = (scalars,) + tuple(operands)
        in_specs = [pl.BlockSpec(memory_space=pltpu.SMEM)] + in_specs
    return pl.pallas_call(
        kernel,
        out_shape=out_shape,
        in_specs=in_specs,
        out_specs=specs,
        scratch_shapes=list(scratch),
        compiler_params=pltpu.CompilerParams(vmem_limit_bytes=VMEM_BYTES),
        cost_estimate=pl.CostEstimate(flops=flops, bytes_accessed=moved, transcendentals=0),
    )(*operands)


def shifted(block, axis, distance):
    size = lax.axis_size(axis)
    return lax.ppermute(block, axis, [(i, (i + distance) % size) for i in range(size)])


def gather_line(block, axis):
    return jnp.stack([block] + [shifted(block, axis, d) for d in SHIFTS[1:]])


def pack_kernel(gain_ref, in_ref, out_ref, pack_ref):
    features, rank = in_ref.shape[1:]
    gain = jnp.broadcast_to(gain_ref[...], (rank, features)).T
    work_in = in_ref[0].astype(LOW).astype(WIDE)
    pack_ref[:, :rank] = (work_in * gain).astype(LOW)
    pack_ref[:, rank:] = out_ref[0].T.astype(LOW)


def project_kernel(rank, place_ref, rows_ref, weight_ref, keep_ref, send_ref):
    groups, both_rows, _ = rows_ref.shape
    layers = weight_ref.shape[0]
    half = both_rows // 2
    columns = keep_ref.shape[0]
    piece = half // (2 * columns)
    core, section = place_ref[0], place_ref[1]
    for layer in range(layers):
        weight = weight_ref[lax.rem(section + layer, layers)]
        base = layer * 3 * rank
        for group in range(groups):
            first = dot_nn(rows_ref[group, :half, :], weight).astype(LOW)
            second = dot_nn(rows_ref[group, half:, :], weight[:, rank:]).astype(LOW)
            for column in range(columns):
                low = 2 * column * piece
                even, odd = slice(low, low + piece), slice(low + piece, low + 2 * piece)
                for value, at, width in ((first, base, 2 * rank), (second, base + 2 * rank, rank)):
                    lanes = slice(at, at + width)
                    keep_ref[column, group, :, lanes] = jnp.where(core == 0, value[even], value[odd])
                    send_ref[column, group, :, lanes] = jnp.where(core == 0, value[odd], value[even])


def recursion_kernel(
    layers, rank, width, place_ref, parts_ref, square_ref, near_ref, far_ref, out_ref, sums_ref, cross_ref
):
    core, column = place_ref[0], place_ref[2]
    count = len(SHIFTS)
    for slot, distance in enumerate(SHIFTS):
        owner = lax.rem(column - distance + count, count)
        for piece_ref, from_core in ((near_ref, core), (far_ref, 1 - core)):
            start = pl.multiple_of((2 * owner + from_core) * rank, rank)
            cross_ref[pl.ds(start, rank), :] = piece_ref[slot]

    total = parts_ref[0].astype(WIDE)
    for source in range(1, parts_ref.shape[0]):
        total = total + parts_ref[source].astype(WIDE)
    sums_ref[...] = total
    rank3 = 3 * rank
    down = [sums_ref[:, k * rank3 : k * rank3 + rank] for k in range(layers)]
    up = [sums_ref[:, k * rank3 + rank : k * rank3 + 2 * rank] for k in range(layers)]
    back = [sums_ref[:, k * rank3 + 2 * rank : (k + 1) * rank3] for k in range(layers)]
    square = square_ref[:, 0:1]

    acts, pres, invs = [], [], []
    for s in range(layers):
        inv = lax.rsqrt(jnp.maximum(square, 0.0) / width + norm_eps)
        pre = inv * down[s]
        act, _ = gelu_pair(pre)
        act = act.astype(LOW)
        acts.append(act)
        pres.append(pre)
        invs.append(inv)
        out_ref[:, s * rank : (s + 1) * rank] = act
        low = s * rank
        forward = dot_nn(act, cross_ref[low : low + rank, low:])
        before = up[s]
        up[s] = before + forward[:, :rank]
        square = square + jnp.sum(act.astype(WIDE) * (before + up[s]), axis=-1, keepdims=True)
        if s + 1 < layers:
            mirrored = dot_nt(act, cross_ref[low + rank :, low : low + rank])
            for k in range(s + 1, layers):
                at = (k - s) * rank
                down[k] = down[k] + forward[:, at : at + rank]
                up[k] = up[k] + mirrored[:, at - rank : at]

    trailing = jnp.zeros_like(square)
    lane = lax.broadcasted_iota(jnp.int32, (square.shape[0], rank), 1)
    tail = jnp.zeros((square.shape[0], rank), WIDE)
    for s in reversed(range(layers)):
        _, slope = gelu_pair(pres[s])
        d_pre = (back[s] - trailing * up[s]) * slope
        coef = invs[s] * invs[s] * (1.0 / width) * jnp.sum(d_pre * pres[s], axis=-1, keepdims=True)
        moved = (invs[s] * d_pre).astype(LOW)
        out_ref[:, (layers + s) * rank : (layers + s + 1) * rank] = moved
        coef_high = coef.astype(LOW).astype(WIDE)
        tail = tail + jnp.where(lane == s, coef_high, 0.0)
        tail = tail + jnp.where(lane == s + layers, coef - coef_high, 0.0)
        if s > 0:
            low = s * rank
            gain_term = dot_nt(moved, cross_ref[:low, low : low + rank])
            scaled_act = (trailing * acts[s].astype(WIDE)).astype(LOW)
            norm_term = dot_nn(scaled_act, cross_ref[low : low + rank, :low])
            for k in range(s):
                sel = slice(k * rank, (k + 1) * rank)
                back[k] = back[k] + gain_term[:, sel] - norm_term[:, sel]
        trailing = trailing + coef
    out_ref[:, 2 * layers * rank :] = tail.astype(LOW)


def expand_kernel(
    layers,
    rank,
    place_ref,
    rows_ref,
    weight_ref,
    near_ref,
    far_ref,
    out_ref,
    grad_ref,
    wide_ref,
    act_ref,
    moved_ref,
    coef_ref,
):
    groups, both_rows, features = rows_ref.shape
    half = both_rows // 2
    piece = near_ref.shape[2]
    span = layers * rank
    core, section, column, line = (place_ref[i] for i in range(4))
    count = len(SHIFTS)
    for group in range(groups):
        base = group * half
        wide_ref[base : base + half, :] = rows_ref[group, :half, :].astype(WIDE)
    for slot_y, step_y in enumerate(SHIFTS):
        group = lax.rem(line - step_y + count, count)
        for slot_x, step_x in enumerate(SHIFTS):
            owner = lax.rem(column - step_x + count, count)
            for coded_ref, from_core in ((near_ref, core), (far_ref, 1 - core)):
                at = pl.multiple_of(group * half + (2 * owner + from_core) * piece, piece)
                dest = pl.ds(at, piece)
                act_ref[dest, :] = coded_ref[slot_y, slot_x, :, :span]
                moved_ref[dest, :] = coded_ref[slot_y, slot_x, :, span : 2 * span]
                coef_ref[dest, :] = coded_ref[slot_y, slot_x, :, 2 * span :].astype(WIDE)

    for layer in range(layers):
        up_weight = weight_ref[lax.rem(section + layer, layers), :, rank:]
        act = act_ref[:, layer * rank : (layer + 1) * rank]
        total = wide_ref[...] + dot_nt(act, up_weight)
        wide_ref[...] = total
        lowered = total.astype(LOW)
        for group in range(groups):
            out_ref[layer, group] = lowered[group * half : (group + 1) * half]

    for group in range(groups):
        base = group * half
        wide_ref[base : base + half, :] = rows_ref[group, half:, :].astype(WIDE)
    for layer in reversed(range(layers)):
        slot = lax.rem(section + layer, layers)
        delta = wide_ref[...].astype(LOW)
        act = act_ref[:, layer * rank : (layer + 1) * rank]
        moved = moved_ref[:, layer * rank : (layer + 1) * rank]
        if layer > 0:
            current = out_ref[layer - 1].reshape(groups * half, features)
        else:
            current = rows_ref[:, :half, :].reshape(groups * half, features)
        grad_ref[slot, :, features:] = dot_tn(act, delta).astype(LOW)
        grad_ref[slot, :, :features] = dot_tn(moved, current).astype(LOW)
        if layer > 0:
            coef = coef_ref[:, layer : layer + 1] + coef_ref[:, layers + layer : layers + layer + 1]
            wide_ref[...] += dot_nt(moved, weight_ref[slot, :, :rank]) - coef * current.astype(WIDE)


def square_kernel(gain_ref, grad_ref, out_ref):
    features = gain_ref.shape[1]
    grad_in = grad_ref[:, :features].astype(WIDE) * gain_ref[...]
    grad_out = grad_ref[:, features:].astype(WIDE)
    total = jnp.sum(grad_in * grad_in) + jnp.sum(grad_out * grad_out)
    out_ref[...] = jnp.full(out_ref.shape, total, WIDE)


def order_kernel(block_ref, out_ref):
    layers, features = block_ref.shape[0], block_ref.shape[3]
    for layer in range(layers):
        out_ref[:, layer * features : (layer + 1) * features] = block_ref[layer, 0]


def update_kernel(limit, sums_ref, gain_ref, grad_ref, *refs):
    features = gain_ref.shape[1]
    sources = refs[:6]
    results = refs[6:]
    total = jnp.sum(sums_ref[...], axis=0, keepdims=True)
    clip = limit / jnp.maximum(jnp.sqrt(total), limit)
    grad_in = (grad_ref[:, :features].astype(WIDE) * gain_ref[...]).T * clip
    updated = adam_update(sources[0][0], sources[1][0], sources[2][0], grad_in)
    for ref, value in zip(results[:3], updated):
        ref[0] = value
    grad_out = grad_ref[:, features:].astype(WIDE) * clip[:, 0:1]
    updated = adam_update(sources[3][0], sources[4][0], sources[5][0], grad_out)
    for ref, value in zip(results[3:], updated):
        ref[0] = value


def shards(
    stack_input,
    out_cotangent,
    norm_gain,
    master_in,
    master_out,
    first_in,
    first_out,
    second_in,
    second_out,
):
    count_x, count_c, count_y, count_z = (lax.axis_size(a) for a in EVERYONE)
    pos_x, pos_c, pos_y, pos_z = (lax.axis_index(a) for a in EVERYONE)
    layers = count_x * count_c
    pos_s = pos_x * count_c + pos_c
    place = jnp.stack([pos_c, pos_s, pos_x, pos_y]).astype(jnp.int32)
    sources = layers * count_y
    tok_rows, model_width = stack_input.shape
    features, rank = master_in.shape[1:]
    piece = tok_rows // layers
    swap_core = [(0, 1), (1, 0)]
    route = [(a * count_z + b, b * count_z + (a + b) % count_z) for a in range(layers) for b in range(count_z)]
    back_route = [(j, i) for i, j in route]
    across = SECTION + ("z",)

    gain_own = lax.dynamic_slice_in_dim(norm_gain, (pos_y * count_z + pos_z) * features, features, 1)
    packed = local_call(
        pack_kernel, jax.ShapeDtypeStruct((features, 2 * rank), LOW), (gain_own, master_in, master_out)
    )
    swapped = lax.ppermute(packed, across, route)
    gain_swapped = lax.ppermute(gain_own, across, route)
    weights = lax.all_gather(swapped, "z", axis=0)

    def blocks_of(rows):
        return jnp.stack(
            [
                lax.dynamic_slice_in_dim(rows, (g * count_z + pos_s) * features, features, 1)
                for g in range(count_y)
            ]
        )

    rows = jnp.concatenate([blocks_of(stack_input), blocks_of(out_cotangent)], axis=1)
    rows = lax.all_to_all(rows, "y", 0, 0, tiled=True)
    own_rows = lax.dynamic_slice_in_dim(stack_input, pos_s * piece, piece, 0).astype(WIDE)
    square = jnp.sum(own_rows * own_rows, axis=-1, keepdims=True)
    square = jnp.broadcast_to(square, (piece, 128))

    lined = gather_line(packed, "x")
    lined = jnp.stack([lined, lax.ppermute(lined, "c", swap_core)])
    cross = lax.dot_general(
        packed[:, rank:], lined, (((0,), (2,)), ((), ())), preferred_element_type=WIDE
    )
    cross = cross.transpose(1, 2, 0, 3)
    ordered = []
    for layer in range(layers):
        owner, from_core = divmod(layer, count_c)
        away = lax.rem(pos_x - owner + count_x, count_x)
        slot = jnp.where(away == count_x - 1, 2, jnp.where(away == 2, 3, away))
        block = lax.dynamic_slice(
            cross, (lax.rem(pos_c + from_core, 2), slot, 0, 0), (1, 1, rank, 2 * rank)
        )[0, 0]
        ordered.append(jnp.where(layer > pos_s, block[:, :rank], block[:, rank:]).astype(LOW))
    cut_r, cut_c = rank // count_z, layers * rank // count_y
    cross = jnp.stack(ordered, axis=1).reshape(count_z, cut_r, count_y, cut_c)
    cross = cross.transpose(2, 0, 1, 3).reshape(count_y * count_z, cut_r, cut_c)
    cross = lax.all_to_all(cross, ("y", "z"), 0, 0, tiled=True)
    cross = jnp.sum(cross.astype(WIDE), axis=0, keepdims=True).astype(LOW)
    cross = jnp.broadcast_to(cross, (count_y * count_z, cut_r, cut_c))
    cross = lax.all_to_all(cross, ("y", "z"), 0, 0, tiled=True)
    cross = cross.reshape(count_y, count_z, cut_r, cut_c).transpose(1, 2, 0, 3)
    cross = cross.reshape(rank, layers * rank)
    cross_near = gather_line(cross, "x")
    cross_far = lax.ppermute(cross_near, "c", swap_core)

    part_shape = jax.ShapeDtypeStruct((count_x, count_y, piece, layers * 3 * rank), LOW)
    keep, send = local_call(
        functools.partial(project_kernel, rank),
        (part_shape, part_shape),
        (rows, weights),
        scalars=place,
        flops=2 * rows.shape[0] * tok_rows * features * layers * rank * 3,
    )
    came = lax.ppermute(send, "c", swap_core)
    parts = (keep.astype(WIDE) + came.astype(WIDE)).astype(LOW)
    parts = parts.reshape(count_x * count_y, piece, layers * 3 * rank)
    parts = lax.all_to_all(parts, ("x", "y"), 0, 0, tiled=True)
    coded_width = 2 * layers * rank + rank
    coded = local_call(
        functools.partial(recursion_kernel, layers, rank, float(model_width)),
        jax.ShapeDtypeStruct((piece, coded_width), LOW),
        (parts, square, cross_near, cross_far),
        scalars=place,
        scratch=[
            pltpu.VMEM((piece, layers * 3 * rank), WIDE),
            pltpu.VMEM((layers * rank, layers * rank), LOW),
        ],
    )
    coded_near = gather_line(gather_line(coded, "x"), "y")
    coded_far = lax.ppermute(coded_near, "c", swap_core)

    group_tokens = count_y * tok_rows
    outputs, grads = local_call(
        functools.partial(expand_kernel, layers, rank),
        (
            jax.ShapeDtypeStruct((layers, count_y, tok_rows, features), LOW),
            jax.ShapeDtypeStruct((layers, rank, 2 * features), LOW),
        ),
        (rows, weights, coded_near, coded_far),
        scalars=place,
        scratch=[
            pltpu.VMEM((group_tokens, features), WIDE),
            pltpu.VMEM((group_tokens, layers * rank), LOW),
            pltpu.VMEM((group_tokens, layers * rank), LOW),
            pltpu.VMEM((group_tokens, rank), WIDE),
        ],
        flops=8 * group_tokens * features * layers * rank,
    )
    grads = lax.psum_scatter(grads, "z", scatter_dimension=0, tiled=True)[0]
    outputs = outputs.reshape(sources, tok_rows, features)
    outputs = lax.all_to_all(outputs, PLANE, 0, 0, tiled=True)
    outputs = outputs.reshape(layers, count_y, tok_rows, features)
    section_rows = pl.pallas_call(
        order_kernel,
        grid=(count_y,),
        out_shape=jax.ShapeDtypeStruct((tok_rows, model_width), LOW),
        in_specs=[pl.BlockSpec((layers, 1, tok_rows, features), lambda i: (0, i, 0, 0))],
        out_specs=pl.BlockSpec((tok_rows, layers * features), lambda i: (0, i)),
        compiler_params=pltpu.CompilerParams(vmem_limit_bytes=VMEM_BYTES),
    )(outputs)

    own_grads = lax.ppermute(grads, across, back_route)
    squares = local_call(
        square_kernel, jax.ShapeDtypeStruct((sources * count_z, 128), WIDE), (gain_swapped, grads)
    )
    squares = lax.all_to_all(squares, EVERYONE, 0, 0, tiled=True)
    norm_limit = clip_rms * math.sqrt(2.0 * model_width * rank * layers)
    shape_in = jax.ShapeDtypeStruct(master_in.shape, WIDE)
    shape_out = jax.ShapeDtypeStruct(master_out.shape, WIDE)
    updated = local_call(
        functools.partial(update_kernel, norm_limit),
        (shape_in,) * 3 + (shape_out,) * 3,
        (squares, gain_own, own_grads, master_in, first_in, second_in, master_out, first_out, second_out),
    )
    new_in, new_first_in, new_second_in, new_out, new_first_out, new_second_out = updated
    return (
        section_rows[None],
        new_in,
        new_out,
        new_first_in,
        new_first_out,
        new_second_in,
        new_second_out,
    )


def solution(mesh):
    layers, groups = mesh.shape["section"], mesh.shape["dp"]
    sizes = (layers // 2, 2, groups // layers, layers)
    fine = Mesh(mesh.devices.reshape(sizes), EVERYONE)
    split = ("y", "z")
    by_rows = P(SECTION, split, None)
    by_cols = P(SECTION, None, split)
    in_specs = (
        P(split, None),
        P(split, None),
        P(SECTION, None),
        by_rows,
        by_cols,
        by_rows,
        by_cols,
        by_rows,
        by_cols,
    )
    out_specs = (by_rows, by_rows, by_cols, by_rows, by_cols, by_rows, by_cols)
    return jax.shard_map(shards, mesh=fine, in_specs=in_specs, out_specs=out_specs, check_vma=False)
```

time: 309 us -> 283 us (0.916)
  waiting for transfers between devices: 155 us -> 131 us
  starting transfers between devices: 49.4 us -> 71.4 us
  blocking collectives: 35.9 us -> 19.3 us
  local copies, waits for them, and re-layouts: 28 us -> 15.5 us
  Pallas kernels: 13.6 us -> 20.1 us
    ppermute x3 -> x19, waiting for transfers between devices: 17.4 us -> 73.8 us  [the longest x12 45.2 us: shifted(): lax.ppermute(block, axis, [(i, (i + distance) % size) for i in range(size)])]
    all_to_all x4 -> x3, waiting for transfers between devices: 50.9 us -> 8.96 us  [the longest x1 8.96 us: shards(): cross = lax.all_to_all(cross, ('y', 'z'), 0, 0, tiled=True)]
    all_gather x1, waiting for transfers between devices: 42 us -> 9.13 us  [shards(): weights = lax.all_gather(swapped, 'z', axis=0)]
    ppermute x3 -> x19, starting transfers between devices: 12.3 us -> 38.4 us  [the longest x12 21.7 us: shifted(): lax.ppermute(block, axis, [(i, (i + distance) % size) for i in range(size)])]
    all_to_all x1, blocking collectives: 35.9 us -> 19.3 us  [shards(): cross = lax.all_to_all(cross, ('y', 'z'), 0, 0, tiled=True)]
    reshape x3 -> x1, local copies, waits for them, and re-layouts: 9.39 us -> 0.17 us  [shards(): cross = jnp.stack(ordered, axis=1).reshape(count_z, cut_r, count_y, cut_c)]
    all_to_all x4 -> x3, starting transfers between devices: 27.9 us -> 21.1 us  [the longest x1 10.1 us: shards(): squares = lax.all_to_all(squares, EVERYONE, 0, 0, tiled=True)]
    pallas_call x3 -> x7, Pallas kernels: 13.6 us -> 20.1 us  [the longest x6 17.6 us: local_call(): pl.pallas_call(kernel, out_shape=out_shape, in_specs=in_specs, out_specs=...]
  transfers between devices with their start and end apart: 12 -> 26, of which waited for: 9 -> 20; matrix products, arithmetic and copies ran while one was open for 6% -> 4% of each run, Pallas kernels for 1% -> 1%
where the time goes in v2:
time: 283 us; the launch traced here: 280 us
  waiting for transfers between devices  131 us (46%)
  starting transfers between devices  71.4 us (25%)
  Pallas kernels  20.1 us (7%)
  blocking collectives  19.3 us (7%)
  local copies, waits for them, and re-layouts  15.5 us (5%)
  between operations  14.3 us (5%)
  other arithmetic  7.28 us (3%)
    ppermute x12, waiting for transfers between devices, shifted(): lax.ppermute(block, axis, [(i, (i + distance) % size) for i in range(size)])  45.2 us
    reduce_scatter x1, waiting for transfers between devices, shards(): grads = lax.psum_scatter(grads, 'z', scatter_dimension=0, tiled=True)[0]  23.1 us
    ppermute x12, starting transfers between devices, shifted(): lax.ppermute(block, axis, [(i, (i + distance) % size) for i in range(size)])  21.7 us
    all_to_all x1, blocking collectives, shards(): cross = lax.all_to_all(cross, ('y', 'z'), 0, 0, tiled=True)  19.3 us
    pallas_call x6, Pallas kernels, local_call(): pl.pallas_call(kernel, out_shape=out_shape, in_specs=in_specs, out_specs=...  17.6 us
    unnamed x35, local copies, waits for them, and re-layouts  11.9 us
    all_to_all x1, waiting for transfers between devices, shards(): rows = lax.all_to_all(rows, 'y', 0, 0, tiled=True)  11.1 us
    ppermute x1, waiting for transfers between devices, shards(): own_grads = lax.ppermute(grads, across, back_route)  10.5 us
  transfers between devices with their start and end apart: 26, of which 20 were waited for; matrix products, arithmetic and copies ran while one was open for 4% of the time, Pallas kernels for 1%

profile of v2, /device:TPU:2, one launch (start us, length us, event | category | flops | bytes accessed | tf_op | source)
XLA Modules:
  0.0 280.4 jit_solution(10053554485325107414)
XLA Ops:
  10.0 5.2 %collective-permute-start = (bf16[384,256]{1,0:T(8,128)(2,1)S(1)}, bf16[384,256]{1,0:T(8,128)(2,1)S(1)}, u32[]{:S(2)}, u32[]{:S(2)}) collective-permute-start(bf16[384,256]{1,0:T(8,128)(2,1)S(1)} %shard_map.144), channel_id=1, source_target_pairs={{0,0},{1,33},{2,66},{3,99},{4,132},{5,165},{6,198},{7,231},{32,1},... | collective-permute-start | bytes 589832 | tf_op jit(solution)/shard_map/ppermute | solution.py:311
  15.2 9.8 %collective-permute-done = bf16[384,256]{1,0:T(8,128)(2,1)S(1)} collective-permute-done((bf16[384,256]{1,0:T(8,128)(2,1)S(1)}, bf16[384,256]{1,0:T(8,128)(2,1)S(1)}, u32[]{:S(2)}, u32[]{:S(2)}) %collective-permute-start) | collective-permute-done | bytes 196640 | tf_op jit(solution)/shard_map/ppermute | solution.py:311
  27.8 6.7 %collective-permute-start.4 = (bf16[384,256]{1,0:T(8,128)(2,1)S(1)}, bf16[384,256]{1,0:T(8,128)(2,1)S(1)}, u32[]{:S(2)}, u32[]{:S(2)}) collective-permute-start(bf16[384,256]{1,0:T(8,128)(2,1)S(1)} %shard_map.144), channel_id=1, source_target_pairs={{0,128},{64,192},{128,0},{192,64},{1,129},{65,193},{129,1},{193,65... | collective-permute-start | bytes 589832 | tf_op jit(solution)/shard_map/ppermute | solution.py:85
  34.5 8.2 %collective-permute-done.3 = bf16[384,256]{1,0:T(8,128)(2,1)S(1)} collective-permute-done((bf16[384,256]{1,0:T(8,128)(2,1)S(1)}, bf16[384,256]{1,0:T(8,128)(2,1)S(1)}, u32[]{:S(2)}, u32[]{:S(2)}) %collective-permute-start.3) | collective-permute-done | bytes 196640 | tf_op jit(solution)/shard_map/ppermute | solution.py:85
  45.2 4.5 %all-to-all-start = ((bf16[4,256,384]{2,1,0:T(8,128)(2,1)}), bf16[4,256,384]{2,1,0:T(8,128)(2,1)S(1)}, u32[]{:S(2)}, u32[]{:S(2)}) async-start(bf16[4,256,384]{2,1,0:T(8,128)(2,1)} %maximum_maximum_fusion), calls=%async_computation | async-start | bytes 1572864 | tf_op jit(solution)/shard_map/all_to_all | solution.py:324
  51.5 11.1 %all-to-all-done.rows_ref = bf16[4,256,384]{2,1,0:T(8,128)(2,1)S(1)} async-done(((bf16[4,256,384]{2,1,0:T(8,128)(2,1)}), bf16[4,256,384]{2,1,0:T(8,128)(2,1)S(1)}, u32[]{:S(2)}, u32[]{:S(2)}) %all-to-all-start) | async-done | bytes 786464 | tf_op jit(solution)/shard_map/all_to_all | solution.py:324
  62.6 9.1 %all-gather.3.cloned.1.call-done = bf16[3072,256]{1,0:T(8,128)(2,1)} async-done(((bf16[384,256]{1,0:T(8,128)(2,1)}), bf16[3072,256]{1,0:T(8,128)(2,1)}) %all-gather.3.cloned.1.call-update) | async-done | bytes 1572880 | tf_op jit(solution)/shard_map/all_gather | solution.py:313
  73.1 4.0 %shard_map.145 = (bf16[4,4,16,3072]{3,2,1,0:T(8,128)(2,1)S(1)}, bf16[4,4,16,3072]{3,2,1,0:T(8,128)(2,1)}) custom-call(s32[4]{0:T(128)S(1)} %pad_add_fusion.place_ref, bf16[4,256,384]{2,1,0:T(8,128)(2,1)S(1)} %all-to-all-done.rows_ref, bf16[8,384,256]{2,1,0:T(8,128)(2,1)S(1)} %bitcast.114), custom_call_target="tpu_custom_call" | custom-call | flops 1207959552 | bytes 5505024 | tf_op jit(solution)/shard_map/pallas_call | solution.py:72
  77.6 19.3 %all_to_all.36 = bf16[32,16,256]{2,1,0:T(8,128)(2,1)S(1)} all-to-all(bf16[32,16,256]{2,1,0:T(8,128)(2,1)S(1)} %bitcast.122), channel_id=1, replica_groups=mesh['x'=4,'c'=2,'y'=4,'z'=8] {'y','z'}, dimensions={0} | all-to-all | bytes 524288 | tf_op jit(solution)/shard_map/all_to_all | solution.py:347
  97.7 5.2 %all-to-all-start.3 = ((bf16[32,16,256]{2,1,0:T(8,128)(2,1)}), bf16[32,16,256]{2,1,0:T(8,128)(2,1)S(1)}, u32[]{:S(2)}, u32[]{:S(2)}) async-start(bf16[32,16,256]{2,1,0:T(8,128)(2,1)} %broadcast_in_dim.7), calls=%async_computation.3 | async-start | bytes 524288 | tf_op jit(solution)/shard_map/all_to_all | solution.py:350
  102.9 3.1 %add_convert_fusion = bf16[4,4,16,3072]{3,2,1,0:T(8,128)(2,1)} fusion(bf16[4,4,16,3072]{3,2,1,0:T(8,128)(2,1)} %collective-permute-done.1, bf16[4,4,16,3072]{3,2,1,0:T(8,128)(2,1)S(1)} %get-tuple-element.17), kind=kLoop, calls=%fused_computation | loop fusion | flops 3145728 | bytes 4718592 | tf_op jit(solution)/shard_map/convert_element_type | solution.py:365
  106.0 9.0 %all-to-all-done.3 = bf16[32,16,256]{2,1,0:T(8,128)(2,1)S(1)} async-done(((bf16[32,16,256]{2,1,0:T(8,128)(2,1)}), bf16[32,16,256]{2,1,0:T(8,128)(2,1)S(1)}, u32[]{:S(2)}, u32[]{:S(2)}) %all-to-all-start.3) | async-done | bytes 262176 | tf_op jit(solution)/shard_map/all_to_all | solution.py:350
  115.0 5.8 %all-to-all-start.1 = ((bf16[16,16,3072]{2,1,0:T(8,128)(2,1)}), bf16[16,16,3072]{2,1,0:T(8,128)(2,1)S(1)}, u32[]{:S(2)}, u32[]{:S(2)}) async-start(bf16[16,16,3072]{2,1,0:T(8,128)(2,1)} %bitcast.116), calls=%async_computation.1 | async-start | bytes 3145728 | tf_op jit(solution)/shard_map/all_to_all | solution.py:367
  123.2 2.1 collective-permute-start.8
  126.1 18.0 %collective-permute-done.6 = bf16[128,1024]{1,0:T(8,128)(2,1)S(1)} collective-permute-done((bf16[128,1024]{1,0:T(8,128)(2,1)S(1)}, bf16[128,1024]{1,0:T(8,128)(2,1)S(1)}, u32[]{:S(2)}, u32[]{:S(2)}) %collective-permute-start.6) | collective-permute-done | bytes 262176 | tf_op jit(solution)/shard_map/ppermute | solution.py:85
  145.1 3.6 %collective-permute-done.8 = bf16[128,1024]{1,0:T(8,128)(2,1)} collective-permute-done((bf16[128,1024]{1,0:T(8,128)(2,1)S(1)}, bf16[128,1024]{1,0:T(8,128)(2,1)}, u32[]{:S(2)}, u32[]{:S(2)}) %collective-permute-start.8) | collective-permute-done | bytes 262176 | tf_op jit(solution)/shard_map/ppermute | solution.py:85
  153.2 4.8 %shard_map.146 = bf16[16,2176]{1,0:T(8,128)(2,1)S(1)} custom-call(s32[4]{0:T(128)S(1)} %pad_add_fusion.place_ref, bf16[16,16,3072]{2,1,0:T(8,128)(2,1)S(1)} %all-to-all-done.1.parts_ref, f32[16,128]{1,0:T(8,128)S(1)} %broadcast_in_dim.6.square_ref, bf16[4,128,1024]{2,1,0:T(8,128)(2,1)S(1)} %pad_maximum_fusion.1.near_ref, ...), custom_call_target="tpu_custom_call" | custom-call | bytes 3747840 | tf_op jit(solution)/shard_map/pallas_call | solution.py:72
  158.0 2.0 collective-permute-start.11
  162.4 3.4 %collective-permute-done.12 = bf16[16,2176]{1,0:T(8,128)(2,1)S(1)} collective-permute-done((bf16[16,2176]{1,0:T(8,128)(2,1)S(1)}, bf16[16,2176]{1,0:T(8,128)(2,1)S(1)}, u32[]{:S(2)}, u32[]{:S(2)}) %collective-permute-start.12) | collective-permute-done | bytes 69664 | tf_op jit(solution)/shard_map/ppermute | solution.py:85
  171.1 4.9 %collective-permute-done.13 = bf16[4,16,2176]{2,1,0:T(8,128)(2,1)S(1)} collective-permute-done((bf16[4,16,2176]{2,1,0:T(8,128)(2,1)S(1)}, bf16[4,16,2176]{2,1,0:T(8,128)(2,1)S(1)}, u32[]{:S(2)}, u32[]{:S(2)}) %collective-permute-start.13) | collective-permute-done | bytes 278560 | tf_op jit(solution)/shard_map/ppermute | solution.py:85
  177.1 4.1 %collective-permute-done.15 = bf16[4,16,2176]{2,1,0:T(8,128)(2,1)S(1)} collective-permute-done((bf16[4,16,2176]{2,1,0:T(8,128)(2,1)S(1)}, bf16[4,16,2176]{2,1,0:T(8,128)(2,1)S(1)}, u32[]{:S(2)}, u32[]{:S(2)}) %collective-permute-start.15) | collective-permute-done | bytes 278560 | tf_op jit(solution)/shard_map/ppermute | solution.py:85
  181.4 2.7 collective-permute-done.16.far_ref
  184.2 6.5 %shard_map.147 = (bf16[8,4,128,384]{3,2,1,0:T(8,128)(2,1)}, bf16[8,128,768]{2,1,0:T(8,128)(2,1)}) custom-call(s32[4]{0:T(128)S(1)} %pad_add_fusion.place_ref, bf16[4,256,384]{2,1,0:T(8,128)(2,1)S(1)} %all-to-all-done.rows_ref, bf16[8,384,256]{2,1,0:T(8,128)(2,1)S(1)} %bitcast.115, bf16[4,4,16,2176]{3,2,1,0:T(8,128)(2,1)S(1)} %pad_maximum_fusion.near_ref, ...), custom_call_target="tpu_custom_call" | custom-call | flops 1610612736 | bytes 9306112 | tf_op jit(solution)/shard_map/pallas_call | solution.py:72
  190.7 7.4 %all-to-all-start.4 = ((bf16[32,128,384]{2,1,0:T(8,128)(2,1)}), bf16[32,128,384]{2,1,0:T(8,128)(2,1)S(1)}, u32[]{:S(2)}, u32[]{:S(2)}) async-start(bf16[32,128,384]{2,1,0:T(8,128)(2,1)} %bitcast.117), calls=%async_computation.4 | async-start | bytes 6291456 | tf_op jit(solution)/shard_map/all_to_all | solution.py:401
  198.1 4.8 %collective-permute-start.17 = (f32[1,384]{1,0:T(1,128)S(1)}, f32[1,384]{1,0:T(1,128)S(1)}, u32[]{:S(2)}, u32[]{:S(2)}) collective-permute-start(f32[1,384]{1,0:T(1,128)S(1)} %constant_dynamic-slice_fusion.gain_ref), channel_id=1, source_target_pairs={{0,0},{1,33},{2,66},{3,99},{4,132},{5,165},{6,198},{7,231},{32,1},... | collective-permute-start | bytes 4616 | tf_op jit(solution)/shard_map/ppermute | solution.py:312
  203.0 4.0 %collective-permute-done.17.gain_ref = f32[1,384]{1,0:T(1,128)S(1)} collective-permute-done((f32[1,384]{1,0:T(1,128)S(1)}, f32[1,384]{1,0:T(1,128)S(1)}, u32[]{:S(2)}, u32[]{:S(2)}) %collective-permute-start.17) | collective-permute-done | bytes 1568 | tf_op jit(solution)/shard_map/ppermute | solution.py:312
  207.0 23.1 %reduce-scatter.2.cloned.1.call-done = bf16[1,128,768]{2,1,0:T(8,128)(2,1)} async-done(((bf16[8,128,768]{2,1,0:T(8,128)(2,1)}), bf16[1,128,768]{2,1,0:T(8,128)(2,1)}) %reduce-scatter.2.cloned.1.call-update) | async-done | bytes 196624 | tf_op jit(solution)/shard_map/reduce_scatter | solution.py:399
  231.9 4.8 %all-to-all-done.4 = bf16[32,128,384]{2,1,0:T(8,128)(2,1)S(1)} async-done(((bf16[32,128,384]{2,1,0:T(8,128)(2,1)}), bf16[32,128,384]{2,1,0:T(8,128)(2,1)S(1)}, u32[]{:S(2)}, u32[]{:S(2)}) %all-to-all-start.4) | async-done | bytes 3145760 | tf_op jit(solution)/shard_map/all_to_all | solution.py:401
  236.7 10.1 %all-to-all-start.5 = ((f32[256,1,128]{2,1,0:T(1,128)}), f32[256,1,128]{2,1,0:T(1,128)S(1)}, u32[]{:S(2)}, u32[]{:S(2)}) async-start(f32[256,1,128]{2,1,0:T(1,128)} %bitcast.58), calls=%async_computation.6 | async-start | bytes 262144 | tf_op jit(solution)/shard_map/all_to_all | solution.py:416
  246.8 6.2 %collective-permute-start.18 = (bf16[128,768]{1,0:T(8,128)(2,1)}, bf16[128,768]{1,0:T(8,128)(2,1)S(1)}, u32[]{:S(2)}, u32[]{:S(2)}) collective-permute-start(bf16[128,768]{1,0:T(8,128)(2,1)} %bitcast.112), channel_id=1, source_target_pairs={{0,0},{33,1},{66,2},{99,3},{132,4},{165,5},{198,6},{231,7},{1,32},... | collective-permute-start | bytes 589832 | tf_op jit(solution)/shard_map/ppermute | solution.py:412
  253.0 2.4 shard_map.148
  255.5 10.5 %collective-permute-done.18.grad_ref = bf16[128,768]{1,0:T(8,128)(2,1)S(1)} collective-permute-done((bf16[128,768]{1,0:T(8,128)(2,1)}, bf16[128,768]{1,0:T(8,128)(2,1)S(1)}, u32[]{:S(2)}, u32[]{:S(2)}) %collective-permute-start.18) | collective-permute-done | bytes 196640 | tf_op jit(solution)/shard_map/ppermute | solution.py:412
  (93 shorter events, 39.5 us)
Async XLA Ops:
  7.2 64.5 %all-gather.3.cloned.1.call-start = ((), (), s32[]{:S(2)}) async-start(), calls=%async_computation.8 | async-start | bytes 1769472 | tf_op jit(solution)/shard_map/all_gather | solution.py:313
  10.0 15.0 %collective-permute-start = (bf16[384,256]{1,0:T(8,128)(2,1)S(1)}, bf16[384,256]{1,0:T(8,128)(2,1)S(1)}, u32[]{:S(2)}, u32[]{:S(2)}) collective-permute-start(bf16[384,256]{1,0:T(8,128)(2,1)S(1)} %shard_map.144), channel_id=1, source_target_pairs={{0,0},{1,33},{2,66},{3,99},{4,132},{5,165},{6,198},{7,231},{32,1},... | collective-permute-start | bytes 589832 | tf_op jit(solution)/shard_map/ppermute | solution.py:311
  25.7 8.8 %collective-permute-start.2 = (bf16[384,256]{1,0:T(8,128)(2,1)S(1)}, bf16[384,256]{1,0:T(8,128)(2,1)S(1)}, u32[]{:S(2)}, u32[]{:S(2)}) collective-permute-start(bf16[384,256]{1,0:T(8,128)(2,1)S(1)} %shard_map.144), channel_id=1, source_target_pairs={{0,64},{64,128},{128,192},{192,0},{1,65},{65,129},{129,193},{193,1... | collective-permute-start | bytes 589832 | tf_op jit(solution)/shard_map/ppermute | solution.py:85
  26.6 16.0 %collective-permute-start.3 = (bf16[384,256]{1,0:T(8,128)(2,1)S(1)}, bf16[384,256]{1,0:T(8,128)(2,1)S(1)}, u32[]{:S(2)}, u32[]{:S(2)}) collective-permute-start(bf16[384,256]{1,0:T(8,128)(2,1)S(1)} %shard_map.144), channel_id=1, source_target_pairs={{0,192},{64,0},{128,64},{192,128},{1,193},{65,1},{129,65},{193,129... | collective-permute-start | bytes 589832 | tf_op jit(solution)/shard_map/ppermute | solution.py:85
  27.8 14.9 %collective-permute-start.4 = (bf16[384,256]{1,0:T(8,128)(2,1)S(1)}, bf16[384,256]{1,0:T(8,128)(2,1)S(1)}, u32[]{:S(2)}, u32[]{:S(2)}) collective-permute-start(bf16[384,256]{1,0:T(8,128)(2,1)S(1)} %shard_map.144), channel_id=1, source_target_pairs={{0,128},{64,192},{128,0},{192,64},{1,129},{65,193},{129,1},{193,65... | collective-permute-start | bytes 589832 | tf_op jit(solution)/shard_map/ppermute | solution.py:85
  42.8 6.9 %collective-permute-start.5 = (bf16[4,384,256]{2,1,0:T(8,128)(2,1)S(1)}, bf16[4,384,256]{2,1,0:T(8,128)(2,1)}, u32[]{:S(2)}, u32[]{:S(2)}) collective-permute-start(bf16[4,384,256]{2,1,0:T(8,128)(2,1)S(1)} %get-tuple-element.36), channel_id=1, source_target_pairs={{0,32},{32,0},{1,33},{33,1},{2,34},{34,2},{3,35},{35,3},{4,36},{36... | collective-permute-start | bytes 2359304 | tf_op jit(solution)/shard_map/ppermute | solution.py:330
  45.2 17.4 %all-to-all-start = ((bf16[4,256,384]{2,1,0:T(8,128)(2,1)}), bf16[4,256,384]{2,1,0:T(8,128)(2,1)S(1)}, u32[]{:S(2)}, u32[]{:S(2)}) async-start(bf16[4,256,384]{2,1,0:T(8,128)(2,1)} %maximum_maximum_fusion), calls=%async_computation | async-start | bytes 1572864 | tf_op jit(solution)/shard_map/all_to_all | solution.py:324
  71.7 1.4 copy-start.12
  77.1 25.8 %collective-permute-start.1 = (bf16[4,4,16,3072]{3,2,1,0:T(8,128)(2,1)}, bf16[4,4,16,3072]{3,2,1,0:T(8,128)(2,1)}, u32[]{:S(2)}, u32[]{:S(2)}) collective-permute-start(bf16[4,4,16,3072]{3,2,1,0:T(8,128)(2,1)} %get-tuple-element.18), channel_id=1, source_target_pairs={{0,32},{32,0},{1,33},{33,1},{2,34},{34,2},{3,35},{35,3},{4,36},{36... | collective-permute-start | bytes 4718600 | tf_op jit(solution)/shard_map/ppermute | solution.py:364
  97.7 17.3 %all-to-all-start.3 = ((bf16[32,16,256]{2,1,0:T(8,128)(2,1)}), bf16[32,16,256]{2,1,0:T(8,128)(2,1)S(1)}, u32[]{:S(2)}, u32[]{:S(2)}) async-start(bf16[32,16,256]{2,1,0:T(8,128)(2,1)} %broadcast_in_dim.7), calls=%async_computation.3 | async-start | bytes 524288 | tf_op jit(solution)/shard_map/all_to_all | solution.py:350
  115.0 38.1 %all-to-all-start.1 = ((bf16[16,16,3072]{2,1,0:T(8,128)(2,1)}), bf16[16,16,3072]{2,1,0:T(8,128)(2,1)S(1)}, u32[]{:S(2)}, u32[]{:S(2)}) async-start(bf16[16,16,3072]{2,1,0:T(8,128)(2,1)} %bitcast.116), calls=%async_computation.1 | async-start | bytes 3145728 | tf_op jit(solution)/shard_map/all_to_all | solution.py:367
  120.8 109.3 %reduce-scatter.2.cloned.1.call-start = ((), (), s32[]{:S(2)}) async-start(), calls=%async_computation.7 | async-start | bytes 1769472 | tf_op jit(solution)/shard_map/reduce_scatter | solution.py:399
  121.0 23.1 %collective-permute-start.6 = (bf16[128,1024]{1,0:T(8,128)(2,1)S(1)}, bf16[128,1024]{1,0:T(8,128)(2,1)S(1)}, u32[]{:S(2)}, u32[]{:S(2)}) collective-permute-start(bf16[128,1024]{1,0:T(8,128)(2,1)S(1)} %bitcast.126), channel_id=1, source_target_pairs={{0,64},{64,128},{128,192},{192,0},{1,65},{65,129},{129,193},{193,1... | collective-permute-start | bytes 786440 | tf_op jit(solution)/shard_map/ppermute | solution.py:85
  122.6 22.5 %collective-permute-start.7 = (bf16[128,1024]{1,0:T(8,128)(2,1)S(1)}, bf16[128,1024]{1,0:T(8,128)(2,1)S(1)}, u32[]{:S(2)}, u32[]{:S(2)}) collective-permute-start(bf16[128,1024]{1,0:T(8,128)(2,1)S(1)} %bitcast.127), channel_id=1, source_target_pairs={{0,192},{64,0},{128,64},{192,128},{1,193},{65,1},{129,65},{193,129... | collective-permute-start | bytes 786440 | tf_op jit(solution)/shard_map/ppermute | solution.py:85
  123.2 25.6 %collective-permute-start.8 = (bf16[128,1024]{1,0:T(8,128)(2,1)S(1)}, bf16[128,1024]{1,0:T(8,128)(2,1)}, u32[]{:S(2)}, u32[]{:S(2)}) collective-permute-start(bf16[128,1024]{1,0:T(8,128)(2,1)S(1)} %bitcast.128), channel_id=1, source_target_pairs={{0,128},{64,192},{128,0},{192,64},{1,129},{65,193},{129,1},{193,65... | collective-permute-start | bytes 786440 | tf_op jit(solution)/shard_map/ppermute | solution.py:85
  144.1 4.6 %copy-start.14 = (bf16[128,1024]{1,0:T(8,128)(2,1)}, bf16[128,1024]{1,0:T(8,128)(2,1)S(1)}, u32[]{:S(2)}) copy-start(bf16[128,1024]{1,0:T(8,128)(2,1)S(1)} %collective-permute-done.6) | copy-start | bytes 786436
  145.1 3.7 %copy-start.15 = (bf16[128,1024]{1,0:T(8,128)(2,1)}, bf16[128,1024]{1,0:T(8,128)(2,1)S(1)}, u32[]{:S(2)}) copy-start(bf16[128,1024]{1,0:T(8,128)(2,1)S(1)} %collective-permute-done.7) | copy-start | bytes 786436
  150.0 3.1 %collective-permute-start.9 = (bf16[4,128,1024]{2,1,0:T(8,128)(2,1)S(1)}, bf16[4,128,1024]{2,1,0:T(8,128)(2,1)}, u32[]{:S(2)}, u32[]{:S(2)}) collective-permute-start(bf16[4,128,1024]{2,1,0:T(8,128)(2,1)S(1)} %pad_maximum_fusion.1.near_ref), channel_id=1, source_target_pairs={{0,32},{32,0},{1,33},{33,1},{2,34},{34,2},{3,35},{35,3},{4,36},{36... | collective-permute-start | bytes 3145736 | tf_op jit(solution)/shard_map/ppermute | solution.py:354
  158.0 26.2 %copy-start.13 = (bf16[3072,256]{1,0:T(8,128)(2,1)S(1)}, bf16[3072,256]{1,0:T(8,128)(2,1)}, u32[]{:S(2)}) copy-start(bf16[3072,256]{1,0:T(8,128)(2,1)} %all-gather.3.cloned.1.call-done) | copy-start | bytes 4718596
  158.0 4.4 %collective-permute-start.10 = (bf16[16,2176]{1,0:T(8,128)(2,1)S(1)}, bf16[16,2176]{1,0:T(8,128)(2,1)S(1)}, u32[]{:S(2)}, u32[]{:S(2)}) collective-permute-start(bf16[16,2176]{1,0:T(8,128)(2,1)S(1)} %shard_map.146), channel_id=1, source_target_pairs={{0,64},{64,128},{128,192},{192,0},{1,65},{65,129},{129,193},{193,1... | collective-permute-start | bytes 208904 | tf_op jit(solution)/shard_map/ppermute | solution.py:85
  158.0 4.4 %collective-permute-start.11 = (bf16[16,2176]{1,0:T(8,128)(2,1)S(1)}, bf16[16,2176]{1,0:T(8,128)(2,1)S(1)}, u32[]{:S(2)}, u32[]{:S(2)}) collective-permute-start(bf16[16,2176]{1,0:T(8,128)(2,1)S(1)} %shard_map.146), channel_id=1, source_target_pairs={{0,192},{64,0},{128,64},{192,128},{1,193},{65,1},{129,65},{193,129... | collective-permute-start | bytes 208904 | tf_op jit(solution)/shard_map/ppermute | solution.py:85
  160.0 5.8 %collective-permute-start.12 = (bf16[16,2176]{1,0:T(8,128)(2,1)S(1)}, bf16[16,2176]{1,0:T(8,128)(2,1)S(1)}, u32[]{:S(2)}, u32[]{:S(2)}) collective-permute-start(bf16[16,2176]{1,0:T(8,128)(2,1)S(1)} %shard_map.146), channel_id=1, source_target_pairs={{0,128},{64,192},{128,0},{192,64},{1,129},{65,193},{129,1},{193,65... | collective-permute-start | bytes 208904 | tf_op jit(solution)/shard_map/ppermute | solution.py:85
  165.9 10.1 %collective-permute-start.13 = (bf16[4,16,2176]{2,1,0:T(8,128)(2,1)S(1)}, bf16[4,16,2176]{2,1,0:T(8,128)(2,1)S(1)}, u32[]{:S(2)}, u32[]{:S(2)}) collective-permute-start(bf16[4,16,2176]{2,1,0:T(8,128)(2,1)S(1)} %get-tuple-element.46), channel_id=1, source_target_pairs={{0,8},{8,16},{16,24},{24,0},{1,9},{9,17},{17,25},{25,1},{2,10},{10... | collective-permute-start | bytes 835592 | tf_op jit(solution)/shard_map/ppermute | solution.py:85
  167.5 9.6 %collective-permute-start.14 = (bf16[4,16,2176]{2,1,0:T(8,128)(2,1)S(1)}, bf16[4,16,2176]{2,1,0:T(8,128)(2,1)S(1)}, u32[]{:S(2)}, u32[]{:S(2)}) collective-permute-start(bf16[4,16,2176]{2,1,0:T(8,128)(2,1)S(1)} %get-tuple-element.46), channel_id=1, source_target_pairs={{0,24},{8,0},{16,8},{24,16},{1,25},{9,1},{17,9},{25,17},{2,26},{10... | collective-permute-start | bytes 835592 | tf_op jit(solution)/shard_map/ppermute | solution.py:85
  169.2 11.9 %collective-permute-start.15 = (bf16[4,16,2176]{2,1,0:T(8,128)(2,1)S(1)}, bf16[4,16,2176]{2,1,0:T(8,128)(2,1)S(1)}, u32[]{:S(2)}, u32[]{:S(2)}) collective-permute-start(bf16[4,16,2176]{2,1,0:T(8,128)(2,1)S(1)} %get-tuple-element.46), channel_id=1, source_target_pairs={{0,16},{8,24},{16,0},{24,8},{1,17},{9,25},{17,1},{25,9},{2,18},{10... | collective-permute-start | bytes 835592 | tf_op jit(solution)/shard_map/ppermute | solution.py:85
  181.3 2.8 %collective-permute-start.16 = (bf16[4,4,16,2176]{3,2,1,0:T(8,128)(2,1)S(1)}, bf16[4,4,16,2176]{3,2,1,0:T(8,128)(2,1)S(1)}, u32[]{:S(2)}, u32[]{:S(2)}) collective-permute-start(bf16[4,4,16,2176]{3,2,1,0:T(8,128)(2,1)S(1)} %pad_maximum_fusion.near_ref), channel_id=1, source_target_pairs={{0,32},{32,0},{1,33},{33,1},{2,34},{34,2},{3,35},{35,3},{4,36},{36... | collective-permute-start | bytes 3342344 | tf_op jit(solution)/shard_map/ppermute | solution.py:380
  190.7 45.9 %all-to-all-start.4 = ((bf16[32,128,384]{2,1,0:T(8,128)(2,1)}), bf16[32,128,384]{2,1,0:T(8,128)(2,1)S(1)}, u32[]{:S(2)}, u32[]{:S(2)}) async-start(bf16[32,128,384]{2,1,0:T(8,128)(2,1)} %bitcast.117), calls=%async_computation.4 | async-start | bytes 6291456 | tf_op jit(solution)/shard_map/all_to_all | solution.py:401
  198.1 8.9 %collective-permute-start.17 = (f32[1,384]{1,0:T(1,128)S(1)}, f32[1,384]{1,0:T(1,128)S(1)}, u32[]{:S(2)}, u32[]{:S(2)}) collective-permute-start(f32[1,384]{1,0:T(1,128)S(1)} %constant_dynamic-slice_fusion.gain_ref), channel_id=1, source_target_pairs={{0,0},{1,33},{2,66},{3,99},{4,132},{5,165},{6,198},{7,231},{32,1},... | collective-permute-start | bytes 4616 | tf_op jit(solution)/shard_map/ppermute | solution.py:312
  236.7 30.0 %all-to-all-start.5 = ((f32[256,1,128]{2,1,0:T(1,128)}), f32[256,1,128]{2,1,0:T(1,128)S(1)}, u32[]{:S(2)}, u32[]{:S(2)}) async-start(f32[256,1,128]{2,1,0:T(1,128)} %bitcast.58), calls=%async_computation.6 | async-start | bytes 262144 | tf_op jit(solution)/shard_map/all_to_all | solution.py:416
  246.8 19.2 %collective-permute-start.18 = (bf16[128,768]{1,0:T(8,128)(2,1)}, bf16[128,768]{1,0:T(8,128)(2,1)S(1)}, u32[]{:S(2)}, u32[]{:S(2)}) collective-permute-start(bf16[128,768]{1,0:T(8,128)(2,1)} %bitcast.112), channel_id=1, source_target_pairs={{0,0},{33,1},{66,2},{99,3},{132,4},{165,5},{198,6},{231,7},{1,32},... | collective-permute-start | bytes 589832 | tf_op jit(solution)/shard_map/ppermute | solution.py:412
  253.0 13.6 %copy-start.2 = (f32[1,384,128]{2,1,0:T(8,128)S(1)}, f32[1,384,128]{2,1,0:T(8,128)}, u32[]{:S(2)}) copy-start(f32[1,384,128]{2,1,0:T(8,128)} %refs_0_.1) | copy-start | bytes 589828
  266.7 0.9 copy-start.4
  (11 other events, 9.6 us)
Sparse Core Ops, SparseCore 0:
  25.8 45.8 all-gather.2
  190.9 39.1 reduce-scatter.1

commit v3 on v2

--- a/solution.py
+++ b/solution.py
@@ -25,6 +25,7 @@
 PLANE = ("x", "c", "y")
 EVERYONE = ("x", "c", "y", "z")
 SHIFTS = (0, 1, -1, 2)
+TURNS = (0, 4, 3, 7, 2, 6, 1, 5)
 VMEM_BYTES = 48 * 1024 * 1024
 
 
@@ -105,7 +106,7 @@
     piece = half // (2 * columns)
     core, section = place_ref[0], place_ref[1]
     for layer in range(layers):
-        weight = weight_ref[lax.rem(section + layer, layers)]
+        weight = weight_ref[lax.rem(section + TURNS[layer], layers)]
         base = layer * 3 * rank
         for group in range(groups):
             first = dot_nn(rows_ref[group, :half, :], weight).astype(LOW)
@@ -222,7 +223,7 @@
                 coef_ref[dest, :] = coded_ref[slot_y, slot_x, :, 2 * span :].astype(WIDE)
 
     for layer in range(layers):
-        up_weight = weight_ref[lax.rem(section + layer, layers), :, rank:]
+        up_weight = weight_ref[lax.rem(section + TURNS[layer], layers), :, rank:]
         act = act_ref[:, layer * rank : (layer + 1) * rank]
         total = wide_ref[...] + dot_nt(act, up_weight)
         wide_ref[...] = total
@@ -234,7 +235,7 @@
         base = group * half
         wide_ref[base : base + half, :] = rows_ref[group, half:, :].astype(WIDE)
     for layer in reversed(range(layers)):
-        slot = lax.rem(section + layer, layers)
+        slot = lax.rem(section + TURNS[layer], layers)
         delta = wide_ref[...].astype(LOW)
         act = act_ref[:, layer * rank : (layer + 1) * rank]
         moved = moved_ref[:, layer * rank : (layer + 1) * rank]
@@ -300,7 +301,11 @@
     features, rank = master_in.shape[1:]
     piece = tok_rows // layers
     swap_core = [(0, 1), (1, 0)]
-    route = [(a * count_z + b, b * count_z + (a + b) % count_z) for a in range(layers) for b in range(count_z)]
+    route = [
+        (a * count_z + b, b * count_z + (b + TURNS[a]) % count_z)
+        for a in range(layers)
+        for b in range(count_z)
+    ]
     back_route = [(j, i) for i, j in route]
     across = SECTION + ("z",)
 
@@ -309,7 +314,8 @@
         pack_kernel, jax.ShapeDtypeStruct((features, 2 * rank), LOW), (gain_own, master_in, master_out)
     )
     swapped = lax.ppermute(packed, across, route)
-    gain_swapped = lax.ppermute(gain_own, across, route)
+    lined = lax.all_gather(packed, SECTION, axis=0)
+    swapped, lined = lax.optimization_barrier((swapped, lined))
     weights = lax.all_gather(swapped, "z", axis=0)
 
     def blocks_of(rows):
@@ -326,30 +332,22 @@
     square = jnp.sum(own_rows * own_rows, axis=-1, keepdims=True)
     square = jnp.broadcast_to(square, (piece, 128))
 
-    lined = gather_line(packed, "x")
-    lined = jnp.stack([lined, lax.ppermute(lined, "c", swap_core)])
     cross = lax.dot_general(
-        packed[:, rank:], lined, (((0,), (2,)), ((), ())), preferred_element_type=WIDE
-    )
-    cross = cross.transpose(1, 2, 0, 3)
-    ordered = []
-    for layer in range(layers):
-        owner, from_core = divmod(layer, count_c)
-        away = lax.rem(pos_x - owner + count_x, count_x)
-        slot = jnp.where(away == count_x - 1, 2, jnp.where(away == 2, 3, away))
-        block = lax.dynamic_slice(
-            cross, (lax.rem(pos_c + from_core, 2), slot, 0, 0), (1, 1, rank, 2 * rank)
-        )[0, 0]
-        ordered.append(jnp.where(layer > pos_s, block[:, :rank], block[:, rank:]).astype(LOW))
+        packed[:, rank:], lined, (((0,), (1,)), ((), ())), preferred_element_type=WIDE
+    )
+    later = (jnp.arange(layers) > pos_s)[None, :, None]
+    cross = jnp.where(later, cross[..., :rank], cross[..., rank:]).astype(LOW)
     cut_r, cut_c = rank // count_z, layers * rank // count_y
-    cross = jnp.stack(ordered, axis=1).reshape(count_z, cut_r, count_y, cut_c)
+    cross = cross.reshape(count_z, cut_r, count_y, cut_c)
     cross = cross.transpose(2, 0, 1, 3).reshape(count_y * count_z, cut_r, cut_c)
+    cross, rows = lax.optimization_barrier((cross, rows))
     cross = lax.all_to_all(cross, ("y", "z"), 0, 0, tiled=True)
     cross = jnp.sum(cross.astype(WIDE), axis=0, keepdims=True).astype(LOW)
     cross = jnp.broadcast_to(cross, (count_y * count_z, cut_r, cut_c))
     cross = lax.all_to_all(cross, ("y", "z"), 0, 0, tiled=True)
     cross = cross.reshape(count_y, count_z, cut_r, cut_c).transpose(1, 2, 0, 3)
     cross = cross.reshape(rank, layers * rank)
+    cross, rows = lax.optimization_barrier((cross, rows))
     cross_near = gather_line(cross, "x")
     cross_far = lax.ppermute(cross_near, "c", swap_core)
 
@@ -411,7 +409,7 @@
 
     own_grads = lax.ppermute(grads, across, back_route)
     squares = local_call(
-        square_kernel, jax.ShapeDtypeStruct((sources * count_z, 128), WIDE), (gain_swapped, grads)
+        square_kernel, jax.ShapeDtypeStruct((sources * count_z, 128), WIDE), (gain_own, own_grads)
     )
     squares = lax.all_to_all(squares, EVERYONE, 0, 0, tiled=True)
     norm_limit = clip_rms * math.sqrt(2.0 * model_width * rank * layers)

time: 283 us -> 282 us (level)
  waiting for transfers between devices: 131 us -> 146 us
  starting transfers between devices: 71.4 us -> 57.7 us
    all_gather x0 -> x1, waiting for transfers between devices: none -> 16.7 us  [shards(): lined = lax.all_gather(packed, SECTION, axis=0)]
    all_to_all x1, waiting for transfers between devices: 0.01 us -> 9.65 us  [shards(): squares = lax.all_to_all(squares, EVERYONE, 0, 0, tiled=True)]
    all_gather x1, waiting for transfers between devices: 9.13 us -> 0.02 us  [shards(): weights = lax.all_gather(swapped, 'z', axis=0)]
    ppermute x12 -> x9, starting transfers between devices: 21.7 us -> 12.9 us  [shifted(): lax.ppermute(block, axis, [(i, (i + distance) % size) for i in range(size)])]
    reduce_scatter x1, waiting for transfers between devices: 23.1 us -> 29.9 us  [shards(): grads = lax.psum_scatter(grads, 'z', scatter_dimension=0, tiled=True)[0]]
    ppermute x2 -> x0, starting transfers between devices: 4.93 us -> none  [the longest x1 4.83 us: shards(): gain_swapped = lax.ppermute(gain_own, across, route)]
    all_to_all x1, waiting for transfers between devices: 4.82 us -> 0.01 us  [shards(): outputs = lax.all_to_all(outputs, PLANE, 0, 0, tiled=True)]
    ppermute x1, waiting for transfers between devices: 9.8 us -> 5.23 us  [shards(): swapped = lax.ppermute(packed, across, route)]
  transfers between devices with their start and end apart: 26 -> 22, of which waited for: 20 -> 17; matrix products, arithmetic and copies ran while one was open for 4% -> 3% of each run, Pallas kernels for 1% -> 1%
where the time goes in v3:
time: 282 us; the launch traced here: 279 us
  waiting for transfers between devices  146 us (52%)
  starting transfers between devices  57.7 us (20%)
  blocking collectives  22 us (8%)
  Pallas kernels  19 us (7%)
  between operations  14 us (5%)
  local copies, waits for them, and re-layouts  13 us (5%)
  other arithmetic  5.45 us (2%)
    ppermute x9, waiting for transfers between devices, shifted(): lax.ppermute(block, axis, [(i, (i + distance) % size) for i in range(size)])  42.2 us
    reduce_scatter x1, waiting for transfers between devices, shards(): grads = lax.psum_scatter(grads, 'z', scatter_dimension=0, tiled=True)[0]  29.9 us
    all_to_all x1, blocking collectives, shards(): cross = lax.all_to_all(cross, ('y', 'z'), 0, 0, tiled=True)  22 us
    all_gather x1, waiting for transfers between devices, shards(): lined = lax.all_gather(packed, SECTION, axis=0)  16.7 us
    pallas_call x6, Pallas kernels, local_call(): pl.pallas_call(kernel, out_shape=out_shape, in_specs=in_specs, out_specs=...  16.6 us
    all_to_all x1, starting transfers between devices, shards(): squares = lax.all_to_all(squares, EVERYONE, 0, 0, tiled=True)  14.2 us
    ppermute x1, waiting for transfers between devices, shards(): own_grads = lax.ppermute(grads, across, back_route)  12.9 us
    ppermute x9, starting transfers between devices, shifted(): lax.ppermute(block, axis, [(i, (i + distance) % size) for i in range(size)])  12.9 us
  transfers between devices with their start and end apart: 22, of which 17 were waited for; matrix products, arithmetic and copies ran while one was open for 3% of the time, Pallas kernels for 1%

profile of v3, /device:TPU:2, one launch (start us, length us, event | category | flops | bytes accessed | tf_op | source)
XLA Modules:
  0.0 279.0 jit_solution(16417088820021118163)
XLA Ops:
  10.7 6.5 %collective-permute-start = (bf16[384,256]{1,0:T(8,128)(2,1)}, bf16[384,256]{1,0:T(8,128)(2,1)S(1)}, u32[]{:S(2)}, u32[]{:S(2)}) collective-permute-start(bf16[384,256]{1,0:T(8,128)(2,1)} %shard_map.144), channel_id=1, source_target_pairs={{0,0},{1,33},{2,66},{3,99},{4,132},{5,165},{6,198},{7,231},{32,4},... | collective-permute-start | bytes 589832 | tf_op jit(solution)/shard_map/ppermute | solution.py:316
  17.3 5.2 %collective-permute-done = bf16[384,256]{1,0:T(8,128)(2,1)S(1)} collective-permute-done((bf16[384,256]{1,0:T(8,128)(2,1)}, bf16[384,256]{1,0:T(8,128)(2,1)S(1)}, u32[]{:S(2)}, u32[]{:S(2)}) %collective-permute-start) | collective-permute-done | bytes 196640 | tf_op jit(solution)/shard_map/ppermute | solution.py:316
  22.5 16.7 %all-gather.5.cloned.1.call-done = bf16[3072,256]{1,0:T(8,128)(2,1)} async-done(((bf16[384,256]{1,0:T(8,128)(2,1)}), bf16[3072,256]{1,0:T(8,128)(2,1)}) %all-gather.5.cloned.1.call-update) | async-done | bytes 1572880 | tf_op jit(solution)/shard_map/all_gather | solution.py:317
  41.6 4.3 %all-to-all-start = ((bf16[4,256,384]{2,1,0:T(8,128)(2,1)}), bf16[4,256,384]{2,1,0:T(8,128)(2,1)S(1)}, u32[]{:S(2)}, u32[]{:S(2)}) async-start(bf16[4,256,384]{2,1,0:T(8,128)(2,1)} %maximum_maximum_fusion), calls=%async_computation | async-start | bytes 1572864 | tf_op jit(solution)/shard_map/all_to_all | solution.py:330
  47.7 10.8 %all-to-all-done.rows_ref = bf16[4,256,384]{2,1,0:T(8,128)(2,1)S(1)} async-done(((bf16[4,256,384]{2,1,0:T(8,128)(2,1)}), bf16[4,256,384]{2,1,0:T(8,128)(2,1)S(1)}, u32[]{:S(2)}, u32[]{:S(2)}) %all-to-all-start) | async-done | bytes 786464 | tf_op jit(solution)/shard_map/all_to_all | solution.py:330
  58.6 22.0 %all_to_all.36 = bf16[32,16,256]{2,1,0:T(8,128)(2,1)S(1)} all-to-all(bf16[32,16,256]{2,1,0:T(8,128)(2,1)S(1)} %bitcast.67), channel_id=1, replica_groups=mesh['x'=4,'c'=2,'y'=4,'z'=8] {'y','z'}, dimensions={0} | all-to-all | bytes 524288 | tf_op jit(solution)/shard_map/all_to_all | solution.py:344
  81.3 5.4 %all-to-all-start.2 = ((bf16[32,16,256]{2,1,0:T(8,128)(2,1)}), bf16[32,16,256]{2,1,0:T(8,128)(2,1)S(1)}, u32[]{:S(2)}, u32[]{:S(2)}) async-start(bf16[32,16,256]{2,1,0:T(8,128)(2,1)} %broadcast_in_dim.15), calls=%async_computation.2 | async-start | bytes 524288 | tf_op jit(solution)/shard_map/all_to_all | solution.py:347
  86.9 11.2 %all-to-all-done.2 = bf16[32,16,256]{2,1,0:T(8,128)(2,1)S(1)} async-done(((bf16[32,16,256]{2,1,0:T(8,128)(2,1)}), bf16[32,16,256]{2,1,0:T(8,128)(2,1)S(1)}, u32[]{:S(2)}, u32[]{:S(2)}) %all-to-all-start.2) | async-done | bytes 262176 | tf_op jit(solution)/shard_map/all_to_all | solution.py:347
  99.9 2.8 %shard_map.145 = (bf16[4,4,16,3072]{3,2,1,0:T(8,128)(2,1)S(1)}, bf16[4,4,16,3072]{3,2,1,0:T(8,128)(2,1)S(1)}) custom-call(s32[4]{0:T(128)S(1)} %pad_add_fusion.place_ref, bf16[4,256,384]{2,1,0:T(8,128)(2,1)S(1)} %all-to-all-done.rows_ref, bf16[8,384,256]{2,1,0:T(8,128)(2,1)S(1)} %bitcast.60), custom_call_target="tpu_custom_call" | custom-call | flops 1207959552 | bytes 5505024 | tf_op jit(solution)/shard_map/pallas_call | solution.py:73
  102.8 3.4 %collective-permute-done.1 = bf16[4,4,16,3072]{3,2,1,0:T(8,128)(2,1)S(1)} collective-permute-done((bf16[4,4,16,3072]{3,2,1,0:T(8,128)(2,1)S(1)}, bf16[4,4,16,3072]{3,2,1,0:T(8,128)(2,1)S(1)}, u32[]{:S(2)}, u32[]{:S(2)}) %collective-permute-start.1) | collective-permute-done | bytes 1572896 | tf_op jit(solution)/shard_map/ppermute | solution.py:362
  106.2 1.7 add_convert_fusion
  107.9 6.3 %all-to-all-start.3 = ((bf16[16,16,3072]{2,1,0:T(8,128)(2,1)}), bf16[16,16,3072]{2,1,0:T(8,128)(2,1)S(1)}, u32[]{:S(2)}, u32[]{:S(2)}) async-start(bf16[16,16,3072]{2,1,0:T(8,128)(2,1)} %bitcast.62), calls=%async_computation.3 | async-start | bytes 3145728 | tf_op jit(solution)/shard_map/all_to_all | solution.py:365
  114.3 2.2 collective-permute-start.4
  118.5 22.4 %collective-permute-done.4 = bf16[128,1024]{1,0:T(8,128)(2,1)S(1)} collective-permute-done((bf16[128,1024]{1,0:T(8,128)(2,1)S(1)}, bf16[128,1024]{1,0:T(8,128)(2,1)S(1)}, u32[]{:S(2)}, u32[]{:S(2)}) %collective-permute-start.4) | collective-permute-done | bytes 262176 | tf_op jit(solution)/shard_map/ppermute | solution.py:86
  140.9 3.6 %collective-permute-done.3 = bf16[128,1024]{1,0:T(8,128)(2,1)S(1)} collective-permute-done((bf16[128,1024]{1,0:T(8,128)(2,1)S(1)}, bf16[128,1024]{1,0:T(8,128)(2,1)S(1)}, u32[]{:S(2)}, u32[]{:S(2)}) %collective-permute-start.3) | collective-permute-done | bytes 262176 | tf_op jit(solution)/shard_map/ppermute | solution.py:86
  148.5 4.8 %shard_map.146 = bf16[16,2176]{1,0:T(8,128)(2,1)S(1)} custom-call(s32[4]{0:T(128)S(1)} %pad_add_fusion.place_ref, bf16[16,16,3072]{2,1,0:T(8,128)(2,1)S(1)} %all-to-all-done.3.parts_ref, f32[16,128]{1,0:T(8,128)S(1)} %broadcast_in_dim.26.square_ref, bf16[4,128,1024]{2,1,0:T(8,128)(2,1)S(1)} %pad_maximum_fusion.1.near_ref, ...), custom_call_target="tpu_custom_call" | custom-call | bytes 3747840 | tf_op jit(solution)/shard_map/pallas_call | solution.py:73
  153.3 1.7 collective-permute-start.8
  155.0 1.9 collective-permute-start.7
  157.0 2.8 %collective-permute-done.8 = bf16[16,2176]{1,0:T(8,128)(2,1)S(1)} collective-permute-done((bf16[16,2176]{1,0:T(8,128)(2,1)S(1)}, bf16[16,2176]{1,0:T(8,128)(2,1)S(1)}, u32[]{:S(2)}, u32[]{:S(2)}) %collective-permute-start.8) | collective-permute-done | bytes 69664 | tf_op jit(solution)/shard_map/ppermute | solution.py:86
  161.3 2.6 collective-permute-start.10
  163.9 2.3 collective-permute-start.11
  166.2 8.7 %collective-permute-done.10 = bf16[4,16,2176]{2,1,0:T(8,128)(2,1)S(1)} collective-permute-done((bf16[4,16,2176]{2,1,0:T(8,128)(2,1)S(1)}, bf16[4,16,2176]{2,1,0:T(8,128)(2,1)S(1)}, u32[]{:S(2)}, u32[]{:S(2)}) %collective-permute-start.10) | collective-permute-done | bytes 278560 | tf_op jit(solution)/shard_map/ppermute | solution.py:86
  174.9 3.4 %collective-permute-done.9 = bf16[4,16,2176]{2,1,0:T(8,128)(2,1)S(1)} collective-permute-done((bf16[4,16,2176]{2,1,0:T(8,128)(2,1)S(1)}, bf16[4,16,2176]{2,1,0:T(8,128)(2,1)S(1)}, u32[]{:S(2)}, u32[]{:S(2)}) %collective-permute-start.9) | collective-permute-done | bytes 278560 | tf_op jit(solution)/shard_map/ppermute | solution.py:86
  178.6 2.7 collective-permute-done.12.far_ref
  181.3 6.6 %shard_map.147 = (bf16[8,4,128,384]{3,2,1,0:T(8,128)(2,1)}, bf16[8,128,768]{2,1,0:T(8,128)(2,1)}) custom-call(s32[4]{0:T(128)S(1)} %pad_add_fusion.place_ref, bf16[4,256,384]{2,1,0:T(8,128)(2,1)S(1)} %all-to-all-done.rows_ref, bf16[8,384,256]{2,1,0:T(8,128)(2,1)S(1)} %bitcast.61, bf16[4,4,16,2176]{3,2,1,0:T(8,128)(2,1)S(1)} %pad_maximum_fusion.near_ref, ...), custom_call_target="tpu_custom_call" | custom-call | flops 1610612736 | bytes 9306112 | tf_op jit(solution)/shard_map/pallas_call | solution.py:73
  187.9 5.8 %all-to-all-start.4 = ((bf16[32,128,384]{2,1,0:T(8,128)(2,1)}), bf16[32,128,384]{2,1,0:T(8,128)(2,1)S(1)}, u32[]{:S(2)}, u32[]{:S(2)}) async-start(bf16[32,128,384]{2,1,0:T(8,128)(2,1)} %bitcast.63), calls=%async_computation.4 | async-start | bytes 6291456 | tf_op jit(solution)/shard_map/all_to_all | solution.py:399
  193.7 29.9 %reduce-scatter.2.cloned.1.call-done = bf16[1,128,768]{2,1,0:T(8,128)(2,1)} async-done(((bf16[8,128,768]{2,1,0:T(8,128)(2,1)}), bf16[1,128,768]{2,1,0:T(8,128)(2,1)}) %reduce-scatter.2.cloned.1.call-update) | async-done | bytes 196624 | tf_op jit(solution)/shard_map/reduce_scatter | solution.py:397
  223.6 1.9 collective-permute-start.13
  225.5 12.9 %collective-permute-done.13.grad_ref = bf16[128,768]{1,0:T(8,128)(2,1)S(1)} collective-permute-done((bf16[128,768]{1,0:T(8,128)(2,1)}, bf16[128,768]{1,0:T(8,128)(2,1)S(1)}, u32[]{:S(2)}, u32[]{:S(2)}) %collective-permute-start.13) | collective-permute-done | bytes 196640 | tf_op jit(solution)/shard_map/ppermute | solution.py:410
  239.3 14.2 %all-to-all-start.5 = ((f32[256,1,128]{2,1,0:T(1,128)}), f32[256,1,128]{2,1,0:T(1,128)S(1)}, u32[]{:S(2)}, u32[]{:S(2)}) async-start(f32[256,1,128]{2,1,0:T(1,128)} %bitcast.58), calls=%async_computation.6 | async-start | bytes 262144 | tf_op jit(solution)/shard_map/all_to_all | solution.py:414
  253.5 2.4 shard_map.148
  255.9 9.7 %all-to-all-done.5 = f32[256,1,128]{2,1,0:T(1,128)S(1)} async-done(((f32[256,1,128]{2,1,0:T(1,128)}), f32[256,1,128]{2,1,0:T(1,128)S(1)}, u32[]{:S(2)}, u32[]{:S(2)}) %all-to-all-start.5) | async-done | bytes 131104 | tf_op jit(solution)/shard_map/all_to_all | solution.py:414
  (73 shorter events, 26.1 us)
Async XLA Ops:
  7.2 32.0 %all-gather.5.cloned.1.call-start = ((), (), s32[]{:S(2)}) async-start(), calls=%async_computation.8 | async-start | bytes 1769472 | tf_op jit(solution)/shard_map/all_gather | solution.py:317
  8.0 0.9 copy-start.1
  8.9 0.9 copy-start.3
  10.7 87.7 %all-gather.7.cloned.1.call-start = ((), (), s32[]{:S(2)}) async-start(), calls=%async_computation.9 | async-start | bytes 1769472 | tf_op jit(solution)/shard_map/all_gather | solution.py:319
  10.7 11.7 %collective-permute-start = (bf16[384,256]{1,0:T(8,128)(2,1)}, bf16[384,256]{1,0:T(8,128)(2,1)S(1)}, u32[]{:S(2)}, u32[]{:S(2)}) collective-permute-start(bf16[384,256]{1,0:T(8,128)(2,1)} %shard_map.144), channel_id=1, source_target_pairs={{0,0},{1,33},{2,66},{3,99},{4,132},{5,165},{6,198},{7,231},{32,4},... | collective-permute-start | bytes 589832 | tf_op jit(solution)/shard_map/ppermute | solution.py:316
  22.5 16.7 %copy-start.14 = (bf16[384,256]{1,0:T(8,128)(2,1)}, bf16[384,256]{1,0:T(8,128)(2,1)S(1)}, u32[]{:S(2)}) copy-start(bf16[384,256]{1,0:T(8,128)(2,1)S(1)} %collective-permute-done) | copy-start | bytes 589828
  40.6 5.3 %copy-start.12 = (bf16[3072,256]{1,0:T(8,128)(2,1)S(1)}, bf16[3072,256]{1,0:T(8,128)(2,1)}, u32[]{:S(2)}) copy-start(bf16[3072,256]{1,0:T(8,128)(2,1)} %all-gather.5.cloned.1.call-done) | copy-start | bytes 4718596
  41.6 17.0 %all-to-all-start = ((bf16[4,256,384]{2,1,0:T(8,128)(2,1)}), bf16[4,256,384]{2,1,0:T(8,128)(2,1)S(1)}, u32[]{:S(2)}, u32[]{:S(2)}) async-start(bf16[4,256,384]{2,1,0:T(8,128)(2,1)} %maximum_maximum_fusion), calls=%async_computation | async-start | bytes 1572864 | tf_op jit(solution)/shard_map/all_to_all | solution.py:330
  81.3 16.8 %all-to-all-start.2 = ((bf16[32,16,256]{2,1,0:T(8,128)(2,1)}), bf16[32,16,256]{2,1,0:T(8,128)(2,1)S(1)}, u32[]{:S(2)}, u32[]{:S(2)}) async-start(bf16[32,16,256]{2,1,0:T(8,128)(2,1)} %broadcast_in_dim.15), calls=%async_computation.2 | async-start | bytes 524288 | tf_op jit(solution)/shard_map/all_to_all | solution.py:347
  98.3 19.6 %copy-start.13 = (bf16[16,8,4,256]{3,1,2,0:T(8,128)(2,1)}, bf16[16,8,4,256]{3,1,2,0:T(8,128)(2,1)S(1)}, u32[]{:S(2)}) copy-start(bf16[16,8,4,256]{3,1,2,0:T(8,128)(2,1)S(1)} %copy.28) | copy-start | bytes 786436
  98.4 1.5 copy-start.10
  102.7 3.5 %collective-permute-start.1 = (bf16[4,4,16,3072]{3,2,1,0:T(8,128)(2,1)S(1)}, bf16[4,4,16,3072]{3,2,1,0:T(8,128)(2,1)S(1)}, u32[]{:S(2)}, u32[]{:S(2)}) collective-permute-start(bf16[4,4,16,3072]{3,2,1,0:T(8,128)(2,1)S(1)} %get-tuple-element.29), channel_id=1, source_target_pairs={{0,32},{32,0},{1,33},{33,1},{2,34},{34,2},{3,35},{35,3},{4,36},{36... | collective-permute-start | bytes 4718600 | tf_op jit(solution)/shard_map/ppermute | solution.py:362
  107.9 40.5 %all-to-all-start.3 = ((bf16[16,16,3072]{2,1,0:T(8,128)(2,1)}), bf16[16,16,3072]{2,1,0:T(8,128)(2,1)S(1)}, u32[]{:S(2)}, u32[]{:S(2)}) async-start(bf16[16,16,3072]{2,1,0:T(8,128)(2,1)} %bitcast.62), calls=%async_computation.3 | async-start | bytes 3145728 | tf_op jit(solution)/shard_map/all_to_all | solution.py:365
  114.2 109.3 %reduce-scatter.2.cloned.1.call-start = ((), (), s32[]{:S(2)}) async-start(), calls=%async_computation.7 | async-start | bytes 1769472 | tf_op jit(solution)/shard_map/reduce_scatter | solution.py:397
  114.3 26.6 %collective-permute-start.4 = (bf16[128,1024]{1,0:T(8,128)(2,1)S(1)}, bf16[128,1024]{1,0:T(8,128)(2,1)S(1)}, u32[]{:S(2)}, u32[]{:S(2)}) collective-permute-start(bf16[128,1024]{1,0:T(8,128)(2,1)S(1)} %bitcast.70), channel_id=1, source_target_pairs={{0,128},{64,192},{128,0},{192,64},{1,129},{65,193},{129,1},{193,65... | collective-permute-start | bytes 786440 | tf_op jit(solution)/shard_map/ppermute | solution.py:86
  116.5 28.0 %collective-permute-start.3 = (bf16[128,1024]{1,0:T(8,128)(2,1)S(1)}, bf16[128,1024]{1,0:T(8,128)(2,1)S(1)}, u32[]{:S(2)}, u32[]{:S(2)}) collective-permute-start(bf16[128,1024]{1,0:T(8,128)(2,1)S(1)} %bitcast.71), channel_id=1, source_target_pairs={{0,192},{64,0},{128,64},{192,128},{1,193},{65,1},{129,65},{193,129... | collective-permute-start | bytes 786440 | tf_op jit(solution)/shard_map/ppermute | solution.py:86
  117.9 26.5 %collective-permute-start.2 = (bf16[128,1024]{1,0:T(8,128)(2,1)S(1)}, bf16[128,1024]{1,0:T(8,128)(2,1)S(1)}, u32[]{:S(2)}, u32[]{:S(2)}) collective-permute-start(bf16[128,1024]{1,0:T(8,128)(2,1)S(1)} %bitcast.72), channel_id=1, source_target_pairs={{0,64},{64,128},{128,192},{192,0},{1,65},{65,129},{129,193},{193,1... | collective-permute-start | bytes 786440 | tf_op jit(solution)/shard_map/ppermute | solution.py:86
  145.5 2.9 %collective-permute-start.5 = (bf16[4,128,1024]{2,1,0:T(8,128)(2,1)S(1)}, bf16[4,128,1024]{2,1,0:T(8,128)(2,1)}, u32[]{:S(2)}, u32[]{:S(2)}) collective-permute-start(bf16[4,128,1024]{2,1,0:T(8,128)(2,1)S(1)} %pad_maximum_fusion.1.near_ref), channel_id=1, source_target_pairs={{0,32},{32,0},{1,33},{33,1},{2,34},{34,2},{3,35},{35,3},{4,36},{36... | collective-permute-start | bytes 3145736 | tf_op jit(solution)/shard_map/ppermute | solution.py:352
  153.3 28.0 %copy-start.11 = (bf16[3072,256]{1,0:T(8,128)(2,1)S(1)}, bf16[3072,256]{1,0:T(8,128)(2,1)}, u32[]{:S(2)}) copy-start(bf16[3072,256]{1,0:T(8,128)(2,1)} %all-gather.7.cloned.1.call-done) | copy-start | bytes 4718596
  153.3 6.6 %collective-permute-start.8 = (bf16[16,2176]{1,0:T(8,128)(2,1)S(1)}, bf16[16,2176]{1,0:T(8,128)(2,1)S(1)}, u32[]{:S(2)}, u32[]{:S(2)}) collective-permute-start(bf16[16,2176]{1,0:T(8,128)(2,1)S(1)} %shard_map.146), channel_id=1, source_target_pairs={{0,128},{64,192},{128,0},{192,64},{1,129},{65,193},{129,1},{193,65... | collective-permute-start | bytes 208904 | tf_op jit(solution)/shard_map/ppermute | solution.py:86
  155.0 5.4 %collective-permute-start.7 = (bf16[16,2176]{1,0:T(8,128)(2,1)S(1)}, bf16[16,2176]{1,0:T(8,128)(2,1)S(1)}, u32[]{:S(2)}, u32[]{:S(2)}) collective-permute-start(bf16[16,2176]{1,0:T(8,128)(2,1)S(1)} %shard_map.146), channel_id=1, source_target_pairs={{0,192},{64,0},{128,64},{192,128},{1,193},{65,1},{129,65},{193,129... | collective-permute-start | bytes 208904 | tf_op jit(solution)/shard_map/ppermute | solution.py:86
  156.9 4.3 %collective-permute-start.6 = (bf16[16,2176]{1,0:T(8,128)(2,1)S(1)}, bf16[16,2176]{1,0:T(8,128)(2,1)S(1)}, u32[]{:S(2)}, u32[]{:S(2)}) collective-permute-start(bf16[16,2176]{1,0:T(8,128)(2,1)S(1)} %shard_map.146), channel_id=1, source_target_pairs={{0,64},{64,128},{128,192},{192,0},{1,65},{65,129},{129,193},{193,1... | collective-permute-start | bytes 208904 | tf_op jit(solution)/shard_map/ppermute | solution.py:86
  161.3 13.6 %collective-permute-start.10 = (bf16[4,16,2176]{2,1,0:T(8,128)(2,1)S(1)}, bf16[4,16,2176]{2,1,0:T(8,128)(2,1)S(1)}, u32[]{:S(2)}, u32[]{:S(2)}) collective-permute-start(bf16[4,16,2176]{2,1,0:T(8,128)(2,1)S(1)} %get-tuple-element.48), channel_id=1, source_target_pairs={{0,24},{8,0},{16,8},{24,16},{1,25},{9,1},{17,9},{25,17},{2,26},{10... | collective-permute-start | bytes 835592 | tf_op jit(solution)/shard_map/ppermute | solution.py:86
  163.9 14.3 %collective-permute-start.9 = (bf16[4,16,2176]{2,1,0:T(8,128)(2,1)S(1)}, bf16[4,16,2176]{2,1,0:T(8,128)(2,1)S(1)}, u32[]{:S(2)}, u32[]{:S(2)}) collective-permute-start(bf16[4,16,2176]{2,1,0:T(8,128)(2,1)S(1)} %get-tuple-element.48), channel_id=1, source_target_pairs={{0,8},{8,16},{16,24},{24,0},{1,9},{9,17},{17,25},{25,1},{2,10},{10... | collective-permute-start | bytes 835592 | tf_op jit(solution)/shard_map/ppermute | solution.py:86
  163.9 14.3 %collective-permute-start.11 = (bf16[4,16,2176]{2,1,0:T(8,128)(2,1)S(1)}, bf16[4,16,2176]{2,1,0:T(8,128)(2,1)S(1)}, u32[]{:S(2)}, u32[]{:S(2)}) collective-permute-start(bf16[4,16,2176]{2,1,0:T(8,128)(2,1)S(1)} %get-tuple-element.48), channel_id=1, source_target_pairs={{0,16},{8,24},{16,0},{24,8},{1,17},{9,25},{17,1},{25,9},{2,18},{10... | collective-permute-start | bytes 835592 | tf_op jit(solution)/shard_map/ppermute | solution.py:86
  178.4 2.8 %collective-permute-start.12 = (bf16[4,4,16,2176]{3,2,1,0:T(8,128)(2,1)S(1)}, bf16[4,4,16,2176]{3,2,1,0:T(8,128)(2,1)S(1)}, u32[]{:S(2)}, u32[]{:S(2)}) collective-permute-start(bf16[4,4,16,2176]{3,2,1,0:T(8,128)(2,1)S(1)} %pad_maximum_fusion.near_ref), channel_id=1, source_target_pairs={{0,32},{32,0},{1,33},{33,1},{2,34},{34,2},{3,35},{35,3},{4,36},{36... | collective-permute-start | bytes 3342344 | tf_op jit(solution)/shard_map/ppermute | solution.py:378
  187.9 51.4 %all-to-all-start.4 = ((bf16[32,128,384]{2,1,0:T(8,128)(2,1)}), bf16[32,128,384]{2,1,0:T(8,128)(2,1)S(1)}, u32[]{:S(2)}, u32[]{:S(2)}) async-start(bf16[32,128,384]{2,1,0:T(8,128)(2,1)} %bitcast.63), calls=%async_computation.4 | async-start | bytes 6291456 | tf_op jit(solution)/shard_map/all_to_all | solution.py:399
  223.6 14.9 %collective-permute-start.13 = (bf16[128,768]{1,0:T(8,128)(2,1)}, bf16[128,768]{1,0:T(8,128)(2,1)S(1)}, u32[]{:S(2)}, u32[]{:S(2)}) collective-permute-start(bf16[128,768]{1,0:T(8,128)(2,1)} %bitcast.83), channel_id=1, source_target_pairs={{0,0},{33,1},{66,2},{99,3},{132,4},{165,5},{198,6},{231,7},{4,32},... | collective-permute-start | bytes 589832 | tf_op jit(solution)/shard_map/ppermute | solution.py:410
  239.3 26.3 %all-to-all-start.5 = ((f32[256,1,128]{2,1,0:T(1,128)}), f32[256,1,128]{2,1,0:T(1,128)S(1)}, u32[]{:S(2)}, u32[]{:S(2)}) async-start(f32[256,1,128]{2,1,0:T(1,128)} %bitcast.58), calls=%async_computation.6 | async-start | bytes 262144 | tf_op jit(solution)/shard_map/all_to_all | solution.py:414
  265.6 0.9 copy-start.2
  266.5 0.9 copy-start.4
  270.2 0.9 copy-start.9
  (5 other events, 4.2 us)
Sparse Core Ops, SparseCore 0:
  10.8 28.3 all-gather.4
  41.6 44.5 all-gather.6
  188.0 35.5 reduce-scatter.1

commit v4 on v3

--- a/solution.py
+++ b/solution.py
@@ -96,6 +96,27 @@
     work_in = in_ref[0].astype(LOW).astype(WIDE)
     pack_ref[:, :rank] = (work_in * gain).astype(LOW)
     pack_ref[:, rank:] = out_ref[0].T.astype(LOW)
+
+
+def cross_kernel(rank, place_ref, own_ref, near_ref, far_ref, out_ref):
+    core, section, column = place_ref[0], place_ref[1], place_ref[2]
+    count = len(SHIFTS)
+    cut = out_ref.shape[1]
+    cuts = rank // cut
+    own = own_ref[:, rank:].T
+    for slot, step in enumerate(SHIFTS):
+        owner = lax.rem(column - step + count, count)
+        blocks = []
+        for line_ref, from_core in ((near_ref, core), (far_ref, 1 - core)):
+            both = dot_nn(own, line_ref[slot])
+            later = 2 * owner + from_core > section
+            blocks.append(jnp.where(later, both[:, :rank], both[:, rank:]).astype(LOW))
+        even = jnp.where(core == 0, blocks[0], blocks[1])
+        odd = jnp.where(core == 0, blocks[1], blocks[0])
+        for k in range(cuts):
+            sel = slice(k * cut, (k + 1) * cut)
+            out_ref[owner * cuts + k, :, :rank] = even[sel]
+            out_ref[owner * cuts + k, :, rank:] = odd[sel]
 
 
 def project_kernel(rank, place_ref, rows_ref, weight_ref, keep_ref, send_ref):
@@ -121,15 +142,20 @@
 
 
 def recursion_kernel(
-    layers, rank, width, place_ref, parts_ref, square_ref, near_ref, far_ref, out_ref, sums_ref, cross_ref
+    layers, rank, width, place_ref, parts_ref, square_ref, near_ref, far_ref, act_ref, moved_ref, sums_ref, cross_ref
 ):
     core, column = place_ref[0], place_ref[2]
     count = len(SHIFTS)
+    pieces, cut = near_ref.shape[1:3]
+    cuts = rank // cut
     for slot, distance in enumerate(SHIFTS):
         owner = lax.rem(column - distance + count, count)
         for piece_ref, from_core in ((near_ref, core), (far_ref, 1 - core)):
-            start = pl.multiple_of((2 * owner + from_core) * rank, rank)
-            cross_ref[pl.ds(start, rank), :] = piece_ref[slot]
+            start = (2 * owner + from_core) * rank
+            for k in range(pieces):
+                at = pl.multiple_of(start + (k % cuts) * cut, cut)
+                low = (k // cuts) * 2 * rank
+                cross_ref[pl.ds(at, cut), low : low + 2 * rank] = piece_ref[slot, k]
 
     total = parts_ref[0].astype(WIDE)
     for source in range(1, parts_ref.shape[0]):
@@ -150,7 +176,7 @@
         acts.append(act)
         pres.append(pre)
         invs.append(inv)
-        out_ref[:, s * rank : (s + 1) * rank] = act
+        act_ref[:, s * rank : (s + 1) * rank] = act
         low = s * rank
         forward = dot_nn(act, cross_ref[low : low + rank, low:])
         before = up[s]
@@ -171,7 +197,7 @@
         d_pre = (back[s] - trailing * up[s]) * slope
         coef = invs[s] * invs[s] * (1.0 / width) * jnp.sum(d_pre * pres[s], axis=-1, keepdims=True)
         moved = (invs[s] * d_pre).astype(LOW)
-        out_ref[:, (layers + s) * rank : (layers + s + 1) * rank] = moved
+        moved_ref[:, s * rank : (s + 1) * rank] = moved
         coef_high = coef.astype(LOW).astype(WIDE)
         tail = tail + jnp.where(lane == s, coef_high, 0.0)
         tail = tail + jnp.where(lane == s + layers, coef - coef_high, 0.0)
@@ -184,7 +210,7 @@
                 sel = slice(k * rank, (k + 1) * rank)
                 back[k] = back[k] + gain_term[:, sel] - norm_term[:, sel]
         trailing = trailing + coef
-    out_ref[:, 2 * layers * rank :] = tail.astype(LOW)
+    act_ref[:, layers * rank :] = tail.astype(LOW)
 
 
 def expand_kernel(
@@ -193,8 +219,10 @@
     place_ref,
     rows_ref,
     weight_ref,
-    near_ref,
-    far_ref,
+    act_near_ref,
+    act_far_ref,
+    move_near_ref,
+    move_far_ref,
     out_ref,
     grad_ref,
     wide_ref,
@@ -204,7 +232,7 @@
 ):
     groups, both_rows, features = rows_ref.shape
     half = both_rows // 2
-    piece = near_ref.shape[2]
+    piece = act_near_ref.shape[2]
     span = layers * rank
     core, section, column, line = (place_ref[i] for i in range(4))
     count = len(SHIFTS)
@@ -215,12 +243,15 @@
         group = lax.rem(line - step_y + count, count)
         for slot_x, step_x in enumerate(SHIFTS):
             owner = lax.rem(column - step_x + count, count)
-            for coded_ref, from_core in ((near_ref, core), (far_ref, 1 - core)):
+            for some_act, some_move, from_core in (
+                (act_near_ref, move_near_ref, core),
+                (act_far_ref, move_far_ref, 1 - core),
+            ):
                 at = pl.multiple_of(group * half + (2 * owner + from_core) * piece, piece)
                 dest = pl.ds(at, piece)
-                act_ref[dest, :] = coded_ref[slot_y, slot_x, :, :span]
-                moved_ref[dest, :] = coded_ref[slot_y, slot_x, :, span : 2 * span]
-                coef_ref[dest, :] = coded_ref[slot_y, slot_x, :, 2 * span :].astype(WIDE)
+                act_ref[dest, :] = some_act[slot_y, slot_x, :, :span]
+                coef_ref[dest, :] = some_act[slot_y, slot_x, :, span:].astype(WIDE)
+                moved_ref[dest, :] = some_move[slot_x, slot_y]
 
     for layer in range(layers):
         up_weight = weight_ref[lax.rem(section + TURNS[layer], layers), :, rank:]
@@ -250,34 +281,20 @@
             wide_ref[...] += dot_nt(moved, weight_ref[slot, :, :rank]) - coef * current.astype(WIDE)
 
 
-def square_kernel(gain_ref, grad_ref, out_ref):
+def settle_kernel(gain_ref, grad_ref, in_ref, out_ref, square_ref):
     features = gain_ref.shape[1]
     grad_in = grad_ref[:, :features].astype(WIDE) * gain_ref[...]
     grad_out = grad_ref[:, features:].astype(WIDE)
+    in_ref[...] = grad_in.T
+    out_ref[...] = grad_out
     total = jnp.sum(grad_in * grad_in) + jnp.sum(grad_out * grad_out)
-    out_ref[...] = jnp.full(out_ref.shape, total, WIDE)
+    square_ref[...] = jnp.full(square_ref.shape, total, WIDE)
 
 
 def order_kernel(block_ref, out_ref):
     layers, features = block_ref.shape[0], block_ref.shape[3]
     for layer in range(layers):
         out_ref[:, layer * features : (layer + 1) * features] = block_ref[layer, 0]
-
-
-def update_kernel(limit, sums_ref, gain_ref, grad_ref, *refs):
-    features = gain_ref.shape[1]
-    sources = refs[:6]
-    results = refs[6:]
-    total = jnp.sum(sums_ref[...], axis=0, keepdims=True)
-    clip = limit / jnp.maximum(jnp.sqrt(total), limit)
-    grad_in = (grad_ref[:, :features].astype(WIDE) * gain_ref[...]).T * clip
-    updated = adam_update(sources[0][0], sources[1][0], sources[2][0], grad_in)
-    for ref, value in zip(results[:3], updated):
-        ref[0] = value
-    grad_out = grad_ref[:, features:].astype(WIDE) * clip[:, 0:1]
-    updated = adam_update(sources[3][0], sources[4][0], sources[5][0], grad_out)
-    for ref, value in zip(results[3:], updated):
-        ref[0] = value
 
 
 def shards(
@@ -314,9 +331,8 @@
         pack_kernel, jax.ShapeDtypeStruct((features, 2 * rank), LOW), (gain_own, master_in, master_out)
     )
     swapped = lax.ppermute(packed, across, route)
-    lined = lax.all_gather(packed, SECTION, axis=0)
-    swapped, lined = lax.optimization_barrier((swapped, lined))
-    weights = lax.all_gather(swapped, "z", axis=0)
+    lined_near = gather_line(packed, "x")
+    lined_far = lax.ppermute(lined_near, "c", swap_core)
 
     def blocks_of(rows):
         return jnp.stack(
@@ -328,27 +344,25 @@
 
     rows = jnp.concatenate([blocks_of(stack_input), blocks_of(out_cotangent)], axis=1)
     rows = lax.all_to_all(rows, "y", 0, 0, tiled=True)
+    swapped, lined_near, lined_far, rows = lax.optimization_barrier((swapped, lined_near, lined_far, rows))
+    weights = lax.all_gather(swapped, "z", axis=0)
     own_rows = lax.dynamic_slice_in_dim(stack_input, pos_s * piece, piece, 0).astype(WIDE)
     square = jnp.sum(own_rows * own_rows, axis=-1, keepdims=True)
     square = jnp.broadcast_to(square, (piece, 128))
 
-    cross = lax.dot_general(
-        packed[:, rank:], lined, (((0,), (1,)), ((), ())), preferred_element_type=WIDE
-    )
-    later = (jnp.arange(layers) > pos_s)[None, :, None]
-    cross = jnp.where(later, cross[..., :rank], cross[..., rank:]).astype(LOW)
-    cut_r, cut_c = rank // count_z, layers * rank // count_y
-    cross = cross.reshape(count_z, cut_r, count_y, cut_c)
-    cross = cross.transpose(2, 0, 1, 3).reshape(count_y * count_z, cut_r, cut_c)
-    cross, rows = lax.optimization_barrier((cross, rows))
+    cut_r, cut_c = rank // count_z, count_c * rank
+    cross = local_call(
+        functools.partial(cross_kernel, rank),
+        jax.ShapeDtypeStruct((count_y * count_z, cut_r, cut_c), LOW),
+        (packed, lined_near, lined_far),
+        scalars=place,
+    )
     cross = lax.all_to_all(cross, ("y", "z"), 0, 0, tiled=True)
     cross = jnp.sum(cross.astype(WIDE), axis=0, keepdims=True).astype(LOW)
     cross = jnp.broadcast_to(cross, (count_y * count_z, cut_r, cut_c))
     cross = lax.all_to_all(cross, ("y", "z"), 0, 0, tiled=True)
-    cross = cross.reshape(count_y, count_z, cut_r, cut_c).transpose(1, 2, 0, 3)
-    cross = cross.reshape(rank, layers * rank)
-    cross, rows = lax.optimization_barrier((cross, rows))
     cross_near = gather_line(cross, "x")
+    cross_near, rows = lax.optimization_barrier((cross_near, rows))
     cross_far = lax.ppermute(cross_near, "c", swap_core)
 
     part_shape = jax.ShapeDtypeStruct((count_x, count_y, piece, layers * 3 * rank), LOW)
@@ -363,10 +377,13 @@
     parts = (keep.astype(WIDE) + came.astype(WIDE)).astype(LOW)
     parts = parts.reshape(count_x * count_y, piece, layers * 3 * rank)
     parts = lax.all_to_all(parts, ("x", "y"), 0, 0, tiled=True)
-    coded_width = 2 * layers * rank + rank
-    coded = local_call(
+    span = layers * rank
+    acts, moves = local_call(
         functools.partial(recursion_kernel, layers, rank, float(model_width)),
-        jax.ShapeDtypeStruct((piece, coded_width), LOW),
+        (
+            jax.ShapeDtypeStruct((piece, span + rank), LOW),
+            jax.ShapeDtypeStruct((piece, span), LOW),
+        ),
         (parts, square, cross_near, cross_far),
         scalars=place,
         scratch=[
@@ -374,8 +391,12 @@
             pltpu.VMEM((layers * rank, layers * rank), LOW),
         ],
     )
-    coded_near = gather_line(gather_line(coded, "x"), "y")
-    coded_far = lax.ppermute(coded_near, "c", swap_core)
+    acts_near = gather_line(acts, "x")
+    moves_near = gather_line(moves, "y")
+    acts_near = gather_line(acts_near, "y")
+    moves_near = gather_line(moves_near, "x")
+    acts_far = lax.ppermute(acts_near, "c", swap_core)
+    moves_far = lax.ppermute(moves_near, "c", swap_core)
 
     group_tokens = count_y * tok_rows
     outputs, grads = local_call(
@@ -384,7 +405,7 @@
             jax.ShapeDtypeStruct((layers, count_y, tok_rows, features), LOW),
             jax.ShapeDtypeStruct((layers, rank, 2 * features), LOW),
         ),
-        (rows, weights, coded_near, coded_far),
+        (rows, weights, acts_near, acts_far, moves_near, moves_far),
         scalars=place,
         scratch=[
             pltpu.VMEM((group_tokens, features), WIDE),
@@ -408,27 +429,33 @@
     )(outputs)
 
     own_grads = lax.ppermute(grads, across, back_route)
-    squares = local_call(
-        square_kernel, jax.ShapeDtypeStruct((sources * count_z, 128), WIDE), (gain_own, own_grads)
+    shard_in, shard_out, squares = local_call(
+        settle_kernel,
+        (
+            jax.ShapeDtypeStruct((features, rank), WIDE),
+            jax.ShapeDtypeStruct((rank, features), WIDE),
+            jax.ShapeDtypeStruct((sources * count_z, 128), WIDE),
+        ),
+        (gain_own, own_grads),
     )
     squares = lax.all_to_all(squares, EVERYONE, 0, 0, tiled=True)
+    total_sq = jnp.sum(squares[:, 0])
     norm_limit = clip_rms * math.sqrt(2.0 * model_width * rank * layers)
-    shape_in = jax.ShapeDtypeStruct(master_in.shape, WIDE)
-    shape_out = jax.ShapeDtypeStruct(master_out.shape, WIDE)
-    updated = local_call(
-        functools.partial(update_kernel, norm_limit),
-        (shape_in,) * 3 + (shape_out,) * 3,
-        (squares, gain_own, own_grads, master_in, first_in, second_in, master_out, first_out, second_out),
-    )
-    new_in, new_first_in, new_second_in, new_out, new_first_out, new_second_out = updated
+    clip_factor = norm_limit / jnp.maximum(jnp.sqrt(total_sq), norm_limit)
+    new_in, new_first_in, new_second_in = adam_update(
+        master_in[0], first_in[0], second_in[0], clip_factor * shard_in
+    )
+    new_out, new_first_out, new_second_out = adam_update(
+        master_out[0], first_out[0], second_out[0], clip_factor * shard_out
+    )
     return (
         section_rows[None],
-        new_in,
-        new_out,
-        new_first_in,
-        new_first_out,
-        new_second_in,
-        new_second_out,
+        new_in[None],
+        new_out[None],
+        new_first_in[None],
+        new_first_out[None],
+        new_second_in[None],
+        new_second_out[None],
     )
 
 

time: 282 us -> 271 us (0.961)
  waiting for transfers between devices: 146 us -> 109 us
  blocking collectives: 22 us -> 45.5 us
  starting transfers between devices: 57.7 us -> 65.7 us
  local copies, waits for them, and re-layouts: 13 us -> 6.84 us
    all_to_all x1 -> x2, blocking collectives: 22 us -> 45.5 us  [shards(): cross = lax.all_to_all(cross, ('y', 'z'), 0, 0, tiled=True)]
    ppermute x9 -> x18, waiting for transfers between devices: 42.2 us -> 22.3 us  [shifted(): lax.ppermute(block, axis, [(i, (i + distance) % size) for i in range(size)])]
    all_to_all x1, waiting for transfers between devices: 0.01 us -> 18.6 us  [shards(): parts = lax.all_to_all(parts, ('x', 'y'), 0, 0, tiled=True)]
    all_gather x1 -> x0, waiting for transfers between devices: 16.7 us -> none  [shards(): lined = lax.all_gather(packed, SECTION, axis=0)]
    ppermute x9 -> x18, starting transfers between devices: 12.9 us -> 24.2 us  [shifted(): lax.ppermute(block, axis, [(i, (i + distance) % size) for i in range(size)])]
    all_to_all x1 -> x0, waiting for transfers between devices: 11.2 us -> none  [shards(): cross = lax.all_to_all(cross, ('y', 'z'), 0, 0, tiled=True)]
    all_to_all x1, waiting for transfers between devices: 10.8 us -> 1.11 us  [shards(): rows = lax.all_to_all(rows, 'y', 0, 0, tiled=True)]
    all_to_all x1 -> x0, starting transfers between devices: 5.45 us -> none  [shards(): cross = lax.all_to_all(cross, ('y', 'z'), 0, 0, tiled=True)]
  transfers between devices with their start and end apart: 22 -> 31, of which waited for: 17 -> 18; matrix products, arithmetic and copies ran while one was open for 3% -> 1% of each run, Pallas kernels for 1% -> 2%
where the time goes in v4:
time: 271 us; the launch traced here: 268 us
  waiting for transfers between devices  109 us (40%)
  starting transfers between devices  65.7 us (24%)
  blocking collectives  45.5 us (17%)
  Pallas kernels  18.7 us (7%)
  between operations  15 us (6%)
  other arithmetic  8.15 us (3%)
  local copies, waits for them, and re-layouts  6.84 us (3%)
    all_to_all x2, blocking collectives, shards(): cross = lax.all_to_all(cross, ('y', 'z'), 0, 0, tiled=True)  45.5 us
    reduce_scatter x1, waiting for transfers between devices, shards(): grads = lax.psum_scatter(grads, 'z', scatter_dimension=0, tiled=True)[0]  31.8 us
    ppermute x18, starting transfers between devices, shifted(): lax.ppermute(block, axis, [(i, (i + distance) % size) for i in range(size)])  24.2 us
    ppermute x18, waiting for transfers between devices, shifted(): lax.ppermute(block, axis, [(i, (i + distance) % size) for i in range(size)])  22.3 us
    all_to_all x1, waiting for transfers between devices, shards(): parts = lax.all_to_all(parts, ('x', 'y'), 0, 0, tiled=True)  18.6 us
    pallas_call x6, Pallas kernels, local_call(): pl.pallas_call(kernel, out_shape=out_shape, in_specs=in_specs, out_specs=...  16.3 us
    all_to_all x1, starting transfers between devices, shards(): squares = lax.all_to_all(squares, EVERYONE, 0, 0, tiled=True)  14.2 us
    ppermute x1, waiting for transfers between devices, shards(): own_grads = lax.ppermute(grads, across, back_route)  12.9 us
  transfers between devices with their start and end apart: 31, of which 18 were waited for; matrix products, arithmetic and copies ran while one was open for 1% of the time, Pallas kernels for 2%

profile of v4, /device:TPU:2, one launch (start us, length us, event | category | flops | bytes accessed | tf_op | source)
XLA Modules:
  0.0 268.4 jit_solution(11457632095653789773)
XLA Ops:
  10.0 2.2 collective-permute-start.3
  14.2 5.2 %collective-permute-done.3 = bf16[384,256]{1,0:T(8,128)(2,1)S(1)} collective-permute-done((bf16[384,256]{1,0:T(8,128)(2,1)S(1)}, bf16[384,256]{1,0:T(8,128)(2,1)S(1)}, u32[]{:S(2)}, u32[]{:S(2)}) %collective-permute-start.3) | collective-permute-done | bytes 196640 | tf_op jit(solution)/shard_map/ppermute | solution.py:86
  19.4 3.0 %collective-permute-done.2 = bf16[384,256]{1,0:T(8,128)(2,1)S(1)} collective-permute-done((bf16[384,256]{1,0:T(8,128)(2,1)S(1)}, bf16[384,256]{1,0:T(8,128)(2,1)S(1)}, u32[]{:S(2)}, u32[]{:S(2)}) %collective-permute-start.2) | collective-permute-done | bytes 196640 | tf_op jit(solution)/shard_map/ppermute | solution.py:86
  25.0 4.5 %all-to-all-start = ((bf16[4,256,384]{2,1,0:T(8,128)(2,1)}), bf16[4,256,384]{2,1,0:T(8,128)(2,1)S(1)}, u32[]{:S(2)}, u32[]{:S(2)}) async-start(bf16[4,256,384]{2,1,0:T(8,128)(2,1)} %maximum_maximum_fusion), calls=%async_computation | async-start | bytes 1572864 | tf_op jit(solution)/shard_map/all_to_all | solution.py:346
  29.5 6.6 %collective-permute-start = (bf16[384,256]{1,0:T(8,128)(2,1)S(1)}, bf16[384,256]{1,0:T(8,128)(2,1)S(1)}, u32[]{:S(2)}, u32[]{:S(2)}) collective-permute-start(bf16[384,256]{1,0:T(8,128)(2,1)S(1)} %shard_map.144.own_ref), channel_id=1, source_target_pairs={{0,0},{1,33},{2,66},{3,99},{4,132},{5,165},{6,198},{7,231},{32,4},... | collective-permute-start | bytes 589832 | tf_op jit(solution)/shard_map/ppermute | solution.py:333
  36.0 5.3 %collective-permute-done = bf16[384,256]{1,0:T(8,128)(2,1)S(1)} collective-permute-done((bf16[384,256]{1,0:T(8,128)(2,1)S(1)}, bf16[384,256]{1,0:T(8,128)(2,1)S(1)}, u32[]{:S(2)}, u32[]{:S(2)}) %collective-permute-start) | collective-permute-done | bytes 196640 | tf_op jit(solution)/shard_map/ppermute | solution.py:333
  43.5 26.3 %all_to_all.37 = bf16[32,16,256]{2,1,0:T(8,128)(2,1)S(1)} all-to-all(bf16[32,16,256]{2,1,0:T(8,128)(2,1)S(1)} %shard_map.145), channel_id=1, replica_groups=mesh['x'=4,'c'=2,'y'=4,'z'=8] {'y','z'}, dimensions={0} | all-to-all | bytes 524288 | tf_op jit(solution)/shard_map/all_to_all | solution.py:360
  69.9 19.2 %all_to_all.38 = bf16[32,16,256]{2,1,0:T(8,128)(2,1)S(1)} all-to-all(bf16[32,16,256]{2,1,0:T(8,128)(2,1)S(1)} %broadcast_in_dim.33), channel_id=1, replica_groups=mesh['x'=4,'c'=2,'y'=4,'z'=8] {'y','z'}, dimensions={0} | all-to-all | bytes 524288 | tf_op jit(solution)/shard_map/all_to_all | solution.py:363
  91.2 7.3 %collective-permute-done.7 = bf16[32,16,256]{2,1,0:T(8,128)(2,1)S(1)} collective-permute-done((bf16[32,16,256]{2,1,0:T(8,128)(2,1)S(1)}, bf16[32,16,256]{2,1,0:T(8,128)(2,1)S(1)}, u32[]{:S(2)}, u32[]{:S(2)}) %collective-permute-start.7) | collective-permute-done | bytes 262176 | tf_op jit(solution)/shard_map/ppermute | solution.py:86
  98.4 2.2 collective-permute-done.6
  102.2 2.8 %shard_map.146 = (bf16[4,4,16,3072]{3,2,1,0:T(8,128)(2,1)S(1)}, bf16[4,4,16,3072]{3,2,1,0:T(8,128)(2,1)S(1)}) custom-call(s32[4]{0:T(128)S(1)} %pad_add_fusion.place_ref, bf16[4,256,384]{2,1,0:T(8,128)(2,1)S(1)} %all-to-all-done.rows_ref, bf16[8,384,256]{2,1,0:T(8,128)(2,1)S(1)} %bitcast.118), custom_call_target="tpu_custom_call" | custom-call | flops 1207959552 | bytes 5505024 | tf_op jit(solution)/shard_map/pallas_call | solution.py:73
  105.1 3.4 %collective-permute-done.8 = bf16[4,4,16,3072]{3,2,1,0:T(8,128)(2,1)S(1)} collective-permute-done((bf16[4,4,16,3072]{3,2,1,0:T(8,128)(2,1)S(1)}, bf16[4,4,16,3072]{3,2,1,0:T(8,128)(2,1)S(1)}, u32[]{:S(2)}, u32[]{:S(2)}) %collective-permute-start.8) | collective-permute-done | bytes 1572896 | tf_op jit(solution)/shard_map/ppermute | solution.py:376
  110.2 6.9 %all-to-all-start.3 = ((bf16[16,16,3072]{2,1,0:T(8,128)(2,1)}), bf16[16,16,3072]{2,1,0:T(8,128)(2,1)S(1)}, u32[]{:S(2)}, u32[]{:S(2)}) async-start(bf16[16,16,3072]{2,1,0:T(8,128)(2,1)} %bitcast.120), calls=%async_computation.3 | async-start | bytes 3145728 | tf_op jit(solution)/shard_map/all_to_all | solution.py:379
  120.2 18.6 %all-to-all-done.3.parts_ref = bf16[16,16,3072]{2,1,0:T(8,128)(2,1)S(1)} async-done(((bf16[16,16,3072]{2,1,0:T(8,128)(2,1)}), bf16[16,16,3072]{2,1,0:T(8,128)(2,1)S(1)}, u32[]{:S(2)}, u32[]{:S(2)}) %all-to-all-start.3) | async-done | bytes 1572896 | tf_op jit(solution)/shard_map/all_to_all | solution.py:379
  138.9 4.9 %shard_map.147 = (bf16[16,1152]{1,0:T(8,128)(2,1)S(1)}, bf16[16,1024]{1,0:T(8,128)(2,1)S(1)}) custom-call(s32[4]{0:T(128)S(1)} %pad_add_fusion.place_ref, bf16[16,16,3072]{2,1,0:T(8,128)(2,1)S(1)} %all-to-all-done.3.parts_ref, f32[16,128]{1,0:T(8,128)S(1)} %broadcast_in_dim.34.square_ref, bf16[4,32,16,256]{3,2,1,0:T(8,128)(2,1)S(1)} %pad_maximum_fusion.near_ref, ...), custom_call_target="tpu_custom_call" | custom-call | bytes 3747840 | tf_op jit(solution)/shard_map/pallas_call | solution.py:73
  143.7 2.3 collective-permute-start.12
  146.0 1.7 collective-permute-start.11
  149.4 1.9 collective-permute-start.18
  151.8 2.9 %collective-permute-start.14 = (bf16[4,16,1152]{2,1,0:T(8,128)(2,1)S(1)}, bf16[4,16,1152]{2,1,0:T(8,128)(2,1)S(1)}, u32[]{:S(2)}, u32[]{:S(2)}) collective-permute-start(bf16[4,16,1152]{2,1,0:T(8,128)(2,1)S(1)} %get-tuple-element.52), channel_id=1, source_target_pairs={{0,24},{8,0},{16,8},{24,16},{1,25},{9,1},{17,9},{25,17},{2,26},{10... | collective-permute-start | bytes 442376 | tf_op jit(solution)/shard_map/ppermute | solution.py:86
  157.7 1.8 collective-permute-start.21
  159.8 3.7 %collective-permute-start.22 = (bf16[4,16,1024]{2,1,0:T(8,128)(2,1)S(1)}, bf16[4,16,1024]{2,1,0:T(8,128)(2,1)S(1)}, u32[]{:S(2)}, u32[]{:S(2)}) collective-permute-start(bf16[4,16,1024]{2,1,0:T(8,128)(2,1)S(1)} %get-tuple-element.54), channel_id=1, source_target_pairs={{0,128},{64,192},{128,0},{192,64},{1,129},{65,193},{129,1},{193,65... | collective-permute-start | bytes 393224 | tf_op jit(solution)/shard_map/ppermute | solution.py:86
  164.5 2.0 collective-permute-done.22
  166.9 1.9 collective-permute-done.23.move_far_ref
  168.8 6.6 %shard_map.148 = (bf16[8,4,128,384]{3,2,1,0:T(8,128)(2,1)}, bf16[8,128,768]{2,1,0:T(8,128)(2,1)}) custom-call(s32[4]{0:T(128)S(1)} %pad_add_fusion.place_ref, bf16[4,256,384]{2,1,0:T(8,128)(2,1)S(1)} %all-to-all-done.rows_ref, bf16[8,384,256]{2,1,0:T(8,128)(2,1)S(1)} %bitcast.119, bf16[4,4,16,1152]{3,2,1,0:T(8,128)(2,1)S(1)} %pad_maximum_fusion.2.act_near_ref, ...), custom_call_target="tpu_custom_call" | custom-call | flops 1610612736 | bytes 9306112 | tf_op jit(solution)/shard_map/pallas_call | solution.py:73
  175.4 6.6 %all-to-all-start.4 = ((bf16[32,128,384]{2,1,0:T(8,128)(2,1)}), bf16[32,128,384]{2,1,0:T(8,128)(2,1)S(1)}, u32[]{:S(2)}, u32[]{:S(2)}) async-start(bf16[32,128,384]{2,1,0:T(8,128)(2,1)} %bitcast.121), calls=%async_computation.4 | async-start | bytes 6291456 | tf_op jit(solution)/shard_map/all_to_all | solution.py:420
  182.1 31.8 %reduce-scatter.2.cloned.1.call-done = bf16[1,128,768]{2,1,0:T(8,128)(2,1)} async-done(((bf16[8,128,768]{2,1,0:T(8,128)(2,1)}), bf16[1,128,768]{2,1,0:T(8,128)(2,1)}) %reduce-scatter.2.cloned.1.call-update) | async-done | bytes 196624 | tf_op jit(solution)/shard_map/reduce_scatter | solution.py:418
  213.9 1.9 collective-permute-start.24
  215.8 12.9 %collective-permute-done.24.grad_ref = bf16[128,768]{1,0:T(8,128)(2,1)S(1)} collective-permute-done((bf16[128,768]{1,0:T(8,128)(2,1)}, bf16[128,768]{1,0:T(8,128)(2,1)S(1)}, u32[]{:S(2)}, u32[]{:S(2)}) %collective-permute-start.24) | collective-permute-done | bytes 196640 | tf_op jit(solution)/shard_map/ppermute | solution.py:431
  230.9 14.2 %all-to-all-start.5 = ((f32[256,1,128]{2,1,0:T(1,128)}), f32[256,1,128]{2,1,0:T(1,128)S(1)}, u32[]{:S(2)}, u32[]{:S(2)}) async-start(f32[256,1,128]{2,1,0:T(1,128)} %bitcast.45), calls=%async_computation.6 | async-start | bytes 262144 | tf_op jit(solution)/shard_map/all_to_all | solution.py:441
  245.1 2.4 shard_map.149
  247.5 9.6 %all-to-all-done.5 = f32[256,1,128]{2,1,0:T(1,128)S(1)} async-done(((f32[256,1,128]{2,1,0:T(1,128)}), f32[256,1,128]{2,1,0:T(1,128)S(1)}, u32[]{:S(2)}, u32[]{:S(2)}) %all-to-all-start.5) | async-done | bytes 131104 | tf_op jit(solution)/shard_map/all_to_all | solution.py:441
  258.5 2.1 fusion.10
  (85 shorter events, 28.8 us)
Async XLA Ops:
  10.0 9.4 %collective-permute-start.3 = (bf16[384,256]{1,0:T(8,128)(2,1)S(1)}, bf16[384,256]{1,0:T(8,128)(2,1)S(1)}, u32[]{:S(2)}, u32[]{:S(2)}) collective-permute-start(bf16[384,256]{1,0:T(8,128)(2,1)S(1)} %shard_map.144.own_ref), channel_id=1, source_target_pairs={{0,128},{64,192},{128,0},{192,64},{1,129},{65,193},{129,1},{193,65... | collective-permute-start | bytes 589832 | tf_op jit(solution)/shard_map/ppermute | solution.py:86
  12.2 10.2 %collective-permute-start.2 = (bf16[384,256]{1,0:T(8,128)(2,1)S(1)}, bf16[384,256]{1,0:T(8,128)(2,1)S(1)}, u32[]{:S(2)}, u32[]{:S(2)}) collective-permute-start(bf16[384,256]{1,0:T(8,128)(2,1)S(1)} %shard_map.144.own_ref), channel_id=1, source_target_pairs={{0,192},{64,0},{128,64},{192,128},{1,193},{65,1},{129,65},{193,129... | collective-permute-start | bytes 589832 | tf_op jit(solution)/shard_map/ppermute | solution.py:86
  13.6 8.9 %collective-permute-start.1 = (bf16[384,256]{1,0:T(8,128)(2,1)S(1)}, bf16[384,256]{1,0:T(8,128)(2,1)S(1)}, u32[]{:S(2)}, u32[]{:S(2)}) collective-permute-start(bf16[384,256]{1,0:T(8,128)(2,1)S(1)} %shard_map.144.own_ref), channel_id=1, source_target_pairs={{0,64},{64,128},{128,192},{192,0},{1,65},{65,129},{129,193},{193,1... | collective-permute-start | bytes 589832 | tf_op jit(solution)/shard_map/ppermute | solution.py:86
  22.6 19.8 %collective-permute-start.4 = (bf16[4,384,256]{2,1,0:T(8,128)(2,1)S(1)}, bf16[4,384,256]{2,1,0:T(8,128)(2,1)S(1)}, u32[]{:S(2)}, u32[]{:S(2)}) collective-permute-start(bf16[4,384,256]{2,1,0:T(8,128)(2,1)S(1)} %pad_maximum_fusion.1.near_ref), channel_id=1, source_target_pairs={{0,32},{32,0},{1,33},{33,1},{2,34},{34,2},{3,35},{35,3},{4,36},{36... | collective-permute-start | bytes 2359304 | tf_op jit(solution)/shard_map/ppermute | solution.py:335
  25.0 17.4 %all-to-all-start = ((bf16[4,256,384]{2,1,0:T(8,128)(2,1)}), bf16[4,256,384]{2,1,0:T(8,128)(2,1)S(1)}, u32[]{:S(2)}, u32[]{:S(2)}) async-start(bf16[4,256,384]{2,1,0:T(8,128)(2,1)} %maximum_maximum_fusion), calls=%async_computation | async-start | bytes 1572864 | tf_op jit(solution)/shard_map/all_to_all | solution.py:346
  29.5 71.3 %all-gather.3.cloned.1.call-start = ((), (), s32[]{:S(2)}) async-start(), calls=%async_computation.8 | async-start | bytes 1769472 | tf_op jit(solution)/shard_map/all_gather | solution.py:348
  29.5 11.8 %collective-permute-start = (bf16[384,256]{1,0:T(8,128)(2,1)S(1)}, bf16[384,256]{1,0:T(8,128)(2,1)S(1)}, u32[]{:S(2)}, u32[]{:S(2)}) collective-permute-start(bf16[384,256]{1,0:T(8,128)(2,1)S(1)} %shard_map.144.own_ref), channel_id=1, source_target_pairs={{0,0},{1,33},{2,66},{3,99},{4,132},{5,165},{6,198},{7,231},{32,4},... | collective-permute-start | bytes 589832 | tf_op jit(solution)/shard_map/ppermute | solution.py:333
  89.1 9.3 %collective-permute-start.7 = (bf16[32,16,256]{2,1,0:T(8,128)(2,1)S(1)}, bf16[32,16,256]{2,1,0:T(8,128)(2,1)S(1)}, u32[]{:S(2)}, u32[]{:S(2)}) collective-permute-start(bf16[32,16,256]{2,1,0:T(8,128)(2,1)S(1)} %all_to_all.38), channel_id=1, source_target_pairs={{0,128},{64,192},{128,0},{192,64},{1,129},{65,193},{129,1},{193,65... | collective-permute-start | bytes 786440 | tf_op jit(solution)/shard_map/ppermute | solution.py:86
  89.1 11.5 %collective-permute-start.6 = (bf16[32,16,256]{2,1,0:T(8,128)(2,1)S(1)}, bf16[32,16,256]{2,1,0:T(8,128)(2,1)S(1)}, u32[]{:S(2)}, u32[]{:S(2)}) collective-permute-start(bf16[32,16,256]{2,1,0:T(8,128)(2,1)S(1)} %all_to_all.38), channel_id=1, source_target_pairs={{0,192},{64,0},{128,64},{192,128},{1,193},{65,1},{129,65},{193,129... | collective-permute-start | bytes 786440 | tf_op jit(solution)/shard_map/ppermute | solution.py:86
  89.5 11.1 %collective-permute-start.5 = (bf16[32,16,256]{2,1,0:T(8,128)(2,1)S(1)}, bf16[32,16,256]{2,1,0:T(8,128)(2,1)S(1)}, u32[]{:S(2)}, u32[]{:S(2)}) collective-permute-start(bf16[32,16,256]{2,1,0:T(8,128)(2,1)S(1)} %all_to_all.38), channel_id=1, source_target_pairs={{0,64},{64,128},{128,192},{192,0},{1,65},{65,129},{129,193},{193,1... | collective-permute-start | bytes 786440 | tf_op jit(solution)/shard_map/ppermute | solution.py:86
  105.0 3.5 %collective-permute-start.8 = (bf16[4,4,16,3072]{3,2,1,0:T(8,128)(2,1)S(1)}, bf16[4,4,16,3072]{3,2,1,0:T(8,128)(2,1)S(1)}, u32[]{:S(2)}, u32[]{:S(2)}) collective-permute-start(bf16[4,4,16,3072]{3,2,1,0:T(8,128)(2,1)S(1)} %get-tuple-element.28), channel_id=1, source_target_pairs={{0,32},{32,0},{1,33},{33,1},{2,34},{34,2},{3,35},{35,3},{4,36},{36... | collective-permute-start | bytes 4718600 | tf_op jit(solution)/shard_map/ppermute | solution.py:376
  110.2 28.5 %all-to-all-start.3 = ((bf16[16,16,3072]{2,1,0:T(8,128)(2,1)}), bf16[16,16,3072]{2,1,0:T(8,128)(2,1)S(1)}, u32[]{:S(2)}, u32[]{:S(2)}) async-start(bf16[16,16,3072]{2,1,0:T(8,128)(2,1)} %bitcast.120), calls=%async_computation.3 | async-start | bytes 3145728 | tf_op jit(solution)/shard_map/all_to_all | solution.py:379
  117.1 96.8 %reduce-scatter.2.cloned.1.call-start = ((), (), s32[]{:S(2)}) async-start(), calls=%async_computation.7 | async-start | bytes 1769472 | tf_op jit(solution)/shard_map/reduce_scatter | solution.py:418
  117.2 3.1 %collective-permute-start.9 = (bf16[4,32,16,256]{3,2,1,0:T(8,128)(2,1)S(1)}, bf16[4,32,16,256]{3,2,1,0:T(8,128)(2,1)}, u32[]{:S(2)}, u32[]{:S(2)}) collective-permute-start(bf16[4,32,16,256]{3,2,1,0:T(8,128)(2,1)S(1)} %pad_maximum_fusion.near_ref), channel_id=1, source_target_pairs={{0,32},{32,0},{1,33},{33,1},{2,34},{34,2},{3,35},{35,3},{4,36},{36... | collective-permute-start | bytes 3145736 | tf_op jit(solution)/shard_map/ppermute | solution.py:366
  143.7 25.1 %copy-start.9 = (bf16[3072,256]{1,0:T(8,128)(2,1)S(1)}, bf16[3072,256]{1,0:T(8,128)(2,1)}, u32[]{:S(2)}) copy-start(bf16[3072,256]{1,0:T(8,128)(2,1)} %all-gather.3.cloned.1.call-done) | copy-start | bytes 4718596
  143.7 7.6 %collective-permute-start.12 = (bf16[16,1152]{1,0:T(8,128)(2,1)S(1)}, bf16[16,1152]{1,0:T(8,128)(2,1)S(1)}, u32[]{:S(2)}, u32[]{:S(2)}) collective-permute-start(bf16[16,1152]{1,0:T(8,128)(2,1)S(1)} %get-tuple-element.30), channel_id=1, source_target_pairs={{0,128},{64,192},{128,0},{192,64},{1,129},{65,193},{129,1},{193,65... | collective-permute-start | bytes 110600 | tf_op jit(solution)/shard_map/ppermute | solution.py:86
  146.0 5.4 %collective-permute-start.11 = (bf16[16,1152]{1,0:T(8,128)(2,1)S(1)}, bf16[16,1152]{1,0:T(8,128)(2,1)S(1)}, u32[]{:S(2)}, u32[]{:S(2)}) collective-permute-start(bf16[16,1152]{1,0:T(8,128)(2,1)S(1)} %get-tuple-element.30), channel_id=1, source_target_pairs={{0,192},{64,0},{128,64},{192,128},{1,193},{65,1},{129,65},{193,129... | collective-permute-start | bytes 110600 | tf_op jit(solution)/shard_map/ppermute | solution.py:86
  147.8 4.0 %collective-permute-start.10 = (bf16[16,1152]{1,0:T(8,128)(2,1)S(1)}, bf16[16,1152]{1,0:T(8,128)(2,1)S(1)}, u32[]{:S(2)}, u32[]{:S(2)}) collective-permute-start(bf16[16,1152]{1,0:T(8,128)(2,1)S(1)} %get-tuple-element.30), channel_id=1, source_target_pairs={{0,64},{64,128},{128,192},{192,0},{1,65},{65,129},{129,193},{193,1... | collective-permute-start | bytes 110600 | tf_op jit(solution)/shard_map/ppermute | solution.py:86
  148.1 6.6 %collective-permute-start.19 = (bf16[16,1024]{1,0:T(8,128)(2,1)S(1)}, bf16[16,1024]{1,0:T(8,128)(2,1)S(1)}, u32[]{:S(2)}, u32[]{:S(2)}) collective-permute-start(bf16[16,1024]{1,0:T(8,128)(2,1)S(1)} %get-tuple-element.31), channel_id=1, source_target_pairs={{0,16},{8,24},{16,0},{24,8},{1,17},{9,25},{17,1},{25,9},{2,18},{10... | collective-permute-start | bytes 98312 | tf_op jit(solution)/shard_map/ppermute | solution.py:86
  149.4 6.8 %collective-permute-start.18 = (bf16[16,1024]{1,0:T(8,128)(2,1)S(1)}, bf16[16,1024]{1,0:T(8,128)(2,1)S(1)}, u32[]{:S(2)}, u32[]{:S(2)}) collective-permute-start(bf16[16,1024]{1,0:T(8,128)(2,1)S(1)} %get-tuple-element.31), channel_id=1, source_target_pairs={{0,24},{8,0},{16,8},{24,16},{1,25},{9,1},{17,9},{25,17},{2,26},{10... | collective-permute-start | bytes 98312 | tf_op jit(solution)/shard_map/ppermute | solution.py:86
  151.3 6.4 %collective-permute-start.17 = (bf16[16,1024]{1,0:T(8,128)(2,1)S(1)}, bf16[16,1024]{1,0:T(8,128)(2,1)S(1)}, u32[]{:S(2)}, u32[]{:S(2)}) collective-permute-start(bf16[16,1024]{1,0:T(8,128)(2,1)S(1)} %get-tuple-element.31), channel_id=1, source_target_pairs={{0,8},{8,16},{16,24},{24,0},{1,9},{9,17},{17,25},{25,1},{2,10},{10... | collective-permute-start | bytes 98312 | tf_op jit(solution)/shard_map/ppermute | solution.py:86
  151.8 8.1 %collective-permute-start.14 = (bf16[4,16,1152]{2,1,0:T(8,128)(2,1)S(1)}, bf16[4,16,1152]{2,1,0:T(8,128)(2,1)S(1)}, u32[]{:S(2)}, u32[]{:S(2)}) collective-permute-start(bf16[4,16,1152]{2,1,0:T(8,128)(2,1)S(1)} %get-tuple-element.52), channel_id=1, source_target_pairs={{0,24},{8,0},{16,8},{24,16},{1,25},{9,1},{17,9},{25,17},{2,26},{10... | collective-permute-start | bytes 442376 | tf_op jit(solution)/shard_map/ppermute | solution.py:86
  154.7 8.9 %collective-permute-start.13 = (bf16[4,16,1152]{2,1,0:T(8,128)(2,1)S(1)}, bf16[4,16,1152]{2,1,0:T(8,128)(2,1)S(1)}, u32[]{:S(2)}, u32[]{:S(2)}) collective-permute-start(bf16[4,16,1152]{2,1,0:T(8,128)(2,1)S(1)} %get-tuple-element.52), channel_id=1, source_target_pairs={{0,8},{8,16},{16,24},{24,0},{1,9},{9,17},{17,25},{25,1},{2,10},{10... | collective-permute-start | bytes 442376 | tf_op jit(solution)/shard_map/ppermute | solution.py:86
  154.7 8.9 %collective-permute-start.15 = (bf16[4,16,1152]{2,1,0:T(8,128)(2,1)S(1)}, bf16[4,16,1152]{2,1,0:T(8,128)(2,1)S(1)}, u32[]{:S(2)}, u32[]{:S(2)}) collective-permute-start(bf16[4,16,1152]{2,1,0:T(8,128)(2,1)S(1)} %get-tuple-element.52), channel_id=1, source_target_pairs={{0,16},{8,24},{16,0},{24,8},{1,17},{9,25},{17,1},{25,9},{2,18},{10... | collective-permute-start | bytes 442376 | tf_op jit(solution)/shard_map/ppermute | solution.py:86
  157.7 6.0 %collective-permute-start.21 = (bf16[4,16,1024]{2,1,0:T(8,128)(2,1)S(1)}, bf16[4,16,1024]{2,1,0:T(8,128)(2,1)S(1)}, u32[]{:S(2)}, u32[]{:S(2)}) collective-permute-start(bf16[4,16,1024]{2,1,0:T(8,128)(2,1)S(1)} %get-tuple-element.54), channel_id=1, source_target_pairs={{0,192},{64,0},{128,64},{192,128},{1,193},{65,1},{129,65},{193,129... | collective-permute-start | bytes 393224 | tf_op jit(solution)/shard_map/ppermute | solution.py:86
  159.5 5.0 %collective-permute-start.20 = (bf16[4,16,1024]{2,1,0:T(8,128)(2,1)S(1)}, bf16[4,16,1024]{2,1,0:T(8,128)(2,1)S(1)}, u32[]{:S(2)}, u32[]{:S(2)}) collective-permute-start(bf16[4,16,1024]{2,1,0:T(8,128)(2,1)S(1)} %get-tuple-element.54), channel_id=1, source_target_pairs={{0,64},{64,128},{128,192},{192,0},{1,65},{65,129},{129,193},{193,1... | collective-permute-start | bytes 393224 | tf_op jit(solution)/shard_map/ppermute | solution.py:86
  159.8 6.7 %collective-permute-start.22 = (bf16[4,16,1024]{2,1,0:T(8,128)(2,1)S(1)}, bf16[4,16,1024]{2,1,0:T(8,128)(2,1)S(1)}, u32[]{:S(2)}, u32[]{:S(2)}) collective-permute-start(bf16[4,16,1024]{2,1,0:T(8,128)(2,1)S(1)} %get-tuple-element.54), channel_id=1, source_target_pairs={{0,128},{64,192},{128,0},{192,64},{1,129},{65,193},{129,1},{193,65... | collective-permute-start | bytes 393224 | tf_op jit(solution)/shard_map/ppermute | solution.py:86
  163.7 5.1 %collective-permute-start.16 = (bf16[4,4,16,1152]{3,2,1,0:T(8,128)(2,1)S(1)}, bf16[4,4,16,1152]{3,2,1,0:T(8,128)(2,1)S(1)}, u32[]{:S(2)}, u32[]{:S(2)}) collective-permute-start(bf16[4,4,16,1152]{3,2,1,0:T(8,128)(2,1)S(1)} %pad_maximum_fusion.2.act_near_ref), channel_id=1, source_target_pairs={{0,32},{32,0},{1,33},{33,1},{2,34},{34,2},{3,35},{35,3},{4,36},{36... | collective-permute-start | bytes 1769480 | tf_op jit(solution)/shard_map/ppermute | solution.py:398
  166.6 2.2 collective-permute-start.23
  175.4 55.5 %all-to-all-start.4 = ((bf16[32,128,384]{2,1,0:T(8,128)(2,1)}), bf16[32,128,384]{2,1,0:T(8,128)(2,1)S(1)}, u32[]{:S(2)}, u32[]{:S(2)}) async-start(bf16[32,128,384]{2,1,0:T(8,128)(2,1)} %bitcast.121), calls=%async_computation.4 | async-start | bytes 6291456 | tf_op jit(solution)/shard_map/all_to_all | solution.py:420
  213.9 14.8 %collective-permute-start.24 = (bf16[128,768]{1,0:T(8,128)(2,1)}, bf16[128,768]{1,0:T(8,128)(2,1)S(1)}, u32[]{:S(2)}, u32[]{:S(2)}) collective-permute-start(bf16[128,768]{1,0:T(8,128)(2,1)} %bitcast.143), channel_id=1, source_target_pairs={{0,0},{33,1},{66,2},{99,3},{132,4},{165,5},{198,6},{231,7},{4,32},... | collective-permute-start | bytes 589832 | tf_op jit(solution)/shard_map/ppermute | solution.py:431
  230.9 26.3 %all-to-all-start.5 = ((f32[256,1,128]{2,1,0:T(1,128)}), f32[256,1,128]{2,1,0:T(1,128)S(1)}, u32[]{:S(2)}, u32[]{:S(2)}) async-start(f32[256,1,128]{2,1,0:T(1,128)} %bitcast.45), calls=%async_computation.6 | async-start | bytes 262144 | tf_op jit(solution)/shard_map/all_to_all | solution.py:441
  (12 other events, 72.4 us)
Sparse Core Ops, SparseCore 0:
  42.6 49.6 all-gather.2
  175.5 38.3 reduce-scatter.1

commit v5 on v4

--- a/solution.py
+++ b/solution.py
@@ -26,6 +26,7 @@
 EVERYONE = ("x", "c", "y", "z")
 SHIFTS = (0, 1, -1, 2)
 TURNS = (0, 4, 3, 7, 2, 6, 1, 5)
+EXTRA = 16
 VMEM_BYTES = 48 * 1024 * 1024
 
 
@@ -94,8 +95,30 @@
     features, rank = in_ref.shape[1:]
     gain = jnp.broadcast_to(gain_ref[...], (rank, features)).T
     work_in = in_ref[0].astype(LOW).astype(WIDE)
-    pack_ref[:, :rank] = (work_in * gain).astype(LOW)
-    pack_ref[:, rank:] = out_ref[0].T.astype(LOW)
+    pack_ref[:features, :rank] = (work_in * gain).astype(LOW)
+    pack_ref[:features, rank:] = out_ref[0].T.astype(LOW)
+    spare = (EXTRA, 2 * rank)
+    row = lax.broadcasted_iota(jnp.int32, spare, 0)
+    rows = jnp.zeros(spare, WIDE)
+    left = gain_ref[...]
+    chunks = features // rank
+    for term in range(3):
+        part = left.astype(LOW).astype(WIDE)
+        left = left - part
+        for k in range(chunks):
+            chunk = part[:, k * rank : (k + 1) * rank]
+            chunk = jnp.broadcast_to(jnp.concatenate([chunk, chunk], axis=1), spare)
+            rows = jnp.where(row == term * chunks + k, chunk, rows)
+    pack_ref[features:, :] = rows.astype(LOW)
+
+
+def packed_gain(tail, chunks):
+    rows = tail.astype(WIDE)
+    parts = []
+    for k in range(chunks):
+        terms = [rows[t * chunks + k : t * chunks + k + 1] for t in range(3)]
+        parts.append(terms[0] + terms[1] + terms[2])
+    return jnp.concatenate(parts, axis=1)
 
 
 def cross_kernel(rank, place_ref, own_ref, near_ref, far_ref, out_ref):
@@ -103,12 +126,13 @@
     count = len(SHIFTS)
     cut = out_ref.shape[1]
     cuts = rank // cut
-    own = own_ref[:, rank:].T
+    features = own_ref.shape[0] - EXTRA
+    own = own_ref[:features, rank:].T
     for slot, step in enumerate(SHIFTS):
         owner = lax.rem(column - step + count, count)
         blocks = []
         for line_ref, from_core in ((near_ref, core), (far_ref, 1 - core)):
-            both = dot_nn(own, line_ref[slot])
+            both = dot_nn(own, line_ref[slot, :features])
             later = 2 * owner + from_core > section
             blocks.append(jnp.where(later, both[:, :rank], both[:, rank:]).astype(LOW))
         even = jnp.where(core == 0, blocks[0], blocks[1])
@@ -120,14 +144,14 @@
 
 
 def project_kernel(rank, place_ref, rows_ref, weight_ref, keep_ref, send_ref):
-    groups, both_rows, _ = rows_ref.shape
+    groups, both_rows, features = rows_ref.shape
     layers = weight_ref.shape[0]
     half = both_rows // 2
     columns = keep_ref.shape[0]
     piece = half // (2 * columns)
     core, section = place_ref[0], place_ref[1]
     for layer in range(layers):
-        weight = weight_ref[lax.rem(section + TURNS[layer], layers)]
+        weight = weight_ref[lax.rem(section + TURNS[layer], layers), :features]
         base = layer * 3 * rank
         for group in range(groups):
             first = dot_nn(rows_ref[group, :half, :], weight).astype(LOW)
@@ -254,7 +278,7 @@
                 moved_ref[dest, :] = some_move[slot_x, slot_y]
 
     for layer in range(layers):
-        up_weight = weight_ref[lax.rem(section + TURNS[layer], layers), :, rank:]
+        up_weight = weight_ref[lax.rem(section + TURNS[layer], layers), :features, rank:]
         act = act_ref[:, layer * rank : (layer + 1) * rank]
         total = wide_ref[...] + dot_nt(act, up_weight)
         wide_ref[...] = total
@@ -275,20 +299,22 @@
         else:
             current = rows_ref[:, :half, :].reshape(groups * half, features)
         grad_ref[slot, :, features:] = dot_tn(act, delta).astype(LOW)
-        grad_ref[slot, :, :features] = dot_tn(moved, current).astype(LOW)
+        gain = packed_gain(weight_ref[slot, features:, :rank], features // rank)
+        grad_ref[slot, :, :features] = (dot_tn(moved, current) * gain).astype(LOW)
         if layer > 0:
             coef = coef_ref[:, layer : layer + 1] + coef_ref[:, layers + layer : layers + layer + 1]
-            wide_ref[...] += dot_nt(moved, weight_ref[slot, :, :rank]) - coef * current.astype(WIDE)
-
-
-def settle_kernel(gain_ref, grad_ref, in_ref, out_ref, square_ref):
-    features = gain_ref.shape[1]
-    grad_in = grad_ref[:, :features].astype(WIDE) * gain_ref[...]
-    grad_out = grad_ref[:, features:].astype(WIDE)
-    in_ref[...] = grad_in.T
-    out_ref[...] = grad_out
-    total = jnp.sum(grad_in * grad_in) + jnp.sum(grad_out * grad_out)
-    square_ref[...] = jnp.full(square_ref.shape, total, WIDE)
+            wide_ref[...] += dot_nt(moved, weight_ref[slot, :features, :rank]) - coef * current.astype(WIDE)
+
+
+def square_kernel(grad_ref, out_ref):
+    grad = grad_ref[...].astype(WIDE)
+    out_ref[...] = jnp.full(out_ref.shape, jnp.sum(grad * grad), WIDE)
+
+
+def settle_kernel(grad_ref, in_ref, out_ref):
+    features = out_ref.shape[1]
+    in_ref[...] = grad_ref[:, :features].astype(WIDE).T
+    out_ref[...] = grad_ref[:, features:].astype(WIDE)
 
 
 def order_kernel(block_ref, out_ref):
@@ -328,7 +354,7 @@
 
     gain_own = lax.dynamic_slice_in_dim(norm_gain, (pos_y * count_z + pos_z) * features, features, 1)
     packed = local_call(
-        pack_kernel, jax.ShapeDtypeStruct((features, 2 * rank), LOW), (gain_own, master_in, master_out)
+        pack_kernel, jax.ShapeDtypeStruct((features + EXTRA, 2 * rank), LOW), (gain_own, master_in, master_out)
     )
     swapped = lax.ppermute(packed, across, route)
     lined_near = gather_line(packed, "x")
@@ -343,8 +369,7 @@
         )
 
     rows = jnp.concatenate([blocks_of(stack_input), blocks_of(out_cotangent)], axis=1)
-    rows = lax.all_to_all(rows, "y", 0, 0, tiled=True)
-    swapped, lined_near, lined_far, rows = lax.optimization_barrier((swapped, lined_near, lined_far, rows))
+    swapped, lined_near, lined_far = lax.optimization_barrier((swapped, lined_near, lined_far))
     weights = lax.all_gather(swapped, "z", axis=0)
     own_rows = lax.dynamic_slice_in_dim(stack_input, pos_s * piece, piece, 0).astype(WIDE)
     square = jnp.sum(own_rows * own_rows, axis=-1, keepdims=True)
@@ -361,6 +386,8 @@
     cross = jnp.sum(cross.astype(WIDE), axis=0, keepdims=True).astype(LOW)
     cross = jnp.broadcast_to(cross, (count_y * count_z, cut_r, cut_c))
     cross = lax.all_to_all(cross, ("y", "z"), 0, 0, tiled=True)
+    cross, rows = lax.optimization_barrier((cross, rows))
+    rows = lax.all_to_all(rows, "y", 0, 0, tiled=True)
     cross_near = gather_line(cross, "x")
     cross_near, rows = lax.optimization_barrier((cross_near, rows))
     cross_far = lax.ppermute(cross_near, "c", swap_core)
@@ -429,17 +456,23 @@
     )(outputs)
 
     own_grads = lax.ppermute(grads, across, back_route)
-    shard_in, shard_out, squares = local_call(
+    squares = local_call(square_kernel, jax.ShapeDtypeStruct((8, 128), WIDE), (grads,))
+    squares = squares + lax.ppermute(squares, "c", swap_core)
+    for axis in ("x", "y"):
+        line = [shifted(squares, axis, d) for d in SHIFTS[1:]]
+        squares = (squares + line[0]) + (line[1] + line[2])
+    squares, own_grads = lax.optimization_barrier((squares, own_grads))
+    shard_in, shard_out = local_call(
         settle_kernel,
         (
             jax.ShapeDtypeStruct((features, rank), WIDE),
             jax.ShapeDtypeStruct((rank, features), WIDE),
-            jax.ShapeDtypeStruct((sources * count_z, 128), WIDE),
         ),
-        (gain_own, own_grads),
-    )
-    squares = lax.all_to_all(squares, EVERYONE, 0, 0, tiled=True)
-    total_sq = jnp.sum(squares[:, 0])
+        (own_grads,),
+    )
+    for distance in (4, 2, 1):
+        squares = squares + shifted(squares, "z", distance)
+    total_sq = squares[0, 0]
     norm_limit = clip_rms * math.sqrt(2.0 * model_width * rank * layers)
     clip_factor = norm_limit / jnp.maximum(jnp.sqrt(total_sq), norm_limit)
     new_in, new_first_in, new_second_in = adam_update(

time: 271 us -> 279 us (1.030)
  waiting for transfers between devices: 109 us -> 129 us
  blocking collectives: 45.5 us -> 26.4 us
  starting transfers between devices: 65.7 us -> 70.2 us
    all_to_all x2 -> x1, blocking collectives: 45.5 us -> 26.4 us  [shards(): cross = lax.all_to_all(cross, ('y', 'z'), 0, 0, tiled=True)]
    ppermute x18 -> x27, waiting for transfers between devices: 22.3 us -> 40.1 us  [shifted(): lax.ppermute(block, axis, [(i, (i + distance) % size) for i in range(size)])]
    ppermute x18 -> x27, starting transfers between devices: 24.2 us -> 36.5 us  [shifted(): lax.ppermute(block, axis, [(i, (i + distance) % size) for i in range(size)])]
    all_to_all x1, starting transfers between devices: 14.2 us -> 6.06 us  [shards(): cross = lax.all_to_all(cross, ('y', 'z'), 0, 0, tiled=True)]
    all_to_all x1, waiting for transfers between devices: 9.63 us -> 12.5 us  [shards(): cross = lax.all_to_all(cross, ('y', 'z'), 0, 0, tiled=True)]
    pallas_call x6 -> x7, Pallas kernels: 16.3 us -> 16.7 us  [local_call(): pl.pallas_call(kernel, out_shape=out_shape, in_specs=in_specs, out_specs=...]
    unnamed x26 -> x24, local copies, waits for them, and re-layouts: 5.42 us -> 5.66 us
  transfers between devices with their start and end apart: 31 -> 41, of which waited for: 18 -> 25; matrix products, arithmetic and copies ran while one was open for 1% -> 2% of each run, Pallas kernels for 2% -> 1%
where the time goes in v5:
time: 279 us; the launch traced here: 275 us
  waiting for transfers between devices  129 us (46%)
  starting transfers between devices  70.2 us (25%)
  blocking collectives  26.4 us (9%)
  Pallas kernels  19.1 us (7%)
  between operations  15.1 us (5%)
  local copies, waits for them, and re-layouts  8.31 us (3%)
  other arithmetic  6.43 us (2%)
    ppermute x27, waiting for transfers between devices, shifted(): lax.ppermute(block, axis, [(i, (i + distance) % size) for i in range(size)])  40.1 us
    ppermute x27, starting transfers between devices, shifted(): lax.ppermute(block, axis, [(i, (i + distance) % size) for i in range(size)])  36.5 us
    reduce_scatter x1, waiting for transfers between devices, shards(): grads = lax.psum_scatter(grads, 'z', scatter_dimension=0, tiled=True)[0]  31.9 us
    all_to_all x1, blocking collectives, shards(): cross = lax.all_to_all(cross, ('y', 'z'), 0, 0, tiled=True)  26.4 us
    all_to_all x1, waiting for transfers between devices, shards(): parts = lax.all_to_all(parts, ('x', 'y'), 0, 0, tiled=True)  18.6 us
    pallas_call x7, Pallas kernels, local_call(): pl.pallas_call(kernel, out_shape=out_shape, in_specs=in_specs, out_specs=...  16.7 us
    ppermute x1, waiting for transfers between devices, shards(): own_grads = lax.ppermute(grads, across, back_route)  12.6 us
    all_to_all x1, waiting for transfers between devices, shards(): cross = lax.all_to_all(cross, ('y', 'z'), 0, 0, tiled=True)  12.5 us
  transfers between devices with their start and end apart: 41, of which 25 were waited for; matrix products, arithmetic and copies ran while one was open for 2% of the time, Pallas kernels for 1%

profile of v5, /device:TPU:2, one launch (start us, length us, event | category | flops | bytes accessed | tf_op | source)
XLA Modules:
  0.0 275.0 jit_solution(11636290428182270033)
XLA Ops:
  10.0 2.2 collective-permute-start.3
  14.2 5.4 %collective-permute-done.3 = bf16[400,256]{1,0:T(8,128)(2,1)S(1)} collective-permute-done((bf16[400,256]{1,0:T(8,128)(2,1)S(1)}, bf16[400,256]{1,0:T(8,128)(2,1)S(1)}, u32[]{:S(2)}, u32[]{:S(2)}) %collective-permute-start.3) | collective-permute-done | bytes 204832 | tf_op jit(solution)/shard_map/ppermute | solution.py:87
  19.6 3.2 %collective-permute-done.2 = bf16[400,256]{1,0:T(8,128)(2,1)S(1)} collective-permute-done((bf16[400,256]{1,0:T(8,128)(2,1)S(1)}, bf16[400,256]{1,0:T(8,128)(2,1)S(1)}, u32[]{:S(2)}, u32[]{:S(2)}) %collective-permute-start.2) | collective-permute-done | bytes 204832 | tf_op jit(solution)/shard_map/ppermute | solution.py:87
  23.1 6.6 %collective-permute-start = (bf16[400,256]{1,0:T(8,128)(2,1)S(1)}, bf16[400,256]{1,0:T(8,128)(2,1)S(1)}, u32[]{:S(2)}, u32[]{:S(2)}) collective-permute-start(bf16[400,256]{1,0:T(8,128)(2,1)S(1)} %shard_map.144.own_ref), channel_id=1, source_target_pairs={{0,0},{1,33},{2,66},{3,99},{4,132},{5,165},{6,198},{7,231},{32,4},... | collective-permute-start | bytes 614408 | tf_op jit(solution)/shard_map/ppermute | solution.py:359
  29.6 5.7 %collective-permute-done = bf16[400,256]{1,0:T(8,128)(2,1)S(1)} collective-permute-done((bf16[400,256]{1,0:T(8,128)(2,1)S(1)}, bf16[400,256]{1,0:T(8,128)(2,1)S(1)}, u32[]{:S(2)}, u32[]{:S(2)}) %collective-permute-start) | collective-permute-done | bytes 204832 | tf_op jit(solution)/shard_map/ppermute | solution.py:359
  37.2 26.4 %all_to_all.25 = bf16[32,16,256]{2,1,0:T(8,128)(2,1)S(1)} all-to-all(bf16[32,16,256]{2,1,0:T(8,128)(2,1)S(1)} %shard_map.145), channel_id=1, replica_groups=mesh['x'=4,'c'=2,'y'=4,'z'=8] {'y','z'}, dimensions={0} | all-to-all | bytes 524288 | tf_op jit(solution)/shard_map/all_to_all | solution.py:385
  64.3 6.1 %all-to-all-start.1 = ((bf16[32,16,256]{2,1,0:T(8,128)(2,1)}), bf16[32,16,256]{2,1,0:T(8,128)(2,1)S(1)}, u32[]{:S(2)}, u32[]{:S(2)}) async-start(bf16[32,16,256]{2,1,0:T(8,128)(2,1)} %broadcast_in_dim.33), calls=%async_computation.1 | async-start | bytes 524288 | tf_op jit(solution)/shard_map/all_to_all | solution.py:388
  72.7 12.5 %all-to-all-done.1 = bf16[32,16,256]{2,1,0:T(8,128)(2,1)S(1)} async-done(((bf16[32,16,256]{2,1,0:T(8,128)(2,1)}), bf16[32,16,256]{2,1,0:T(8,128)(2,1)S(1)}, u32[]{:S(2)}, u32[]{:S(2)}) %all-to-all-start.1) | async-done | bytes 262176 | tf_op jit(solution)/shard_map/all_to_all | solution.py:388
  85.2 3.5 %all-to-all-start.2 = ((bf16[4,256,384]{2,1,0:T(8,128)(2,1)}), bf16[4,256,384]{2,1,0:T(8,128)(2,1)S(1)}, u32[]{:S(2)}, u32[]{:S(2)}) async-start(bf16[4,256,384]{2,1,0:T(8,128)(2,1)} %maximum_maximum_fusion), calls=%async_computation.2 | async-start | bytes 1572864 | tf_op jit(solution)/shard_map/all_to_all | solution.py:390
  88.9 2.0 collective-permute-start.5
  90.9 8.2 %collective-permute-done.7 = bf16[32,16,256]{2,1,0:T(8,128)(2,1)S(1)} collective-permute-done((bf16[32,16,256]{2,1,0:T(8,128)(2,1)S(1)}, bf16[32,16,256]{2,1,0:T(8,128)(2,1)S(1)}, u32[]{:S(2)}, u32[]{:S(2)}) %collective-permute-start.7) | collective-permute-done | bytes 262176 | tf_op jit(solution)/shard_map/ppermute | solution.py:87
  102.1 2.8 %shard_map.146 = (bf16[4,4,16,3072]{3,2,1,0:T(8,128)(2,1)S(1)}, bf16[4,4,16,3072]{3,2,1,0:T(8,128)(2,1)S(1)}) custom-call(s32[4]{0:T(128)S(1)} %pad_add_fusion.place_ref, bf16[4,256,384]{2,1,0:T(8,128)(2,1)S(1)} %all-to-all-done.2.rows_ref, bf16[8,400,256]{2,1,0:T(8,128)(2,1)S(1)} %bitcast.118), custom_call_target="tpu_custom_call" | custom-call | flops 1207959552 | bytes 5570560 | tf_op jit(solution)/shard_map/pallas_call | solution.py:74
  105.0 3.4 %collective-permute-done.8 = bf16[4,4,16,3072]{3,2,1,0:T(8,128)(2,1)S(1)} collective-permute-done((bf16[4,4,16,3072]{3,2,1,0:T(8,128)(2,1)S(1)}, bf16[4,4,16,3072]{3,2,1,0:T(8,128)(2,1)S(1)}, u32[]{:S(2)}, u32[]{:S(2)}) %collective-permute-start.8) | collective-permute-done | bytes 1572896 | tf_op jit(solution)/shard_map/ppermute | solution.py:403
  110.2 7.9 %all-to-all-start.3 = ((bf16[16,16,3072]{2,1,0:T(8,128)(2,1)}), bf16[16,16,3072]{2,1,0:T(8,128)(2,1)S(1)}, u32[]{:S(2)}, u32[]{:S(2)}) async-start(bf16[16,16,3072]{2,1,0:T(8,128)(2,1)} %bitcast.119), calls=%async_computation.3 | async-start | bytes 3145728 | tf_op jit(solution)/shard_map/all_to_all | solution.py:406
  121.2 18.6 %all-to-all-done.3.parts_ref = bf16[16,16,3072]{2,1,0:T(8,128)(2,1)S(1)} async-done(((bf16[16,16,3072]{2,1,0:T(8,128)(2,1)}), bf16[16,16,3072]{2,1,0:T(8,128)(2,1)S(1)}, u32[]{:S(2)}, u32[]{:S(2)}) %all-to-all-start.3) | async-done | bytes 1572896 | tf_op jit(solution)/shard_map/all_to_all | solution.py:406
  139.9 4.9 %shard_map.147 = (bf16[16,1152]{1,0:T(8,128)(2,1)S(1)}, bf16[16,1024]{1,0:T(8,128)(2,1)S(1)}) custom-call(s32[4]{0:T(128)S(1)} %pad_add_fusion.place_ref, bf16[16,16,3072]{2,1,0:T(8,128)(2,1)S(1)} %all-to-all-done.3.parts_ref, f32[16,128]{1,0:T(8,128)S(1)} %broadcast_in_dim.34.square_ref, bf16[4,32,16,256]{3,2,1,0:T(8,128)(2,1)S(1)} %pad_maximum_fusion.near_ref, ...), custom_call_target="tpu_custom_call" | custom-call | bytes 3747840 | tf_op jit(solution)/shard_map/pallas_call | solution.py:74
  144.7 2.3 collective-permute-start.12
  150.4 1.9 collective-permute-start.18
  152.7 2.9 %collective-permute-start.14 = (bf16[4,16,1152]{2,1,0:T(8,128)(2,1)S(1)}, bf16[4,16,1152]{2,1,0:T(8,128)(2,1)S(1)}, u32[]{:S(2)}, u32[]{:S(2)}) collective-permute-start(bf16[4,16,1152]{2,1,0:T(8,128)(2,1)S(1)} %get-tuple-element.56), channel_id=1, source_target_pairs={{0,24},{8,0},{16,8},{24,16},{1,25},{9,1},{17,9},{25,17},{2,26},{10... | collective-permute-start | bytes 442376 | tf_op jit(solution)/shard_map/ppermute | solution.py:87
  160.8 3.7 %collective-permute-start.22 = (bf16[4,16,1024]{2,1,0:T(8,128)(2,1)S(1)}, bf16[4,16,1024]{2,1,0:T(8,128)(2,1)S(1)}, u32[]{:S(2)}, u32[]{:S(2)}) collective-permute-start(bf16[4,16,1024]{2,1,0:T(8,128)(2,1)S(1)} %get-tuple-element.58), channel_id=1, source_target_pairs={{0,128},{64,192},{128,0},{192,64},{1,129},{65,193},{129,1},{193,65... | collective-permute-start | bytes 393224 | tf_op jit(solution)/shard_map/ppermute | solution.py:87
  165.5 2.0 collective-permute-done.22
  169.8 7.4 %shard_map.148 = (bf16[8,4,128,384]{3,2,1,0:T(8,128)(2,1)}, bf16[8,128,768]{2,1,0:T(8,128)(2,1)}) custom-call(s32[4]{0:T(128)S(1)} %pad_add_fusion.place_ref, bf16[4,256,384]{2,1,0:T(8,128)(2,1)S(1)} %all-to-all-done.2.rows_ref, bf16[8,400,256]{2,1,0:T(8,128)(2,1)} %bitcast.117, bf16[4,4,16,1152]{3,2,1,0:T(8,128)(2,1)S(1)} %pad_maximum_fusion.2.act_near_ref, ...), custom_call_target="tpu_custom_call" | custom-call | flops 1610612736 | bytes 9371648 | tf_op jit(solution)/shard_map/pallas_call | solution.py:74
  177.3 6.6 %all-to-all-start.4 = ((bf16[32,128,384]{2,1,0:T(8,128)(2,1)}), bf16[32,128,384]{2,1,0:T(8,128)(2,1)S(1)}, u32[]{:S(2)}, u32[]{:S(2)}) async-start(bf16[32,128,384]{2,1,0:T(8,128)(2,1)} %bitcast.120), calls=%async_computation.4 | async-start | bytes 6291456 | tf_op jit(solution)/shard_map/all_to_all | solution.py:447
  183.9 31.9 %reduce-scatter.2.cloned.1.call-done = bf16[1,128,768]{2,1,0:T(8,128)(2,1)} async-done(((bf16[8,128,768]{2,1,0:T(8,128)(2,1)}), bf16[1,128,768]{2,1,0:T(8,128)(2,1)}) %reduce-scatter.2.cloned.1.call-update) | async-done | bytes 196624 | tf_op jit(solution)/shard_map/reduce_scatter | solution.py:445
  218.2 2.0 collective-permute-start.27
  225.3 3.1 %collective-permute-start.30 = (f32[8,128]{1,0:T(8,128)S(1)}, f32[8,128]{1,0:T(8,128)S(1)}, u32[]{:S(2)}, u32[]{:S(2)}) collective-permute-start(f32[8,128]{1,0:T(8,128)S(1)} %add_add_fusion.1), channel_id=1, source_target_pairs={{0,16},{8,24},{16,0},{24,8},{1,17},{9,25},{17,1},{25,9},{2,18},{10... | collective-permute-start | bytes 12296 | tf_op jit(solution)/shard_map/ppermute | solution.py:87
  234.3 12.6 %collective-permute-done.31.grad_ref = bf16[128,768]{1,0:T(8,128)(2,1)S(1)} collective-permute-done((bf16[128,768]{1,0:T(8,128)(2,1)S(1)}, bf16[128,768]{1,0:T(8,128)(2,1)S(1)}, u32[]{:S(2)}, u32[]{:S(2)}) %collective-permute-start.31) | collective-permute-done | bytes 196640 | tf_op jit(solution)/shard_map/ppermute | solution.py:458
  246.9 2.2 collective-permute-start.32
  249.0 5.3 %collective-permute-done.32 = f32[8,128]{1,0:T(8,128)S(1)} collective-permute-done((f32[8,128]{1,0:T(8,128)S(1)}, f32[8,128]{1,0:T(8,128)S(1)}, u32[]{:S(2)}, u32[]{:S(2)}) %collective-permute-start.32) | collective-permute-done | bytes 4128 | tf_op jit(solution)/shard_map/ppermute | solution.py:87
  255.2 4.9 %collective-permute-done.33 = f32[8,128]{1,0:T(8,128)S(1)} collective-permute-done((f32[8,128]{1,0:T(8,128)S(1)}, f32[8,128]{1,0:T(8,128)S(1)}, u32[]{:S(2)}, u32[]{:S(2)}) %collective-permute-start.33) | collective-permute-done | bytes 4128 | tf_op jit(solution)/shard_map/ppermute | solution.py:87
  260.1 2.4 shard_map.149
  262.7 2.2 collective-permute-done.34
  (109 shorter events, 46.9 us)
Async XLA Ops:
  7.2 93.4 %all-gather.3.cloned.1.call-start = ((), (), s32[]{:S(2)}) async-start(), calls=%async_computation.7 | async-start | bytes 1843200 | tf_op jit(solution)/shard_map/all_gather | solution.py:373
  10.0 9.6 %collective-permute-start.3 = (bf16[400,256]{1,0:T(8,128)(2,1)S(1)}, bf16[400,256]{1,0:T(8,128)(2,1)S(1)}, u32[]{:S(2)}, u32[]{:S(2)}) collective-permute-start(bf16[400,256]{1,0:T(8,128)(2,1)S(1)} %shard_map.144.own_ref), channel_id=1, source_target_pairs={{0,128},{64,192},{128,0},{192,64},{1,129},{65,193},{129,1},{193,65... | collective-permute-start | bytes 614408 | tf_op jit(solution)/shard_map/ppermute | solution.py:87
  12.2 10.6 %collective-permute-start.2 = (bf16[400,256]{1,0:T(8,128)(2,1)S(1)}, bf16[400,256]{1,0:T(8,128)(2,1)S(1)}, u32[]{:S(2)}, u32[]{:S(2)}) collective-permute-start(bf16[400,256]{1,0:T(8,128)(2,1)S(1)} %shard_map.144.own_ref), channel_id=1, source_target_pairs={{0,192},{64,0},{128,64},{192,128},{1,193},{65,1},{129,65},{193,129... | collective-permute-start | bytes 614408 | tf_op jit(solution)/shard_map/ppermute | solution.py:87
  13.6 9.2 %collective-permute-start.1 = (bf16[400,256]{1,0:T(8,128)(2,1)S(1)}, bf16[400,256]{1,0:T(8,128)(2,1)S(1)}, u32[]{:S(2)}, u32[]{:S(2)}) collective-permute-start(bf16[400,256]{1,0:T(8,128)(2,1)S(1)} %shard_map.144.own_ref), channel_id=1, source_target_pairs={{0,64},{64,128},{128,192},{192,0},{1,65},{65,129},{129,193},{193,1... | collective-permute-start | bytes 614408 | tf_op jit(solution)/shard_map/ppermute | solution.py:87
  23.0 12.4 %collective-permute-start.4 = (bf16[4,400,256]{2,1,0:T(8,128)(2,1)S(1)}, bf16[4,400,256]{2,1,0:T(8,128)(2,1)S(1)}, u32[]{:S(2)}, u32[]{:S(2)}) collective-permute-start(bf16[4,400,256]{2,1,0:T(8,128)(2,1)S(1)} %pad_maximum_fusion.1.near_ref), channel_id=1, source_target_pairs={{0,32},{32,0},{1,33},{33,1},{2,34},{34,2},{3,35},{35,3},{4,36},{36... | collective-permute-start | bytes 2457608 | tf_op jit(solution)/shard_map/ppermute | solution.py:361
  23.1 12.3 %collective-permute-start = (bf16[400,256]{1,0:T(8,128)(2,1)S(1)}, bf16[400,256]{1,0:T(8,128)(2,1)S(1)}, u32[]{:S(2)}, u32[]{:S(2)}) collective-permute-start(bf16[400,256]{1,0:T(8,128)(2,1)S(1)} %shard_map.144.own_ref), channel_id=1, source_target_pairs={{0,0},{1,33},{2,66},{3,99},{4,132},{5,165},{6,198},{7,231},{32,4},... | collective-permute-start | bytes 614408 | tf_op jit(solution)/shard_map/ppermute | solution.py:359
  64.3 20.9 %all-to-all-start.1 = ((bf16[32,16,256]{2,1,0:T(8,128)(2,1)}), bf16[32,16,256]{2,1,0:T(8,128)(2,1)S(1)}, u32[]{:S(2)}, u32[]{:S(2)}) async-start(bf16[32,16,256]{2,1,0:T(8,128)(2,1)} %broadcast_in_dim.33), calls=%async_computation.1 | async-start | bytes 524288 | tf_op jit(solution)/shard_map/all_to_all | solution.py:388
  85.2 15.4 %all-to-all-start.2 = ((bf16[4,256,384]{2,1,0:T(8,128)(2,1)}), bf16[4,256,384]{2,1,0:T(8,128)(2,1)S(1)}, u32[]{:S(2)}, u32[]{:S(2)}) async-start(bf16[4,256,384]{2,1,0:T(8,128)(2,1)} %maximum_maximum_fusion), calls=%async_computation.2 | async-start | bytes 1572864 | tf_op jit(solution)/shard_map/all_to_all | solution.py:390
  88.7 10.4 %collective-permute-start.7 = (bf16[32,16,256]{2,1,0:T(8,128)(2,1)S(1)}, bf16[32,16,256]{2,1,0:T(8,128)(2,1)S(1)}, u32[]{:S(2)}, u32[]{:S(2)}) collective-permute-start(bf16[32,16,256]{2,1,0:T(8,128)(2,1)S(1)} %all-to-all-done.1), channel_id=1, source_target_pairs={{0,128},{64,192},{128,0},{192,64},{1,129},{65,193},{129,1},{193,65... | collective-permute-start | bytes 786440 | tf_op jit(solution)/shard_map/ppermute | solution.py:87
  88.8 11.6 %collective-permute-start.6 = (bf16[32,16,256]{2,1,0:T(8,128)(2,1)S(1)}, bf16[32,16,256]{2,1,0:T(8,128)(2,1)S(1)}, u32[]{:S(2)}, u32[]{:S(2)}) collective-permute-start(bf16[32,16,256]{2,1,0:T(8,128)(2,1)S(1)} %all-to-all-done.1), channel_id=1, source_target_pairs={{0,192},{64,0},{128,64},{192,128},{1,193},{65,1},{129,65},{193,129... | collective-permute-start | bytes 786440 | tf_op jit(solution)/shard_map/ppermute | solution.py:87
  88.9 11.5 %collective-permute-start.5 = (bf16[32,16,256]{2,1,0:T(8,128)(2,1)S(1)}, bf16[32,16,256]{2,1,0:T(8,128)(2,1)S(1)}, u32[]{:S(2)}, u32[]{:S(2)}) collective-permute-start(bf16[32,16,256]{2,1,0:T(8,128)(2,1)S(1)} %all-to-all-done.1), channel_id=1, source_target_pairs={{0,64},{64,128},{128,192},{192,0},{1,65},{65,129},{129,193},{193,1... | collective-permute-start | bytes 786440 | tf_op jit(solution)/shard_map/ppermute | solution.py:87
  110.2 29.6 %all-to-all-start.3 = ((bf16[16,16,3072]{2,1,0:T(8,128)(2,1)}), bf16[16,16,3072]{2,1,0:T(8,128)(2,1)S(1)}, u32[]{:S(2)}, u32[]{:S(2)}) async-start(bf16[16,16,3072]{2,1,0:T(8,128)(2,1)} %bitcast.119), calls=%async_computation.3 | async-start | bytes 3145728 | tf_op jit(solution)/shard_map/all_to_all | solution.py:406
  118.1 97.7 %reduce-scatter.2.cloned.1.call-start = ((), (), s32[]{:S(2)}) async-start(), calls=%async_computation.6 | async-start | bytes 1769472 | tf_op jit(solution)/shard_map/reduce_scatter | solution.py:445
  144.7 7.5 %collective-permute-start.12 = (bf16[16,1152]{1,0:T(8,128)(2,1)S(1)}, bf16[16,1152]{1,0:T(8,128)(2,1)S(1)}, u32[]{:S(2)}, u32[]{:S(2)}) collective-permute-start(bf16[16,1152]{1,0:T(8,128)(2,1)S(1)} %get-tuple-element.33), channel_id=1, source_target_pairs={{0,128},{64,192},{128,0},{192,64},{1,129},{65,193},{129,1},{193,65... | collective-permute-start | bytes 110600 | tf_op jit(solution)/shard_map/ppermute | solution.py:87
  147.0 5.4 %collective-permute-start.11 = (bf16[16,1152]{1,0:T(8,128)(2,1)S(1)}, bf16[16,1152]{1,0:T(8,128)(2,1)S(1)}, u32[]{:S(2)}, u32[]{:S(2)}) collective-permute-start(bf16[16,1152]{1,0:T(8,128)(2,1)S(1)} %get-tuple-element.33), channel_id=1, source_target_pairs={{0,192},{64,0},{128,64},{192,128},{1,193},{65,1},{129,65},{193,129... | collective-permute-start | bytes 110600 | tf_op jit(solution)/shard_map/ppermute | solution.py:87
  149.0 6.6 %collective-permute-start.19 = (bf16[16,1024]{1,0:T(8,128)(2,1)S(1)}, bf16[16,1024]{1,0:T(8,128)(2,1)S(1)}, u32[]{:S(2)}, u32[]{:S(2)}) collective-permute-start(bf16[16,1024]{1,0:T(8,128)(2,1)S(1)} %get-tuple-element.34), channel_id=1, source_target_pairs={{0,16},{8,24},{16,0},{24,8},{1,17},{9,25},{17,1},{25,9},{2,18},{10... | collective-permute-start | bytes 98312 | tf_op jit(solution)/shard_map/ppermute | solution.py:87
  150.4 6.8 %collective-permute-start.18 = (bf16[16,1024]{1,0:T(8,128)(2,1)S(1)}, bf16[16,1024]{1,0:T(8,128)(2,1)S(1)}, u32[]{:S(2)}, u32[]{:S(2)}) collective-permute-start(bf16[16,1024]{1,0:T(8,128)(2,1)S(1)} %get-tuple-element.34), channel_id=1, source_target_pairs={{0,24},{8,0},{16,8},{24,16},{1,25},{9,1},{17,9},{25,17},{2,26},{10... | collective-permute-start | bytes 98312 | tf_op jit(solution)/shard_map/ppermute | solution.py:87
  152.3 6.4 %collective-permute-start.17 = (bf16[16,1024]{1,0:T(8,128)(2,1)S(1)}, bf16[16,1024]{1,0:T(8,128)(2,1)S(1)}, u32[]{:S(2)}, u32[]{:S(2)}) collective-permute-start(bf16[16,1024]{1,0:T(8,128)(2,1)S(1)} %get-tuple-element.34), channel_id=1, source_target_pairs={{0,8},{8,16},{16,24},{24,0},{1,9},{9,17},{17,25},{25,1},{2,10},{10... | collective-permute-start | bytes 98312 | tf_op jit(solution)/shard_map/ppermute | solution.py:87
  152.7 8.1 %collective-permute-start.14 = (bf16[4,16,1152]{2,1,0:T(8,128)(2,1)S(1)}, bf16[4,16,1152]{2,1,0:T(8,128)(2,1)S(1)}, u32[]{:S(2)}, u32[]{:S(2)}) collective-permute-start(bf16[4,16,1152]{2,1,0:T(8,128)(2,1)S(1)} %get-tuple-element.56), channel_id=1, source_target_pairs={{0,24},{8,0},{16,8},{24,16},{1,25},{9,1},{17,9},{25,17},{2,26},{10... | collective-permute-start | bytes 442376 | tf_op jit(solution)/shard_map/ppermute | solution.py:87
  155.6 8.9 %collective-permute-start.13 = (bf16[4,16,1152]{2,1,0:T(8,128)(2,1)S(1)}, bf16[4,16,1152]{2,1,0:T(8,128)(2,1)S(1)}, u32[]{:S(2)}, u32[]{:S(2)}) collective-permute-start(bf16[4,16,1152]{2,1,0:T(8,128)(2,1)S(1)} %get-tuple-element.56), channel_id=1, source_target_pairs={{0,8},{8,16},{16,24},{24,0},{1,9},{9,17},{17,25},{25,1},{2,10},{10... | collective-permute-start | bytes 442376 | tf_op jit(solution)/shard_map/ppermute | solution.py:87
  155.6 8.9 %collective-permute-start.15 = (bf16[4,16,1152]{2,1,0:T(8,128)(2,1)S(1)}, bf16[4,16,1152]{2,1,0:T(8,128)(2,1)S(1)}, u32[]{:S(2)}, u32[]{:S(2)}) collective-permute-start(bf16[4,16,1152]{2,1,0:T(8,128)(2,1)S(1)} %get-tuple-element.56), channel_id=1, source_target_pairs={{0,16},{8,24},{16,0},{24,8},{1,17},{9,25},{17,1},{25,9},{2,18},{10... | collective-permute-start | bytes 442376 | tf_op jit(solution)/shard_map/ppermute | solution.py:87
  158.7 6.0 %collective-permute-start.21 = (bf16[4,16,1024]{2,1,0:T(8,128)(2,1)S(1)}, bf16[4,16,1024]{2,1,0:T(8,128)(2,1)S(1)}, u32[]{:S(2)}, u32[]{:S(2)}) collective-permute-start(bf16[4,16,1024]{2,1,0:T(8,128)(2,1)S(1)} %get-tuple-element.58), channel_id=1, source_target_pairs={{0,192},{64,0},{128,64},{192,128},{1,193},{65,1},{129,65},{193,129... | collective-permute-start | bytes 393224 | tf_op jit(solution)/shard_map/ppermute | solution.py:87
  160.5 5.0 %collective-permute-start.20 = (bf16[4,16,1024]{2,1,0:T(8,128)(2,1)S(1)}, bf16[4,16,1024]{2,1,0:T(8,128)(2,1)S(1)}, u32[]{:S(2)}, u32[]{:S(2)}) collective-permute-start(bf16[4,16,1024]{2,1,0:T(8,128)(2,1)S(1)} %get-tuple-element.58), channel_id=1, source_target_pairs={{0,64},{64,128},{128,192},{192,0},{1,65},{65,129},{129,193},{193,1... | collective-permute-start | bytes 393224 | tf_op jit(solution)/shard_map/ppermute | solution.py:87
  160.8 6.7 %collective-permute-start.22 = (bf16[4,16,1024]{2,1,0:T(8,128)(2,1)S(1)}, bf16[4,16,1024]{2,1,0:T(8,128)(2,1)S(1)}, u32[]{:S(2)}, u32[]{:S(2)}) collective-permute-start(bf16[4,16,1024]{2,1,0:T(8,128)(2,1)S(1)} %get-tuple-element.58), channel_id=1, source_target_pairs={{0,128},{64,192},{128,0},{192,64},{1,129},{65,193},{129,1},{193,65... | collective-permute-start | bytes 393224 | tf_op jit(solution)/shard_map/ppermute | solution.py:87
  164.7 5.1 %collective-permute-start.16 = (bf16[4,4,16,1152]{3,2,1,0:T(8,128)(2,1)S(1)}, bf16[4,4,16,1152]{3,2,1,0:T(8,128)(2,1)S(1)}, u32[]{:S(2)}, u32[]{:S(2)}) collective-permute-start(bf16[4,4,16,1152]{3,2,1,0:T(8,128)(2,1)S(1)} %pad_maximum_fusion.2.act_near_ref), channel_id=1, source_target_pairs={{0,32},{32,0},{1,33},{33,1},{2,34},{34,2},{3,35},{35,3},{4,36},{36... | collective-permute-start | bytes 1769480 | tf_op jit(solution)/shard_map/ppermute | solution.py:425
  177.3 82.8 %all-to-all-start.4 = ((bf16[32,128,384]{2,1,0:T(8,128)(2,1)}), bf16[32,128,384]{2,1,0:T(8,128)(2,1)S(1)}, u32[]{:S(2)}, u32[]{:S(2)}) async-start(bf16[32,128,384]{2,1,0:T(8,128)(2,1)} %bitcast.120), calls=%async_computation.4 | async-start | bytes 6291456 | tf_op jit(solution)/shard_map/all_to_all | solution.py:447
  218.2 5.1 %collective-permute-start.27 = (f32[8,128]{1,0:T(8,128)S(1)}, f32[8,128]{1,0:T(8,128)S(1)}, u32[]{:S(2)}, u32[]{:S(2)}) collective-permute-start(f32[8,128]{1,0:T(8,128)S(1)} %add.117), channel_id=1, source_target_pairs={{0,128},{64,192},{128,0},{192,64},{1,129},{65,193},{129,1},{193,65... | collective-permute-start | bytes 12296 | tf_op jit(solution)/shard_map/ppermute | solution.py:87
  225.3 7.1 %collective-permute-start.30 = (f32[8,128]{1,0:T(8,128)S(1)}, f32[8,128]{1,0:T(8,128)S(1)}, u32[]{:S(2)}, u32[]{:S(2)}) collective-permute-start(f32[8,128]{1,0:T(8,128)S(1)} %add_add_fusion.1), channel_id=1, source_target_pairs={{0,16},{8,24},{16,0},{24,8},{1,17},{9,25},{17,1},{25,9},{2,18},{10... | collective-permute-start | bytes 12296 | tf_op jit(solution)/shard_map/ppermute | solution.py:87
  229.4 4.8 %collective-permute-start.28 = (f32[8,128]{1,0:T(8,128)S(1)}, f32[8,128]{1,0:T(8,128)S(1)}, u32[]{:S(2)}, u32[]{:S(2)}) collective-permute-start(f32[8,128]{1,0:T(8,128)S(1)} %add_add_fusion.1), channel_id=1, source_target_pairs={{0,8},{8,16},{16,24},{24,0},{1,9},{9,17},{17,25},{25,1},{2,10},{10... | collective-permute-start | bytes 12296 | tf_op jit(solution)/shard_map/ppermute | solution.py:87
  230.4 16.4 %collective-permute-start.31 = (bf16[128,768]{1,0:T(8,128)(2,1)S(1)}, bf16[128,768]{1,0:T(8,128)(2,1)S(1)}, u32[]{:S(2)}, u32[]{:S(2)}) collective-permute-start(bf16[128,768]{1,0:T(8,128)(2,1)S(1)} %bitcast.114), channel_id=1, source_target_pairs={{0,0},{33,1},{66,2},{99,3},{132,4},{165,5},{198,6},{231,7},{4,32},... | collective-permute-start | bytes 589832 | tf_op jit(solution)/shard_map/ppermute | solution.py:458
  246.9 7.5 %collective-permute-start.32 = (f32[8,128]{1,0:T(8,128)S(1)}, f32[8,128]{1,0:T(8,128)S(1)}, u32[]{:S(2)}, u32[]{:S(2)}) collective-permute-start(f32[8,128]{1,0:T(8,128)S(1)} %add_add_fusion), channel_id=1, source_target_pairs={{0,4},{1,5},{2,6},{3,7},{4,0},{5,1},{6,2},{7,3},{8,12},{9,13},{10,... | collective-permute-start | bytes 12296 | tf_op jit(solution)/shard_map/ppermute | solution.py:87
  254.4 5.7 %collective-permute-start.33 = (f32[8,128]{1,0:T(8,128)S(1)}, f32[8,128]{1,0:T(8,128)S(1)}, u32[]{:S(2)}, u32[]{:S(2)}) collective-permute-start(f32[8,128]{1,0:T(8,128)S(1)} %add.124), channel_id=1, source_target_pairs={{0,2},{1,3},{2,4},{3,5},{4,6},{5,7},{6,0},{7,1},{8,10},{9,11},{10,... | collective-permute-start | bytes 12296 | tf_op jit(solution)/shard_map/ppermute | solution.py:87
  (21 other events, 67.6 us)
Sparse Core Ops, SparseCore 0:
  36.2 50.5 all-gather.2
  177.4 38.4 reduce-scatter.1

commit v6 on v5

--- a/solution.py
+++ b/solution.py
@@ -344,20 +344,21 @@
     features, rank = master_in.shape[1:]
     piece = tok_rows // layers
     swap_core = [(0, 1), (1, 0)]
-    route = [
-        (a * count_z + b, b * count_z + (b + TURNS[a]) % count_z)
-        for a in range(layers)
-        for b in range(count_z)
-    ]
-    back_route = [(j, i) for i, j in route]
+    grid = [(a, b) for a in range(layers) for b in range(count_z)]
+    turned = {(a, b): (b + TURNS[a]) % count_z for a, b in grid}
+    turn = [(a * count_z + b, a * count_z + turned[a, b]) for a, b in grid]
+    move = [(a * count_z + turned[a, b], b * count_z + turned[a, b]) for a, b in grid]
+    turn_back, move_back = ([(j, i) for i, j in route] for route in (turn, move))
     across = SECTION + ("z",)
 
     gain_own = lax.dynamic_slice_in_dim(norm_gain, (pos_y * count_z + pos_z) * features, features, 1)
     packed = local_call(
         pack_kernel, jax.ShapeDtypeStruct((features + EXTRA, 2 * rank), LOW), (gain_own, master_in, master_out)
     )
-    swapped = lax.ppermute(packed, across, route)
+    swapped = lax.ppermute(packed, across, turn)
     lined_near = gather_line(packed, "x")
+    swapped, lined_near = lax.optimization_barrier((swapped, lined_near))
+    swapped = lax.ppermute(swapped, across, move)
     lined_far = lax.ppermute(lined_near, "c", swap_core)
 
     def blocks_of(rows):
@@ -369,7 +370,6 @@
         )
 
     rows = jnp.concatenate([blocks_of(stack_input), blocks_of(out_cotangent)], axis=1)
-    swapped, lined_near, lined_far = lax.optimization_barrier((swapped, lined_near, lined_far))
     weights = lax.all_gather(swapped, "z", axis=0)
     own_rows = lax.dynamic_slice_in_dim(stack_input, pos_s * piece, piece, 0).astype(WIDE)
     square = jnp.sum(own_rows * own_rows, axis=-1, keepdims=True)
@@ -455,13 +455,13 @@
         compiler_params=pltpu.CompilerParams(vmem_limit_bytes=VMEM_BYTES),
     )(outputs)
 
-    own_grads = lax.ppermute(grads, across, back_route)
-    squares = local_call(square_kernel, jax.ShapeDtypeStruct((8, 128), WIDE), (grads,))
-    squares = squares + lax.ppermute(squares, "c", swap_core)
-    for axis in ("x", "y"):
-        line = [shifted(squares, axis, d) for d in SHIFTS[1:]]
-        squares = (squares + line[0]) + (line[1] + line[2])
-    squares, own_grads = lax.optimization_barrier((squares, own_grads))
+    grads = lax.ppermute(grads, across, move_back)
+    squares = local_call(
+        square_kernel, jax.ShapeDtypeStruct((sources * count_z, 128), WIDE), (grads,)
+    )
+    squares = lax.all_to_all(squares, EVERYONE, 0, 0, tiled=True)
+    total_sq = jnp.sum(squares[:, 0])
+    own_grads = lax.ppermute(grads, across, turn_back)
     shard_in, shard_out = local_call(
         settle_kernel,
         (
@@ -470,9 +470,6 @@
         ),
         (own_grads,),
     )
-    for distance in (4, 2, 1):
-        squares = squares + shifted(squares, "z", distance)
-    total_sq = squares[0, 0]
     norm_limit = clip_rms * math.sqrt(2.0 * model_width * rank * layers)
     clip_factor = norm_limit / jnp.maximum(jnp.sqrt(total_sq), norm_limit)
     new_in, new_first_in, new_second_in = adam_update(

time: 279 us -> 266 us (0.953); the launches traced: 275 us -> 265 us
  waiting for transfers between devices: 129 us -> 108 us
  starting transfers between devices: 70.2 us -> 81 us
    ppermute x27 -> x18, waiting for transfers between devices: 40.1 us -> 15.6 us  [shifted(): lax.ppermute(block, axis, [(i, (i + distance) % size) for i in range(size)])]
    ppermute x27 -> x18, starting transfers between devices: 36.5 us -> 24.5 us  [shifted(): lax.ppermute(block, axis, [(i, (i + distance) % size) for i in range(size)])]
    all_to_all x0 -> x1, starting transfers between devices: none -> 11.8 us  [shards(): squares = lax.all_to_all(squares, EVERYONE, 0, 0, tiled=True)]
    ppermute x3 -> x4, starting transfers between devices: 8.57 us -> 17.9 us  [the longest x1 7.6 us: shards(): own_grads = lax.ppermute(grads, across, turn_back)]
    ppermute x3 -> x4, waiting for transfers between devices: 19.5 us -> 21.1 us  [the longest x1 6.53 us: shards(): grads = lax.ppermute(grads, across, move_back)]
    unnamed x24 -> x18, local copies, waits for them, and re-layouts: 5.66 us -> 4.72 us
  transfers between devices with their start and end apart: 41 -> 34, of which waited for: 25 -> 19; matrix products, arithmetic and copies ran while one was open for 2% -> 2% of each run, Pallas kernels for 1% -> 2%
where the time goes in v6:
time: 266 us; the launch traced here: 265 us
  waiting for transfers between devices  108 us (41%)
  starting transfers between devices  81 us (30%)
  blocking collectives  25.6 us (10%)
  Pallas kernels  20.7 us (8%)
  between operations  15 us (6%)
  other arithmetic  8.05 us (3%)
  local copies, waits for them, and re-layouts  6.83 us (3%)
    reduce_scatter x1, waiting for transfers between devices, shards(): grads = lax.psum_scatter(grads, 'z', scatter_dimension=0, tiled=True)[0]  31.7 us
    all_to_all x1, blocking collectives, shards(): cross = lax.all_to_all(cross, ('y', 'z'), 0, 0, tiled=True)  25.6 us
    ppermute x18, starting transfers between devices, shifted(): lax.ppermute(block, axis, [(i, (i + distance) % size) for i in range(size)])  24.5 us
    all_to_all x1, waiting for transfers between devices, shards(): parts = lax.all_to_all(parts, ('x', 'y'), 0, 0, tiled=True)  18.6 us
    pallas_call x7, Pallas kernels, local_call(): pl.pallas_call(kernel, out_shape=out_shape, in_specs=in_specs, out_specs=...  18.2 us
    ppermute x18, waiting for transfers between devices, shifted(): lax.ppermute(block, axis, [(i, (i + distance) % size) for i in range(size)])  15.6 us
    all_to_all x1, waiting for transfers between devices, shards(): cross = lax.all_to_all(cross, ('y', 'z'), 0, 0, tiled=True)  12.4 us
    all_to_all x1, starting transfers between devices, shards(): squares = lax.all_to_all(squares, EVERYONE, 0, 0, tiled=True)  11.8 us
  transfers between devices with their start and end apart: 34, of which 19 were waited for; matrix products, arithmetic and copies ran while one was open for 2% of the time, Pallas kernels for 2%

profile of v6, /device:TPU:2, one launch (start us, length us, event | category | flops | bytes accessed | tf_op | source)
XLA Modules:
  0.0 265.4 jit_solution(17544486823573442596)
XLA Ops:
  10.0 2.2 collective-permute-start.3
  14.2 6.5 %collective-permute-start = (bf16[400,256]{1,0:T(8,128)(2,1)S(1)}, bf16[400,256]{1,0:T(8,128)(2,1)S(1)}, u32[]{:S(2)}, u32[]{:S(2)}) collective-permute-start(bf16[400,256]{1,0:T(8,128)(2,1)S(1)} %shard_map.144.own_ref), channel_id=1, source_target_pairs={{0,0},{1,1},{2,2},{3,3},{4,4},{5,5},{6,6},{7,7},{32,36},{33,37},{3... | collective-permute-start | bytes 614408 | tf_op jit(solution)/shard_map/ppermute | solution.py:358
  20.8 2.0 collective-permute-done.2
  23.0 3.8 %collective-permute-done = bf16[400,256]{1,0:T(8,128)(2,1)S(1)} collective-permute-done((bf16[400,256]{1,0:T(8,128)(2,1)S(1)}, bf16[400,256]{1,0:T(8,128)(2,1)S(1)}, u32[]{:S(2)}, u32[]{:S(2)}) %collective-permute-start) | collective-permute-done | bytes 204832 | tf_op jit(solution)/shard_map/ppermute | solution.py:358
  26.8 1.9 collective-permute-start.8
  28.7 5.4 %collective-permute-done.8 = bf16[400,256]{1,0:T(8,128)(2,1)S(1)} collective-permute-done((bf16[400,256]{1,0:T(8,128)(2,1)S(1)}, bf16[400,256]{1,0:T(8,128)(2,1)S(1)}, u32[]{:S(2)}, u32[]{:S(2)}) %collective-permute-start.8) | collective-permute-done | bytes 204832 | tf_op jit(solution)/shard_map/ppermute | solution.py:361
  34.9 2.0 collective-permute-start.4
  39.8 25.6 %all_to_all.37 = bf16[32,16,256]{2,1,0:T(8,128)(2,1)S(1)} all-to-all(bf16[32,16,256]{2,1,0:T(8,128)(2,1)S(1)} %shard_map.145), channel_id=1, replica_groups=mesh['x'=4,'c'=2,'y'=4,'z'=8] {'y','z'}, dimensions={0} | all-to-all | bytes 524288 | tf_op jit(solution)/shard_map/all_to_all | solution.py:385
  66.2 5.8 %all-to-all-start.1 = ((bf16[32,16,256]{2,1,0:T(8,128)(2,1)}), bf16[32,16,256]{2,1,0:T(8,128)(2,1)S(1)}, u32[]{:S(2)}, u32[]{:S(2)}) async-start(bf16[32,16,256]{2,1,0:T(8,128)(2,1)} %broadcast_in_dim.33), calls=%async_computation.1 | async-start | bytes 524288 | tf_op jit(solution)/shard_map/all_to_all | solution.py:388
  74.3 12.4 %all-to-all-done.1 = bf16[32,16,256]{2,1,0:T(8,128)(2,1)S(1)} async-done(((bf16[32,16,256]{2,1,0:T(8,128)(2,1)}), bf16[32,16,256]{2,1,0:T(8,128)(2,1)S(1)}, u32[]{:S(2)}, u32[]{:S(2)}) %all-to-all-start.1) | async-done | bytes 262176 | tf_op jit(solution)/shard_map/all_to_all | solution.py:388
  86.7 3.5 %all-to-all-start.2 = ((bf16[4,256,384]{2,1,0:T(8,128)(2,1)}), bf16[4,256,384]{2,1,0:T(8,128)(2,1)S(1)}, u32[]{:S(2)}, u32[]{:S(2)}) async-start(bf16[4,256,384]{2,1,0:T(8,128)(2,1)} %maximum_maximum_fusion), calls=%async_computation.2 | async-start | bytes 1572864 | tf_op jit(solution)/shard_map/all_to_all | solution.py:390
  92.6 7.7 %collective-permute-done.7 = bf16[32,16,256]{2,1,0:T(8,128)(2,1)S(1)} collective-permute-done((bf16[32,16,256]{2,1,0:T(8,128)(2,1)S(1)}, bf16[32,16,256]{2,1,0:T(8,128)(2,1)S(1)}, u32[]{:S(2)}, u32[]{:S(2)}) %collective-permute-start.7) | collective-permute-done | bytes 262176 | tf_op jit(solution)/shard_map/ppermute | solution.py:87
  103.1 2.9 %shard_map.146 = (bf16[4,4,16,3072]{3,2,1,0:T(8,128)(2,1)S(1)}, bf16[4,4,16,3072]{3,2,1,0:T(8,128)(2,1)S(1)}) custom-call(s32[4]{0:T(128)S(1)} %pad_add_fusion.place_ref, bf16[4,256,384]{2,1,0:T(8,128)(2,1)S(1)} %all-to-all-done.2.rows_ref, bf16[8,400,256]{2,1,0:T(8,128)(2,1)S(1)} %bitcast.119), custom_call_target="tpu_custom_call" | custom-call | flops 1207959552 | bytes 5570560 | tf_op jit(solution)/shard_map/pallas_call | solution.py:74
  106.1 3.4 %collective-permute-done.9 = bf16[4,4,16,3072]{3,2,1,0:T(8,128)(2,1)S(1)} collective-permute-done((bf16[4,4,16,3072]{3,2,1,0:T(8,128)(2,1)S(1)}, bf16[4,4,16,3072]{3,2,1,0:T(8,128)(2,1)S(1)}, u32[]{:S(2)}, u32[]{:S(2)}) %collective-permute-start.9) | collective-permute-done | bytes 1572896 | tf_op jit(solution)/shard_map/ppermute | solution.py:403
  111.2 8.0 %all-to-all-start.3 = ((bf16[16,16,3072]{2,1,0:T(8,128)(2,1)}), bf16[16,16,3072]{2,1,0:T(8,128)(2,1)S(1)}, u32[]{:S(2)}, u32[]{:S(2)}) async-start(bf16[16,16,3072]{2,1,0:T(8,128)(2,1)} %bitcast.120), calls=%async_computation.3 | async-start | bytes 3145728 | tf_op jit(solution)/shard_map/all_to_all | solution.py:406
  122.3 18.6 %all-to-all-done.3.parts_ref = bf16[16,16,3072]{2,1,0:T(8,128)(2,1)S(1)} async-done(((bf16[16,16,3072]{2,1,0:T(8,128)(2,1)}), bf16[16,16,3072]{2,1,0:T(8,128)(2,1)S(1)}, u32[]{:S(2)}, u32[]{:S(2)}) %all-to-all-start.3) | async-done | bytes 1572896 | tf_op jit(solution)/shard_map/all_to_all | solution.py:406
  141.0 4.9 %shard_map.147 = (bf16[16,1152]{1,0:T(8,128)(2,1)S(1)}, bf16[16,1024]{1,0:T(8,128)(2,1)S(1)}) custom-call(s32[4]{0:T(128)S(1)} %pad_add_fusion.place_ref, bf16[16,16,3072]{2,1,0:T(8,128)(2,1)S(1)} %all-to-all-done.3.parts_ref, f32[16,128]{1,0:T(8,128)S(1)} %broadcast_in_dim.34.square_ref, bf16[4,32,16,256]{3,2,1,0:T(8,128)(2,1)S(1)} %pad_maximum_fusion.near_ref, ...), custom_call_target="tpu_custom_call" | custom-call | bytes 3747840 | tf_op jit(solution)/shard_map/pallas_call | solution.py:74
  145.8 2.3 collective-permute-start.13
  151.5 1.9 collective-permute-start.19
  153.8 2.9 %collective-permute-start.15 = (bf16[4,16,1152]{2,1,0:T(8,128)(2,1)S(1)}, bf16[4,16,1152]{2,1,0:T(8,128)(2,1)S(1)}, u32[]{:S(2)}, u32[]{:S(2)}) collective-permute-start(bf16[4,16,1152]{2,1,0:T(8,128)(2,1)S(1)} %get-tuple-element.50), channel_id=1, source_target_pairs={{0,24},{8,0},{16,8},{24,16},{1,25},{9,1},{17,9},{25,17},{2,26},{10... | collective-permute-start | bytes 442376 | tf_op jit(solution)/shard_map/ppermute | solution.py:87
  161.9 3.7 %collective-permute-start.23 = (bf16[4,16,1024]{2,1,0:T(8,128)(2,1)S(1)}, bf16[4,16,1024]{2,1,0:T(8,128)(2,1)S(1)}, u32[]{:S(2)}, u32[]{:S(2)}) collective-permute-start(bf16[4,16,1024]{2,1,0:T(8,128)(2,1)S(1)} %get-tuple-element.52), channel_id=1, source_target_pairs={{0,128},{64,192},{128,0},{192,64},{1,129},{65,193},{129,1},{193,65... | collective-permute-start | bytes 393224 | tf_op jit(solution)/shard_map/ppermute | solution.py:87
  166.6 2.0 collective-permute-done.23
  170.9 7.4 %shard_map.148 = (bf16[8,4,128,384]{3,2,1,0:T(8,128)(2,1)}, bf16[8,128,768]{2,1,0:T(8,128)(2,1)}) custom-call(s32[4]{0:T(128)S(1)} %pad_add_fusion.place_ref, bf16[4,256,384]{2,1,0:T(8,128)(2,1)S(1)} %all-to-all-done.2.rows_ref, bf16[8,400,256]{2,1,0:T(8,128)(2,1)} %bitcast.118, bf16[4,4,16,1152]{3,2,1,0:T(8,128)(2,1)S(1)} %pad_maximum_fusion.2.act_near_ref, ...), custom_call_target="tpu_custom_call" | custom-call | flops 1610612736 | bytes 9371648 | tf_op jit(solution)/shard_map/pallas_call | solution.py:74
  178.3 6.6 %all-to-all-start.4 = ((bf16[32,128,384]{2,1,0:T(8,128)(2,1)}), bf16[32,128,384]{2,1,0:T(8,128)(2,1)S(1)}, u32[]{:S(2)}, u32[]{:S(2)}) async-start(bf16[32,128,384]{2,1,0:T(8,128)(2,1)} %bitcast.122), calls=%async_computation.4 | async-start | bytes 6291456 | tf_op jit(solution)/shard_map/all_to_all | solution.py:447
  185.0 31.7 %reduce-scatter.2.cloned.1.call-done = bf16[1,128,768]{2,1,0:T(8,128)(2,1)} async-done(((bf16[8,128,768]{2,1,0:T(8,128)(2,1)}), bf16[1,128,768]{2,1,0:T(8,128)(2,1)}) %reduce-scatter.2.cloned.1.call-update) | async-done | bytes 196624 | tf_op jit(solution)/shard_map/reduce_scatter | solution.py:445
  216.7 1.9 collective-permute-start.25
  218.6 6.5 %collective-permute-done.25.grad_ref = bf16[128,768]{1,0:T(8,128)(2,1)} collective-permute-done((bf16[128,768]{1,0:T(8,128)(2,1)}, bf16[128,768]{1,0:T(8,128)(2,1)}, u32[]{:S(2)}, u32[]{:S(2)}) %collective-permute-start.25) | collective-permute-done | bytes 196640 | tf_op jit(solution)/shard_map/ppermute | solution.py:458
  227.0 11.8 %all-to-all-start.5 = ((f32[256,1,128]{2,1,0:T(1,128)}), f32[256,1,128]{2,1,0:T(1,128)S(1)}, u32[]{:S(2)}, u32[]{:S(2)}) async-start(f32[256,1,128]{2,1,0:T(1,128)} %bitcast.45), calls=%async_computation.6 | async-start | bytes 262144 | tf_op jit(solution)/shard_map/all_to_all | solution.py:462
  238.8 7.6 %collective-permute-start.26 = (bf16[128,768]{1,0:T(8,128)(2,1)}, bf16[128,768]{1,0:T(8,128)(2,1)S(1)}, u32[]{:S(2)}, u32[]{:S(2)}) collective-permute-start(bf16[128,768]{1,0:T(8,128)(2,1)} %collective-permute-done.25.grad_ref), channel_id=1, source_target_pairs={{0,0},{1,1},{2,2},{3,3},{4,4},{5,5},{6,6},{7,7},{36,32},{37,33},{3... | collective-permute-start | bytes 589832 | tf_op jit(solution)/shard_map/ppermute | solution.py:464
  246.4 2.4 shard_map.149
  248.9 5.3 %collective-permute-done.26.grad_ref = bf16[128,768]{1,0:T(8,128)(2,1)S(1)} collective-permute-done((bf16[128,768]{1,0:T(8,128)(2,1)}, bf16[128,768]{1,0:T(8,128)(2,1)S(1)}, u32[]{:S(2)}, u32[]{:S(2)}) %collective-permute-start.26) | collective-permute-done | bytes 196640 | tf_op jit(solution)/shard_map/ppermute | solution.py:464
  255.6 2.0 fusion.11
  (83 shorter events, 37.6 us)
Async XLA Ops:
  7.2 94.5 %all-gather.3.cloned.1.call-start = ((), (), s32[]{:S(2)}) async-start(), calls=%async_computation.8 | async-start | bytes 1843200 | tf_op jit(solution)/shard_map/all_gather | solution.py:373
  10.0 10.8 %collective-permute-start.3 = (bf16[400,256]{1,0:T(8,128)(2,1)S(1)}, bf16[400,256]{1,0:T(8,128)(2,1)S(1)}, u32[]{:S(2)}, u32[]{:S(2)}) collective-permute-start(bf16[400,256]{1,0:T(8,128)(2,1)S(1)} %shard_map.144.own_ref), channel_id=1, source_target_pairs={{0,128},{64,192},{128,0},{192,64},{1,129},{65,193},{129,1},{193,65... | collective-permute-start | bytes 614408 | tf_op jit(solution)/shard_map/ppermute | solution.py:87
  12.2 10.6 %collective-permute-start.2 = (bf16[400,256]{1,0:T(8,128)(2,1)S(1)}, bf16[400,256]{1,0:T(8,128)(2,1)S(1)}, u32[]{:S(2)}, u32[]{:S(2)}) collective-permute-start(bf16[400,256]{1,0:T(8,128)(2,1)S(1)} %shard_map.144.own_ref), channel_id=1, source_target_pairs={{0,192},{64,0},{128,64},{192,128},{1,193},{65,1},{129,65},{193,129... | collective-permute-start | bytes 614408 | tf_op jit(solution)/shard_map/ppermute | solution.py:87
  13.6 9.2 %collective-permute-start.1 = (bf16[400,256]{1,0:T(8,128)(2,1)S(1)}, bf16[400,256]{1,0:T(8,128)(2,1)S(1)}, u32[]{:S(2)}, u32[]{:S(2)}) collective-permute-start(bf16[400,256]{1,0:T(8,128)(2,1)S(1)} %shard_map.144.own_ref), channel_id=1, source_target_pairs={{0,64},{64,128},{128,192},{192,0},{1,65},{65,129},{129,193},{193,1... | collective-permute-start | bytes 614408 | tf_op jit(solution)/shard_map/ppermute | solution.py:87
  14.2 12.6 %collective-permute-start = (bf16[400,256]{1,0:T(8,128)(2,1)S(1)}, bf16[400,256]{1,0:T(8,128)(2,1)S(1)}, u32[]{:S(2)}, u32[]{:S(2)}) collective-permute-start(bf16[400,256]{1,0:T(8,128)(2,1)S(1)} %shard_map.144.own_ref), channel_id=1, source_target_pairs={{0,0},{1,1},{2,2},{3,3},{4,4},{5,5},{6,6},{7,7},{32,36},{33,37},{3... | collective-permute-start | bytes 614408 | tf_op jit(solution)/shard_map/ppermute | solution.py:358
  26.8 7.4 %collective-permute-start.8 = (bf16[400,256]{1,0:T(8,128)(2,1)S(1)}, bf16[400,256]{1,0:T(8,128)(2,1)S(1)}, u32[]{:S(2)}, u32[]{:S(2)}) collective-permute-start(bf16[400,256]{1,0:T(8,128)(2,1)S(1)} %collective-permute-done), channel_id=1, source_target_pairs={{0,0},{1,33},{2,66},{3,99},{4,132},{5,165},{6,198},{7,231},{36,4},... | collective-permute-start | bytes 614408 | tf_op jit(solution)/shard_map/ppermute | solution.py:361
  34.9 3.9 %collective-permute-start.4 = (bf16[4,400,256]{2,1,0:T(8,128)(2,1)S(1)}, bf16[4,400,256]{2,1,0:T(8,128)(2,1)S(1)}, u32[]{:S(2)}, u32[]{:S(2)}) collective-permute-start(bf16[4,400,256]{2,1,0:T(8,128)(2,1)S(1)} %pad_maximum_fusion.1.near_ref), channel_id=1, source_target_pairs={{0,32},{32,0},{1,33},{33,1},{2,34},{34,2},{3,35},{35,3},{4,36},{36... | collective-permute-start | bytes 2457608 | tf_op jit(solution)/shard_map/ppermute | solution.py:362
  66.2 20.5 %all-to-all-start.1 = ((bf16[32,16,256]{2,1,0:T(8,128)(2,1)}), bf16[32,16,256]{2,1,0:T(8,128)(2,1)S(1)}, u32[]{:S(2)}, u32[]{:S(2)}) async-start(bf16[32,16,256]{2,1,0:T(8,128)(2,1)} %broadcast_in_dim.33), calls=%async_computation.1 | async-start | bytes 524288 | tf_op jit(solution)/shard_map/all_to_all | solution.py:388
  86.7 14.9 %all-to-all-start.2 = ((bf16[4,256,384]{2,1,0:T(8,128)(2,1)}), bf16[4,256,384]{2,1,0:T(8,128)(2,1)S(1)}, u32[]{:S(2)}, u32[]{:S(2)}) async-start(bf16[4,256,384]{2,1,0:T(8,128)(2,1)} %maximum_maximum_fusion), calls=%async_computation.2 | async-start | bytes 1572864 | tf_op jit(solution)/shard_map/all_to_all | solution.py:390
  90.2 10.1 %collective-permute-start.7 = (bf16[32,16,256]{2,1,0:T(8,128)(2,1)S(1)}, bf16[32,16,256]{2,1,0:T(8,128)(2,1)S(1)}, u32[]{:S(2)}, u32[]{:S(2)}) collective-permute-start(bf16[32,16,256]{2,1,0:T(8,128)(2,1)S(1)} %all-to-all-done.1), channel_id=1, source_target_pairs={{0,128},{64,192},{128,0},{192,64},{1,129},{65,193},{129,1},{193,65... | collective-permute-start | bytes 786440 | tf_op jit(solution)/shard_map/ppermute | solution.py:87
  90.5 11.0 %collective-permute-start.6 = (bf16[32,16,256]{2,1,0:T(8,128)(2,1)S(1)}, bf16[32,16,256]{2,1,0:T(8,128)(2,1)S(1)}, u32[]{:S(2)}, u32[]{:S(2)}) collective-permute-start(bf16[32,16,256]{2,1,0:T(8,128)(2,1)S(1)} %all-to-all-done.1), channel_id=1, source_target_pairs={{0,192},{64,0},{128,64},{192,128},{1,193},{65,1},{129,65},{193,129... | collective-permute-start | bytes 786440 | tf_op jit(solution)/shard_map/ppermute | solution.py:87
  92.2 9.3 %collective-permute-start.5 = (bf16[32,16,256]{2,1,0:T(8,128)(2,1)S(1)}, bf16[32,16,256]{2,1,0:T(8,128)(2,1)S(1)}, u32[]{:S(2)}, u32[]{:S(2)}) collective-permute-start(bf16[32,16,256]{2,1,0:T(8,128)(2,1)S(1)} %all-to-all-done.1), channel_id=1, source_target_pairs={{0,64},{64,128},{128,192},{192,0},{1,65},{65,129},{129,193},{193,1... | collective-permute-start | bytes 786440 | tf_op jit(solution)/shard_map/ppermute | solution.py:87
  106.0 3.5 %collective-permute-start.9 = (bf16[4,4,16,3072]{3,2,1,0:T(8,128)(2,1)S(1)}, bf16[4,4,16,3072]{3,2,1,0:T(8,128)(2,1)S(1)}, u32[]{:S(2)}, u32[]{:S(2)}) collective-permute-start(bf16[4,4,16,3072]{3,2,1,0:T(8,128)(2,1)S(1)} %get-tuple-element.27), channel_id=1, source_target_pairs={{0,32},{32,0},{1,33},{33,1},{2,34},{34,2},{3,35},{35,3},{4,36},{36... | collective-permute-start | bytes 4718600 | tf_op jit(solution)/shard_map/ppermute | solution.py:403
  111.2 29.7 %all-to-all-start.3 = ((bf16[16,16,3072]{2,1,0:T(8,128)(2,1)}), bf16[16,16,3072]{2,1,0:T(8,128)(2,1)S(1)}, u32[]{:S(2)}, u32[]{:S(2)}) async-start(bf16[16,16,3072]{2,1,0:T(8,128)(2,1)} %bitcast.120), calls=%async_computation.3 | async-start | bytes 3145728 | tf_op jit(solution)/shard_map/all_to_all | solution.py:406
  119.2 97.5 %reduce-scatter.2.cloned.1.call-start = ((), (), s32[]{:S(2)}) async-start(), calls=%async_computation.7 | async-start | bytes 1769472 | tf_op jit(solution)/shard_map/reduce_scatter | solution.py:445
  145.8 7.5 %collective-permute-start.13 = (bf16[16,1152]{1,0:T(8,128)(2,1)S(1)}, bf16[16,1152]{1,0:T(8,128)(2,1)S(1)}, u32[]{:S(2)}, u32[]{:S(2)}) collective-permute-start(bf16[16,1152]{1,0:T(8,128)(2,1)S(1)} %get-tuple-element.29), channel_id=1, source_target_pairs={{0,128},{64,192},{128,0},{192,64},{1,129},{65,193},{129,1},{193,65... | collective-permute-start | bytes 110600 | tf_op jit(solution)/shard_map/ppermute | solution.py:87
  148.1 5.4 %collective-permute-start.12 = (bf16[16,1152]{1,0:T(8,128)(2,1)S(1)}, bf16[16,1152]{1,0:T(8,128)(2,1)S(1)}, u32[]{:S(2)}, u32[]{:S(2)}) collective-permute-start(bf16[16,1152]{1,0:T(8,128)(2,1)S(1)} %get-tuple-element.29), channel_id=1, source_target_pairs={{0,192},{64,0},{128,64},{192,128},{1,193},{65,1},{129,65},{193,129... | collective-permute-start | bytes 110600 | tf_op jit(solution)/shard_map/ppermute | solution.py:87
  149.9 4.0 %collective-permute-start.11 = (bf16[16,1152]{1,0:T(8,128)(2,1)S(1)}, bf16[16,1152]{1,0:T(8,128)(2,1)S(1)}, u32[]{:S(2)}, u32[]{:S(2)}) collective-permute-start(bf16[16,1152]{1,0:T(8,128)(2,1)S(1)} %get-tuple-element.29), channel_id=1, source_target_pairs={{0,64},{64,128},{128,192},{192,0},{1,65},{65,129},{129,193},{193,1... | collective-permute-start | bytes 110600 | tf_op jit(solution)/shard_map/ppermute | solution.py:87
  150.1 6.6 %collective-permute-start.20 = (bf16[16,1024]{1,0:T(8,128)(2,1)S(1)}, bf16[16,1024]{1,0:T(8,128)(2,1)S(1)}, u32[]{:S(2)}, u32[]{:S(2)}) collective-permute-start(bf16[16,1024]{1,0:T(8,128)(2,1)S(1)} %get-tuple-element.30), channel_id=1, source_target_pairs={{0,16},{8,24},{16,0},{24,8},{1,17},{9,25},{17,1},{25,9},{2,18},{10... | collective-permute-start | bytes 98312 | tf_op jit(solution)/shard_map/ppermute | solution.py:87
  151.5 6.8 %collective-permute-start.19 = (bf16[16,1024]{1,0:T(8,128)(2,1)S(1)}, bf16[16,1024]{1,0:T(8,128)(2,1)S(1)}, u32[]{:S(2)}, u32[]{:S(2)}) collective-permute-start(bf16[16,1024]{1,0:T(8,128)(2,1)S(1)} %get-tuple-element.30), channel_id=1, source_target_pairs={{0,24},{8,0},{16,8},{24,16},{1,25},{9,1},{17,9},{25,17},{2,26},{10... | collective-permute-start | bytes 98312 | tf_op jit(solution)/shard_map/ppermute | solution.py:87
  153.4 6.4 %collective-permute-start.18 = (bf16[16,1024]{1,0:T(8,128)(2,1)S(1)}, bf16[16,1024]{1,0:T(8,128)(2,1)S(1)}, u32[]{:S(2)}, u32[]{:S(2)}) collective-permute-start(bf16[16,1024]{1,0:T(8,128)(2,1)S(1)} %get-tuple-element.30), channel_id=1, source_target_pairs={{0,8},{8,16},{16,24},{24,0},{1,9},{9,17},{17,25},{25,1},{2,10},{10... | collective-permute-start | bytes 98312 | tf_op jit(solution)/shard_map/ppermute | solution.py:87
  153.8 8.1 %collective-permute-start.15 = (bf16[4,16,1152]{2,1,0:T(8,128)(2,1)S(1)}, bf16[4,16,1152]{2,1,0:T(8,128)(2,1)S(1)}, u32[]{:S(2)}, u32[]{:S(2)}) collective-permute-start(bf16[4,16,1152]{2,1,0:T(8,128)(2,1)S(1)} %get-tuple-element.50), channel_id=1, source_target_pairs={{0,24},{8,0},{16,8},{24,16},{1,25},{9,1},{17,9},{25,17},{2,26},{10... | collective-permute-start | bytes 442376 | tf_op jit(solution)/shard_map/ppermute | solution.py:87
  156.7 8.9 %collective-permute-start.14 = (bf16[4,16,1152]{2,1,0:T(8,128)(2,1)S(1)}, bf16[4,16,1152]{2,1,0:T(8,128)(2,1)S(1)}, u32[]{:S(2)}, u32[]{:S(2)}) collective-permute-start(bf16[4,16,1152]{2,1,0:T(8,128)(2,1)S(1)} %get-tuple-element.50), channel_id=1, source_target_pairs={{0,8},{8,16},{16,24},{24,0},{1,9},{9,17},{17,25},{25,1},{2,10},{10... | collective-permute-start | bytes 442376 | tf_op jit(solution)/shard_map/ppermute | solution.py:87
  156.7 8.9 %collective-permute-start.16 = (bf16[4,16,1152]{2,1,0:T(8,128)(2,1)S(1)}, bf16[4,16,1152]{2,1,0:T(8,128)(2,1)S(1)}, u32[]{:S(2)}, u32[]{:S(2)}) collective-permute-start(bf16[4,16,1152]{2,1,0:T(8,128)(2,1)S(1)} %get-tuple-element.50), channel_id=1, source_target_pairs={{0,16},{8,24},{16,0},{24,8},{1,17},{9,25},{17,1},{25,9},{2,18},{10... | collective-permute-start | bytes 442376 | tf_op jit(solution)/shard_map/ppermute | solution.py:87
  159.8 6.0 %collective-permute-start.22 = (bf16[4,16,1024]{2,1,0:T(8,128)(2,1)S(1)}, bf16[4,16,1024]{2,1,0:T(8,128)(2,1)S(1)}, u32[]{:S(2)}, u32[]{:S(2)}) collective-permute-start(bf16[4,16,1024]{2,1,0:T(8,128)(2,1)S(1)} %get-tuple-element.52), channel_id=1, source_target_pairs={{0,192},{64,0},{128,64},{192,128},{1,193},{65,1},{129,65},{193,129... | collective-permute-start | bytes 393224 | tf_op jit(solution)/shard_map/ppermute | solution.py:87
  161.6 5.0 %collective-permute-start.21 = (bf16[4,16,1024]{2,1,0:T(8,128)(2,1)S(1)}, bf16[4,16,1024]{2,1,0:T(8,128)(2,1)S(1)}, u32[]{:S(2)}, u32[]{:S(2)}) collective-permute-start(bf16[4,16,1024]{2,1,0:T(8,128)(2,1)S(1)} %get-tuple-element.52), channel_id=1, source_target_pairs={{0,64},{64,128},{128,192},{192,0},{1,65},{65,129},{129,193},{193,1... | collective-permute-start | bytes 393224 | tf_op jit(solution)/shard_map/ppermute | solution.py:87
  161.9 6.7 %collective-permute-start.23 = (bf16[4,16,1024]{2,1,0:T(8,128)(2,1)S(1)}, bf16[4,16,1024]{2,1,0:T(8,128)(2,1)S(1)}, u32[]{:S(2)}, u32[]{:S(2)}) collective-permute-start(bf16[4,16,1024]{2,1,0:T(8,128)(2,1)S(1)} %get-tuple-element.52), channel_id=1, source_target_pairs={{0,128},{64,192},{128,0},{192,64},{1,129},{65,193},{129,1},{193,65... | collective-permute-start | bytes 393224 | tf_op jit(solution)/shard_map/ppermute | solution.py:87
  165.8 5.1 %collective-permute-start.17 = (bf16[4,4,16,1152]{3,2,1,0:T(8,128)(2,1)S(1)}, bf16[4,4,16,1152]{3,2,1,0:T(8,128)(2,1)S(1)}, u32[]{:S(2)}, u32[]{:S(2)}) collective-permute-start(bf16[4,4,16,1152]{3,2,1,0:T(8,128)(2,1)S(1)} %pad_maximum_fusion.2.act_near_ref), channel_id=1, source_target_pairs={{0,32},{32,0},{1,33},{33,1},{2,34},{34,2},{3,35},{35,3},{4,36},{36... | collective-permute-start | bytes 1769480 | tf_op jit(solution)/shard_map/ppermute | solution.py:425
  178.3 48.6 %all-to-all-start.4 = ((bf16[32,128,384]{2,1,0:T(8,128)(2,1)}), bf16[32,128,384]{2,1,0:T(8,128)(2,1)S(1)}, u32[]{:S(2)}, u32[]{:S(2)}) async-start(bf16[32,128,384]{2,1,0:T(8,128)(2,1)} %bitcast.122), calls=%async_computation.4 | async-start | bytes 6291456 | tf_op jit(solution)/shard_map/all_to_all | solution.py:447
  216.7 8.4 %collective-permute-start.25 = (bf16[128,768]{1,0:T(8,128)(2,1)}, bf16[128,768]{1,0:T(8,128)(2,1)}, u32[]{:S(2)}, u32[]{:S(2)}) collective-permute-start(bf16[128,768]{1,0:T(8,128)(2,1)} %bitcast.143), channel_id=1, source_target_pairs={{0,0},{33,1},{66,2},{99,3},{132,4},{165,5},{198,6},{231,7},{4,36},... | collective-permute-start | bytes 589832 | tf_op jit(solution)/shard_map/ppermute | solution.py:458
  227.0 27.2 %all-to-all-start.5 = ((f32[256,1,128]{2,1,0:T(1,128)}), f32[256,1,128]{2,1,0:T(1,128)S(1)}, u32[]{:S(2)}, u32[]{:S(2)}) async-start(f32[256,1,128]{2,1,0:T(1,128)} %bitcast.45), calls=%async_computation.6 | async-start | bytes 262144 | tf_op jit(solution)/shard_map/all_to_all | solution.py:462
  238.8 15.3 %collective-permute-start.26 = (bf16[128,768]{1,0:T(8,128)(2,1)}, bf16[128,768]{1,0:T(8,128)(2,1)S(1)}, u32[]{:S(2)}, u32[]{:S(2)}) collective-permute-start(bf16[128,768]{1,0:T(8,128)(2,1)} %collective-permute-done.25.grad_ref), channel_id=1, source_target_pairs={{0,0},{1,1},{2,2},{3,3},{4,4},{5,5},{6,6},{7,7},{36,32},{37,33},{3... | collective-permute-start | bytes 589832 | tf_op jit(solution)/shard_map/ppermute | solution.py:464
  (11 other events, 45.4 us)
Sparse Core Ops, SparseCore 0:
  35.0 48.8 all-gather.2
  178.5 38.2 reduce-scatter.1

commit v7 on v6

--- a/solution.py
+++ b/solution.py
@@ -26,6 +26,7 @@
 EVERYONE = ("x", "c", "y", "z")
 SHIFTS = (0, 1, -1, 2)
 TURNS = (0, 4, 3, 7, 2, 6, 1, 5)
+FIRST = (0, 2, 2, -1, 1, -1, 1, -2)
 EXTRA = 16
 VMEM_BYTES = 48 * 1024 * 1024
 
@@ -89,6 +90,13 @@
 
 def gather_line(block, axis):
     return jnp.stack([block] + [shifted(block, axis, d) for d in SHIFTS[1:]])
+
+
+def gather_line_both_ways(block, axis):
+    before, after = shifted(block, axis, 1), shifted(block, axis, -1)
+    half = block.shape[0] // 2
+    far = [shifted(before[:half], axis, 1), shifted(after[half:], axis, -1)]
+    return jnp.stack([block, before, after, jnp.concatenate(far)])
 
 
 def pack_kernel(gain_ref, in_ref, out_ref, pack_ref):
@@ -348,19 +356,12 @@
     turned = {(a, b): (b + TURNS[a]) % count_z for a, b in grid}
     turn = [(a * count_z + b, a * count_z + turned[a, b]) for a, b in grid]
     move = [(a * count_z + turned[a, b], b * count_z + turned[a, b]) for a, b in grid]
-    turn_back, move_back = ([(j, i) for i, j in route] for route in (turn, move))
+    move_back = [(j, i) for i, j in move]
+    first_back = [(a * count_z + b, a * count_z + (b - FIRST[a]) % count_z) for a, b in grid]
+    last_back = [(a * count_z + b, a * count_z + (b - TURNS[a] + FIRST[a]) % count_z) for a, b in grid]
     across = SECTION + ("z",)
 
     gain_own = lax.dynamic_slice_in_dim(norm_gain, (pos_y * count_z + pos_z) * features, features, 1)
-    packed = local_call(
-        pack_kernel, jax.ShapeDtypeStruct((features + EXTRA, 2 * rank), LOW), (gain_own, master_in, master_out)
-    )
-    swapped = lax.ppermute(packed, across, turn)
-    lined_near = gather_line(packed, "x")
-    swapped, lined_near = lax.optimization_barrier((swapped, lined_near))
-    swapped = lax.ppermute(swapped, across, move)
-    lined_far = lax.ppermute(lined_near, "c", swap_core)
-
     def blocks_of(rows):
         return jnp.stack(
             [
@@ -370,7 +371,19 @@
         )
 
     rows = jnp.concatenate([blocks_of(stack_input), blocks_of(out_cotangent)], axis=1)
+    gain_own, rows = lax.optimization_barrier((gain_own, rows))
+    rows = lax.all_to_all(rows, "y", 0, 0, tiled=True)
+    packed = local_call(
+        pack_kernel, jax.ShapeDtypeStruct((features + EXTRA, 2 * rank), LOW), (gain_own, master_in, master_out)
+    )
+    swapped = lax.ppermute(packed, across, turn)
+    lined_near = gather_line(packed, "x")
+    swapped, lined_near, rows = lax.optimization_barrier((swapped, lined_near, rows))
+    swapped = lax.ppermute(swapped, across, move)
+    lined_far = lax.ppermute(lined_near, "c", swap_core)
+    swapped, lined_far = lax.optimization_barrier((swapped, lined_far))
     weights = lax.all_gather(swapped, "z", axis=0)
+
     own_rows = lax.dynamic_slice_in_dim(stack_input, pos_s * piece, piece, 0).astype(WIDE)
     square = jnp.sum(own_rows * own_rows, axis=-1, keepdims=True)
     square = jnp.broadcast_to(square, (piece, 128))
@@ -386,9 +399,7 @@
     cross = jnp.sum(cross.astype(WIDE), axis=0, keepdims=True).astype(LOW)
     cross = jnp.broadcast_to(cross, (count_y * count_z, cut_r, cut_c))
     cross = lax.all_to_all(cross, ("y", "z"), 0, 0, tiled=True)
-    cross, rows = lax.optimization_barrier((cross, rows))
-    rows = lax.all_to_all(rows, "y", 0, 0, tiled=True)
-    cross_near = gather_line(cross, "x")
+    cross_near = gather_line_both_ways(cross, "x")
     cross_near, rows = lax.optimization_barrier((cross_near, rows))
     cross_far = lax.ppermute(cross_near, "c", swap_core)
 
@@ -461,7 +472,7 @@
     )
     squares = lax.all_to_all(squares, EVERYONE, 0, 0, tiled=True)
     total_sq = jnp.sum(squares[:, 0])
-    own_grads = lax.ppermute(grads, across, turn_back)
+    own_grads = lax.ppermute(lax.ppermute(grads, across, first_back), across, last_back)
     shard_in, shard_out = local_call(
         settle_kernel,
         (

time: 266 us -> 268 us (level)
  blocking collectives: 25.6 us -> 46.7 us
  waiting for transfers between devices: 108 us -> 93.4 us
  starting transfers between devices: 81 us -> 76.9 us
    all_to_all x1 -> x2, blocking collectives: 25.6 us -> 46.7 us  [shards(): cross = lax.all_to_all(cross, ('y', 'z'), 0, 0, tiled=True)]
    all_to_all x1 -> x0, waiting for transfers between devices: 12.4 us -> none  [shards(): cross = lax.all_to_all(cross, ('y', 'z'), 0, 0, tiled=True)]
    all_to_all x1 -> x0, starting transfers between devices: 5.82 us -> none  [shards(): cross = lax.all_to_all(cross, ('y', 'z'), 0, 0, tiled=True)]
    ppermute x1 -> x2, waiting for transfers between devices: 5.25 us -> 0.01 us  [the longest x1 0.01 us: shards(): lax.ppermute(grads, across, first_back)]
    all_to_all x1, waiting for transfers between devices: 0.01 us -> 3.28 us  [shards(): squares = lax.all_to_all(squares, EVERYONE, 0, 0, tiled=True)]
    ppermute x18 -> x19, starting transfers between devices: 24.5 us -> 26.3 us  [shifted(): lax.ppermute(block, axis, [(i, (i + distance) % size) for i in range(size)])]
    ppermute x1 -> x2, starting transfers between devices: 7.6 us -> 8.57 us  [the longest x1 6.34 us: shards(): lax.ppermute(lax.ppermute(grads, across, first_back), across, last_back)]
    ppermute x18 -> x19, waiting for transfers between devices: 15.6 us -> 15.1 us  [shifted(): lax.ppermute(block, axis, [(i, (i + distance) % size) for i in range(size)])]
  transfers between devices with their start and end apart: 34 -> 35, of which waited for: 19 -> 18; matrix products, arithmetic and copies ran while one was open for 2% -> 1% of each run, Pallas kernels for 2% -> 2%
where the time goes in v7:
time: 268 us; the launch traced here: 265 us
  waiting for transfers between devices  93.4 us (35%)
  starting transfers between devices  76.9 us (29%)
  blocking collectives  46.7 us (17%)
  Pallas kernels  20.6 us (8%)
  between operations  15.1 us (6%)
  other arithmetic  8.09 us (3%)
  local copies, waits for them, and re-layouts  4.33 us (2%)
    all_to_all x2, blocking collectives, shards(): cross = lax.all_to_all(cross, ('y', 'z'), 0, 0, tiled=True)  46.7 us
    reduce_scatter x1, waiting for transfers between devices, shards(): grads = lax.psum_scatter(grads, 'z', scatter_dimension=0, tiled=True)[0]  31 us
    ppermute x19, starting transfers between devices, shifted(): lax.ppermute(block, axis, [(i, (i + distance) % size) for i in range(size)])  26.3 us
    all_to_all x1, waiting for transfers between devices, shards(): parts = lax.all_to_all(parts, ('x', 'y'), 0, 0, tiled=True)  18.6 us
    pallas_call x7, Pallas kernels, local_call(): pl.pallas_call(kernel, out_shape=out_shape, in_specs=in_specs, out_specs=...  18.2 us
    ppermute x19, waiting for transfers between devices, shifted(): lax.ppermute(block, axis, [(i, (i + distance) % size) for i in range(size)])  15.1 us
    all_to_all x1, starting transfers between devices, shards(): squares = lax.all_to_all(squares, EVERYONE, 0, 0, tiled=True)  13.4 us
    ppermute x1, waiting for transfers between devices, shards(): swapped = lax.ppermute(swapped, across, move)  7.29 us
  transfers between devices with their start and end apart: 35, of which 18 were waited for; matrix products, arithmetic and copies ran while one was open for 1% of the time, Pallas kernels for 2%

profile of v7, /device:TPU:2, one launch (start us, length us, event | category | flops | bytes accessed | tf_op | source)
XLA Modules:
  0.0 265.1 jit_solution(4254236416410765699)
XLA Ops:
  10.3 4.5 %all-to-all-start = ((bf16[4,256,384]{2,1,0:T(8,128)(2,1)}), bf16[4,256,384]{2,1,0:T(8,128)(2,1)S(1)}, u32[]{:S(2)}, u32[]{:S(2)}) async-start(bf16[4,256,384]{2,1,0:T(8,128)(2,1)} %maximum_maximum_fusion), calls=%async_computation | async-start | bytes 1572864 | tf_op jit(solution)/shard_map/all_to_all | solution.py:375
  14.9 2.2 collective-permute-start.3
  19.2 6.5 %collective-permute-start = (bf16[400,256]{1,0:T(8,128)(2,1)S(1)}, bf16[400,256]{1,0:T(8,128)(2,1)S(1)}, u32[]{:S(2)}, u32[]{:S(2)}) collective-permute-start(bf16[400,256]{1,0:T(8,128)(2,1)S(1)} %shard_map.144.own_ref), channel_id=1, source_target_pairs={{0,0},{1,1},{2,2},{3,3},{4,4},{5,5},{6,6},{7,7},{32,36},{33,37},{3... | collective-permute-start | bytes 614408 | tf_op jit(solution)/shard_map/ppermute | solution.py:379
  27.6 4.1 %collective-permute-done = bf16[400,256]{1,0:T(8,128)(2,1)S(1)} collective-permute-done((bf16[400,256]{1,0:T(8,128)(2,1)S(1)}, bf16[400,256]{1,0:T(8,128)(2,1)S(1)}, u32[]{:S(2)}, u32[]{:S(2)}) %collective-permute-start) | collective-permute-done | bytes 204832 | tf_op jit(solution)/shard_map/ppermute | solution.py:379
  31.7 2.0 collective-permute-start.4
  33.7 7.3 %collective-permute-done.4 = bf16[400,256]{1,0:T(8,128)(2,1)S(1)} collective-permute-done((bf16[400,256]{1,0:T(8,128)(2,1)S(1)}, bf16[400,256]{1,0:T(8,128)(2,1)S(1)}, u32[]{:S(2)}, u32[]{:S(2)}) %collective-permute-start.4) | collective-permute-done | bytes 204832 | tf_op jit(solution)/shard_map/ppermute | solution.py:382
  42.8 27.1 %all_to_all.37 = bf16[32,16,256]{2,1,0:T(8,128)(2,1)S(1)} all-to-all(bf16[32,16,256]{2,1,0:T(8,128)(2,1)S(1)} %shard_map.145), channel_id=1, replica_groups=mesh['x'=4,'c'=2,'y'=4,'z'=8] {'y','z'}, dimensions={0} | all-to-all | bytes 524288 | tf_op jit(solution)/shard_map/all_to_all | solution.py:398
  69.9 19.6 %all_to_all.38 = bf16[32,16,256]{2,1,0:T(8,128)(2,1)S(1)} all-to-all(bf16[32,16,256]{2,1,0:T(8,128)(2,1)S(1)} %broadcast_in_dim.33), channel_id=1, replica_groups=mesh['x'=4,'c'=2,'y'=4,'z'=8] {'y','z'}, dimensions={0} | all-to-all | bytes 524288 | tf_op jit(solution)/shard_map/all_to_all | solution.py:401
  89.6 2.0 collective-permute-start.6
  91.6 5.8 %collective-permute-done.7 = bf16[32,16,256]{2,1,0:T(8,128)(2,1)S(1)} collective-permute-done((bf16[32,16,256]{2,1,0:T(8,128)(2,1)S(1)}, bf16[32,16,256]{2,1,0:T(8,128)(2,1)S(1)}, u32[]{:S(2)}, u32[]{:S(2)}) %collective-permute-start.7) | collective-permute-done | bytes 262176 | tf_op jit(solution)/shard_map/ppermute | solution.py:88
  97.5 2.1 collective-permute-start.8
  99.6 2.8 %collective-permute-done.9 = bf16[16,16,256]{2,1,0:T(8,128)(2,1)S(1)} collective-permute-done((bf16[16,16,256]{2,1,0:T(8,128)(2,1)S(1)}, bf16[16,16,256]{2,1,0:T(8,128)(2,1)S(1)}, u32[]{:S(2)}, u32[]{:S(2)}) %collective-permute-start.9) | collective-permute-done | bytes 131104 | tf_op jit(solution)/shard_map/ppermute | solution.py:88
  104.2 2.8 %shard_map.146 = (bf16[4,4,16,3072]{3,2,1,0:T(8,128)(2,1)S(1)}, bf16[4,4,16,3072]{3,2,1,0:T(8,128)(2,1)S(1)}) custom-call(s32[4]{0:T(128)S(1)} %pad_add_fusion.place_ref, bf16[4,256,384]{2,1,0:T(8,128)(2,1)S(1)} %all-to-all-done.rows_ref, bf16[8,400,256]{2,1,0:T(8,128)(2,1)S(1)} %bitcast.120), custom_call_target="tpu_custom_call" | custom-call | flops 1207959552 | bytes 5570560 | tf_op jit(solution)/shard_map/pallas_call | solution.py:75
  107.1 3.4 %collective-permute-done.10 = bf16[4,4,16,3072]{3,2,1,0:T(8,128)(2,1)S(1)} collective-permute-done((bf16[4,4,16,3072]{3,2,1,0:T(8,128)(2,1)S(1)}, bf16[4,4,16,3072]{3,2,1,0:T(8,128)(2,1)S(1)}, u32[]{:S(2)}, u32[]{:S(2)}) %collective-permute-start.10) | collective-permute-done | bytes 1572896 | tf_op jit(solution)/shard_map/ppermute | solution.py:414
  112.3 6.2 %all-to-all-start.3 = ((bf16[16,16,3072]{2,1,0:T(8,128)(2,1)}), bf16[16,16,3072]{2,1,0:T(8,128)(2,1)S(1)}, u32[]{:S(2)}, u32[]{:S(2)}) async-start(bf16[16,16,3072]{2,1,0:T(8,128)(2,1)} %bitcast.121), calls=%async_computation.3 | async-start | bytes 3145728 | tf_op jit(solution)/shard_map/all_to_all | solution.py:417
  121.6 18.6 %all-to-all-done.3.parts_ref = bf16[16,16,3072]{2,1,0:T(8,128)(2,1)S(1)} async-done(((bf16[16,16,3072]{2,1,0:T(8,128)(2,1)}), bf16[16,16,3072]{2,1,0:T(8,128)(2,1)S(1)}, u32[]{:S(2)}, u32[]{:S(2)}) %all-to-all-start.3) | async-done | bytes 1572896 | tf_op jit(solution)/shard_map/all_to_all | solution.py:417
  140.2 4.9 %shard_map.147 = (bf16[16,1152]{1,0:T(8,128)(2,1)S(1)}, bf16[16,1024]{1,0:T(8,128)(2,1)S(1)}) custom-call(s32[4]{0:T(128)S(1)} %pad_add_fusion.place_ref, bf16[16,16,3072]{2,1,0:T(8,128)(2,1)S(1)} %all-to-all-done.3.parts_ref, f32[16,128]{1,0:T(8,128)S(1)} %broadcast_in_dim.34.square_ref, bf16[4,32,16,256]{3,2,1,0:T(8,128)(2,1)S(1)} %pad_maximum_fusion.near_ref, ...), custom_call_target="tpu_custom_call" | custom-call | bytes 3747840 | tf_op jit(solution)/shard_map/pallas_call | solution.py:75
  145.1 2.3 collective-permute-start.14
  150.7 1.9 collective-permute-start.20
  153.1 2.9 %collective-permute-start.16 = (bf16[4,16,1152]{2,1,0:T(8,128)(2,1)S(1)}, bf16[4,16,1152]{2,1,0:T(8,128)(2,1)S(1)}, u32[]{:S(2)}, u32[]{:S(2)}) collective-permute-start(bf16[4,16,1152]{2,1,0:T(8,128)(2,1)S(1)} %get-tuple-element.56), channel_id=1, source_target_pairs={{0,24},{8,0},{16,8},{24,16},{1,25},{9,1},{17,9},{25,17},{2,26},{10... | collective-permute-start | bytes 442376 | tf_op jit(solution)/shard_map/ppermute | solution.py:88
  161.2 3.7 %collective-permute-start.24 = (bf16[4,16,1024]{2,1,0:T(8,128)(2,1)S(1)}, bf16[4,16,1024]{2,1,0:T(8,128)(2,1)S(1)}, u32[]{:S(2)}, u32[]{:S(2)}) collective-permute-start(bf16[4,16,1024]{2,1,0:T(8,128)(2,1)S(1)} %get-tuple-element.58), channel_id=1, source_target_pairs={{0,128},{64,192},{128,0},{192,64},{1,129},{65,193},{129,1},{193,65... | collective-permute-start | bytes 393224 | tf_op jit(solution)/shard_map/ppermute | solution.py:88
  165.8 2.0 collective-permute-done.24
  170.2 7.4 %shard_map.148 = (bf16[8,4,128,384]{3,2,1,0:T(8,128)(2,1)}, bf16[8,128,768]{2,1,0:T(8,128)(2,1)}) custom-call(s32[4]{0:T(128)S(1)} %pad_add_fusion.place_ref, bf16[4,256,384]{2,1,0:T(8,128)(2,1)S(1)} %all-to-all-done.rows_ref, bf16[8,400,256]{2,1,0:T(8,128)(2,1)} %bitcast.119, bf16[4,4,16,1152]{3,2,1,0:T(8,128)(2,1)S(1)} %pad_maximum_fusion.2.act_near_ref, ...), custom_call_target="tpu_custom_call" | custom-call | flops 1610612736 | bytes 9371648 | tf_op jit(solution)/shard_map/pallas_call | solution.py:75
  177.6 6.6 %all-to-all-start.4 = ((bf16[32,128,384]{2,1,0:T(8,128)(2,1)}), bf16[32,128,384]{2,1,0:T(8,128)(2,1)S(1)}, u32[]{:S(2)}, u32[]{:S(2)}) async-start(bf16[32,128,384]{2,1,0:T(8,128)(2,1)} %bitcast.123), calls=%async_computation.4 | async-start | bytes 6291456 | tf_op jit(solution)/shard_map/all_to_all | solution.py:458
  184.2 31.0 %reduce-scatter.2.cloned.1.call-done = bf16[1,128,768]{2,1,0:T(8,128)(2,1)} async-done(((bf16[8,128,768]{2,1,0:T(8,128)(2,1)}), bf16[1,128,768]{2,1,0:T(8,128)(2,1)}) %reduce-scatter.2.cloned.1.call-update) | async-done | bytes 196624 | tf_op jit(solution)/shard_map/reduce_scatter | solution.py:456
  217.1 7.2 %collective-permute-done.26.grad_ref = bf16[128,768]{1,0:T(8,128)(2,1)S(1)} collective-permute-done((bf16[128,768]{1,0:T(8,128)(2,1)}, bf16[128,768]{1,0:T(8,128)(2,1)S(1)}, u32[]{:S(2)}, u32[]{:S(2)}) %collective-permute-start.26) | collective-permute-done | bytes 196640 | tf_op jit(solution)/shard_map/ppermute | solution.py:469
  224.3 2.2 collective-permute-start.27
  227.4 13.4 %all-to-all-start.5 = ((f32[256,1,128]{2,1,0:T(1,128)}), f32[256,1,128]{2,1,0:T(1,128)S(1)}, u32[]{:S(2)}, u32[]{:S(2)}) async-start(f32[256,1,128]{2,1,0:T(1,128)} %bitcast.45), calls=%async_computation.6 | async-start | bytes 262144 | tf_op jit(solution)/shard_map/all_to_all | solution.py:473
  240.9 6.3 %collective-permute-start.28 = (bf16[128,768]{1,0:T(8,128)(2,1)}, bf16[128,768]{1,0:T(8,128)(2,1)}, u32[]{:S(2)}, u32[]{:S(2)}) collective-permute-start(bf16[128,768]{1,0:T(8,128)(2,1)} %collective-permute-done.27), channel_id=1, source_target_pairs={{0,0},{1,1},{2,2},{3,3},{4,4},{5,5},{6,6},{7,7},{32,38},{33,39},{3... | collective-permute-start | bytes 589832 | tf_op jit(solution)/shard_map/ppermute | solution.py:475
  247.2 2.4 shard_map.149
  249.6 3.3 %all-to-all-done.5 = f32[256,1,128]{2,1,0:T(1,128)S(1)} async-done(((f32[256,1,128]{2,1,0:T(1,128)}), f32[256,1,128]{2,1,0:T(1,128)S(1)}, u32[]{:S(2)}, u32[]{:S(2)}) %all-to-all-start.5) | async-done | bytes 131104 | tf_op jit(solution)/shard_map/all_to_all | solution.py:473
  255.4 2.0 fusion.11
  (89 shorter events, 33.4 us)
Async XLA Ops:
  10.3 21.5 %all-to-all-start = ((bf16[4,256,384]{2,1,0:T(8,128)(2,1)}), bf16[4,256,384]{2,1,0:T(8,128)(2,1)S(1)}, u32[]{:S(2)}, u32[]{:S(2)}) async-start(bf16[4,256,384]{2,1,0:T(8,128)(2,1)} %maximum_maximum_fusion), calls=%async_computation | async-start | bytes 1572864 | tf_op jit(solution)/shard_map/all_to_all | solution.py:375
  14.7 88.0 %all-gather.3.cloned.1.call-start = ((), (), s32[]{:S(2)}) async-start(), calls=%async_computation.8 | async-start | bytes 1843200 | tf_op jit(solution)/shard_map/all_gather | solution.py:385
  14.9 10.8 %collective-permute-start.3 = (bf16[400,256]{1,0:T(8,128)(2,1)S(1)}, bf16[400,256]{1,0:T(8,128)(2,1)S(1)}, u32[]{:S(2)}, u32[]{:S(2)}) collective-permute-start(bf16[400,256]{1,0:T(8,128)(2,1)S(1)} %shard_map.144.own_ref), channel_id=1, source_target_pairs={{0,128},{64,192},{128,0},{192,64},{1,129},{65,193},{129,1},{193,65... | collective-permute-start | bytes 614408 | tf_op jit(solution)/shard_map/ppermute | solution.py:88
  17.1 10.3 %collective-permute-start.2 = (bf16[400,256]{1,0:T(8,128)(2,1)S(1)}, bf16[400,256]{1,0:T(8,128)(2,1)S(1)}, u32[]{:S(2)}, u32[]{:S(2)}) collective-permute-start(bf16[400,256]{1,0:T(8,128)(2,1)S(1)} %shard_map.144.own_ref), channel_id=1, source_target_pairs={{0,192},{64,0},{128,64},{192,128},{1,193},{65,1},{129,65},{193,129... | collective-permute-start | bytes 614408 | tf_op jit(solution)/shard_map/ppermute | solution.py:88
  18.6 8.9 %collective-permute-start.1 = (bf16[400,256]{1,0:T(8,128)(2,1)S(1)}, bf16[400,256]{1,0:T(8,128)(2,1)S(1)}, u32[]{:S(2)}, u32[]{:S(2)}) collective-permute-start(bf16[400,256]{1,0:T(8,128)(2,1)S(1)} %shard_map.144.own_ref), channel_id=1, source_target_pairs={{0,64},{64,128},{128,192},{192,0},{1,65},{65,129},{129,193},{193,1... | collective-permute-start | bytes 614408 | tf_op jit(solution)/shard_map/ppermute | solution.py:88
  19.2 12.6 %collective-permute-start = (bf16[400,256]{1,0:T(8,128)(2,1)S(1)}, bf16[400,256]{1,0:T(8,128)(2,1)S(1)}, u32[]{:S(2)}, u32[]{:S(2)}) collective-permute-start(bf16[400,256]{1,0:T(8,128)(2,1)S(1)} %shard_map.144.own_ref), channel_id=1, source_target_pairs={{0,0},{1,1},{2,2},{3,3},{4,4},{5,5},{6,6},{7,7},{32,36},{33,37},{3... | collective-permute-start | bytes 614408 | tf_op jit(solution)/shard_map/ppermute | solution.py:379
  31.7 9.3 %collective-permute-start.5 = (bf16[4,400,256]{2,1,0:T(8,128)(2,1)S(1)}, bf16[4,400,256]{2,1,0:T(8,128)(2,1)S(1)}, u32[]{:S(2)}, u32[]{:S(2)}) collective-permute-start(bf16[4,400,256]{2,1,0:T(8,128)(2,1)S(1)} %pad_maximum_fusion.1.near_ref), channel_id=1, source_target_pairs={{0,32},{32,0},{1,33},{33,1},{2,34},{34,2},{3,35},{35,3},{4,36},{36... | collective-permute-start | bytes 2457608 | tf_op jit(solution)/shard_map/ppermute | solution.py:383
  31.7 9.3 %collective-permute-start.4 = (bf16[400,256]{1,0:T(8,128)(2,1)S(1)}, bf16[400,256]{1,0:T(8,128)(2,1)S(1)}, u32[]{:S(2)}, u32[]{:S(2)}) collective-permute-start(bf16[400,256]{1,0:T(8,128)(2,1)S(1)} %collective-permute-done), channel_id=1, source_target_pairs={{0,0},{1,33},{2,66},{3,99},{4,132},{5,165},{6,198},{7,231},{36,4},... | collective-permute-start | bytes 614408 | tf_op jit(solution)/shard_map/ppermute | solution.py:382
  89.6 7.8 %collective-permute-start.7 = (bf16[32,16,256]{2,1,0:T(8,128)(2,1)S(1)}, bf16[32,16,256]{2,1,0:T(8,128)(2,1)S(1)}, u32[]{:S(2)}, u32[]{:S(2)}) collective-permute-start(bf16[32,16,256]{2,1,0:T(8,128)(2,1)S(1)} %all_to_all.38), channel_id=1, source_target_pairs={{0,192},{64,0},{128,64},{192,128},{1,193},{65,1},{129,65},{193,129... | collective-permute-start | bytes 786440 | tf_op jit(solution)/shard_map/ppermute | solution.py:88
  89.6 7.9 %collective-permute-start.6 = (bf16[32,16,256]{2,1,0:T(8,128)(2,1)S(1)}, bf16[32,16,256]{2,1,0:T(8,128)(2,1)S(1)}, u32[]{:S(2)}, u32[]{:S(2)}) collective-permute-start(bf16[32,16,256]{2,1,0:T(8,128)(2,1)S(1)} %all_to_all.38), channel_id=1, source_target_pairs={{0,64},{64,128},{128,192},{192,0},{1,65},{65,129},{129,193},{193,1... | collective-permute-start | bytes 786440 | tf_op jit(solution)/shard_map/ppermute | solution.py:88
  97.4 5.0 %collective-permute-start.9 = (bf16[16,16,256]{2,1,0:T(8,128)(2,1)S(1)}, bf16[16,16,256]{2,1,0:T(8,128)(2,1)S(1)}, u32[]{:S(2)}, u32[]{:S(2)}) collective-permute-start(bf16[16,16,256]{2,1,0:T(8,128)(2,1)S(1)} %slice.13), channel_id=1, source_target_pairs={{0,192},{64,0},{128,64},{192,128},{1,193},{65,1},{129,65},{193,129... | collective-permute-start | bytes 393224 | tf_op jit(solution)/shard_map/ppermute | solution.py:88
  97.5 5.0 %collective-permute-start.8 = (bf16[16,16,256]{2,1,0:T(8,128)(2,1)S(1)}, bf16[16,16,256]{2,1,0:T(8,128)(2,1)S(1)}, u32[]{:S(2)}, u32[]{:S(2)}) collective-permute-start(bf16[16,16,256]{2,1,0:T(8,128)(2,1)S(1)} %slice.12), channel_id=1, source_target_pairs={{0,64},{64,128},{128,192},{192,0},{1,65},{65,129},{129,193},{193,1... | collective-permute-start | bytes 393224 | tf_op jit(solution)/shard_map/ppermute | solution.py:88
  112.3 27.9 %all-to-all-start.3 = ((bf16[16,16,3072]{2,1,0:T(8,128)(2,1)}), bf16[16,16,3072]{2,1,0:T(8,128)(2,1)S(1)}, u32[]{:S(2)}, u32[]{:S(2)}) async-start(bf16[16,16,3072]{2,1,0:T(8,128)(2,1)} %bitcast.121), calls=%async_computation.3 | async-start | bytes 3145728 | tf_op jit(solution)/shard_map/all_to_all | solution.py:417
  118.5 96.7 %reduce-scatter.2.cloned.1.call-start = ((), (), s32[]{:S(2)}) async-start(), calls=%async_computation.7 | async-start | bytes 1769472 | tf_op jit(solution)/shard_map/reduce_scatter | solution.py:456
  145.1 7.5 %collective-permute-start.14 = (bf16[16,1152]{1,0:T(8,128)(2,1)S(1)}, bf16[16,1152]{1,0:T(8,128)(2,1)S(1)}, u32[]{:S(2)}, u32[]{:S(2)}) collective-permute-start(bf16[16,1152]{1,0:T(8,128)(2,1)S(1)} %get-tuple-element.35), channel_id=1, source_target_pairs={{0,128},{64,192},{128,0},{192,64},{1,129},{65,193},{129,1},{193,65... | collective-permute-start | bytes 110600 | tf_op jit(solution)/shard_map/ppermute | solution.py:88
  147.4 5.4 %collective-permute-start.13 = (bf16[16,1152]{1,0:T(8,128)(2,1)S(1)}, bf16[16,1152]{1,0:T(8,128)(2,1)S(1)}, u32[]{:S(2)}, u32[]{:S(2)}) collective-permute-start(bf16[16,1152]{1,0:T(8,128)(2,1)S(1)} %get-tuple-element.35), channel_id=1, source_target_pairs={{0,192},{64,0},{128,64},{192,128},{1,193},{65,1},{129,65},{193,129... | collective-permute-start | bytes 110600 | tf_op jit(solution)/shard_map/ppermute | solution.py:88
  149.1 4.0 %collective-permute-start.12 = (bf16[16,1152]{1,0:T(8,128)(2,1)S(1)}, bf16[16,1152]{1,0:T(8,128)(2,1)S(1)}, u32[]{:S(2)}, u32[]{:S(2)}) collective-permute-start(bf16[16,1152]{1,0:T(8,128)(2,1)S(1)} %get-tuple-element.35), channel_id=1, source_target_pairs={{0,64},{64,128},{128,192},{192,0},{1,65},{65,129},{129,193},{193,1... | collective-permute-start | bytes 110600 | tf_op jit(solution)/shard_map/ppermute | solution.py:88
  149.4 6.6 %collective-permute-start.21 = (bf16[16,1024]{1,0:T(8,128)(2,1)S(1)}, bf16[16,1024]{1,0:T(8,128)(2,1)S(1)}, u32[]{:S(2)}, u32[]{:S(2)}) collective-permute-start(bf16[16,1024]{1,0:T(8,128)(2,1)S(1)} %get-tuple-element.36), channel_id=1, source_target_pairs={{0,16},{8,24},{16,0},{24,8},{1,17},{9,25},{17,1},{25,9},{2,18},{10... | collective-permute-start | bytes 98312 | tf_op jit(solution)/shard_map/ppermute | solution.py:88
  150.7 6.8 %collective-permute-start.20 = (bf16[16,1024]{1,0:T(8,128)(2,1)S(1)}, bf16[16,1024]{1,0:T(8,128)(2,1)S(1)}, u32[]{:S(2)}, u32[]{:S(2)}) collective-permute-start(bf16[16,1024]{1,0:T(8,128)(2,1)S(1)} %get-tuple-element.36), channel_id=1, source_target_pairs={{0,24},{8,0},{16,8},{24,16},{1,25},{9,1},{17,9},{25,17},{2,26},{10... | collective-permute-start | bytes 98312 | tf_op jit(solution)/shard_map/ppermute | solution.py:88
  152.6 6.4 %collective-permute-start.19 = (bf16[16,1024]{1,0:T(8,128)(2,1)S(1)}, bf16[16,1024]{1,0:T(8,128)(2,1)S(1)}, u32[]{:S(2)}, u32[]{:S(2)}) collective-permute-start(bf16[16,1024]{1,0:T(8,128)(2,1)S(1)} %get-tuple-element.36), channel_id=1, source_target_pairs={{0,8},{8,16},{16,24},{24,0},{1,9},{9,17},{17,25},{25,1},{2,10},{10... | collective-permute-start | bytes 98312 | tf_op jit(solution)/shard_map/ppermute | solution.py:88
  153.1 8.1 %collective-permute-start.16 = (bf16[4,16,1152]{2,1,0:T(8,128)(2,1)S(1)}, bf16[4,16,1152]{2,1,0:T(8,128)(2,1)S(1)}, u32[]{:S(2)}, u32[]{:S(2)}) collective-permute-start(bf16[4,16,1152]{2,1,0:T(8,128)(2,1)S(1)} %get-tuple-element.56), channel_id=1, source_target_pairs={{0,24},{8,0},{16,8},{24,16},{1,25},{9,1},{17,9},{25,17},{2,26},{10... | collective-permute-start | bytes 442376 | tf_op jit(solution)/shard_map/ppermute | solution.py:88
  156.0 8.9 %collective-permute-start.15 = (bf16[4,16,1152]{2,1,0:T(8,128)(2,1)S(1)}, bf16[4,16,1152]{2,1,0:T(8,128)(2,1)S(1)}, u32[]{:S(2)}, u32[]{:S(2)}) collective-permute-start(bf16[4,16,1152]{2,1,0:T(8,128)(2,1)S(1)} %get-tuple-element.56), channel_id=1, source_target_pairs={{0,8},{8,16},{16,24},{24,0},{1,9},{9,17},{17,25},{25,1},{2,10},{10... | collective-permute-start | bytes 442376 | tf_op jit(solution)/shard_map/ppermute | solution.py:88
  156.0 8.9 %collective-permute-start.17 = (bf16[4,16,1152]{2,1,0:T(8,128)(2,1)S(1)}, bf16[4,16,1152]{2,1,0:T(8,128)(2,1)S(1)}, u32[]{:S(2)}, u32[]{:S(2)}) collective-permute-start(bf16[4,16,1152]{2,1,0:T(8,128)(2,1)S(1)} %get-tuple-element.56), channel_id=1, source_target_pairs={{0,16},{8,24},{16,0},{24,8},{1,17},{9,25},{17,1},{25,9},{2,18},{10... | collective-permute-start | bytes 442376 | tf_op jit(solution)/shard_map/ppermute | solution.py:88
  159.1 6.0 %collective-permute-start.23 = (bf16[4,16,1024]{2,1,0:T(8,128)(2,1)S(1)}, bf16[4,16,1024]{2,1,0:T(8,128)(2,1)S(1)}, u32[]{:S(2)}, u32[]{:S(2)}) collective-permute-start(bf16[4,16,1024]{2,1,0:T(8,128)(2,1)S(1)} %get-tuple-element.58), channel_id=1, source_target_pairs={{0,192},{64,0},{128,64},{192,128},{1,193},{65,1},{129,65},{193,129... | collective-permute-start | bytes 393224 | tf_op jit(solution)/shard_map/ppermute | solution.py:88
  160.8 5.0 %collective-permute-start.22 = (bf16[4,16,1024]{2,1,0:T(8,128)(2,1)S(1)}, bf16[4,16,1024]{2,1,0:T(8,128)(2,1)S(1)}, u32[]{:S(2)}, u32[]{:S(2)}) collective-permute-start(bf16[4,16,1024]{2,1,0:T(8,128)(2,1)S(1)} %get-tuple-element.58), channel_id=1, source_target_pairs={{0,64},{64,128},{128,192},{192,0},{1,65},{65,129},{129,193},{193,1... | collective-permute-start | bytes 393224 | tf_op jit(solution)/shard_map/ppermute | solution.py:88
  161.2 6.7 %collective-permute-start.24 = (bf16[4,16,1024]{2,1,0:T(8,128)(2,1)S(1)}, bf16[4,16,1024]{2,1,0:T(8,128)(2,1)S(1)}, u32[]{:S(2)}, u32[]{:S(2)}) collective-permute-start(bf16[4,16,1024]{2,1,0:T(8,128)(2,1)S(1)} %get-tuple-element.58), channel_id=1, source_target_pairs={{0,128},{64,192},{128,0},{192,64},{1,129},{65,193},{129,1},{193,65... | collective-permute-start | bytes 393224 | tf_op jit(solution)/shard_map/ppermute | solution.py:88
  165.0 5.1 %collective-permute-start.18 = (bf16[4,4,16,1152]{3,2,1,0:T(8,128)(2,1)S(1)}, bf16[4,4,16,1152]{3,2,1,0:T(8,128)(2,1)S(1)}, u32[]{:S(2)}, u32[]{:S(2)}) collective-permute-start(bf16[4,4,16,1152]{3,2,1,0:T(8,128)(2,1)S(1)} %pad_maximum_fusion.2.act_near_ref), channel_id=1, source_target_pairs={{0,32},{32,0},{1,33},{33,1},{2,34},{34,2},{3,35},{35,3},{4,36},{36... | collective-permute-start | bytes 1769480 | tf_op jit(solution)/shard_map/ppermute | solution.py:436
  177.6 49.8 %all-to-all-start.4 = ((bf16[32,128,384]{2,1,0:T(8,128)(2,1)}), bf16[32,128,384]{2,1,0:T(8,128)(2,1)S(1)}, u32[]{:S(2)}, u32[]{:S(2)}) async-start(bf16[32,128,384]{2,1,0:T(8,128)(2,1)} %bitcast.123), calls=%async_computation.4 | async-start | bytes 6291456 | tf_op jit(solution)/shard_map/all_to_all | solution.py:458
  215.2 9.1 %collective-permute-start.26 = (bf16[128,768]{1,0:T(8,128)(2,1)}, bf16[128,768]{1,0:T(8,128)(2,1)S(1)}, u32[]{:S(2)}, u32[]{:S(2)}) collective-permute-start(bf16[128,768]{1,0:T(8,128)(2,1)} %bitcast.143), channel_id=1, source_target_pairs={{0,0},{33,1},{66,2},{99,3},{132,4},{165,5},{198,6},{231,7},{4,36},... | collective-permute-start | bytes 589832 | tf_op jit(solution)/shard_map/ppermute | solution.py:469
  224.3 16.6 %collective-permute-start.27 = (bf16[128,768]{1,0:T(8,128)(2,1)S(1)}, bf16[128,768]{1,0:T(8,128)(2,1)}, u32[]{:S(2)}, u32[]{:S(2)}) collective-permute-start(bf16[128,768]{1,0:T(8,128)(2,1)S(1)} %collective-permute-done.26.grad_ref), channel_id=1, source_target_pairs={{0,0},{1,1},{2,2},{3,3},{4,4},{5,5},{6,6},{7,7},{32,38},{33,39},{3... | collective-permute-start | bytes 589832 | tf_op jit(solution)/shard_map/ppermute | solution.py:475
  227.4 25.5 %all-to-all-start.5 = ((f32[256,1,128]{2,1,0:T(1,128)}), f32[256,1,128]{2,1,0:T(1,128)S(1)}, u32[]{:S(2)}, u32[]{:S(2)}) async-start(f32[256,1,128]{2,1,0:T(1,128)} %bitcast.45), calls=%async_computation.6 | async-start | bytes 262144 | tf_op jit(solution)/shard_map/all_to_all | solution.py:473
  240.9 13.4 %collective-permute-start.28 = (bf16[128,768]{1,0:T(8,128)(2,1)}, bf16[128,768]{1,0:T(8,128)(2,1)}, u32[]{:S(2)}, u32[]{:S(2)}) collective-permute-start(bf16[128,768]{1,0:T(8,128)(2,1)} %collective-permute-done.27), channel_id=1, source_target_pairs={{0,0},{1,1},{2,2},{3,3},{4,4},{5,5},{6,6},{7,7},{32,38},{33,39},{3... | collective-permute-start | bytes 589832 | tf_op jit(solution)/shard_map/ppermute | solution.py:475
  (12 other events, 53.8 us)
Sparse Core Ops, SparseCore 0:
  41.8 49.7 all-gather.2
  177.7 37.4 reduce-scatter.1

commit v8 on v7

--- a/solution.py
+++ b/solution.py
@@ -90,13 +90,6 @@
 
 def gather_line(block, axis):
     return jnp.stack([block] + [shifted(block, axis, d) for d in SHIFTS[1:]])
-
-
-def gather_line_both_ways(block, axis):
-    before, after = shifted(block, axis, 1), shifted(block, axis, -1)
-    half = block.shape[0] // 2
-    far = [shifted(before[:half], axis, 1), shifted(after[half:], axis, -1)]
-    return jnp.stack([block, before, after, jnp.concatenate(far)])
 
 
 def pack_kernel(gain_ref, in_ref, out_ref, pack_ref):
@@ -354,7 +347,7 @@
     swap_core = [(0, 1), (1, 0)]
     grid = [(a, b) for a in range(layers) for b in range(count_z)]
     turned = {(a, b): (b + TURNS[a]) % count_z for a, b in grid}
-    turn = [(a * count_z + b, a * count_z + turned[a, b]) for a, b in grid]
+    swap = [(a * count_z + b, b * count_z + turned[a, b]) for a, b in grid]
     move = [(a * count_z + turned[a, b], b * count_z + turned[a, b]) for a, b in grid]
     move_back = [(j, i) for i, j in move]
     first_back = [(a * count_z + b, a * count_z + (b - FIRST[a]) % count_z) for a, b in grid]
@@ -376,12 +369,10 @@
     packed = local_call(
         pack_kernel, jax.ShapeDtypeStruct((features + EXTRA, 2 * rank), LOW), (gain_own, master_in, master_out)
     )
-    swapped = lax.ppermute(packed, across, turn)
+    swapped = lax.ppermute(packed, across, swap)
     lined_near = gather_line(packed, "x")
     swapped, lined_near, rows = lax.optimization_barrier((swapped, lined_near, rows))
-    swapped = lax.ppermute(swapped, across, move)
     lined_far = lax.ppermute(lined_near, "c", swap_core)
-    swapped, lined_far = lax.optimization_barrier((swapped, lined_far))
     weights = lax.all_gather(swapped, "z", axis=0)
 
     own_rows = lax.dynamic_slice_in_dim(stack_input, pos_s * piece, piece, 0).astype(WIDE)
@@ -399,9 +390,11 @@
     cross = jnp.sum(cross.astype(WIDE), axis=0, keepdims=True).astype(LOW)
     cross = jnp.broadcast_to(cross, (count_y * count_z, cut_r, cut_c))
     cross = lax.all_to_all(cross, ("y", "z"), 0, 0, tiled=True)
-    cross_near = gather_line_both_ways(cross, "x")
-    cross_near, rows = lax.optimization_barrier((cross_near, rows))
-    cross_far = lax.ppermute(cross_near, "c", swap_core)
+    before, after = shifted(cross, "x", 1), shifted(cross, "x", -1)
+    before, after, rows = lax.optimization_barrier((before, after, rows))
+    half = cross.shape[0] // 2
+    beyond = [shifted(before[:half], "x", 1), shifted(after[half:], "x", -1)]
+    cross_near = jnp.stack([cross, before, after, jnp.concatenate(beyond)])
 
     part_shape = jax.ShapeDtypeStruct((count_x, count_y, piece, layers * 3 * rank), LOW)
     keep, send = local_call(
@@ -414,6 +407,8 @@
     came = lax.ppermute(send, "c", swap_core)
     parts = (keep.astype(WIDE) + came.astype(WIDE)).astype(LOW)
     parts = parts.reshape(count_x * count_y, piece, layers * 3 * rank)
+    parts, cross_near = lax.optimization_barrier((parts, cross_near))
+    cross_far = lax.ppermute(cross_near, "c", swap_core)
     parts = lax.all_to_all(parts, ("x", "y"), 0, 0, tiled=True)
     span = layers * rank
     acts, moves = local_call(

time: 268 us -> 260 us (0.970)
  waiting for transfers between devices: 93.4 us -> 85 us
    ppermute x2 -> x1, waiting for transfers between devices: 11.4 us -> 0.01 us  [shards(): swapped = lax.ppermute(packed, across, swap)]
    ppermute x19, waiting for transfers between devices: 15.1 us -> 20.2 us  [shifted(): lax.ppermute(block, axis, [(i, (i + distance) % size) for i in range(size)])]
    ppermute x1, waiting for transfers between devices: 3.4 us -> 0.01 us  [shards(): came = lax.ppermute(send, 'c', swap_core)]
    ppermute x2 -> x1, starting transfers between devices: 8.48 us -> 7.39 us  [shards(): swapped = lax.ppermute(packed, across, swap)]
  transfers between devices with their start and end apart: 35 -> 34, of which waited for: 18 -> 16; matrix products, arithmetic and copies ran while one was open for 1% -> 1% of each run, Pallas kernels for 2% -> 2%
where the time goes in v8:
time: 260 us; the launch traced here: 258 us
  waiting for transfers between devices  85 us (33%)
  starting transfers between devices  76.1 us (29%)
  blocking collectives  47.1 us (18%)
  Pallas kernels  20.6 us (8%)
  between operations  15.1 us (6%)
  other arithmetic  9.19 us (4%)
  local copies, waits for them, and re-layouts  4.44 us (2%)
    all_to_all x2, blocking collectives, shards(): cross = lax.all_to_all(cross, ('y', 'z'), 0, 0, tiled=True)  47.1 us
    reduce_scatter x1, waiting for transfers between devices, shards(): grads = lax.psum_scatter(grads, 'z', scatter_dimension=0, tiled=True)[0]  31.8 us
    ppermute x19, starting transfers between devices, shifted(): lax.ppermute(block, axis, [(i, (i + distance) % size) for i in range(size)])  26.7 us
    ppermute x19, waiting for transfers between devices, shifted(): lax.ppermute(block, axis, [(i, (i + distance) % size) for i in range(size)])  20.2 us
    pallas_call x7, Pallas kernels, local_call(): pl.pallas_call(kernel, out_shape=out_shape, in_specs=in_specs, out_specs=...  18.2 us
    all_to_all x1, waiting for transfers between devices, shards(): parts = lax.all_to_all(parts, ('x', 'y'), 0, 0, tiled=True)  17.7 us
    all_to_all x1, starting transfers between devices, shards(): squares = lax.all_to_all(squares, EVERYONE, 0, 0, tiled=True)  12.3 us
    ppermute x1, starting transfers between devices, shards(): swapped = lax.ppermute(packed, across, swap)  7.39 us
  transfers between devices with their start and end apart: 34, of which 16 were waited for; matrix products, arithmetic and copies ran while one was open for 1% of the time, Pallas kernels for 2%

profile of v8, /device:TPU:2, one launch (start us, length us, event | category | flops | bytes accessed | tf_op | source)
XLA Modules:
  0.0 257.7 jit_solution(15905354766103724158)
XLA Ops:
  10.3 4.5 %all-to-all-start = ((bf16[4,256,384]{2,1,0:T(8,128)(2,1)}), bf16[4,256,384]{2,1,0:T(8,128)(2,1)S(1)}, u32[]{:S(2)}, u32[]{:S(2)}) async-start(bf16[4,256,384]{2,1,0:T(8,128)(2,1)} %maximum_maximum_fusion), calls=%async_computation | async-start | bytes 1572864 | tf_op jit(solution)/shard_map/all_to_all | solution.py:368
  14.9 2.2 collective-permute-start.3
  19.2 7.4 %collective-permute-start = (bf16[400,256]{1,0:T(8,128)(2,1)S(1)}, bf16[400,256]{1,0:T(8,128)(2,1)S(1)}, u32[]{:S(2)}, u32[]{:S(2)}) collective-permute-start(bf16[400,256]{1,0:T(8,128)(2,1)S(1)} %shard_map.144.own_ref), channel_id=1, source_target_pairs={{0,0},{1,33},{2,66},{3,99},{4,132},{5,165},{6,198},{7,231},{32,4},... | collective-permute-start | bytes 614408 | tf_op jit(solution)/shard_map/ppermute | solution.py:372
  26.6 5.3 %collective-permute-done.2 = bf16[400,256]{1,0:T(8,128)(2,1)S(1)} collective-permute-done((bf16[400,256]{1,0:T(8,128)(2,1)S(1)}, bf16[400,256]{1,0:T(8,128)(2,1)S(1)}, u32[]{:S(2)}, u32[]{:S(2)}) %collective-permute-start.2) | collective-permute-done | bytes 204832 | tf_op jit(solution)/shard_map/ppermute | solution.py:88
  32.9 2.2 collective-permute-done.4.far_ref
  36.1 27.5 %all_to_all.37 = bf16[32,16,256]{2,1,0:T(8,128)(2,1)S(1)} all-to-all(bf16[32,16,256]{2,1,0:T(8,128)(2,1)S(1)} %shard_map.145), channel_id=1, replica_groups=mesh['x'=4,'c'=2,'y'=4,'z'=8] {'y','z'}, dimensions={0} | all-to-all | bytes 524288 | tf_op jit(solution)/shard_map/all_to_all | solution.py:389
  63.7 19.6 %all_to_all.38 = bf16[32,16,256]{2,1,0:T(8,128)(2,1)S(1)} all-to-all(bf16[32,16,256]{2,1,0:T(8,128)(2,1)S(1)} %broadcast_in_dim.33), channel_id=1, replica_groups=mesh['x'=4,'c'=2,'y'=4,'z'=8] {'y','z'}, dimensions={0} | all-to-all | bytes 524288 | tf_op jit(solution)/shard_map/all_to_all | solution.py:392
  85.3 4.3 %collective-permute-done.6 = bf16[32,16,256]{2,1,0:T(8,128)(2,1)S(1)} collective-permute-done((bf16[32,16,256]{2,1,0:T(8,128)(2,1)S(1)}, bf16[32,16,256]{2,1,0:T(8,128)(2,1)S(1)}, u32[]{:S(2)}, u32[]{:S(2)}) %collective-permute-start.6) | collective-permute-done | bytes 262176 | tf_op jit(solution)/shard_map/ppermute | solution.py:88
  92.6 2.8 %shard_map.146 = (bf16[4,4,16,3072]{3,2,1,0:T(8,128)(2,1)S(1)}, bf16[4,4,16,3072]{3,2,1,0:T(8,128)(2,1)S(1)}) custom-call(s32[4]{0:T(128)S(1)} %pad_add_fusion.place_ref, bf16[4,256,384]{2,1,0:T(8,128)(2,1)S(1)} %all-to-all-done.rows_ref, bf16[8,400,256]{2,1,0:T(8,128)(2,1)S(1)} %bitcast.120), custom_call_target="tpu_custom_call" | custom-call | flops 1207959552 | bytes 5570560 | tf_op jit(solution)/shard_map/pallas_call | solution.py:75
  97.7 3.9 %collective-permute-done.9 = bf16[16,16,256]{2,1,0:T(8,128)(2,1)S(1)} collective-permute-done((bf16[16,16,256]{2,1,0:T(8,128)(2,1)S(1)}, bf16[16,16,256]{2,1,0:T(8,128)(2,1)S(1)}, u32[]{:S(2)}, u32[]{:S(2)}) %collective-permute-start.9) | collective-permute-done | bytes 131104 | tf_op jit(solution)/shard_map/ppermute | solution.py:88
  105.6 5.5 %all-to-all-start.3 = ((bf16[16,16,3072]{2,1,0:T(8,128)(2,1)}), bf16[16,16,3072]{2,1,0:T(8,128)(2,1)S(1)}, u32[]{:S(2)}, u32[]{:S(2)}) async-start(bf16[16,16,3072]{2,1,0:T(8,128)(2,1)} %bitcast.121), calls=%async_computation.3 | async-start | bytes 3145728 | tf_op jit(solution)/shard_map/all_to_all | solution.py:412
  114.2 17.7 %all-to-all-done.3.parts_ref = bf16[16,16,3072]{2,1,0:T(8,128)(2,1)S(1)} async-done(((bf16[16,16,3072]{2,1,0:T(8,128)(2,1)}), bf16[16,16,3072]{2,1,0:T(8,128)(2,1)S(1)}, u32[]{:S(2)}, u32[]{:S(2)}) %all-to-all-start.3) | async-done | bytes 1572896 | tf_op jit(solution)/shard_map/all_to_all | solution.py:412
  132.0 4.9 %shard_map.147 = (bf16[16,1152]{1,0:T(8,128)(2,1)S(1)}, bf16[16,1024]{1,0:T(8,128)(2,1)S(1)}) custom-call(s32[4]{0:T(128)S(1)} %pad_add_fusion.place_ref, bf16[16,16,3072]{2,1,0:T(8,128)(2,1)S(1)} %all-to-all-done.3.parts_ref, f32[16,128]{1,0:T(8,128)S(1)} %broadcast_in_dim.34.square_ref, bf16[4,32,16,256]{3,2,1,0:T(8,128)(2,1)S(1)} %pad_maximum_fusion.near_ref, ...), custom_call_target="tpu_custom_call" | custom-call | bytes 3747840 | tf_op jit(solution)/shard_map/pallas_call | solution.py:75
  136.8 2.5 collective-permute-start.13
  139.3 1.8 collective-permute-start.12
  142.5 2.1 collective-permute-start.19
  145.2 2.8 %collective-permute-start.15 = (bf16[4,16,1152]{2,1,0:T(8,128)(2,1)S(1)}, bf16[4,16,1152]{2,1,0:T(8,128)(2,1)S(1)}, u32[]{:S(2)}, u32[]{:S(2)}) collective-permute-start(bf16[4,16,1152]{2,1,0:T(8,128)(2,1)S(1)} %get-tuple-element.58), channel_id=1, source_target_pairs={{0,24},{8,0},{16,8},{24,16},{1,25},{9,1},{17,9},{25,17},{2,26},{10... | collective-permute-start | bytes 442376 | tf_op jit(solution)/shard_map/ppermute | solution.py:88
  150.6 2.1 collective-permute-start.22
  152.8 4.0 %collective-permute-start.23 = (bf16[4,16,1024]{2,1,0:T(8,128)(2,1)S(1)}, bf16[4,16,1024]{2,1,0:T(8,128)(2,1)S(1)}, u32[]{:S(2)}, u32[]{:S(2)}) collective-permute-start(bf16[4,16,1024]{2,1,0:T(8,128)(2,1)S(1)} %get-tuple-element.60), channel_id=1, source_target_pairs={{0,128},{64,192},{128,0},{192,64},{1,129},{65,193},{129,1},{193,65... | collective-permute-start | bytes 393224 | tf_op jit(solution)/shard_map/ppermute | solution.py:88
  157.7 2.1 collective-permute-done.23
  160.1 1.9 collective-permute-done.24.move_far_ref
  162.0 7.4 %shard_map.148 = (bf16[8,4,128,384]{3,2,1,0:T(8,128)(2,1)}, bf16[8,128,768]{2,1,0:T(8,128)(2,1)}) custom-call(s32[4]{0:T(128)S(1)} %pad_add_fusion.place_ref, bf16[4,256,384]{2,1,0:T(8,128)(2,1)S(1)} %all-to-all-done.rows_ref, bf16[8,400,256]{2,1,0:T(8,128)(2,1)} %bitcast.119, bf16[4,4,16,1152]{3,2,1,0:T(8,128)(2,1)S(1)} %pad_maximum_fusion.2.act_near_ref, ...), custom_call_target="tpu_custom_call" | custom-call | flops 1610612736 | bytes 9371648 | tf_op jit(solution)/shard_map/pallas_call | solution.py:75
  169.5 6.5 %all-to-all-start.4 = ((bf16[32,128,384]{2,1,0:T(8,128)(2,1)}), bf16[32,128,384]{2,1,0:T(8,128)(2,1)S(1)}, u32[]{:S(2)}, u32[]{:S(2)}) async-start(bf16[32,128,384]{2,1,0:T(8,128)(2,1)} %bitcast.123), calls=%async_computation.4 | async-start | bytes 6291456 | tf_op jit(solution)/shard_map/all_to_all | solution.py:453
  176.0 31.8 %reduce-scatter.2.cloned.1.call-done = bf16[1,128,768]{2,1,0:T(8,128)(2,1)} async-done(((bf16[8,128,768]{2,1,0:T(8,128)(2,1)}), bf16[1,128,768]{2,1,0:T(8,128)(2,1)}) %reduce-scatter.2.cloned.1.call-update) | async-done | bytes 196624 | tf_op jit(solution)/shard_map/reduce_scatter | solution.py:451
  207.8 1.9 collective-permute-start.25
  209.7 6.3 %collective-permute-done.25.grad_ref = bf16[128,768]{1,0:T(8,128)(2,1)S(1)} collective-permute-done((bf16[128,768]{1,0:T(8,128)(2,1)}, bf16[128,768]{1,0:T(8,128)(2,1)S(1)}, u32[]{:S(2)}, u32[]{:S(2)}) %collective-permute-start.25) | collective-permute-done | bytes 196640 | tf_op jit(solution)/shard_map/ppermute | solution.py:464
  216.0 4.1 %collective-permute-start.26 = (bf16[128,768]{1,0:T(8,128)(2,1)S(1)}, bf16[128,768]{1,0:T(8,128)(2,1)}, u32[]{:S(2)}, u32[]{:S(2)}) collective-permute-start(bf16[128,768]{1,0:T(8,128)(2,1)S(1)} %collective-permute-done.25.grad_ref), channel_id=1, source_target_pairs={{0,0},{1,1},{2,2},{3,3},{4,4},{5,5},{6,6},{7,7},{32,38},{33,39},{3... | collective-permute-start | bytes 589832 | tf_op jit(solution)/shard_map/ppermute | solution.py:470
  221.0 12.3 %all-to-all-start.5 = ((f32[256,1,128]{2,1,0:T(1,128)}), f32[256,1,128]{2,1,0:T(1,128)S(1)}, u32[]{:S(2)}, u32[]{:S(2)}) async-start(f32[256,1,128]{2,1,0:T(1,128)} %bitcast.45), calls=%async_computation.6 | async-start | bytes 262144 | tf_op jit(solution)/shard_map/all_to_all | solution.py:468
  233.4 6.3 %collective-permute-start.27 = (bf16[128,768]{1,0:T(8,128)(2,1)}, bf16[128,768]{1,0:T(8,128)(2,1)}, u32[]{:S(2)}, u32[]{:S(2)}) collective-permute-start(bf16[128,768]{1,0:T(8,128)(2,1)} %collective-permute-done.26), channel_id=1, source_target_pairs={{0,0},{1,1},{2,2},{3,3},{4,4},{5,5},{6,6},{7,7},{32,38},{33,39},{3... | collective-permute-start | bytes 589832 | tf_op jit(solution)/shard_map/ppermute | solution.py:470
  239.7 2.4 shard_map.149
  242.2 3.3 %all-to-all-done.5 = f32[256,1,128]{2,1,0:T(1,128)S(1)} async-done(((f32[256,1,128]{2,1,0:T(1,128)}), f32[256,1,128]{2,1,0:T(1,128)S(1)}, u32[]{:S(2)}, u32[]{:S(2)}) %all-to-all-start.5) | async-done | bytes 131104 | tf_op jit(solution)/shard_map/all_to_all | solution.py:468
  247.9 2.0 fusion.11
  (93 shorter events, 31.0 us)
Async XLA Ops:
  10.3 21.7 %all-to-all-start = ((bf16[4,256,384]{2,1,0:T(8,128)(2,1)}), bf16[4,256,384]{2,1,0:T(8,128)(2,1)S(1)}, u32[]{:S(2)}, u32[]{:S(2)}) async-start(bf16[4,256,384]{2,1,0:T(8,128)(2,1)} %maximum_maximum_fusion), calls=%async_computation | async-start | bytes 1572864 | tf_op jit(solution)/shard_map/all_to_all | solution.py:368
  14.7 76.4 %all-gather.3.cloned.1.call-start = ((), (), s32[]{:S(2)}) async-start(), calls=%async_computation.8 | async-start | bytes 1843200 | tf_op jit(solution)/shard_map/all_gather | solution.py:376
  14.9 11.6 %collective-permute-start.3 = (bf16[400,256]{1,0:T(8,128)(2,1)S(1)}, bf16[400,256]{1,0:T(8,128)(2,1)S(1)}, u32[]{:S(2)}, u32[]{:S(2)}) collective-permute-start(bf16[400,256]{1,0:T(8,128)(2,1)S(1)} %shard_map.144.own_ref), channel_id=1, source_target_pairs={{0,128},{64,192},{128,0},{192,64},{1,129},{65,193},{129,1},{193,65... | collective-permute-start | bytes 614408 | tf_op jit(solution)/shard_map/ppermute | solution.py:88
  17.1 14.7 %collective-permute-start.2 = (bf16[400,256]{1,0:T(8,128)(2,1)S(1)}, bf16[400,256]{1,0:T(8,128)(2,1)S(1)}, u32[]{:S(2)}, u32[]{:S(2)}) collective-permute-start(bf16[400,256]{1,0:T(8,128)(2,1)S(1)} %shard_map.144.own_ref), channel_id=1, source_target_pairs={{0,192},{64,0},{128,64},{192,128},{1,193},{65,1},{129,65},{193,129... | collective-permute-start | bytes 614408 | tf_op jit(solution)/shard_map/ppermute | solution.py:88
  18.6 13.3 %collective-permute-start.1 = (bf16[400,256]{1,0:T(8,128)(2,1)S(1)}, bf16[400,256]{1,0:T(8,128)(2,1)S(1)}, u32[]{:S(2)}, u32[]{:S(2)}) collective-permute-start(bf16[400,256]{1,0:T(8,128)(2,1)S(1)} %shard_map.144.own_ref), channel_id=1, source_target_pairs={{0,64},{64,128},{128,192},{192,0},{1,65},{65,129},{129,193},{193,1... | collective-permute-start | bytes 614408 | tf_op jit(solution)/shard_map/ppermute | solution.py:88
  19.2 12.8 %collective-permute-start = (bf16[400,256]{1,0:T(8,128)(2,1)S(1)}, bf16[400,256]{1,0:T(8,128)(2,1)S(1)}, u32[]{:S(2)}, u32[]{:S(2)}) collective-permute-start(bf16[400,256]{1,0:T(8,128)(2,1)S(1)} %shard_map.144.own_ref), channel_id=1, source_target_pairs={{0,0},{1,33},{2,66},{3,99},{4,132},{5,165},{6,198},{7,231},{32,4},... | collective-permute-start | bytes 614408 | tf_op jit(solution)/shard_map/ppermute | solution.py:372
  83.3 6.4 %collective-permute-start.6 = (bf16[32,16,256]{2,1,0:T(8,128)(2,1)S(1)}, bf16[32,16,256]{2,1,0:T(8,128)(2,1)S(1)}, u32[]{:S(2)}, u32[]{:S(2)}) collective-permute-start(bf16[32,16,256]{2,1,0:T(8,128)(2,1)S(1)} %all_to_all.38), channel_id=1, source_target_pairs={{0,192},{64,0},{128,64},{192,128},{1,193},{65,1},{129,65},{193,129... | collective-permute-start | bytes 786440 | tf_op jit(solution)/shard_map/ppermute | solution.py:88
  84.7 6.4 %collective-permute-start.5 = (bf16[32,16,256]{2,1,0:T(8,128)(2,1)S(1)}, bf16[32,16,256]{2,1,0:T(8,128)(2,1)S(1)}, u32[]{:S(2)}, u32[]{:S(2)}) collective-permute-start(bf16[32,16,256]{2,1,0:T(8,128)(2,1)S(1)} %all_to_all.38), channel_id=1, source_target_pairs={{0,64},{64,128},{128,192},{192,0},{1,65},{65,129},{129,193},{193,1... | collective-permute-start | bytes 786440 | tf_op jit(solution)/shard_map/ppermute | solution.py:88
  95.5 8.3 %collective-permute-start.7 = (bf16[4,4,16,3072]{3,2,1,0:T(8,128)(2,1)S(1)}, bf16[4,4,16,3072]{3,2,1,0:T(8,128)(2,1)S(1)}, u32[]{:S(2)}, u32[]{:S(2)}) collective-permute-start(bf16[4,4,16,3072]{3,2,1,0:T(8,128)(2,1)S(1)} %get-tuple-element.32), channel_id=1, source_target_pairs={{0,32},{32,0},{1,33},{33,1},{2,34},{34,2},{3,35},{35,3},{4,36},{36... | collective-permute-start | bytes 4718600 | tf_op jit(solution)/shard_map/ppermute | solution.py:407
  95.6 6.0 %collective-permute-start.9 = (bf16[16,16,256]{2,1,0:T(8,128)(2,1)S(1)}, bf16[16,16,256]{2,1,0:T(8,128)(2,1)S(1)}, u32[]{:S(2)}, u32[]{:S(2)}) collective-permute-start(bf16[16,16,256]{2,1,0:T(8,128)(2,1)S(1)} %slice.10), channel_id=1, source_target_pairs={{0,192},{64,0},{128,64},{192,128},{1,193},{65,1},{129,65},{193,129... | collective-permute-start | bytes 393224 | tf_op jit(solution)/shard_map/ppermute | solution.py:88
  96.9 5.6 %collective-permute-start.8 = (bf16[16,16,256]{2,1,0:T(8,128)(2,1)S(1)}, bf16[16,16,256]{2,1,0:T(8,128)(2,1)S(1)}, u32[]{:S(2)}, u32[]{:S(2)}) collective-permute-start(bf16[16,16,256]{2,1,0:T(8,128)(2,1)S(1)} %slice.9), channel_id=1, source_target_pairs={{0,64},{64,128},{128,192},{192,0},{1,65},{65,129},{129,193},{193,1... | collective-permute-start | bytes 393224 | tf_op jit(solution)/shard_map/ppermute | solution.py:88
  105.6 26.3 %all-to-all-start.3 = ((bf16[16,16,3072]{2,1,0:T(8,128)(2,1)}), bf16[16,16,3072]{2,1,0:T(8,128)(2,1)S(1)}, u32[]{:S(2)}, u32[]{:S(2)}) async-start(bf16[16,16,3072]{2,1,0:T(8,128)(2,1)} %bitcast.121), calls=%async_computation.3 | async-start | bytes 3145728 | tf_op jit(solution)/shard_map/all_to_all | solution.py:412
  111.1 96.7 %reduce-scatter.2.cloned.1.call-start = ((), (), s32[]{:S(2)}) async-start(), calls=%async_computation.7 | async-start | bytes 1769472 | tf_op jit(solution)/shard_map/reduce_scatter | solution.py:451
  111.2 3.1 %collective-permute-start.10 = (bf16[4,32,16,256]{3,2,1,0:T(8,128)(2,1)S(1)}, bf16[4,32,16,256]{3,2,1,0:T(8,128)(2,1)}, u32[]{:S(2)}, u32[]{:S(2)}) collective-permute-start(bf16[4,32,16,256]{3,2,1,0:T(8,128)(2,1)S(1)} %pad_maximum_fusion.near_ref), channel_id=1, source_target_pairs={{0,32},{32,0},{1,33},{33,1},{2,34},{34,2},{3,35},{35,3},{4,36},{36... | collective-permute-start | bytes 3145736 | tf_op jit(solution)/shard_map/ppermute | solution.py:411
  136.8 7.8 %collective-permute-start.13 = (bf16[16,1152]{1,0:T(8,128)(2,1)S(1)}, bf16[16,1152]{1,0:T(8,128)(2,1)S(1)}, u32[]{:S(2)}, u32[]{:S(2)}) collective-permute-start(bf16[16,1152]{1,0:T(8,128)(2,1)S(1)} %get-tuple-element.37), channel_id=1, source_target_pairs={{0,128},{64,192},{128,0},{192,64},{1,129},{65,193},{129,1},{193,65... | collective-permute-start | bytes 110600 | tf_op jit(solution)/shard_map/ppermute | solution.py:88
  139.3 5.3 %collective-permute-start.12 = (bf16[16,1152]{1,0:T(8,128)(2,1)S(1)}, bf16[16,1152]{1,0:T(8,128)(2,1)S(1)}, u32[]{:S(2)}, u32[]{:S(2)}) collective-permute-start(bf16[16,1152]{1,0:T(8,128)(2,1)S(1)} %get-tuple-element.37), channel_id=1, source_target_pairs={{0,192},{64,0},{128,64},{192,128},{1,193},{65,1},{129,65},{193,129... | collective-permute-start | bytes 110600 | tf_op jit(solution)/shard_map/ppermute | solution.py:88
  141.2 4.0 %collective-permute-start.11 = (bf16[16,1152]{1,0:T(8,128)(2,1)S(1)}, bf16[16,1152]{1,0:T(8,128)(2,1)S(1)}, u32[]{:S(2)}, u32[]{:S(2)}) collective-permute-start(bf16[16,1152]{1,0:T(8,128)(2,1)S(1)} %get-tuple-element.37), channel_id=1, source_target_pairs={{0,64},{64,128},{128,192},{192,0},{1,65},{65,129},{129,193},{193,1... | collective-permute-start | bytes 110600 | tf_op jit(solution)/shard_map/ppermute | solution.py:88
  141.4 6.6 %collective-permute-start.20 = (bf16[16,1024]{1,0:T(8,128)(2,1)S(1)}, bf16[16,1024]{1,0:T(8,128)(2,1)S(1)}, u32[]{:S(2)}, u32[]{:S(2)}) collective-permute-start(bf16[16,1024]{1,0:T(8,128)(2,1)S(1)} %get-tuple-element.38), channel_id=1, source_target_pairs={{0,16},{8,24},{16,0},{24,8},{1,17},{9,25},{17,1},{25,9},{2,18},{10... | collective-permute-start | bytes 98312 | tf_op jit(solution)/shard_map/ppermute | solution.py:88
  142.5 7.1 %collective-permute-start.19 = (bf16[16,1024]{1,0:T(8,128)(2,1)S(1)}, bf16[16,1024]{1,0:T(8,128)(2,1)S(1)}, u32[]{:S(2)}, u32[]{:S(2)}) collective-permute-start(bf16[16,1024]{1,0:T(8,128)(2,1)S(1)} %get-tuple-element.38), channel_id=1, source_target_pairs={{0,24},{8,0},{16,8},{24,16},{1,25},{9,1},{17,9},{25,17},{2,26},{10... | collective-permute-start | bytes 98312 | tf_op jit(solution)/shard_map/ppermute | solution.py:88
  144.6 6.0 %collective-permute-start.18 = (bf16[16,1024]{1,0:T(8,128)(2,1)S(1)}, bf16[16,1024]{1,0:T(8,128)(2,1)S(1)}, u32[]{:S(2)}, u32[]{:S(2)}) collective-permute-start(bf16[16,1024]{1,0:T(8,128)(2,1)S(1)} %get-tuple-element.38), channel_id=1, source_target_pairs={{0,8},{8,16},{16,24},{24,0},{1,9},{9,17},{17,25},{25,1},{2,10},{10... | collective-permute-start | bytes 98312 | tf_op jit(solution)/shard_map/ppermute | solution.py:88
  145.2 7.6 %collective-permute-start.15 = (bf16[4,16,1152]{2,1,0:T(8,128)(2,1)S(1)}, bf16[4,16,1152]{2,1,0:T(8,128)(2,1)S(1)}, u32[]{:S(2)}, u32[]{:S(2)}) collective-permute-start(bf16[4,16,1152]{2,1,0:T(8,128)(2,1)S(1)} %get-tuple-element.58), channel_id=1, source_target_pairs={{0,24},{8,0},{16,8},{24,16},{1,25},{9,1},{17,9},{25,17},{2,26},{10... | collective-permute-start | bytes 442376 | tf_op jit(solution)/shard_map/ppermute | solution.py:88
  148.0 8.8 %collective-permute-start.14 = (bf16[4,16,1152]{2,1,0:T(8,128)(2,1)S(1)}, bf16[4,16,1152]{2,1,0:T(8,128)(2,1)S(1)}, u32[]{:S(2)}, u32[]{:S(2)}) collective-permute-start(bf16[4,16,1152]{2,1,0:T(8,128)(2,1)S(1)} %get-tuple-element.58), channel_id=1, source_target_pairs={{0,8},{8,16},{16,24},{24,0},{1,9},{9,17},{17,25},{25,1},{2,10},{10... | collective-permute-start | bytes 442376 | tf_op jit(solution)/shard_map/ppermute | solution.py:88
  148.0 8.8 %collective-permute-start.16 = (bf16[4,16,1152]{2,1,0:T(8,128)(2,1)S(1)}, bf16[4,16,1152]{2,1,0:T(8,128)(2,1)S(1)}, u32[]{:S(2)}, u32[]{:S(2)}) collective-permute-start(bf16[4,16,1152]{2,1,0:T(8,128)(2,1)S(1)} %get-tuple-element.58), channel_id=1, source_target_pairs={{0,16},{8,24},{16,0},{24,8},{1,17},{9,25},{17,1},{25,9},{2,18},{10... | collective-permute-start | bytes 442376 | tf_op jit(solution)/shard_map/ppermute | solution.py:88
  150.6 6.4 %collective-permute-start.22 = (bf16[4,16,1024]{2,1,0:T(8,128)(2,1)S(1)}, bf16[4,16,1024]{2,1,0:T(8,128)(2,1)S(1)}, u32[]{:S(2)}, u32[]{:S(2)}) collective-permute-start(bf16[4,16,1024]{2,1,0:T(8,128)(2,1)S(1)} %get-tuple-element.60), channel_id=1, source_target_pairs={{0,192},{64,0},{128,64},{192,128},{1,193},{65,1},{129,65},{193,129... | collective-permute-start | bytes 393224 | tf_op jit(solution)/shard_map/ppermute | solution.py:88
  152.7 5.0 %collective-permute-start.21 = (bf16[4,16,1024]{2,1,0:T(8,128)(2,1)S(1)}, bf16[4,16,1024]{2,1,0:T(8,128)(2,1)S(1)}, u32[]{:S(2)}, u32[]{:S(2)}) collective-permute-start(bf16[4,16,1024]{2,1,0:T(8,128)(2,1)S(1)} %get-tuple-element.60), channel_id=1, source_target_pairs={{0,64},{64,128},{128,192},{192,0},{1,65},{65,129},{129,193},{193,1... | collective-permute-start | bytes 393224 | tf_op jit(solution)/shard_map/ppermute | solution.py:88
  152.8 7.0 %collective-permute-start.23 = (bf16[4,16,1024]{2,1,0:T(8,128)(2,1)S(1)}, bf16[4,16,1024]{2,1,0:T(8,128)(2,1)S(1)}, u32[]{:S(2)}, u32[]{:S(2)}) collective-permute-start(bf16[4,16,1024]{2,1,0:T(8,128)(2,1)S(1)} %get-tuple-element.60), channel_id=1, source_target_pairs={{0,128},{64,192},{128,0},{192,64},{1,129},{65,193},{129,1},{193,65... | collective-permute-start | bytes 393224 | tf_op jit(solution)/shard_map/ppermute | solution.py:88
  156.9 5.1 %collective-permute-start.17 = (bf16[4,4,16,1152]{3,2,1,0:T(8,128)(2,1)S(1)}, bf16[4,4,16,1152]{3,2,1,0:T(8,128)(2,1)S(1)}, u32[]{:S(2)}, u32[]{:S(2)}) collective-permute-start(bf16[4,4,16,1152]{3,2,1,0:T(8,128)(2,1)S(1)} %pad_maximum_fusion.2.act_near_ref), channel_id=1, source_target_pairs={{0,32},{32,0},{1,33},{33,1},{2,34},{34,2},{3,35},{35,3},{4,36},{36... | collective-permute-start | bytes 1769480 | tf_op jit(solution)/shard_map/ppermute | solution.py:431
  169.5 51.5 %all-to-all-start.4 = ((bf16[32,128,384]{2,1,0:T(8,128)(2,1)}), bf16[32,128,384]{2,1,0:T(8,128)(2,1)S(1)}, u32[]{:S(2)}, u32[]{:S(2)}) async-start(bf16[32,128,384]{2,1,0:T(8,128)(2,1)} %bitcast.123), calls=%async_computation.4 | async-start | bytes 6291456 | tf_op jit(solution)/shard_map/all_to_all | solution.py:453
  207.8 8.3 %collective-permute-start.25 = (bf16[128,768]{1,0:T(8,128)(2,1)}, bf16[128,768]{1,0:T(8,128)(2,1)S(1)}, u32[]{:S(2)}, u32[]{:S(2)}) collective-permute-start(bf16[128,768]{1,0:T(8,128)(2,1)} %bitcast.143), channel_id=1, source_target_pairs={{0,0},{33,1},{66,2},{99,3},{132,4},{165,5},{198,6},{231,7},{4,36},... | collective-permute-start | bytes 589832 | tf_op jit(solution)/shard_map/ppermute | solution.py:464
  216.0 17.3 %collective-permute-start.26 = (bf16[128,768]{1,0:T(8,128)(2,1)S(1)}, bf16[128,768]{1,0:T(8,128)(2,1)}, u32[]{:S(2)}, u32[]{:S(2)}) collective-permute-start(bf16[128,768]{1,0:T(8,128)(2,1)S(1)} %collective-permute-done.25.grad_ref), channel_id=1, source_target_pairs={{0,0},{1,1},{2,2},{3,3},{4,4},{5,5},{6,6},{7,7},{32,38},{33,39},{3... | collective-permute-start | bytes 589832 | tf_op jit(solution)/shard_map/ppermute | solution.py:470
  221.0 24.4 %all-to-all-start.5 = ((f32[256,1,128]{2,1,0:T(1,128)}), f32[256,1,128]{2,1,0:T(1,128)S(1)}, u32[]{:S(2)}, u32[]{:S(2)}) async-start(f32[256,1,128]{2,1,0:T(1,128)} %bitcast.45), calls=%async_computation.6 | async-start | bytes 262144 | tf_op jit(solution)/shard_map/all_to_all | solution.py:468
  233.4 13.4 %collective-permute-start.27 = (bf16[128,768]{1,0:T(8,128)(2,1)}, bf16[128,768]{1,0:T(8,128)(2,1)}, u32[]{:S(2)}, u32[]{:S(2)}) collective-permute-start(bf16[128,768]{1,0:T(8,128)(2,1)} %collective-permute-done.26), channel_id=1, source_target_pairs={{0,0},{1,1},{2,2},{3,3},{4,4},{5,5},{6,6},{7,7},{32,38},{33,39},{3... | collective-permute-start | bytes 589832 | tf_op jit(solution)/shard_map/ppermute | solution.py:470
  (14 other events, 86.5 us)
Sparse Core Ops, SparseCore 0:
  32.8 49.0 all-gather.2
  169.6 38.1 reduce-scatter.1

commit v9 on v8

--- a/solution.py
+++ b/solution.py
@@ -26,7 +26,7 @@
 EVERYONE = ("x", "c", "y", "z")
 SHIFTS = (0, 1, -1, 2)
 TURNS = (0, 4, 3, 7, 2, 6, 1, 5)
-FIRST = (0, 2, 2, -1, 1, -1, 1, -2)
+FIRST = (0, 3, 3, -1, 2, -2, 1, -3)
 EXTRA = 16
 VMEM_BYTES = 48 * 1024 * 1024
 
@@ -391,10 +391,6 @@
     cross = jnp.broadcast_to(cross, (count_y * count_z, cut_r, cut_c))
     cross = lax.all_to_all(cross, ("y", "z"), 0, 0, tiled=True)
     before, after = shifted(cross, "x", 1), shifted(cross, "x", -1)
-    before, after, rows = lax.optimization_barrier((before, after, rows))
-    half = cross.shape[0] // 2
-    beyond = [shifted(before[:half], "x", 1), shifted(after[half:], "x", -1)]
-    cross_near = jnp.stack([cross, before, after, jnp.concatenate(beyond)])
 
     part_shape = jax.ShapeDtypeStruct((count_x, count_y, piece, layers * 3 * rank), LOW)
     keep, send = local_call(
@@ -404,10 +400,14 @@
         scalars=place,
         flops=2 * rows.shape[0] * tok_rows * features * layers * rank * 3,
     )
+    send, before, after = lax.optimization_barrier((send, before, after))
     came = lax.ppermute(send, "c", swap_core)
+    half = cross.shape[0] // 2
+    beyond = [shifted(before[:half], "x", 1), shifted(after[half:], "x", -1)]
     parts = (keep.astype(WIDE) + came.astype(WIDE)).astype(LOW)
     parts = parts.reshape(count_x * count_y, piece, layers * 3 * rank)
-    parts, cross_near = lax.optimization_barrier((parts, cross_near))
+    parts, *beyond = lax.optimization_barrier((parts, *beyond))
+    cross_near = jnp.stack([cross, before, after, jnp.concatenate(beyond)])
     cross_far = lax.ppermute(cross_near, "c", swap_core)
     parts = lax.all_to_all(parts, ("x", "y"), 0, 0, tiled=True)
     span = layers * rank

time: 260 us -> 254 us (0.977)
  waiting for transfers between devices: 85 us -> 81.2 us
  starting transfers between devices: 76.1 us -> 72.9 us
    ppermute x19, waiting for transfers between devices: 20.2 us -> 12.9 us  [shifted(): lax.ppermute(block, axis, [(i, (i + distance) % size) for i in range(size)])]
    all_to_all x1, waiting for transfers between devices: 3.28 us -> 6.65 us  [shards(): squares = lax.all_to_all(squares, EVERYONE, 0, 0, tiled=True)]
    ppermute x1, starting transfers between devices: 6.34 us -> 2.99 us  [shards(): lax.ppermute(lax.ppermute(grads, across, first_back), across, last_back)]
  transfers between devices with their start and end apart: 34 -> 34, of which waited for: 16 -> 17; matrix products, arithmetic and copies ran while one was open for 1% -> 2% of each run, Pallas kernels for 2% -> 3%
where the time goes in v9:
time: 254 us; the launch traced here: 251 us
  waiting for transfers between devices  81.2 us (32%)
  starting transfers between devices  72.9 us (29%)
  blocking collectives  47.2 us (19%)
  Pallas kernels  20.6 us (8%)
  between operations  15.1 us (6%)
  other arithmetic  9.2 us (4%)
  local copies, waits for them, and re-layouts  5 us (2%)
    all_to_all x2, blocking collectives, shards(): cross = lax.all_to_all(cross, ('y', 'z'), 0, 0, tiled=True)  47.2 us
    reduce_scatter x1, waiting for transfers between devices, shards(): grads = lax.psum_scatter(grads, 'z', scatter_dimension=0, tiled=True)[0]  32.1 us
    ppermute x19, starting transfers between devices, shifted(): lax.ppermute(block, axis, [(i, (i + distance) % size) for i in range(size)])  26.6 us
    pallas_call x7, Pallas kernels, local_call(): pl.pallas_call(kernel, out_shape=out_shape, in_specs=in_specs, out_specs=...  18.2 us
    all_to_all x1, waiting for transfers between devices, shards(): parts = lax.all_to_all(parts, ('x', 'y'), 0, 0, tiled=True)  16.5 us
    all_to_all x1, starting transfers between devices, shards(): squares = lax.all_to_all(squares, EVERYONE, 0, 0, tiled=True)  14.7 us
    ppermute x19, waiting for transfers between devices, shifted(): lax.ppermute(block, axis, [(i, (i + distance) % size) for i in range(size)])  12.9 us
    ppermute x1, starting transfers between devices, shards(): swapped = lax.ppermute(packed, across, swap)  7.39 us
  transfers between devices with their start and end apart: 34, of which 17 were waited for; matrix products, arithmetic and copies ran while one was open for 2% of the time, Pallas kernels for 3%

profile of v9, /device:TPU:2, one launch (start us, length us, event | category | flops | bytes accessed | tf_op | source)
XLA Modules:
  0.0 251.2 jit_solution(10755359520944313628)
XLA Ops:
  10.3 4.5 %all-to-all-start = ((bf16[4,256,384]{2,1,0:T(8,128)(2,1)}), bf16[4,256,384]{2,1,0:T(8,128)(2,1)S(1)}, u32[]{:S(2)}, u32[]{:S(2)}) async-start(bf16[4,256,384]{2,1,0:T(8,128)(2,1)} %maximum_maximum_fusion), calls=%async_computation | async-start | bytes 1572864 | tf_op jit(solution)/shard_map/all_to_all | solution.py:368
  14.9 2.2 collective-permute-start.3
  19.2 7.4 %collective-permute-start = (bf16[400,256]{1,0:T(8,128)(2,1)S(1)}, bf16[400,256]{1,0:T(8,128)(2,1)S(1)}, u32[]{:S(2)}, u32[]{:S(2)}) collective-permute-start(bf16[400,256]{1,0:T(8,128)(2,1)S(1)} %shard_map.144.own_ref), channel_id=1, source_target_pairs={{0,0},{1,33},{2,66},{3,99},{4,132},{5,165},{6,198},{7,231},{32,4},... | collective-permute-start | bytes 614408 | tf_op jit(solution)/shard_map/ppermute | solution.py:372
  26.6 5.3 %collective-permute-done.2 = bf16[400,256]{1,0:T(8,128)(2,1)S(1)} collective-permute-done((bf16[400,256]{1,0:T(8,128)(2,1)S(1)}, bf16[400,256]{1,0:T(8,128)(2,1)S(1)}, u32[]{:S(2)}, u32[]{:S(2)}) %collective-permute-start.2) | collective-permute-done | bytes 204832 | tf_op jit(solution)/shard_map/ppermute | solution.py:88
  32.8 2.2 collective-permute-done.4.far_ref
  36.1 27.5 %all_to_all.37 = bf16[32,16,256]{2,1,0:T(8,128)(2,1)S(1)} all-to-all(bf16[32,16,256]{2,1,0:T(8,128)(2,1)S(1)} %shard_map.146), channel_id=1, replica_groups=mesh['x'=4,'c'=2,'y'=4,'z'=8] {'y','z'}, dimensions={0} | all-to-all | bytes 524288 | tf_op jit(solution)/shard_map/all_to_all | solution.py:389
  63.7 19.6 %all_to_all.38 = bf16[32,16,256]{2,1,0:T(8,128)(2,1)S(1)} all-to-all(bf16[32,16,256]{2,1,0:T(8,128)(2,1)S(1)} %broadcast_in_dim.33), channel_id=1, replica_groups=mesh['x'=4,'c'=2,'y'=4,'z'=8] {'y','z'}, dimensions={0} | all-to-all | bytes 524288 | tf_op jit(solution)/shard_map/all_to_all | solution.py:392
  86.8 2.8 %shard_map.145 = (bf16[4,4,16,3072]{3,2,1,0:T(8,128)(2,1)S(1)}, bf16[4,4,16,3072]{3,2,1,0:T(8,128)(2,1)S(1)}) custom-call(s32[4]{0:T(128)S(1)} %pad_add_fusion.place_ref, bf16[4,256,384]{2,1,0:T(8,128)(2,1)S(1)} %all-to-all-done.rows_ref, bf16[8,400,256]{2,1,0:T(8,128)(2,1)S(1)} %bitcast.120), custom_call_target="tpu_custom_call" | custom-call | flops 1207959552 | bytes 5570560 | tf_op jit(solution)/shard_map/pallas_call | solution.py:75
  94.5 1.7 add_convert_fusion
  98.7 5.6 %all-to-all-start.3 = ((bf16[16,16,3072]{2,1,0:T(8,128)(2,1)}), bf16[16,16,3072]{2,1,0:T(8,128)(2,1)S(1)}, u32[]{:S(2)}, u32[]{:S(2)}) async-start(bf16[16,16,3072]{2,1,0:T(8,128)(2,1)} %bitcast.121), calls=%async_computation.3 | async-start | bytes 3145728 | tf_op jit(solution)/shard_map/all_to_all | solution.py:412
  107.2 1.6 collective-permute-done.10.far_ref
  108.8 16.5 %all-to-all-done.3.parts_ref = bf16[16,16,3072]{2,1,0:T(8,128)(2,1)S(1)} async-done(((bf16[16,16,3072]{2,1,0:T(8,128)(2,1)}), bf16[16,16,3072]{2,1,0:T(8,128)(2,1)S(1)}, u32[]{:S(2)}, u32[]{:S(2)}) %all-to-all-start.3) | async-done | bytes 1572896 | tf_op jit(solution)/shard_map/all_to_all | solution.py:412
  125.3 4.9 %shard_map.147 = (bf16[16,1152]{1,0:T(8,128)(2,1)S(1)}, bf16[16,1024]{1,0:T(8,128)(2,1)S(1)}) custom-call(s32[4]{0:T(128)S(1)} %pad_add_fusion.place_ref, bf16[16,16,3072]{2,1,0:T(8,128)(2,1)S(1)} %all-to-all-done.3.parts_ref, f32[16,128]{1,0:T(8,128)S(1)} %broadcast_in_dim.34.square_ref, bf16[4,32,16,256]{3,2,1,0:T(8,128)(2,1)S(1)} %pad_maximum_fusion.near_ref, ...), custom_call_target="tpu_custom_call" | custom-call | bytes 3747840 | tf_op jit(solution)/shard_map/pallas_call | solution.py:75
  130.2 2.5 collective-permute-start.13
  132.7 1.8 collective-permute-start.12
  135.9 2.1 collective-permute-start.19
  138.5 2.8 %collective-permute-start.15 = (bf16[4,16,1152]{2,1,0:T(8,128)(2,1)S(1)}, bf16[4,16,1152]{2,1,0:T(8,128)(2,1)S(1)}, u32[]{:S(2)}, u32[]{:S(2)}) collective-permute-start(bf16[4,16,1152]{2,1,0:T(8,128)(2,1)S(1)} %get-tuple-element.60), channel_id=1, source_target_pairs={{0,24},{8,0},{16,8},{24,16},{1,25},{9,1},{17,9},{25,17},{2,26},{10... | collective-permute-start | bytes 442376 | tf_op jit(solution)/shard_map/ppermute | solution.py:88
  144.0 2.1 collective-permute-start.22
  146.1 4.0 %collective-permute-start.23 = (bf16[4,16,1024]{2,1,0:T(8,128)(2,1)S(1)}, bf16[4,16,1024]{2,1,0:T(8,128)(2,1)S(1)}, u32[]{:S(2)}, u32[]{:S(2)}) collective-permute-start(bf16[4,16,1024]{2,1,0:T(8,128)(2,1)S(1)} %get-tuple-element.62), channel_id=1, source_target_pairs={{0,128},{64,192},{128,0},{192,64},{1,129},{65,193},{129,1},{193,65... | collective-permute-start | bytes 393224 | tf_op jit(solution)/shard_map/ppermute | solution.py:88
  151.1 2.1 collective-permute-done.23
  153.5 1.9 collective-permute-done.24.move_far_ref
  155.4 7.4 %shard_map.148 = (bf16[8,4,128,384]{3,2,1,0:T(8,128)(2,1)}, bf16[8,128,768]{2,1,0:T(8,128)(2,1)}) custom-call(s32[4]{0:T(128)S(1)} %pad_add_fusion.place_ref, bf16[4,256,384]{2,1,0:T(8,128)(2,1)S(1)} %all-to-all-done.rows_ref, bf16[8,400,256]{2,1,0:T(8,128)(2,1)} %bitcast.119, bf16[4,4,16,1152]{3,2,1,0:T(8,128)(2,1)S(1)} %pad_maximum_fusion.2.act_near_ref, ...), custom_call_target="tpu_custom_call" | custom-call | flops 1610612736 | bytes 9371648 | tf_op jit(solution)/shard_map/pallas_call | solution.py:75
  162.8 6.5 %all-to-all-start.4 = ((bf16[32,128,384]{2,1,0:T(8,128)(2,1)}), bf16[32,128,384]{2,1,0:T(8,128)(2,1)S(1)}, u32[]{:S(2)}, u32[]{:S(2)}) async-start(bf16[32,128,384]{2,1,0:T(8,128)(2,1)} %bitcast.123), calls=%async_computation.4 | async-start | bytes 6291456 | tf_op jit(solution)/shard_map/all_to_all | solution.py:453
  169.3 32.1 %reduce-scatter.2.cloned.1.call-done = bf16[1,128,768]{2,1,0:T(8,128)(2,1)} async-done(((bf16[8,128,768]{2,1,0:T(8,128)(2,1)}), bf16[1,128,768]{2,1,0:T(8,128)(2,1)}) %reduce-scatter.2.cloned.1.call-update) | async-done | bytes 196624 | tf_op jit(solution)/shard_map/reduce_scatter | solution.py:451
  201.4 1.9 collective-permute-start.25
  203.3 6.1 %collective-permute-done.25.grad_ref = bf16[128,768]{1,0:T(8,128)(2,1)S(1)} collective-permute-done((bf16[128,768]{1,0:T(8,128)(2,1)}, bf16[128,768]{1,0:T(8,128)(2,1)S(1)}, u32[]{:S(2)}, u32[]{:S(2)}) %collective-permute-start.25) | collective-permute-done | bytes 196640 | tf_op jit(solution)/shard_map/ppermute | solution.py:464
  209.4 1.9 collective-permute-start.26
  212.2 14.7 %all-to-all-start.5 = ((f32[256,1,128]{2,1,0:T(1,128)}), f32[256,1,128]{2,1,0:T(1,128)S(1)}, u32[]{:S(2)}, u32[]{:S(2)}) async-start(f32[256,1,128]{2,1,0:T(1,128)} %bitcast.45), calls=%async_computation.6 | async-start | bytes 262144 | tf_op jit(solution)/shard_map/all_to_all | solution.py:468
  226.9 3.0 %collective-permute-start.27 = (bf16[128,768]{1,0:T(8,128)(2,1)}, bf16[128,768]{1,0:T(8,128)(2,1)}, u32[]{:S(2)}, u32[]{:S(2)}) collective-permute-start(bf16[128,768]{1,0:T(8,128)(2,1)} %collective-permute-done.26), channel_id=1, source_target_pairs={{0,0},{1,1},{2,2},{3,3},{4,4},{5,5},{6,6},{7,7},{32,39},{33,32},{3... | collective-permute-start | bytes 589832 | tf_op jit(solution)/shard_map/ppermute | solution.py:470
  229.9 2.4 shard_map.149
  232.3 6.7 %all-to-all-done.5 = f32[256,1,128]{2,1,0:T(1,128)S(1)} async-done(((f32[256,1,128]{2,1,0:T(1,128)}), f32[256,1,128]{2,1,0:T(1,128)S(1)}, u32[]{:S(2)}, u32[]{:S(2)}) %all-to-all-start.5) | async-done | bytes 131104 | tf_op jit(solution)/shard_map/all_to_all | solution.py:468
  241.4 2.0 fusion.11
  (101 shorter events, 30.4 us)
Async XLA Ops:
  10.3 21.7 %all-to-all-start = ((bf16[4,256,384]{2,1,0:T(8,128)(2,1)}), bf16[4,256,384]{2,1,0:T(8,128)(2,1)S(1)}, u32[]{:S(2)}, u32[]{:S(2)}) async-start(bf16[4,256,384]{2,1,0:T(8,128)(2,1)} %maximum_maximum_fusion), calls=%async_computation | async-start | bytes 1572864 | tf_op jit(solution)/shard_map/all_to_all | solution.py:368
  14.7 70.6 %all-gather.3.cloned.1.call-start = ((), (), s32[]{:S(2)}) async-start(), calls=%async_computation.8 | async-start | bytes 1843200 | tf_op jit(solution)/shard_map/all_gather | solution.py:376
  14.9 11.6 %collective-permute-start.3 = (bf16[400,256]{1,0:T(8,128)(2,1)S(1)}, bf16[400,256]{1,0:T(8,128)(2,1)S(1)}, u32[]{:S(2)}, u32[]{:S(2)}) collective-permute-start(bf16[400,256]{1,0:T(8,128)(2,1)S(1)} %shard_map.144.own_ref), channel_id=1, source_target_pairs={{0,128},{64,192},{128,0},{192,64},{1,129},{65,193},{129,1},{193,65... | collective-permute-start | bytes 614408 | tf_op jit(solution)/shard_map/ppermute | solution.py:88
  17.1 14.7 %collective-permute-start.2 = (bf16[400,256]{1,0:T(8,128)(2,1)S(1)}, bf16[400,256]{1,0:T(8,128)(2,1)S(1)}, u32[]{:S(2)}, u32[]{:S(2)}) collective-permute-start(bf16[400,256]{1,0:T(8,128)(2,1)S(1)} %shard_map.144.own_ref), channel_id=1, source_target_pairs={{0,192},{64,0},{128,64},{192,128},{1,193},{65,1},{129,65},{193,129... | collective-permute-start | bytes 614408 | tf_op jit(solution)/shard_map/ppermute | solution.py:88
  18.6 13.3 %collective-permute-start.1 = (bf16[400,256]{1,0:T(8,128)(2,1)S(1)}, bf16[400,256]{1,0:T(8,128)(2,1)S(1)}, u32[]{:S(2)}, u32[]{:S(2)}) collective-permute-start(bf16[400,256]{1,0:T(8,128)(2,1)S(1)} %shard_map.144.own_ref), channel_id=1, source_target_pairs={{0,64},{64,128},{128,192},{192,0},{1,65},{65,129},{129,193},{193,1... | collective-permute-start | bytes 614408 | tf_op jit(solution)/shard_map/ppermute | solution.py:88
  19.2 12.8 %collective-permute-start = (bf16[400,256]{1,0:T(8,128)(2,1)S(1)}, bf16[400,256]{1,0:T(8,128)(2,1)S(1)}, u32[]{:S(2)}, u32[]{:S(2)}) collective-permute-start(bf16[400,256]{1,0:T(8,128)(2,1)S(1)} %shard_map.144.own_ref), channel_id=1, source_target_pairs={{0,0},{1,33},{2,66},{3,99},{4,132},{5,165},{6,198},{7,231},{32,4},... | collective-permute-start | bytes 614408 | tf_op jit(solution)/shard_map/ppermute | solution.py:372
  83.4 6.4 %collective-permute-start.6 = (bf16[32,16,256]{2,1,0:T(8,128)(2,1)S(1)}, bf16[32,16,256]{2,1,0:T(8,128)(2,1)S(1)}, u32[]{:S(2)}, u32[]{:S(2)}) collective-permute-start(bf16[32,16,256]{2,1,0:T(8,128)(2,1)S(1)} %all_to_all.38), channel_id=1, source_target_pairs={{0,192},{64,0},{128,64},{192,128},{1,193},{65,1},{129,65},{193,129... | collective-permute-start | bytes 786440 | tf_op jit(solution)/shard_map/ppermute | solution.py:88
  84.7 6.4 %collective-permute-start.5 = (bf16[32,16,256]{2,1,0:T(8,128)(2,1)S(1)}, bf16[32,16,256]{2,1,0:T(8,128)(2,1)S(1)}, u32[]{:S(2)}, u32[]{:S(2)}) collective-permute-start(bf16[32,16,256]{2,1,0:T(8,128)(2,1)S(1)} %all_to_all.38), channel_id=1, source_target_pairs={{0,64},{64,128},{128,192},{192,0},{1,65},{65,129},{129,193},{193,1... | collective-permute-start | bytes 786440 | tf_op jit(solution)/shard_map/ppermute | solution.py:88
  91.1 3.4 %collective-permute-start.7 = (bf16[4,4,16,3072]{3,2,1,0:T(8,128)(2,1)S(1)}, bf16[4,4,16,3072]{3,2,1,0:T(8,128)(2,1)S(1)}, u32[]{:S(2)}, u32[]{:S(2)}) collective-permute-start(bf16[4,4,16,3072]{3,2,1,0:T(8,128)(2,1)S(1)} %get-tuple-element.33), channel_id=1, source_target_pairs={{0,32},{32,0},{1,33},{33,1},{2,34},{34,2},{3,35},{35,3},{4,36},{36... | collective-permute-start | bytes 4718600 | tf_op jit(solution)/shard_map/ppermute | solution.py:404
  91.2 6.0 %collective-permute-start.9 = (bf16[16,16,256]{2,1,0:T(8,128)(2,1)S(1)}, bf16[16,16,256]{2,1,0:T(8,128)(2,1)S(1)}, u32[]{:S(2)}, u32[]{:S(2)}) collective-permute-start(bf16[16,16,256]{2,1,0:T(8,128)(2,1)S(1)} %slice.10), channel_id=1, source_target_pairs={{0,192},{64,0},{128,64},{192,128},{1,193},{65,1},{129,65},{193,129... | collective-permute-start | bytes 393224 | tf_op jit(solution)/shard_map/ppermute | solution.py:88
  92.4 5.6 %collective-permute-start.8 = (bf16[16,16,256]{2,1,0:T(8,128)(2,1)S(1)}, bf16[16,16,256]{2,1,0:T(8,128)(2,1)S(1)}, u32[]{:S(2)}, u32[]{:S(2)}) collective-permute-start(bf16[16,16,256]{2,1,0:T(8,128)(2,1)S(1)} %slice.9), channel_id=1, source_target_pairs={{0,64},{64,128},{128,192},{192,0},{1,65},{65,129},{129,193},{193,1... | collective-permute-start | bytes 393224 | tf_op jit(solution)/shard_map/ppermute | solution.py:88
  98.7 26.5 %all-to-all-start.3 = ((bf16[16,16,3072]{2,1,0:T(8,128)(2,1)}), bf16[16,16,3072]{2,1,0:T(8,128)(2,1)S(1)}, u32[]{:S(2)}, u32[]{:S(2)}) async-start(bf16[16,16,3072]{2,1,0:T(8,128)(2,1)} %bitcast.121), calls=%async_computation.3 | async-start | bytes 3145728 | tf_op jit(solution)/shard_map/all_to_all | solution.py:412
  104.4 97.0 %reduce-scatter.2.cloned.1.call-start = ((), (), s32[]{:S(2)}) async-start(), calls=%async_computation.7 | async-start | bytes 1769472 | tf_op jit(solution)/shard_map/reduce_scatter | solution.py:451
  105.7 3.1 %collective-permute-start.10 = (bf16[4,32,16,256]{3,2,1,0:T(8,128)(2,1)S(1)}, bf16[4,32,16,256]{3,2,1,0:T(8,128)(2,1)}, u32[]{:S(2)}, u32[]{:S(2)}) collective-permute-start(bf16[4,32,16,256]{3,2,1,0:T(8,128)(2,1)S(1)} %pad_maximum_fusion.near_ref), channel_id=1, source_target_pairs={{0,32},{32,0},{1,33},{33,1},{2,34},{34,2},{3,35},{35,3},{4,36},{36... | collective-permute-start | bytes 3145736 | tf_op jit(solution)/shard_map/ppermute | solution.py:411
  130.2 7.7 %collective-permute-start.13 = (bf16[16,1152]{1,0:T(8,128)(2,1)S(1)}, bf16[16,1152]{1,0:T(8,128)(2,1)S(1)}, u32[]{:S(2)}, u32[]{:S(2)}) collective-permute-start(bf16[16,1152]{1,0:T(8,128)(2,1)S(1)} %get-tuple-element.39), channel_id=1, source_target_pairs={{0,128},{64,192},{128,0},{192,64},{1,129},{65,193},{129,1},{193,65... | collective-permute-start | bytes 110600 | tf_op jit(solution)/shard_map/ppermute | solution.py:88
  132.7 5.3 %collective-permute-start.12 = (bf16[16,1152]{1,0:T(8,128)(2,1)S(1)}, bf16[16,1152]{1,0:T(8,128)(2,1)S(1)}, u32[]{:S(2)}, u32[]{:S(2)}) collective-permute-start(bf16[16,1152]{1,0:T(8,128)(2,1)S(1)} %get-tuple-element.39), channel_id=1, source_target_pairs={{0,192},{64,0},{128,64},{192,128},{1,193},{65,1},{129,65},{193,129... | collective-permute-start | bytes 110600 | tf_op jit(solution)/shard_map/ppermute | solution.py:88
  134.5 4.0 %collective-permute-start.11 = (bf16[16,1152]{1,0:T(8,128)(2,1)S(1)}, bf16[16,1152]{1,0:T(8,128)(2,1)S(1)}, u32[]{:S(2)}, u32[]{:S(2)}) collective-permute-start(bf16[16,1152]{1,0:T(8,128)(2,1)S(1)} %get-tuple-element.39), channel_id=1, source_target_pairs={{0,64},{64,128},{128,192},{192,0},{1,65},{65,129},{129,193},{193,1... | collective-permute-start | bytes 110600 | tf_op jit(solution)/shard_map/ppermute | solution.py:88
  134.7 6.6 %collective-permute-start.20 = (bf16[16,1024]{1,0:T(8,128)(2,1)S(1)}, bf16[16,1024]{1,0:T(8,128)(2,1)S(1)}, u32[]{:S(2)}, u32[]{:S(2)}) collective-permute-start(bf16[16,1024]{1,0:T(8,128)(2,1)S(1)} %get-tuple-element.40), channel_id=1, source_target_pairs={{0,16},{8,24},{16,0},{24,8},{1,17},{9,25},{17,1},{25,9},{2,18},{10... | collective-permute-start | bytes 98312 | tf_op jit(solution)/shard_map/ppermute | solution.py:88
  135.9 7.0 %collective-permute-start.19 = (bf16[16,1024]{1,0:T(8,128)(2,1)S(1)}, bf16[16,1024]{1,0:T(8,128)(2,1)S(1)}, u32[]{:S(2)}, u32[]{:S(2)}) collective-permute-start(bf16[16,1024]{1,0:T(8,128)(2,1)S(1)} %get-tuple-element.40), channel_id=1, source_target_pairs={{0,24},{8,0},{16,8},{24,16},{1,25},{9,1},{17,9},{25,17},{2,26},{10... | collective-permute-start | bytes 98312 | tf_op jit(solution)/shard_map/ppermute | solution.py:88
  138.0 6.0 %collective-permute-start.18 = (bf16[16,1024]{1,0:T(8,128)(2,1)S(1)}, bf16[16,1024]{1,0:T(8,128)(2,1)S(1)}, u32[]{:S(2)}, u32[]{:S(2)}) collective-permute-start(bf16[16,1024]{1,0:T(8,128)(2,1)S(1)} %get-tuple-element.40), channel_id=1, source_target_pairs={{0,8},{8,16},{16,24},{24,0},{1,9},{9,17},{17,25},{25,1},{2,10},{10... | collective-permute-start | bytes 98312 | tf_op jit(solution)/shard_map/ppermute | solution.py:88
  138.5 7.6 %collective-permute-start.15 = (bf16[4,16,1152]{2,1,0:T(8,128)(2,1)S(1)}, bf16[4,16,1152]{2,1,0:T(8,128)(2,1)S(1)}, u32[]{:S(2)}, u32[]{:S(2)}) collective-permute-start(bf16[4,16,1152]{2,1,0:T(8,128)(2,1)S(1)} %get-tuple-element.60), channel_id=1, source_target_pairs={{0,24},{8,0},{16,8},{24,16},{1,25},{9,1},{17,9},{25,17},{2,26},{10... | collective-permute-start | bytes 442376 | tf_op jit(solution)/shard_map/ppermute | solution.py:88
  141.3 8.8 %collective-permute-start.14 = (bf16[4,16,1152]{2,1,0:T(8,128)(2,1)S(1)}, bf16[4,16,1152]{2,1,0:T(8,128)(2,1)S(1)}, u32[]{:S(2)}, u32[]{:S(2)}) collective-permute-start(bf16[4,16,1152]{2,1,0:T(8,128)(2,1)S(1)} %get-tuple-element.60), channel_id=1, source_target_pairs={{0,8},{8,16},{16,24},{24,0},{1,9},{9,17},{17,25},{25,1},{2,10},{10... | collective-permute-start | bytes 442376 | tf_op jit(solution)/shard_map/ppermute | solution.py:88
  141.3 8.8 %collective-permute-start.16 = (bf16[4,16,1152]{2,1,0:T(8,128)(2,1)S(1)}, bf16[4,16,1152]{2,1,0:T(8,128)(2,1)S(1)}, u32[]{:S(2)}, u32[]{:S(2)}) collective-permute-start(bf16[4,16,1152]{2,1,0:T(8,128)(2,1)S(1)} %get-tuple-element.60), channel_id=1, source_target_pairs={{0,16},{8,24},{16,0},{24,8},{1,17},{9,25},{17,1},{25,9},{2,18},{10... | collective-permute-start | bytes 442376 | tf_op jit(solution)/shard_map/ppermute | solution.py:88
  144.0 6.4 %collective-permute-start.22 = (bf16[4,16,1024]{2,1,0:T(8,128)(2,1)S(1)}, bf16[4,16,1024]{2,1,0:T(8,128)(2,1)S(1)}, u32[]{:S(2)}, u32[]{:S(2)}) collective-permute-start(bf16[4,16,1024]{2,1,0:T(8,128)(2,1)S(1)} %get-tuple-element.62), channel_id=1, source_target_pairs={{0,192},{64,0},{128,64},{192,128},{1,193},{65,1},{129,65},{193,129... | collective-permute-start | bytes 393224 | tf_op jit(solution)/shard_map/ppermute | solution.py:88
  146.1 5.0 %collective-permute-start.21 = (bf16[4,16,1024]{2,1,0:T(8,128)(2,1)S(1)}, bf16[4,16,1024]{2,1,0:T(8,128)(2,1)S(1)}, u32[]{:S(2)}, u32[]{:S(2)}) collective-permute-start(bf16[4,16,1024]{2,1,0:T(8,128)(2,1)S(1)} %get-tuple-element.62), channel_id=1, source_target_pairs={{0,64},{64,128},{128,192},{192,0},{1,65},{65,129},{129,193},{193,1... | collective-permute-start | bytes 393224 | tf_op jit(solution)/shard_map/ppermute | solution.py:88
  146.1 7.0 %collective-permute-start.23 = (bf16[4,16,1024]{2,1,0:T(8,128)(2,1)S(1)}, bf16[4,16,1024]{2,1,0:T(8,128)(2,1)S(1)}, u32[]{:S(2)}, u32[]{:S(2)}) collective-permute-start(bf16[4,16,1024]{2,1,0:T(8,128)(2,1)S(1)} %get-tuple-element.62), channel_id=1, source_target_pairs={{0,128},{64,192},{128,0},{192,64},{1,129},{65,193},{129,1},{193,65... | collective-permute-start | bytes 393224 | tf_op jit(solution)/shard_map/ppermute | solution.py:88
  150.3 5.1 %collective-permute-start.17 = (bf16[4,4,16,1152]{3,2,1,0:T(8,128)(2,1)S(1)}, bf16[4,4,16,1152]{3,2,1,0:T(8,128)(2,1)S(1)}, u32[]{:S(2)}, u32[]{:S(2)}) collective-permute-start(bf16[4,4,16,1152]{3,2,1,0:T(8,128)(2,1)S(1)} %pad_maximum_fusion.2.act_near_ref), channel_id=1, source_target_pairs={{0,32},{32,0},{1,33},{33,1},{2,34},{34,2},{3,35},{35,3},{4,36},{36... | collective-permute-start | bytes 1769480 | tf_op jit(solution)/shard_map/ppermute | solution.py:431
  162.8 49.4 %all-to-all-start.4 = ((bf16[32,128,384]{2,1,0:T(8,128)(2,1)}), bf16[32,128,384]{2,1,0:T(8,128)(2,1)S(1)}, u32[]{:S(2)}, u32[]{:S(2)}) async-start(bf16[32,128,384]{2,1,0:T(8,128)(2,1)} %bitcast.123), calls=%async_computation.4 | async-start | bytes 6291456 | tf_op jit(solution)/shard_map/all_to_all | solution.py:453
  201.4 8.0 %collective-permute-start.25 = (bf16[128,768]{1,0:T(8,128)(2,1)}, bf16[128,768]{1,0:T(8,128)(2,1)S(1)}, u32[]{:S(2)}, u32[]{:S(2)}) collective-permute-start(bf16[128,768]{1,0:T(8,128)(2,1)} %bitcast.143), channel_id=1, source_target_pairs={{0,0},{33,1},{66,2},{99,3},{132,4},{165,5},{198,6},{231,7},{4,36},... | collective-permute-start | bytes 589832 | tf_op jit(solution)/shard_map/ppermute | solution.py:464
  209.4 17.5 %collective-permute-start.26 = (bf16[128,768]{1,0:T(8,128)(2,1)S(1)}, bf16[128,768]{1,0:T(8,128)(2,1)}, u32[]{:S(2)}, u32[]{:S(2)}) collective-permute-start(bf16[128,768]{1,0:T(8,128)(2,1)S(1)} %collective-permute-done.25.grad_ref), channel_id=1, source_target_pairs={{0,0},{1,1},{2,2},{3,3},{4,4},{5,5},{6,6},{7,7},{32,37},{33,38},{3... | collective-permute-start | bytes 589832 | tf_op jit(solution)/shard_map/ppermute | solution.py:470
  212.2 26.8 %all-to-all-start.5 = ((f32[256,1,128]{2,1,0:T(1,128)}), f32[256,1,128]{2,1,0:T(1,128)S(1)}, u32[]{:S(2)}, u32[]{:S(2)}) async-start(f32[256,1,128]{2,1,0:T(1,128)} %bitcast.45), calls=%async_computation.6 | async-start | bytes 262144 | tf_op jit(solution)/shard_map/all_to_all | solution.py:468
  226.9 13.4 %collective-permute-start.27 = (bf16[128,768]{1,0:T(8,128)(2,1)}, bf16[128,768]{1,0:T(8,128)(2,1)}, u32[]{:S(2)}, u32[]{:S(2)}) collective-permute-start(bf16[128,768]{1,0:T(8,128)(2,1)} %collective-permute-done.26), channel_id=1, source_target_pairs={{0,0},{1,1},{2,2},{3,3},{4,4},{5,5},{6,6},{7,7},{32,39},{33,32},{3... | collective-permute-start | bytes 589832 | tf_op jit(solution)/shard_map/ppermute | solution.py:470
  (18 other events, 109.0 us)
Sparse Core Ops, SparseCore 0:
  32.8 49.0 all-gather.2
  162.9 38.4 reduce-scatter.1

commit v10 on v9

--- a/solution.py
+++ b/solution.py
@@ -348,9 +348,9 @@
     grid = [(a, b) for a in range(layers) for b in range(count_z)]
     turned = {(a, b): (b + TURNS[a]) % count_z for a, b in grid}
     swap = [(a * count_z + b, b * count_z + turned[a, b]) for a, b in grid]
-    move = [(a * count_z + turned[a, b], b * count_z + turned[a, b]) for a, b in grid]
-    move_back = [(j, i) for i, j in move]
-    first_back = [(a * count_z + b, a * count_z + (b - FIRST[a]) % count_z) for a, b in grid]
+    most_back = [
+        (b * count_z + turned[a, b], a * count_z + (turned[a, b] - FIRST[a]) % count_z) for a, b in grid
+    ]
     last_back = [(a * count_z + b, a * count_z + (b - TURNS[a] + FIRST[a]) % count_z) for a, b in grid]
     across = SECTION + ("z",)
 
@@ -461,13 +461,12 @@
         compiler_params=pltpu.CompilerParams(vmem_limit_bytes=VMEM_BYTES),
     )(outputs)
 
-    grads = lax.ppermute(grads, across, move_back)
     squares = local_call(
         square_kernel, jax.ShapeDtypeStruct((sources * count_z, 128), WIDE), (grads,)
     )
     squares = lax.all_to_all(squares, EVERYONE, 0, 0, tiled=True)
     total_sq = jnp.sum(squares[:, 0])
-    own_grads = lax.ppermute(lax.ppermute(grads, across, first_back), across, last_back)
+    own_grads = lax.ppermute(lax.ppermute(grads, across, most_back), across, last_back)
     shard_in, shard_out = local_call(
         settle_kernel,
         (

time: 254 us -> 250 us (0.984)
  waiting for transfers between devices: 81.2 us -> 77.9 us
    ppermute x3 -> x2, waiting for transfers between devices: 6.1 us -> 0.01 us  [the longest x1 0.01 us: shards(): lax.ppermute(lax.ppermute(grads, across, most_back), across, last_back)]
    all_to_all x1, waiting for transfers between devices: 0.01 us -> 2.75 us  [shards(): outputs = lax.all_to_all(outputs, PLANE, 0, 0, tiled=True)]
    ppermute x3 -> x2, starting transfers between devices: 6.81 us -> 4.91 us  [the longest x1 3 us: shards(): lax.ppermute(lax.ppermute(grads, across, most_back), across, last_back)]
  transfers between devices with their start and end apart: 34 -> 33, of which waited for: 17 -> 17; matrix products, arithmetic and copies ran while one was open for 2% -> 2% of each run, Pallas kernels for 3% -> 3%
where the time goes in v10:
time: 250 us; the launch traced here: 247 us
  waiting for transfers between devices  77.9 us (31%)
  starting transfers between devices  71.3 us (29%)
  blocking collectives  47.2 us (19%)
  Pallas kernels  20.6 us (8%)
  between operations  15.1 us (6%)
  other arithmetic  9.2 us (4%)
  local copies, waits for them, and re-layouts  5.93 us (2%)
    all_to_all x2, blocking collectives, shards(): cross = lax.all_to_all(cross, ('y', 'z'), 0, 0, tiled=True)  47.2 us
    reduce_scatter x1, waiting for transfers between devices, shards(): grads = lax.psum_scatter(grads, 'z', scatter_dimension=0, tiled=True)[0]  32.1 us
    ppermute x19, starting transfers between devices, shifted(): lax.ppermute(block, axis, [(i, (i + distance) % size) for i in range(size)])  26.6 us
    pallas_call x7, Pallas kernels, local_call(): pl.pallas_call(kernel, out_shape=out_shape, in_specs=in_specs, out_specs=...  18.2 us
    all_to_all x1, waiting for transfers between devices, shards(): parts = lax.all_to_all(parts, ('x', 'y'), 0, 0, tiled=True)  16.5 us
    all_to_all x1, starting transfers between devices, shards(): squares = lax.all_to_all(squares, EVERYONE, 0, 0, tiled=True)  14.9 us
    ppermute x19, waiting for transfers between devices, shifted(): lax.ppermute(block, axis, [(i, (i + distance) % size) for i in range(size)])  12.9 us
    ppermute x1, starting transfers between devices, shards(): swapped = lax.ppermute(packed, across, swap)  7.39 us
  transfers between devices with their start and end apart: 33, of which 17 were waited for; matrix products, arithmetic and copies ran while one was open for 2% of the time, Pallas kernels for 3%

profile of v10, /device:TPU:2, one launch (start us, length us, event | category | flops | bytes accessed | tf_op | source)
XLA Modules:
  0.0 247.1 jit_solution(7704200524643403648)
XLA Ops:
  10.3 4.5 %all-to-all-start = ((bf16[4,256,384]{2,1,0:T(8,128)(2,1)}), bf16[4,256,384]{2,1,0:T(8,128)(2,1)S(1)}, u32[]{:S(2)}, u32[]{:S(2)}) async-start(bf16[4,256,384]{2,1,0:T(8,128)(2,1)} %maximum_maximum_fusion), calls=%async_computation | async-start | bytes 1572864 | tf_op jit(solution)/shard_map/all_to_all | solution.py:368
  14.9 2.2 collective-permute-start.3
  19.2 7.4 %collective-permute-start = (bf16[400,256]{1,0:T(8,128)(2,1)S(1)}, bf16[400,256]{1,0:T(8,128)(2,1)S(1)}, u32[]{:S(2)}, u32[]{:S(2)}) collective-permute-start(bf16[400,256]{1,0:T(8,128)(2,1)S(1)} %shard_map.144.own_ref), channel_id=1, source_target_pairs={{0,0},{1,33},{2,66},{3,99},{4,132},{5,165},{6,198},{7,231},{32,4},... | collective-permute-start | bytes 614408 | tf_op jit(solution)/shard_map/ppermute | solution.py:372
  26.6 5.3 %collective-permute-done.2 = bf16[400,256]{1,0:T(8,128)(2,1)S(1)} collective-permute-done((bf16[400,256]{1,0:T(8,128)(2,1)S(1)}, bf16[400,256]{1,0:T(8,128)(2,1)S(1)}, u32[]{:S(2)}, u32[]{:S(2)}) %collective-permute-start.2) | collective-permute-done | bytes 204832 | tf_op jit(solution)/shard_map/ppermute | solution.py:88
  32.8 2.2 collective-permute-done.4.far_ref
  36.1 27.5 %all_to_all.37 = bf16[32,16,256]{2,1,0:T(8,128)(2,1)S(1)} all-to-all(bf16[32,16,256]{2,1,0:T(8,128)(2,1)S(1)} %shard_map.146), channel_id=1, replica_groups=mesh['x'=4,'c'=2,'y'=4,'z'=8] {'y','z'}, dimensions={0} | all-to-all | bytes 524288 | tf_op jit(solution)/shard_map/all_to_all | solution.py:389
  63.7 19.6 %all_to_all.38 = bf16[32,16,256]{2,1,0:T(8,128)(2,1)S(1)} all-to-all(bf16[32,16,256]{2,1,0:T(8,128)(2,1)S(1)} %broadcast_in_dim.33), channel_id=1, replica_groups=mesh['x'=4,'c'=2,'y'=4,'z'=8] {'y','z'}, dimensions={0} | all-to-all | bytes 524288 | tf_op jit(solution)/shard_map/all_to_all | solution.py:392
  86.8 2.8 %shard_map.145 = (bf16[4,4,16,3072]{3,2,1,0:T(8,128)(2,1)S(1)}, bf16[4,4,16,3072]{3,2,1,0:T(8,128)(2,1)S(1)}) custom-call(s32[4]{0:T(128)S(1)} %pad_add_fusion.place_ref, bf16[4,256,384]{2,1,0:T(8,128)(2,1)S(1)} %all-to-all-done.rows_ref, bf16[8,400,256]{2,1,0:T(8,128)(2,1)S(1)} %bitcast.122), custom_call_target="tpu_custom_call" | custom-call | flops 1207959552 | bytes 5570560 | tf_op jit(solution)/shard_map/pallas_call | solution.py:75
  94.5 1.7 add_convert_fusion
  98.7 5.6 %all-to-all-start.3 = ((bf16[16,16,3072]{2,1,0:T(8,128)(2,1)}), bf16[16,16,3072]{2,1,0:T(8,128)(2,1)S(1)}, u32[]{:S(2)}, u32[]{:S(2)}) async-start(bf16[16,16,3072]{2,1,0:T(8,128)(2,1)} %bitcast.123), calls=%async_computation.3 | async-start | bytes 3145728 | tf_op jit(solution)/shard_map/all_to_all | solution.py:412
  107.2 1.6 collective-permute-done.10.far_ref
  108.8 16.5 %all-to-all-done.3.parts_ref = bf16[16,16,3072]{2,1,0:T(8,128)(2,1)S(1)} async-done(((bf16[16,16,3072]{2,1,0:T(8,128)(2,1)}), bf16[16,16,3072]{2,1,0:T(8,128)(2,1)S(1)}, u32[]{:S(2)}, u32[]{:S(2)}) %all-to-all-start.3) | async-done | bytes 1572896 | tf_op jit(solution)/shard_map/all_to_all | solution.py:412
  125.3 4.9 %shard_map.147 = (bf16[16,1152]{1,0:T(8,128)(2,1)S(1)}, bf16[16,1024]{1,0:T(8,128)(2,1)S(1)}) custom-call(s32[4]{0:T(128)S(1)} %pad_add_fusion.place_ref, bf16[16,16,3072]{2,1,0:T(8,128)(2,1)S(1)} %all-to-all-done.3.parts_ref, f32[16,128]{1,0:T(8,128)S(1)} %broadcast_in_dim.34.square_ref, bf16[4,32,16,256]{3,2,1,0:T(8,128)(2,1)S(1)} %pad_maximum_fusion.near_ref, ...), custom_call_target="tpu_custom_call" | custom-call | bytes 3747840 | tf_op jit(solution)/shard_map/pallas_call | solution.py:75
  130.2 2.5 collective-permute-start.13
  132.7 1.8 collective-permute-start.12
  135.9 2.1 collective-permute-start.19
  138.5 2.8 %collective-permute-start.15 = (bf16[4,16,1152]{2,1,0:T(8,128)(2,1)S(1)}, bf16[4,16,1152]{2,1,0:T(8,128)(2,1)S(1)}, u32[]{:S(2)}, u32[]{:S(2)}) collective-permute-start(bf16[4,16,1152]{2,1,0:T(8,128)(2,1)S(1)} %get-tuple-element.60), channel_id=1, source_target_pairs={{0,24},{8,0},{16,8},{24,16},{1,25},{9,1},{17,9},{25,17},{2,26},{10... | collective-permute-start | bytes 442376 | tf_op jit(solution)/shard_map/ppermute | solution.py:88
  141.3 1.6 collective-permute-start.16
  144.0 2.1 collective-permute-start.22
  146.1 4.0 %collective-permute-start.23 = (bf16[4,16,1024]{2,1,0:T(8,128)(2,1)S(1)}, bf16[4,16,1024]{2,1,0:T(8,128)(2,1)S(1)}, u32[]{:S(2)}, u32[]{:S(2)}) collective-permute-start(bf16[4,16,1024]{2,1,0:T(8,128)(2,1)S(1)} %get-tuple-element.62), channel_id=1, source_target_pairs={{0,128},{64,192},{128,0},{192,64},{1,129},{65,193},{129,1},{193,65... | collective-permute-start | bytes 393224 | tf_op jit(solution)/shard_map/ppermute | solution.py:88
  151.1 2.1 collective-permute-done.23
  153.5 1.9 collective-permute-done.24.move_far_ref
  155.4 7.4 %shard_map.148 = (bf16[8,4,128,384]{3,2,1,0:T(8,128)(2,1)}, bf16[8,128,768]{2,1,0:T(8,128)(2,1)}) custom-call(s32[4]{0:T(128)S(1)} %pad_add_fusion.place_ref, bf16[4,256,384]{2,1,0:T(8,128)(2,1)S(1)} %all-to-all-done.rows_ref, bf16[8,400,256]{2,1,0:T(8,128)(2,1)} %bitcast.121, bf16[4,4,16,1152]{3,2,1,0:T(8,128)(2,1)S(1)} %pad_maximum_fusion.2.act_near_ref, ...), custom_call_target="tpu_custom_call" | custom-call | flops 1610612736 | bytes 9371648 | tf_op jit(solution)/shard_map/pallas_call | solution.py:75
  162.8 6.5 %all-to-all-start.4 = ((bf16[32,128,384]{2,1,0:T(8,128)(2,1)}), bf16[32,128,384]{2,1,0:T(8,128)(2,1)S(1)}, u32[]{:S(2)}, u32[]{:S(2)}) async-start(bf16[32,128,384]{2,1,0:T(8,128)(2,1)} %bitcast.125), calls=%async_computation.4 | async-start | bytes 6291456 | tf_op jit(solution)/shard_map/all_to_all | solution.py:453
  169.3 32.1 %reduce-scatter.2.cloned.1.call-done = bf16[1,128,768]{2,1,0:T(8,128)(2,1)} async-done(((bf16[8,128,768]{2,1,0:T(8,128)(2,1)}), bf16[1,128,768]{2,1,0:T(8,128)(2,1)}) %reduce-scatter.2.cloned.1.call-update) | async-done | bytes 196624 | tf_op jit(solution)/shard_map/reduce_scatter | solution.py:451
  201.4 1.9 collective-permute-start.25
  205.1 2.7 %all-to-all-done.4 = bf16[32,128,384]{2,1,0:T(8,128)(2,1)S(1)} async-done(((bf16[32,128,384]{2,1,0:T(8,128)(2,1)}), bf16[32,128,384]{2,1,0:T(8,128)(2,1)S(1)}, u32[]{:S(2)}, u32[]{:S(2)}) %all-to-all-start.4) | async-done | bytes 3145760 | tf_op jit(solution)/shard_map/all_to_all | solution.py:453
  207.9 14.9 %all-to-all-start.5 = ((f32[256,1,128]{2,1,0:T(1,128)}), f32[256,1,128]{2,1,0:T(1,128)S(1)}, u32[]{:S(2)}, u32[]{:S(2)}) async-start(f32[256,1,128]{2,1,0:T(1,128)} %bitcast.45), calls=%async_computation.6 | async-start | bytes 262144 | tf_op jit(solution)/shard_map/all_to_all | solution.py:467
  222.8 3.0 %collective-permute-start.26 = (bf16[128,768]{1,0:T(8,128)(2,1)}, bf16[128,768]{1,0:T(8,128)(2,1)}, u32[]{:S(2)}, u32[]{:S(2)}) collective-permute-start(bf16[128,768]{1,0:T(8,128)(2,1)} %collective-permute-done.25), channel_id=1, source_target_pairs={{0,0},{1,1},{2,2},{3,3},{4,4},{5,5},{6,6},{7,7},{32,39},{33,32},{3... | collective-permute-start | bytes 589832 | tf_op jit(solution)/shard_map/ppermute | solution.py:469
  225.8 2.4 shard_map.149
  228.3 6.6 %all-to-all-done.5 = f32[256,1,128]{2,1,0:T(1,128)S(1)} async-done(((f32[256,1,128]{2,1,0:T(1,128)}), f32[256,1,128]{2,1,0:T(1,128)S(1)}, u32[]{:S(2)}, u32[]{:S(2)}) %all-to-all-start.5) | async-done | bytes 131104 | tf_op jit(solution)/shard_map/all_to_all | solution.py:467
  237.3 2.0 fusion.11
  (101 shorter events, 29.8 us)
Async XLA Ops:
  10.3 21.7 %all-to-all-start = ((bf16[4,256,384]{2,1,0:T(8,128)(2,1)}), bf16[4,256,384]{2,1,0:T(8,128)(2,1)S(1)}, u32[]{:S(2)}, u32[]{:S(2)}) async-start(bf16[4,256,384]{2,1,0:T(8,128)(2,1)} %maximum_maximum_fusion), calls=%async_computation | async-start | bytes 1572864 | tf_op jit(solution)/shard_map/all_to_all | solution.py:368
  14.7 70.6 %all-gather.3.cloned.1.call-start = ((), (), s32[]{:S(2)}) async-start(), calls=%async_computation.8 | async-start | bytes 1843200 | tf_op jit(solution)/shard_map/all_gather | solution.py:376
  14.9 11.6 %collective-permute-start.3 = (bf16[400,256]{1,0:T(8,128)(2,1)S(1)}, bf16[400,256]{1,0:T(8,128)(2,1)S(1)}, u32[]{:S(2)}, u32[]{:S(2)}) collective-permute-start(bf16[400,256]{1,0:T(8,128)(2,1)S(1)} %shard_map.144.own_ref), channel_id=1, source_target_pairs={{0,128},{64,192},{128,0},{192,64},{1,129},{65,193},{129,1},{193,65... | collective-permute-start | bytes 614408 | tf_op jit(solution)/shard_map/ppermute | solution.py:88
  17.1 14.7 %collective-permute-start.2 = (bf16[400,256]{1,0:T(8,128)(2,1)S(1)}, bf16[400,256]{1,0:T(8,128)(2,1)S(1)}, u32[]{:S(2)}, u32[]{:S(2)}) collective-permute-start(bf16[400,256]{1,0:T(8,128)(2,1)S(1)} %shard_map.144.own_ref), channel_id=1, source_target_pairs={{0,192},{64,0},{128,64},{192,128},{1,193},{65,1},{129,65},{193,129... | collective-permute-start | bytes 614408 | tf_op jit(solution)/shard_map/ppermute | solution.py:88
  18.6 13.3 %collective-permute-start.1 = (bf16[400,256]{1,0:T(8,128)(2,1)S(1)}, bf16[400,256]{1,0:T(8,128)(2,1)S(1)}, u32[]{:S(2)}, u32[]{:S(2)}) collective-permute-start(bf16[400,256]{1,0:T(8,128)(2,1)S(1)} %shard_map.144.own_ref), channel_id=1, source_target_pairs={{0,64},{64,128},{128,192},{192,0},{1,65},{65,129},{129,193},{193,1... | collective-permute-start | bytes 614408 | tf_op jit(solution)/shard_map/ppermute | solution.py:88
  19.2 12.8 %collective-permute-start = (bf16[400,256]{1,0:T(8,128)(2,1)S(1)}, bf16[400,256]{1,0:T(8,128)(2,1)S(1)}, u32[]{:S(2)}, u32[]{:S(2)}) collective-permute-start(bf16[400,256]{1,0:T(8,128)(2,1)S(1)} %shard_map.144.own_ref), channel_id=1, source_target_pairs={{0,0},{1,33},{2,66},{3,99},{4,132},{5,165},{6,198},{7,231},{32,4},... | collective-permute-start | bytes 614408 | tf_op jit(solution)/shard_map/ppermute | solution.py:372
  32.7 2.4 collective-permute-start.4
  83.4 6.4 %collective-permute-start.6 = (bf16[32,16,256]{2,1,0:T(8,128)(2,1)S(1)}, bf16[32,16,256]{2,1,0:T(8,128)(2,1)S(1)}, u32[]{:S(2)}, u32[]{:S(2)}) collective-permute-start(bf16[32,16,256]{2,1,0:T(8,128)(2,1)S(1)} %all_to_all.38), channel_id=1, source_target_pairs={{0,192},{64,0},{128,64},{192,128},{1,193},{65,1},{129,65},{193,129... | collective-permute-start | bytes 786440 | tf_op jit(solution)/shard_map/ppermute | solution.py:88
  84.7 6.4 %collective-permute-start.5 = (bf16[32,16,256]{2,1,0:T(8,128)(2,1)S(1)}, bf16[32,16,256]{2,1,0:T(8,128)(2,1)S(1)}, u32[]{:S(2)}, u32[]{:S(2)}) collective-permute-start(bf16[32,16,256]{2,1,0:T(8,128)(2,1)S(1)} %all_to_all.38), channel_id=1, source_target_pairs={{0,64},{64,128},{128,192},{192,0},{1,65},{65,129},{129,193},{193,1... | collective-permute-start | bytes 786440 | tf_op jit(solution)/shard_map/ppermute | solution.py:88
  91.1 3.4 %collective-permute-start.7 = (bf16[4,4,16,3072]{3,2,1,0:T(8,128)(2,1)S(1)}, bf16[4,4,16,3072]{3,2,1,0:T(8,128)(2,1)S(1)}, u32[]{:S(2)}, u32[]{:S(2)}) collective-permute-start(bf16[4,4,16,3072]{3,2,1,0:T(8,128)(2,1)S(1)} %get-tuple-element.33), channel_id=1, source_target_pairs={{0,32},{32,0},{1,33},{33,1},{2,34},{34,2},{3,35},{35,3},{4,36},{36... | collective-permute-start | bytes 4718600 | tf_op jit(solution)/shard_map/ppermute | solution.py:404
  91.2 6.0 %collective-permute-start.9 = (bf16[16,16,256]{2,1,0:T(8,128)(2,1)S(1)}, bf16[16,16,256]{2,1,0:T(8,128)(2,1)S(1)}, u32[]{:S(2)}, u32[]{:S(2)}) collective-permute-start(bf16[16,16,256]{2,1,0:T(8,128)(2,1)S(1)} %slice.10), channel_id=1, source_target_pairs={{0,192},{64,0},{128,64},{192,128},{1,193},{65,1},{129,65},{193,129... | collective-permute-start | bytes 393224 | tf_op jit(solution)/shard_map/ppermute | solution.py:88
  92.4 5.6 %collective-permute-start.8 = (bf16[16,16,256]{2,1,0:T(8,128)(2,1)S(1)}, bf16[16,16,256]{2,1,0:T(8,128)(2,1)S(1)}, u32[]{:S(2)}, u32[]{:S(2)}) collective-permute-start(bf16[16,16,256]{2,1,0:T(8,128)(2,1)S(1)} %slice.9), channel_id=1, source_target_pairs={{0,64},{64,128},{128,192},{192,0},{1,65},{65,129},{129,193},{193,1... | collective-permute-start | bytes 393224 | tf_op jit(solution)/shard_map/ppermute | solution.py:88
  98.7 26.5 %all-to-all-start.3 = ((bf16[16,16,3072]{2,1,0:T(8,128)(2,1)}), bf16[16,16,3072]{2,1,0:T(8,128)(2,1)S(1)}, u32[]{:S(2)}, u32[]{:S(2)}) async-start(bf16[16,16,3072]{2,1,0:T(8,128)(2,1)} %bitcast.123), calls=%async_computation.3 | async-start | bytes 3145728 | tf_op jit(solution)/shard_map/all_to_all | solution.py:412
  104.4 97.0 %reduce-scatter.2.cloned.1.call-start = ((), (), s32[]{:S(2)}) async-start(), calls=%async_computation.7 | async-start | bytes 1769472 | tf_op jit(solution)/shard_map/reduce_scatter | solution.py:451
  105.7 3.1 %collective-permute-start.10 = (bf16[4,32,16,256]{3,2,1,0:T(8,128)(2,1)S(1)}, bf16[4,32,16,256]{3,2,1,0:T(8,128)(2,1)}, u32[]{:S(2)}, u32[]{:S(2)}) collective-permute-start(bf16[4,32,16,256]{3,2,1,0:T(8,128)(2,1)S(1)} %pad_maximum_fusion.near_ref), channel_id=1, source_target_pairs={{0,32},{32,0},{1,33},{33,1},{2,34},{34,2},{3,35},{35,3},{4,36},{36... | collective-permute-start | bytes 3145736 | tf_op jit(solution)/shard_map/ppermute | solution.py:411
  130.2 7.7 %collective-permute-start.13 = (bf16[16,1152]{1,0:T(8,128)(2,1)S(1)}, bf16[16,1152]{1,0:T(8,128)(2,1)S(1)}, u32[]{:S(2)}, u32[]{:S(2)}) collective-permute-start(bf16[16,1152]{1,0:T(8,128)(2,1)S(1)} %get-tuple-element.39), channel_id=1, source_target_pairs={{0,128},{64,192},{128,0},{192,64},{1,129},{65,193},{129,1},{193,65... | collective-permute-start | bytes 110600 | tf_op jit(solution)/shard_map/ppermute | solution.py:88
  132.7 5.3 %collective-permute-start.12 = (bf16[16,1152]{1,0:T(8,128)(2,1)S(1)}, bf16[16,1152]{1,0:T(8,128)(2,1)S(1)}, u32[]{:S(2)}, u32[]{:S(2)}) collective-permute-start(bf16[16,1152]{1,0:T(8,128)(2,1)S(1)} %get-tuple-element.39), channel_id=1, source_target_pairs={{0,192},{64,0},{128,64},{192,128},{1,193},{65,1},{129,65},{193,129... | collective-permute-start | bytes 110600 | tf_op jit(solution)/shard_map/ppermute | solution.py:88
  134.5 4.0 %collective-permute-start.11 = (bf16[16,1152]{1,0:T(8,128)(2,1)S(1)}, bf16[16,1152]{1,0:T(8,128)(2,1)S(1)}, u32[]{:S(2)}, u32[]{:S(2)}) collective-permute-start(bf16[16,1152]{1,0:T(8,128)(2,1)S(1)} %get-tuple-element.39), channel_id=1, source_target_pairs={{0,64},{64,128},{128,192},{192,0},{1,65},{65,129},{129,193},{193,1... | collective-permute-start | bytes 110600 | tf_op jit(solution)/shard_map/ppermute | solution.py:88
  134.7 6.6 %collective-permute-start.20 = (bf16[16,1024]{1,0:T(8,128)(2,1)S(1)}, bf16[16,1024]{1,0:T(8,128)(2,1)S(1)}, u32[]{:S(2)}, u32[]{:S(2)}) collective-permute-start(bf16[16,1024]{1,0:T(8,128)(2,1)S(1)} %get-tuple-element.40), channel_id=1, source_target_pairs={{0,16},{8,24},{16,0},{24,8},{1,17},{9,25},{17,1},{25,9},{2,18},{10... | collective-permute-start | bytes 98312 | tf_op jit(solution)/shard_map/ppermute | solution.py:88
  135.9 7.0 %collective-permute-start.19 = (bf16[16,1024]{1,0:T(8,128)(2,1)S(1)}, bf16[16,1024]{1,0:T(8,128)(2,1)S(1)}, u32[]{:S(2)}, u32[]{:S(2)}) collective-permute-start(bf16[16,1024]{1,0:T(8,128)(2,1)S(1)} %get-tuple-element.40), channel_id=1, source_target_pairs={{0,24},{8,0},{16,8},{24,16},{1,25},{9,1},{17,9},{25,17},{2,26},{10... | collective-permute-start | bytes 98312 | tf_op jit(solution)/shard_map/ppermute | solution.py:88
  138.0 6.0 %collective-permute-start.18 = (bf16[16,1024]{1,0:T(8,128)(2,1)S(1)}, bf16[16,1024]{1,0:T(8,128)(2,1)S(1)}, u32[]{:S(2)}, u32[]{:S(2)}) collective-permute-start(bf16[16,1024]{1,0:T(8,128)(2,1)S(1)} %get-tuple-element.40), channel_id=1, source_target_pairs={{0,8},{8,16},{16,24},{24,0},{1,9},{9,17},{17,25},{25,1},{2,10},{10... | collective-permute-start | bytes 98312 | tf_op jit(solution)/shard_map/ppermute | solution.py:88
  138.5 7.6 %collective-permute-start.15 = (bf16[4,16,1152]{2,1,0:T(8,128)(2,1)S(1)}, bf16[4,16,1152]{2,1,0:T(8,128)(2,1)S(1)}, u32[]{:S(2)}, u32[]{:S(2)}) collective-permute-start(bf16[4,16,1152]{2,1,0:T(8,128)(2,1)S(1)} %get-tuple-element.60), channel_id=1, source_target_pairs={{0,24},{8,0},{16,8},{24,16},{1,25},{9,1},{17,9},{25,17},{2,26},{10... | collective-permute-start | bytes 442376 | tf_op jit(solution)/shard_map/ppermute | solution.py:88
  141.3 8.8 %collective-permute-start.14 = (bf16[4,16,1152]{2,1,0:T(8,128)(2,1)S(1)}, bf16[4,16,1152]{2,1,0:T(8,128)(2,1)S(1)}, u32[]{:S(2)}, u32[]{:S(2)}) collective-permute-start(bf16[4,16,1152]{2,1,0:T(8,128)(2,1)S(1)} %get-tuple-element.60), channel_id=1, source_target_pairs={{0,8},{8,16},{16,24},{24,0},{1,9},{9,17},{17,25},{25,1},{2,10},{10... | collective-permute-start | bytes 442376 | tf_op jit(solution)/shard_map/ppermute | solution.py:88
  141.3 8.8 %collective-permute-start.16 = (bf16[4,16,1152]{2,1,0:T(8,128)(2,1)S(1)}, bf16[4,16,1152]{2,1,0:T(8,128)(2,1)S(1)}, u32[]{:S(2)}, u32[]{:S(2)}) collective-permute-start(bf16[4,16,1152]{2,1,0:T(8,128)(2,1)S(1)} %get-tuple-element.60), channel_id=1, source_target_pairs={{0,16},{8,24},{16,0},{24,8},{1,17},{9,25},{17,1},{25,9},{2,18},{10... | collective-permute-start | bytes 442376 | tf_op jit(solution)/shard_map/ppermute | solution.py:88
  144.0 6.4 %collective-permute-start.22 = (bf16[4,16,1024]{2,1,0:T(8,128)(2,1)S(1)}, bf16[4,16,1024]{2,1,0:T(8,128)(2,1)S(1)}, u32[]{:S(2)}, u32[]{:S(2)}) collective-permute-start(bf16[4,16,1024]{2,1,0:T(8,128)(2,1)S(1)} %get-tuple-element.62), channel_id=1, source_target_pairs={{0,192},{64,0},{128,64},{192,128},{1,193},{65,1},{129,65},{193,129... | collective-permute-start | bytes 393224 | tf_op jit(solution)/shard_map/ppermute | solution.py:88
  146.1 5.0 %collective-permute-start.21 = (bf16[4,16,1024]{2,1,0:T(8,128)(2,1)S(1)}, bf16[4,16,1024]{2,1,0:T(8,128)(2,1)S(1)}, u32[]{:S(2)}, u32[]{:S(2)}) collective-permute-start(bf16[4,16,1024]{2,1,0:T(8,128)(2,1)S(1)} %get-tuple-element.62), channel_id=1, source_target_pairs={{0,64},{64,128},{128,192},{192,0},{1,65},{65,129},{129,193},{193,1... | collective-permute-start | bytes 393224 | tf_op jit(solution)/shard_map/ppermute | solution.py:88
  146.1 7.0 %collective-permute-start.23 = (bf16[4,16,1024]{2,1,0:T(8,128)(2,1)S(1)}, bf16[4,16,1024]{2,1,0:T(8,128)(2,1)S(1)}, u32[]{:S(2)}, u32[]{:S(2)}) collective-permute-start(bf16[4,16,1024]{2,1,0:T(8,128)(2,1)S(1)} %get-tuple-element.62), channel_id=1, source_target_pairs={{0,128},{64,192},{128,0},{192,64},{1,129},{65,193},{129,1},{193,65... | collective-permute-start | bytes 393224 | tf_op jit(solution)/shard_map/ppermute | solution.py:88
  150.3 5.1 %collective-permute-start.17 = (bf16[4,4,16,1152]{3,2,1,0:T(8,128)(2,1)S(1)}, bf16[4,4,16,1152]{3,2,1,0:T(8,128)(2,1)S(1)}, u32[]{:S(2)}, u32[]{:S(2)}) collective-permute-start(bf16[4,4,16,1152]{3,2,1,0:T(8,128)(2,1)S(1)} %pad_maximum_fusion.2.act_near_ref), channel_id=1, source_target_pairs={{0,32},{32,0},{1,33},{33,1},{2,34},{34,2},{3,35},{35,3},{4,36},{36... | collective-permute-start | bytes 1769480 | tf_op jit(solution)/shard_map/ppermute | solution.py:431
  162.8 45.1 %all-to-all-start.4 = ((bf16[32,128,384]{2,1,0:T(8,128)(2,1)}), bf16[32,128,384]{2,1,0:T(8,128)(2,1)S(1)}, u32[]{:S(2)}, u32[]{:S(2)}) async-start(bf16[32,128,384]{2,1,0:T(8,128)(2,1)} %bitcast.125), calls=%async_computation.4 | async-start | bytes 6291456 | tf_op jit(solution)/shard_map/all_to_all | solution.py:453
  201.4 21.4 %collective-permute-start.25 = (bf16[128,768]{1,0:T(8,128)(2,1)}, bf16[128,768]{1,0:T(8,128)(2,1)}, u32[]{:S(2)}, u32[]{:S(2)}) collective-permute-start(bf16[128,768]{1,0:T(8,128)(2,1)} %bitcast.117), channel_id=1, source_target_pairs={{0,0},{33,1},{66,2},{99,3},{132,4},{165,5},{198,6},{231,7},{4,33},... | collective-permute-start | bytes 589832 | tf_op jit(solution)/shard_map/ppermute | solution.py:469
  207.9 27.0 %all-to-all-start.5 = ((f32[256,1,128]{2,1,0:T(1,128)}), f32[256,1,128]{2,1,0:T(1,128)S(1)}, u32[]{:S(2)}, u32[]{:S(2)}) async-start(f32[256,1,128]{2,1,0:T(1,128)} %bitcast.45), calls=%async_computation.6 | async-start | bytes 262144 | tf_op jit(solution)/shard_map/all_to_all | solution.py:467
  222.8 13.4 %collective-permute-start.26 = (bf16[128,768]{1,0:T(8,128)(2,1)}, bf16[128,768]{1,0:T(8,128)(2,1)}, u32[]{:S(2)}, u32[]{:S(2)}) collective-permute-start(bf16[128,768]{1,0:T(8,128)(2,1)} %collective-permute-done.25), channel_id=1, source_target_pairs={{0,0},{1,1},{2,2},{3,3},{4,4},{5,5},{6,6},{7,7},{32,39},{33,32},{3... | collective-permute-start | bytes 589832 | tf_op jit(solution)/shard_map/ppermute | solution.py:469
  (18 other events, 107.5 us)
Sparse Core Ops, SparseCore 0:
  32.8 49.0 all-gather.2
  162.9 38.4 reduce-scatter.1

commit v11 on v10

--- a/solution.py
+++ b/solution.py
@@ -26,7 +26,6 @@
 EVERYONE = ("x", "c", "y", "z")
 SHIFTS = (0, 1, -1, 2)
 TURNS = (0, 4, 3, 7, 2, 6, 1, 5)
-FIRST = (0, 3, 3, -1, 2, -2, 1, -3)
 EXTRA = 16
 VMEM_BYTES = 48 * 1024 * 1024
 
@@ -348,10 +347,7 @@
     grid = [(a, b) for a in range(layers) for b in range(count_z)]
     turned = {(a, b): (b + TURNS[a]) % count_z for a, b in grid}
     swap = [(a * count_z + b, b * count_z + turned[a, b]) for a, b in grid]
-    most_back = [
-        (b * count_z + turned[a, b], a * count_z + (turned[a, b] - FIRST[a]) % count_z) for a, b in grid
-    ]
-    last_back = [(a * count_z + b, a * count_z + (b - TURNS[a] + FIRST[a]) % count_z) for a, b in grid]
+    home = [(j, i) for i, j in swap]
     across = SECTION + ("z",)
 
     gain_own = lax.dynamic_slice_in_dim(norm_gain, (pos_y * count_z + pos_z) * features, features, 1)
@@ -462,11 +458,13 @@
     )(outputs)
 
     squares = local_call(
-        square_kernel, jax.ShapeDtypeStruct((sources * count_z, 128), WIDE), (grads,)
-    )
-    squares = lax.all_to_all(squares, EVERYONE, 0, 0, tiled=True)
+        square_kernel, jax.ShapeDtypeStruct((sources, 128), WIDE), (grads,)
+    )
+    for distance in (4, 2, 1):
+        squares = squares + shifted(squares, "z", distance)
+    squares = lax.all_to_all(squares, PLANE, 0, 0, tiled=True)
     total_sq = jnp.sum(squares[:, 0])
-    own_grads = lax.ppermute(lax.ppermute(grads, across, most_back), across, last_back)
+    own_grads = lax.ppermute(grads, across, home)
     shard_in, shard_out = local_call(
         settle_kernel,
         (

time: 250 us -> 254 us (1.016)
  waiting for transfers between devices: 77.9 us -> 86.1 us
  starting transfers between devices: 71.3 us -> 67.8 us
    ppermute x19 -> x22, waiting for transfers between devices: 12.9 us -> 26.9 us  [shifted(): lax.ppermute(block, axis, [(i, (i + distance) % size) for i in range(size)])]
    all_to_all x1, starting transfers between devices: 14.9 us -> 7.37 us  [shards(): squares = lax.all_to_all(squares, PLANE, 0, 0, tiled=True)]
    ppermute x19 -> x22, starting transfers between devices: 26.6 us -> 33.7 us  [shifted(): lax.ppermute(block, axis, [(i, (i + distance) % size) for i in range(size)])]
    all_to_all x1, waiting for transfers between devices: 6.65 us -> 3.64 us  [shards(): squares = lax.all_to_all(squares, PLANE, 0, 0, tiled=True)]
    ppermute x2 -> x1, starting transfers between devices: 4.91 us -> 1.91 us  [shards(): own_grads = lax.ppermute(grads, across, home)]
    all_to_all x1, waiting for transfers between devices: 2.75 us -> 0.01 us  [shards(): outputs = lax.all_to_all(outputs, PLANE, 0, 0, tiled=True)]
  transfers between devices with their start and end apart: 33 -> 35, of which waited for: 17 -> 19; matrix products, arithmetic and copies ran while one was open for 2% -> 2% of each run, Pallas kernels for 3% -> 3%
where the time goes in v11:
time: 254 us; the launch traced here: 252 us
  waiting for transfers between devices  86.1 us (34%)
  starting transfers between devices  67.8 us (27%)
  blocking collectives  47.1 us (19%)
  Pallas kernels  20 us (8%)
  between operations  15.1 us (6%)
  other arithmetic  9.78 us (4%)
  local copies, waits for them, and re-layouts  5.92 us (2%)
    all_to_all x2, blocking collectives, shards(): cross = lax.all_to_all(cross, ('y', 'z'), 0, 0, tiled=True)  47.1 us
    ppermute x22, starting transfers between devices, shifted(): lax.ppermute(block, axis, [(i, (i + distance) % size) for i in range(size)])  33.7 us
    reduce_scatter x1, waiting for transfers between devices, shards(): grads = lax.psum_scatter(grads, 'z', scatter_dimension=0, tiled=True)[0]  32.1 us
    ppermute x22, waiting for transfers between devices, shifted(): lax.ppermute(block, axis, [(i, (i + distance) % size) for i in range(size)])  26.9 us
    pallas_call x7, Pallas kernels, local_call(): pl.pallas_call(kernel, out_shape=out_shape, in_specs=in_specs, out_specs=...  17.5 us
    all_to_all x1, waiting for transfers between devices, shards(): parts = lax.all_to_all(parts, ('x', 'y'), 0, 0, tiled=True)  16.4 us
    ppermute x1, starting transfers between devices, shards(): swapped = lax.ppermute(packed, across, swap)  7.39 us
    all_to_all x1, starting transfers between devices, shards(): squares = lax.all_to_all(squares, PLANE, 0, 0, tiled=True)  7.37 us
  transfers between devices with their start and end apart: 35, of which 19 were waited for; matrix products, arithmetic and copies ran while one was open for 2% of the time, Pallas kernels for 3%

profile of v11, /device:TPU:2, one launch (start us, length us, event | category | flops | bytes accessed | tf_op | source)
XLA Modules:
  0.0 251.8 jit_solution(9702481045902199545)
XLA Ops:
  10.3 4.5 %all-to-all-start = ((bf16[4,256,384]{2,1,0:T(8,128)(2,1)}), bf16[4,256,384]{2,1,0:T(8,128)(2,1)S(1)}, u32[]{:S(2)}, u32[]{:S(2)}) async-start(bf16[4,256,384]{2,1,0:T(8,128)(2,1)} %maximum_maximum_fusion), calls=%async_computation | async-start | bytes 1572864 | tf_op jit(solution)/shard_map/all_to_all | solution.py:364
  14.9 2.2 collective-permute-start.3
  19.2 7.4 %collective-permute-start = (bf16[400,256]{1,0:T(8,128)(2,1)S(1)}, bf16[400,256]{1,0:T(8,128)(2,1)S(1)}, u32[]{:S(2)}, u32[]{:S(2)}) collective-permute-start(bf16[400,256]{1,0:T(8,128)(2,1)S(1)} %shard_map.144.own_ref), channel_id=1, source_target_pairs={{0,0},{1,33},{2,66},{3,99},{4,132},{5,165},{6,198},{7,231},{32,4},... | collective-permute-start | bytes 614408 | tf_op jit(solution)/shard_map/ppermute | solution.py:368
  26.6 5.3 %collective-permute-done.2 = bf16[400,256]{1,0:T(8,128)(2,1)S(1)} collective-permute-done((bf16[400,256]{1,0:T(8,128)(2,1)S(1)}, bf16[400,256]{1,0:T(8,128)(2,1)S(1)}, u32[]{:S(2)}, u32[]{:S(2)}) %collective-permute-start.2) | collective-permute-done | bytes 204832 | tf_op jit(solution)/shard_map/ppermute | solution.py:87
  32.8 2.2 collective-permute-done.4.far_ref
  36.1 27.5 %all_to_all.37 = bf16[32,16,256]{2,1,0:T(8,128)(2,1)S(1)} all-to-all(bf16[32,16,256]{2,1,0:T(8,128)(2,1)S(1)} %shard_map.146), channel_id=1, replica_groups=mesh['x'=4,'c'=2,'y'=4,'z'=8] {'y','z'}, dimensions={0} | all-to-all | bytes 524288 | tf_op jit(solution)/shard_map/all_to_all | solution.py:385
  63.7 19.6 %all_to_all.38 = bf16[32,16,256]{2,1,0:T(8,128)(2,1)S(1)} all-to-all(bf16[32,16,256]{2,1,0:T(8,128)(2,1)S(1)} %broadcast_in_dim.33), channel_id=1, replica_groups=mesh['x'=4,'c'=2,'y'=4,'z'=8] {'y','z'}, dimensions={0} | all-to-all | bytes 524288 | tf_op jit(solution)/shard_map/all_to_all | solution.py:388
  86.7 2.8 %shard_map.145 = (bf16[4,4,16,3072]{3,2,1,0:T(8,128)(2,1)S(1)}, bf16[4,4,16,3072]{3,2,1,0:T(8,128)(2,1)S(1)}) custom-call(s32[4]{0:T(128)S(1)} %pad_add_fusion.place_ref, bf16[4,256,384]{2,1,0:T(8,128)(2,1)S(1)} %all-to-all-done.rows_ref, bf16[8,400,256]{2,1,0:T(8,128)(2,1)S(1)} %bitcast.122), custom_call_target="tpu_custom_call" | custom-call | flops 1207959552 | bytes 5570560 | tf_op jit(solution)/shard_map/pallas_call | solution.py:74
  94.5 1.7 add_convert_fusion
  98.7 5.7 %all-to-all-start.3 = ((bf16[16,16,3072]{2,1,0:T(8,128)(2,1)}), bf16[16,16,3072]{2,1,0:T(8,128)(2,1)S(1)}, u32[]{:S(2)}, u32[]{:S(2)}) async-start(bf16[16,16,3072]{2,1,0:T(8,128)(2,1)} %bitcast.123), calls=%async_computation.3 | async-start | bytes 3145728 | tf_op jit(solution)/shard_map/all_to_all | solution.py:408
  108.8 16.4 %all-to-all-done.3.parts_ref = bf16[16,16,3072]{2,1,0:T(8,128)(2,1)S(1)} async-done(((bf16[16,16,3072]{2,1,0:T(8,128)(2,1)}), bf16[16,16,3072]{2,1,0:T(8,128)(2,1)S(1)}, u32[]{:S(2)}, u32[]{:S(2)}) %all-to-all-start.3) | async-done | bytes 1572896 | tf_op jit(solution)/shard_map/all_to_all | solution.py:408
  125.3 4.9 %shard_map.147 = (bf16[16,1152]{1,0:T(8,128)(2,1)S(1)}, bf16[16,1024]{1,0:T(8,128)(2,1)S(1)}) custom-call(s32[4]{0:T(128)S(1)} %pad_add_fusion.place_ref, bf16[16,16,3072]{2,1,0:T(8,128)(2,1)S(1)} %all-to-all-done.3.parts_ref, f32[16,128]{1,0:T(8,128)S(1)} %broadcast_in_dim.34.square_ref, bf16[4,32,16,256]{3,2,1,0:T(8,128)(2,1)S(1)} %pad_maximum_fusion.near_ref, ...), custom_call_target="tpu_custom_call" | custom-call | bytes 3747840 | tf_op jit(solution)/shard_map/pallas_call | solution.py:74
  130.2 2.5 collective-permute-start.13
  132.7 1.8 collective-permute-start.12
  135.8 2.1 collective-permute-start.19
  138.5 2.8 %collective-permute-start.15 = (bf16[4,16,1152]{2,1,0:T(8,128)(2,1)S(1)}, bf16[4,16,1152]{2,1,0:T(8,128)(2,1)S(1)}, u32[]{:S(2)}, u32[]{:S(2)}) collective-permute-start(bf16[4,16,1152]{2,1,0:T(8,128)(2,1)S(1)} %get-tuple-element.60), channel_id=1, source_target_pairs={{0,24},{8,0},{16,8},{24,16},{1,25},{9,1},{17,9},{25,17},{2,26},{10... | collective-permute-start | bytes 442376 | tf_op jit(solution)/shard_map/ppermute | solution.py:87
  144.0 2.1 collective-permute-start.22
  146.1 4.0 %collective-permute-start.23 = (bf16[4,16,1024]{2,1,0:T(8,128)(2,1)S(1)}, bf16[4,16,1024]{2,1,0:T(8,128)(2,1)S(1)}, u32[]{:S(2)}, u32[]{:S(2)}) collective-permute-start(bf16[4,16,1024]{2,1,0:T(8,128)(2,1)S(1)} %get-tuple-element.62), channel_id=1, source_target_pairs={{0,128},{64,192},{128,0},{192,64},{1,129},{65,193},{129,1},{193,65... | collective-permute-start | bytes 393224 | tf_op jit(solution)/shard_map/ppermute | solution.py:87
  151.0 2.0 collective-permute-done.23
  153.5 1.9 collective-permute-done.24.move_far_ref
  155.4 7.4 %shard_map.148 = (bf16[8,4,128,384]{3,2,1,0:T(8,128)(2,1)}, bf16[8,128,768]{2,1,0:T(8,128)(2,1)}) custom-call(s32[4]{0:T(128)S(1)} %pad_add_fusion.place_ref, bf16[4,256,384]{2,1,0:T(8,128)(2,1)S(1)} %all-to-all-done.rows_ref, bf16[8,400,256]{2,1,0:T(8,128)(2,1)} %bitcast.121, bf16[4,4,16,1152]{3,2,1,0:T(8,128)(2,1)S(1)} %pad_maximum_fusion.2.act_near_ref, ...), custom_call_target="tpu_custom_call" | custom-call | flops 1610612736 | bytes 9371648 | tf_op jit(solution)/shard_map/pallas_call | solution.py:74
  162.8 6.5 %all-to-all-start.4 = ((bf16[32,128,384]{2,1,0:T(8,128)(2,1)}), bf16[32,128,384]{2,1,0:T(8,128)(2,1)S(1)}, u32[]{:S(2)}, u32[]{:S(2)}) async-start(bf16[32,128,384]{2,1,0:T(8,128)(2,1)} %bitcast.124), calls=%async_computation.4 | async-start | bytes 6291456 | tf_op jit(solution)/shard_map/all_to_all | solution.py:449
  169.3 32.1 %reduce-scatter.2.cloned.1.call-done = bf16[1,128,768]{2,1,0:T(8,128)(2,1)} async-done(((bf16[8,128,768]{2,1,0:T(8,128)(2,1)}), bf16[1,128,768]{2,1,0:T(8,128)(2,1)}) %reduce-scatter.2.cloned.1.call-update) | async-done | bytes 196624 | tf_op jit(solution)/shard_map/reduce_scatter | solution.py:447
  201.4 1.9 collective-permute-start.28
  204.5 5.2 %collective-permute-start.25 = (f32[32,128]{1,0:T(8,128)S(1)}, f32[32,128]{1,0:T(8,128)S(1)}, u32[]{:S(2)}, u32[]{:S(2)}) collective-permute-start(f32[32,128]{1,0:T(8,128)S(1)} %shard_map.150), channel_id=1, source_target_pairs={{0,4},{1,5},{2,6},{3,7},{4,0},{5,1},{6,2},{7,3},{8,12},{9,13},{10,... | collective-permute-start | bytes 49160 | tf_op jit(solution)/shard_map/ppermute | solution.py:87
  209.7 4.9 %collective-permute-done.25 = f32[32,128]{1,0:T(8,128)S(1)} collective-permute-done((f32[32,128]{1,0:T(8,128)S(1)}, f32[32,128]{1,0:T(8,128)S(1)}, u32[]{:S(2)}, u32[]{:S(2)}) %collective-permute-start.25) | collective-permute-done | bytes 16416 | tf_op jit(solution)/shard_map/ppermute | solution.py:87
  215.0 5.6 %collective-permute-done.26 = f32[32,128]{1,0:T(8,128)S(1)} collective-permute-done((f32[32,128]{1,0:T(8,128)S(1)}, f32[32,128]{1,0:T(8,128)S(1)}, u32[]{:S(2)}, u32[]{:S(2)}) %collective-permute-start.26) | collective-permute-done | bytes 16416 | tf_op jit(solution)/shard_map/ppermute | solution.py:87
  222.1 3.4 %collective-permute-done.27 = f32[32,128]{1,0:T(8,128)S(1)} collective-permute-done((f32[32,128]{1,0:T(8,128)S(1)}, f32[32,128]{1,0:T(8,128)S(1)}, u32[]{:S(2)}, u32[]{:S(2)}) %collective-permute-start.27) | collective-permute-done | bytes 16416 | tf_op jit(solution)/shard_map/ppermute | solution.py:87
  226.2 7.4 %all-to-all-start.5 = ((f32[32,1,128]{2,1,0:T(1,128)}), f32[32,1,128]{2,1,0:T(1,128)S(1)}, u32[]{:S(2)}, u32[]{:S(2)}) async-start(f32[32,1,128]{2,1,0:T(1,128)} %bitcast.45), calls=%async_computation.6 | async-start | bytes 32768 | tf_op jit(solution)/shard_map/all_to_all | solution.py:465
  233.6 2.4 shard_map.149
  236.0 3.6 %all-to-all-done.5 = f32[32,1,128]{2,1,0:T(1,128)S(1)} async-done(((f32[32,1,128]{2,1,0:T(1,128)}), f32[32,1,128]{2,1,0:T(1,128)S(1)}, u32[]{:S(2)}, u32[]{:S(2)}) %all-to-all-start.5) | async-done | bytes 16416 | tf_op jit(solution)/shard_map/all_to_all | solution.py:465
  242.0 2.0 fusion.11
  (108 shorter events, 34.7 us)
Async XLA Ops:
  10.3 21.7 %all-to-all-start = ((bf16[4,256,384]{2,1,0:T(8,128)(2,1)}), bf16[4,256,384]{2,1,0:T(8,128)(2,1)S(1)}, u32[]{:S(2)}, u32[]{:S(2)}) async-start(bf16[4,256,384]{2,1,0:T(8,128)(2,1)} %maximum_maximum_fusion), calls=%async_computation | async-start | bytes 1572864 | tf_op jit(solution)/shard_map/all_to_all | solution.py:364
  14.7 70.6 %all-gather.3.cloned.1.call-start = ((), (), s32[]{:S(2)}) async-start(), calls=%async_computation.8 | async-start | bytes 1843200 | tf_op jit(solution)/shard_map/all_gather | solution.py:372
  14.9 11.6 %collective-permute-start.3 = (bf16[400,256]{1,0:T(8,128)(2,1)S(1)}, bf16[400,256]{1,0:T(8,128)(2,1)S(1)}, u32[]{:S(2)}, u32[]{:S(2)}) collective-permute-start(bf16[400,256]{1,0:T(8,128)(2,1)S(1)} %shard_map.144.own_ref), channel_id=1, source_target_pairs={{0,128},{64,192},{128,0},{192,64},{1,129},{65,193},{129,1},{193,65... | collective-permute-start | bytes 614408 | tf_op jit(solution)/shard_map/ppermute | solution.py:87
  17.1 14.7 %collective-permute-start.2 = (bf16[400,256]{1,0:T(8,128)(2,1)S(1)}, bf16[400,256]{1,0:T(8,128)(2,1)S(1)}, u32[]{:S(2)}, u32[]{:S(2)}) collective-permute-start(bf16[400,256]{1,0:T(8,128)(2,1)S(1)} %shard_map.144.own_ref), channel_id=1, source_target_pairs={{0,192},{64,0},{128,64},{192,128},{1,193},{65,1},{129,65},{193,129... | collective-permute-start | bytes 614408 | tf_op jit(solution)/shard_map/ppermute | solution.py:87
  18.6 13.3 %collective-permute-start.1 = (bf16[400,256]{1,0:T(8,128)(2,1)S(1)}, bf16[400,256]{1,0:T(8,128)(2,1)S(1)}, u32[]{:S(2)}, u32[]{:S(2)}) collective-permute-start(bf16[400,256]{1,0:T(8,128)(2,1)S(1)} %shard_map.144.own_ref), channel_id=1, source_target_pairs={{0,64},{64,128},{128,192},{192,0},{1,65},{65,129},{129,193},{193,1... | collective-permute-start | bytes 614408 | tf_op jit(solution)/shard_map/ppermute | solution.py:87
  19.2 12.8 %collective-permute-start = (bf16[400,256]{1,0:T(8,128)(2,1)S(1)}, bf16[400,256]{1,0:T(8,128)(2,1)S(1)}, u32[]{:S(2)}, u32[]{:S(2)}) collective-permute-start(bf16[400,256]{1,0:T(8,128)(2,1)S(1)} %shard_map.144.own_ref), channel_id=1, source_target_pairs={{0,0},{1,33},{2,66},{3,99},{4,132},{5,165},{6,198},{7,231},{32,4},... | collective-permute-start | bytes 614408 | tf_op jit(solution)/shard_map/ppermute | solution.py:368
  83.3 6.4 %collective-permute-start.6 = (bf16[32,16,256]{2,1,0:T(8,128)(2,1)S(1)}, bf16[32,16,256]{2,1,0:T(8,128)(2,1)S(1)}, u32[]{:S(2)}, u32[]{:S(2)}) collective-permute-start(bf16[32,16,256]{2,1,0:T(8,128)(2,1)S(1)} %all_to_all.38), channel_id=1, source_target_pairs={{0,192},{64,0},{128,64},{192,128},{1,193},{65,1},{129,65},{193,129... | collective-permute-start | bytes 786440 | tf_op jit(solution)/shard_map/ppermute | solution.py:87
  84.7 6.4 %collective-permute-start.5 = (bf16[32,16,256]{2,1,0:T(8,128)(2,1)S(1)}, bf16[32,16,256]{2,1,0:T(8,128)(2,1)S(1)}, u32[]{:S(2)}, u32[]{:S(2)}) collective-permute-start(bf16[32,16,256]{2,1,0:T(8,128)(2,1)S(1)} %all_to_all.38), channel_id=1, source_target_pairs={{0,64},{64,128},{128,192},{192,0},{1,65},{65,129},{129,193},{193,1... | collective-permute-start | bytes 786440 | tf_op jit(solution)/shard_map/ppermute | solution.py:87
  91.1 3.4 %collective-permute-start.7 = (bf16[4,4,16,3072]{3,2,1,0:T(8,128)(2,1)S(1)}, bf16[4,4,16,3072]{3,2,1,0:T(8,128)(2,1)S(1)}, u32[]{:S(2)}, u32[]{:S(2)}) collective-permute-start(bf16[4,4,16,3072]{3,2,1,0:T(8,128)(2,1)S(1)} %get-tuple-element.33), channel_id=1, source_target_pairs={{0,32},{32,0},{1,33},{33,1},{2,34},{34,2},{3,35},{35,3},{4,36},{36... | collective-permute-start | bytes 4718600 | tf_op jit(solution)/shard_map/ppermute | solution.py:400
  91.1 6.0 %collective-permute-start.9 = (bf16[16,16,256]{2,1,0:T(8,128)(2,1)S(1)}, bf16[16,16,256]{2,1,0:T(8,128)(2,1)S(1)}, u32[]{:S(2)}, u32[]{:S(2)}) collective-permute-start(bf16[16,16,256]{2,1,0:T(8,128)(2,1)S(1)} %slice.10), channel_id=1, source_target_pairs={{0,192},{64,0},{128,64},{192,128},{1,193},{65,1},{129,65},{193,129... | collective-permute-start | bytes 393224 | tf_op jit(solution)/shard_map/ppermute | solution.py:87
  92.4 5.6 %collective-permute-start.8 = (bf16[16,16,256]{2,1,0:T(8,128)(2,1)S(1)}, bf16[16,16,256]{2,1,0:T(8,128)(2,1)S(1)}, u32[]{:S(2)}, u32[]{:S(2)}) collective-permute-start(bf16[16,16,256]{2,1,0:T(8,128)(2,1)S(1)} %slice.9), channel_id=1, source_target_pairs={{0,64},{64,128},{128,192},{192,0},{1,65},{65,129},{129,193},{193,1... | collective-permute-start | bytes 393224 | tf_op jit(solution)/shard_map/ppermute | solution.py:87
  98.7 26.5 %all-to-all-start.3 = ((bf16[16,16,3072]{2,1,0:T(8,128)(2,1)}), bf16[16,16,3072]{2,1,0:T(8,128)(2,1)S(1)}, u32[]{:S(2)}, u32[]{:S(2)}) async-start(bf16[16,16,3072]{2,1,0:T(8,128)(2,1)} %bitcast.123), calls=%async_computation.3 | async-start | bytes 3145728 | tf_op jit(solution)/shard_map/all_to_all | solution.py:408
  104.4 97.0 %reduce-scatter.2.cloned.1.call-start = ((), (), s32[]{:S(2)}) async-start(), calls=%async_computation.7 | async-start | bytes 1769472 | tf_op jit(solution)/shard_map/reduce_scatter | solution.py:447
  130.2 7.8 %collective-permute-start.13 = (bf16[16,1152]{1,0:T(8,128)(2,1)S(1)}, bf16[16,1152]{1,0:T(8,128)(2,1)S(1)}, u32[]{:S(2)}, u32[]{:S(2)}) collective-permute-start(bf16[16,1152]{1,0:T(8,128)(2,1)S(1)} %get-tuple-element.39), channel_id=1, source_target_pairs={{0,128},{64,192},{128,0},{192,64},{1,129},{65,193},{129,1},{193,65... | collective-permute-start | bytes 110600 | tf_op jit(solution)/shard_map/ppermute | solution.py:87
  132.7 5.3 %collective-permute-start.12 = (bf16[16,1152]{1,0:T(8,128)(2,1)S(1)}, bf16[16,1152]{1,0:T(8,128)(2,1)S(1)}, u32[]{:S(2)}, u32[]{:S(2)}) collective-permute-start(bf16[16,1152]{1,0:T(8,128)(2,1)S(1)} %get-tuple-element.39), channel_id=1, source_target_pairs={{0,192},{64,0},{128,64},{192,128},{1,193},{65,1},{129,65},{193,129... | collective-permute-start | bytes 110600 | tf_op jit(solution)/shard_map/ppermute | solution.py:87
  134.5 4.0 %collective-permute-start.11 = (bf16[16,1152]{1,0:T(8,128)(2,1)S(1)}, bf16[16,1152]{1,0:T(8,128)(2,1)S(1)}, u32[]{:S(2)}, u32[]{:S(2)}) collective-permute-start(bf16[16,1152]{1,0:T(8,128)(2,1)S(1)} %get-tuple-element.39), channel_id=1, source_target_pairs={{0,64},{64,128},{128,192},{192,0},{1,65},{65,129},{129,193},{193,1... | collective-permute-start | bytes 110600 | tf_op jit(solution)/shard_map/ppermute | solution.py:87
  134.7 6.6 %collective-permute-start.20 = (bf16[16,1024]{1,0:T(8,128)(2,1)S(1)}, bf16[16,1024]{1,0:T(8,128)(2,1)S(1)}, u32[]{:S(2)}, u32[]{:S(2)}) collective-permute-start(bf16[16,1024]{1,0:T(8,128)(2,1)S(1)} %get-tuple-element.40), channel_id=1, source_target_pairs={{0,16},{8,24},{16,0},{24,8},{1,17},{9,25},{17,1},{25,9},{2,18},{10... | collective-permute-start | bytes 98312 | tf_op jit(solution)/shard_map/ppermute | solution.py:87
  135.8 7.0 %collective-permute-start.19 = (bf16[16,1024]{1,0:T(8,128)(2,1)S(1)}, bf16[16,1024]{1,0:T(8,128)(2,1)S(1)}, u32[]{:S(2)}, u32[]{:S(2)}) collective-permute-start(bf16[16,1024]{1,0:T(8,128)(2,1)S(1)} %get-tuple-element.40), channel_id=1, source_target_pairs={{0,24},{8,0},{16,8},{24,16},{1,25},{9,1},{17,9},{25,17},{2,26},{10... | collective-permute-start | bytes 98312 | tf_op jit(solution)/shard_map/ppermute | solution.py:87
  137.9 6.0 %collective-permute-start.18 = (bf16[16,1024]{1,0:T(8,128)(2,1)S(1)}, bf16[16,1024]{1,0:T(8,128)(2,1)S(1)}, u32[]{:S(2)}, u32[]{:S(2)}) collective-permute-start(bf16[16,1024]{1,0:T(8,128)(2,1)S(1)} %get-tuple-element.40), channel_id=1, source_target_pairs={{0,8},{8,16},{16,24},{24,0},{1,9},{9,17},{17,25},{25,1},{2,10},{10... | collective-permute-start | bytes 98312 | tf_op jit(solution)/shard_map/ppermute | solution.py:87
  138.5 7.6 %collective-permute-start.15 = (bf16[4,16,1152]{2,1,0:T(8,128)(2,1)S(1)}, bf16[4,16,1152]{2,1,0:T(8,128)(2,1)S(1)}, u32[]{:S(2)}, u32[]{:S(2)}) collective-permute-start(bf16[4,16,1152]{2,1,0:T(8,128)(2,1)S(1)} %get-tuple-element.60), channel_id=1, source_target_pairs={{0,24},{8,0},{16,8},{24,16},{1,25},{9,1},{17,9},{25,17},{2,26},{10... | collective-permute-start | bytes 442376 | tf_op jit(solution)/shard_map/ppermute | solution.py:87
  141.3 8.8 %collective-permute-start.14 = (bf16[4,16,1152]{2,1,0:T(8,128)(2,1)S(1)}, bf16[4,16,1152]{2,1,0:T(8,128)(2,1)S(1)}, u32[]{:S(2)}, u32[]{:S(2)}) collective-permute-start(bf16[4,16,1152]{2,1,0:T(8,128)(2,1)S(1)} %get-tuple-element.60), channel_id=1, source_target_pairs={{0,8},{8,16},{16,24},{24,0},{1,9},{9,17},{17,25},{25,1},{2,10},{10... | collective-permute-start | bytes 442376 | tf_op jit(solution)/shard_map/ppermute | solution.py:87
  141.3 8.8 %collective-permute-start.16 = (bf16[4,16,1152]{2,1,0:T(8,128)(2,1)S(1)}, bf16[4,16,1152]{2,1,0:T(8,128)(2,1)S(1)}, u32[]{:S(2)}, u32[]{:S(2)}) collective-permute-start(bf16[4,16,1152]{2,1,0:T(8,128)(2,1)S(1)} %get-tuple-element.60), channel_id=1, source_target_pairs={{0,16},{8,24},{16,0},{24,8},{1,17},{9,25},{17,1},{25,9},{2,18},{10... | collective-permute-start | bytes 442376 | tf_op jit(solution)/shard_map/ppermute | solution.py:87
  144.0 6.4 %collective-permute-start.22 = (bf16[4,16,1024]{2,1,0:T(8,128)(2,1)S(1)}, bf16[4,16,1024]{2,1,0:T(8,128)(2,1)S(1)}, u32[]{:S(2)}, u32[]{:S(2)}) collective-permute-start(bf16[4,16,1024]{2,1,0:T(8,128)(2,1)S(1)} %get-tuple-element.62), channel_id=1, source_target_pairs={{0,192},{64,0},{128,64},{192,128},{1,193},{65,1},{129,65},{193,129... | collective-permute-start | bytes 393224 | tf_op jit(solution)/shard_map/ppermute | solution.py:87
  146.1 5.0 %collective-permute-start.21 = (bf16[4,16,1024]{2,1,0:T(8,128)(2,1)S(1)}, bf16[4,16,1024]{2,1,0:T(8,128)(2,1)S(1)}, u32[]{:S(2)}, u32[]{:S(2)}) collective-permute-start(bf16[4,16,1024]{2,1,0:T(8,128)(2,1)S(1)} %get-tuple-element.62), channel_id=1, source_target_pairs={{0,64},{64,128},{128,192},{192,0},{1,65},{65,129},{129,193},{193,1... | collective-permute-start | bytes 393224 | tf_op jit(solution)/shard_map/ppermute | solution.py:87
  146.1 7.0 %collective-permute-start.23 = (bf16[4,16,1024]{2,1,0:T(8,128)(2,1)S(1)}, bf16[4,16,1024]{2,1,0:T(8,128)(2,1)S(1)}, u32[]{:S(2)}, u32[]{:S(2)}) collective-permute-start(bf16[4,16,1024]{2,1,0:T(8,128)(2,1)S(1)} %get-tuple-element.62), channel_id=1, source_target_pairs={{0,128},{64,192},{128,0},{192,64},{1,129},{65,193},{129,1},{193,65... | collective-permute-start | bytes 393224 | tf_op jit(solution)/shard_map/ppermute | solution.py:87
  150.2 5.1 %collective-permute-start.17 = (bf16[4,4,16,1152]{3,2,1,0:T(8,128)(2,1)S(1)}, bf16[4,4,16,1152]{3,2,1,0:T(8,128)(2,1)S(1)}, u32[]{:S(2)}, u32[]{:S(2)}) collective-permute-start(bf16[4,4,16,1152]{3,2,1,0:T(8,128)(2,1)S(1)} %pad_maximum_fusion.2.act_near_ref), channel_id=1, source_target_pairs={{0,32},{32,0},{1,33},{33,1},{2,34},{34,2},{3,35},{35,3},{4,36},{36... | collective-permute-start | bytes 1769480 | tf_op jit(solution)/shard_map/ppermute | solution.py:427
  162.8 63.4 %all-to-all-start.4 = ((bf16[32,128,384]{2,1,0:T(8,128)(2,1)}), bf16[32,128,384]{2,1,0:T(8,128)(2,1)S(1)}, u32[]{:S(2)}, u32[]{:S(2)}) async-start(bf16[32,128,384]{2,1,0:T(8,128)(2,1)} %bitcast.124), calls=%async_computation.4 | async-start | bytes 6291456 | tf_op jit(solution)/shard_map/all_to_all | solution.py:449
  201.4 39.5 %collective-permute-start.28 = (bf16[128,768]{1,0:T(8,128)(2,1)}, bf16[128,768]{1,0:T(8,128)(2,1)}, u32[]{:S(2)}, u32[]{:S(2)}) collective-permute-start(bf16[128,768]{1,0:T(8,128)(2,1)} %bitcast.117), channel_id=1, source_target_pairs={{0,0},{33,1},{66,2},{99,3},{132,4},{165,5},{198,6},{231,7},{4,32},... | collective-permute-start | bytes 589832 | tf_op jit(solution)/shard_map/ppermute | solution.py:467
  204.5 10.1 %collective-permute-start.25 = (f32[32,128]{1,0:T(8,128)S(1)}, f32[32,128]{1,0:T(8,128)S(1)}, u32[]{:S(2)}, u32[]{:S(2)}) collective-permute-start(f32[32,128]{1,0:T(8,128)S(1)} %shard_map.150), channel_id=1, source_target_pairs={{0,4},{1,5},{2,6},{3,7},{4,0},{5,1},{6,2},{7,3},{8,12},{9,13},{10,... | collective-permute-start | bytes 49160 | tf_op jit(solution)/shard_map/ppermute | solution.py:87
  214.7 6.0 %collective-permute-start.26 = (f32[32,128]{1,0:T(8,128)S(1)}, f32[32,128]{1,0:T(8,128)S(1)}, u32[]{:S(2)}, u32[]{:S(2)}) collective-permute-start(f32[32,128]{1,0:T(8,128)S(1)} %add.96), channel_id=1, source_target_pairs={{0,2},{1,3},{2,4},{3,5},{4,6},{5,7},{6,0},{7,1},{8,10},{9,11},{10,... | collective-permute-start | bytes 49160 | tf_op jit(solution)/shard_map/ppermute | solution.py:87
  220.6 4.9 %collective-permute-start.27 = (f32[32,128]{1,0:T(8,128)S(1)}, f32[32,128]{1,0:T(8,128)S(1)}, u32[]{:S(2)}, u32[]{:S(2)}) collective-permute-start(f32[32,128]{1,0:T(8,128)S(1)} %add.97), channel_id=1, source_target_pairs={{0,1},{1,2},{2,3},{3,4},{4,5},{5,6},{6,7},{7,0},{8,9},{9,10},{10,1... | collective-permute-start | bytes 49160 | tf_op jit(solution)/shard_map/ppermute | solution.py:87
  226.2 13.5 %all-to-all-start.5 = ((f32[32,1,128]{2,1,0:T(1,128)}), f32[32,1,128]{2,1,0:T(1,128)S(1)}, u32[]{:S(2)}, u32[]{:S(2)}) async-start(f32[32,1,128]{2,1,0:T(1,128)} %bitcast.45), calls=%async_computation.6 | async-start | bytes 32768 | tf_op jit(solution)/shard_map/all_to_all | solution.py:465
  (20 other events, 101.0 us)
Sparse Core Ops, SparseCore 0:
  32.8 49.0 all-gather.2
  162.9 38.4 reduce-scatter.1

commit v12 on v10

--- a/solution.py
+++ b/solution.py
@@ -406,7 +406,6 @@
     beyond = [shifted(before[:half], "x", 1), shifted(after[half:], "x", -1)]
     parts = (keep.astype(WIDE) + came.astype(WIDE)).astype(LOW)
     parts = parts.reshape(count_x * count_y, piece, layers * 3 * rank)
-    parts, *beyond = lax.optimization_barrier((parts, *beyond))
     cross_near = jnp.stack([cross, before, after, jnp.concatenate(beyond)])
     cross_far = lax.ppermute(cross_near, "c", swap_core)
     parts = lax.all_to_all(parts, ("x", "y"), 0, 0, tiled=True)

time: 250 us -> 253 us (1.012)
    ppermute x19, waiting for transfers between devices: 12.9 us -> 29.6 us  [shifted(): lax.ppermute(block, axis, [(i, (i + distance) % size) for i in range(size)])]
    all_to_all x1, waiting for transfers between devices: 16.5 us -> 0.01 us  [shards(): parts = lax.all_to_all(parts, ('x', 'y'), 0, 0, tiled=True)]
  transfers between devices with their start and end apart: 33 -> 33, of which waited for: 17 -> 15; matrix products, arithmetic and copies ran while one was open for 2% -> 1% of each run, Pallas kernels for 3% -> 3%
where the time goes in v12:
time: 253 us; the launch traced here: 250 us
  waiting for transfers between devices  80.2 us (32%)
  starting transfers between devices  72.2 us (29%)
  blocking collectives  47.2 us (19%)
  Pallas kernels  20.6 us (8%)
  between operations  15.1 us (6%)
  other arithmetic  9.19 us (4%)
  local copies, waits for them, and re-layouts  5.25 us (2%)
    all_to_all x2, blocking collectives, shards(): cross = lax.all_to_all(cross, ('y', 'z'), 0, 0, tiled=True)  47.2 us
    reduce_scatter x1, waiting for transfers between devices, shards(): grads = lax.psum_scatter(grads, 'z', scatter_dimension=0, tiled=True)[0]  32.4 us
    ppermute x19, waiting for transfers between devices, shifted(): lax.ppermute(block, axis, [(i, (i + distance) % size) for i in range(size)])  29.6 us
    ppermute x19, starting transfers between devices, shifted(): lax.ppermute(block, axis, [(i, (i + distance) % size) for i in range(size)])  27.2 us
    pallas_call x7, Pallas kernels, local_call(): pl.pallas_call(kernel, out_shape=out_shape, in_specs=in_specs, out_specs=...  18.2 us
    all_to_all x1, starting transfers between devices, shards(): squares = lax.all_to_all(squares, EVERYONE, 0, 0, tiled=True)  13.7 us
    all_to_all x1, starting transfers between devices, shards(): outputs = lax.all_to_all(outputs, PLANE, 0, 0, tiled=True)  8.4 us
    ppermute x1, starting transfers between devices, shards(): swapped = lax.ppermute(packed, across, swap)  7.39 us
  transfers between devices with their start and end apart: 33, of which 15 were waited for; matrix products, arithmetic and copies ran while one was open for 1% of the time, Pallas kernels for 3%

profile of v12, /device:TPU:2, one launch (start us, length us, event | category | flops | bytes accessed | tf_op | source)
XLA Modules:
  0.0 249.7 jit_solution(11481633600363330711)
XLA Ops:
  10.3 4.5 %all-to-all-start = ((bf16[4,256,384]{2,1,0:T(8,128)(2,1)}), bf16[4,256,384]{2,1,0:T(8,128)(2,1)S(1)}, u32[]{:S(2)}, u32[]{:S(2)}) async-start(bf16[4,256,384]{2,1,0:T(8,128)(2,1)} %maximum_maximum_fusion), calls=%async_computation | async-start | bytes 1572864 | tf_op jit(solution)/shard_map/all_to_all | solution.py:368
  14.9 2.2 collective-permute-start.3
  19.2 7.4 %collective-permute-start = (bf16[400,256]{1,0:T(8,128)(2,1)S(1)}, bf16[400,256]{1,0:T(8,128)(2,1)S(1)}, u32[]{:S(2)}, u32[]{:S(2)}) collective-permute-start(bf16[400,256]{1,0:T(8,128)(2,1)S(1)} %shard_map.144.own_ref), channel_id=1, source_target_pairs={{0,0},{1,33},{2,66},{3,99},{4,132},{5,165},{6,198},{7,231},{32,4},... | collective-permute-start | bytes 614408 | tf_op jit(solution)/shard_map/ppermute | solution.py:372
  26.6 5.3 %collective-permute-done.2 = bf16[400,256]{1,0:T(8,128)(2,1)S(1)} collective-permute-done((bf16[400,256]{1,0:T(8,128)(2,1)S(1)}, bf16[400,256]{1,0:T(8,128)(2,1)S(1)}, u32[]{:S(2)}, u32[]{:S(2)}) %collective-permute-start.2) | collective-permute-done | bytes 204832 | tf_op jit(solution)/shard_map/ppermute | solution.py:88
  32.8 2.2 collective-permute-done.4.far_ref
  36.1 27.5 %all_to_all.37 = bf16[32,16,256]{2,1,0:T(8,128)(2,1)S(1)} all-to-all(bf16[32,16,256]{2,1,0:T(8,128)(2,1)S(1)} %shard_map.146), channel_id=1, replica_groups=mesh['x'=4,'c'=2,'y'=4,'z'=8] {'y','z'}, dimensions={0} | all-to-all | bytes 524288 | tf_op jit(solution)/shard_map/all_to_all | solution.py:389
  63.7 19.7 %all_to_all.38 = bf16[32,16,256]{2,1,0:T(8,128)(2,1)S(1)} all-to-all(bf16[32,16,256]{2,1,0:T(8,128)(2,1)S(1)} %broadcast_in_dim.33), channel_id=1, replica_groups=mesh['x'=4,'c'=2,'y'=4,'z'=8] {'y','z'}, dimensions={0} | all-to-all | bytes 524288 | tf_op jit(solution)/shard_map/all_to_all | solution.py:392
  86.8 2.8 %shard_map.145 = (bf16[4,4,16,3072]{3,2,1,0:T(8,128)(2,1)S(1)}, bf16[4,4,16,3072]{3,2,1,0:T(8,128)(2,1)S(1)}) custom-call(s32[4]{0:T(128)S(1)} %pad_add_fusion.place_ref, bf16[4,256,384]{2,1,0:T(8,128)(2,1)S(1)} %all-to-all-done.rows_ref, bf16[8,400,256]{2,1,0:T(8,128)(2,1)S(1)} %bitcast.122), custom_call_target="tpu_custom_call" | custom-call | flops 1207959552 | bytes 5570560 | tf_op jit(solution)/shard_map/pallas_call | solution.py:75
  91.1 3.4 %collective-permute-done.7 = bf16[4,4,16,3072]{3,2,1,0:T(8,128)(2,1)S(1)} collective-permute-done((bf16[4,4,16,3072]{3,2,1,0:T(8,128)(2,1)S(1)}, bf16[4,4,16,3072]{3,2,1,0:T(8,128)(2,1)S(1)}, u32[]{:S(2)}, u32[]{:S(2)}) %collective-permute-start.7) | collective-permute-done | bytes 1572896 | tf_op jit(solution)/shard_map/ppermute | solution.py:404
  94.5 1.7 add_convert_fusion
  96.2 5.3 %all-to-all-start.3 = ((bf16[16,16,3072]{2,1,0:T(8,128)(2,1)}), bf16[16,16,3072]{2,1,0:T(8,128)(2,1)S(1)}, u32[]{:S(2)}, u32[]{:S(2)}) async-start(bf16[16,16,3072]{2,1,0:T(8,128)(2,1)} %bitcast.123), calls=%async_computation.3 | async-start | bytes 3145728 | tf_op jit(solution)/shard_map/all_to_all | solution.py:411
  101.8 1.9 collective-permute-start.8
  103.8 19.6 %collective-permute-done.9 = bf16[16,16,256]{2,1,0:T(8,128)(2,1)S(1)} collective-permute-done((bf16[16,16,256]{2,1,0:T(8,128)(2,1)S(1)}, bf16[16,16,256]{2,1,0:T(8,128)(2,1)S(1)}, u32[]{:S(2)}, u32[]{:S(2)}) %collective-permute-start.9) | collective-permute-done | bytes 131104 | tf_op jit(solution)/shard_map/ppermute | solution.py:88
  127.7 4.9 %shard_map.147 = (bf16[16,1152]{1,0:T(8,128)(2,1)S(1)}, bf16[16,1024]{1,0:T(8,128)(2,1)S(1)}) custom-call(s32[4]{0:T(128)S(1)} %pad_add_fusion.place_ref, bf16[16,16,3072]{2,1,0:T(8,128)(2,1)S(1)} %all-to-all-done.3.parts_ref, f32[16,128]{1,0:T(8,128)S(1)} %broadcast_in_dim.34.square_ref, bf16[4,32,16,256]{3,2,1,0:T(8,128)(2,1)S(1)} %pad_maximum_fusion.near_ref, ...), custom_call_target="tpu_custom_call" | custom-call | bytes 3747840 | tf_op jit(solution)/shard_map/pallas_call | solution.py:75
  132.6 1.7 collective-permute-start.13
  134.3 1.9 collective-permute-start.12
  136.4 2.8 %collective-permute-start.20 = (bf16[16,1024]{1,0:T(8,128)(2,1)S(1)}, bf16[16,1024]{1,0:T(8,128)(2,1)S(1)}, u32[]{:S(2)}, u32[]{:S(2)}) collective-permute-start(bf16[16,1024]{1,0:T(8,128)(2,1)S(1)} %get-tuple-element.34), channel_id=1, source_target_pairs={{0,16},{8,24},{16,0},{24,8},{1,17},{9,25},{17,1},{25,9},{2,18},{10... | collective-permute-start | bytes 98312 | tf_op jit(solution)/shard_map/ppermute | solution.py:88
  141.2 2.6 %collective-permute-start.15 = (bf16[4,16,1152]{2,1,0:T(8,128)(2,1)S(1)}, bf16[4,16,1152]{2,1,0:T(8,128)(2,1)S(1)}, u32[]{:S(2)}, u32[]{:S(2)}) collective-permute-start(bf16[4,16,1152]{2,1,0:T(8,128)(2,1)S(1)} %get-tuple-element.54), channel_id=1, source_target_pairs={{0,24},{8,0},{16,8},{24,16},{1,25},{9,1},{17,9},{25,17},{2,26},{10... | collective-permute-start | bytes 442376 | tf_op jit(solution)/shard_map/ppermute | solution.py:88
  145.6 2.1 collective-permute-start.22
  148.1 3.9 %collective-permute-start.23 = (bf16[4,16,1024]{2,1,0:T(8,128)(2,1)S(1)}, bf16[4,16,1024]{2,1,0:T(8,128)(2,1)S(1)}, u32[]{:S(2)}, u32[]{:S(2)}) collective-permute-start(bf16[4,16,1024]{2,1,0:T(8,128)(2,1)S(1)} %get-tuple-element.56), channel_id=1, source_target_pairs={{0,128},{64,192},{128,0},{192,64},{1,129},{65,193},{129,1},{193,65... | collective-permute-start | bytes 393224 | tf_op jit(solution)/shard_map/ppermute | solution.py:88
  152.9 2.1 collective-permute-done.23
  155.4 1.9 collective-permute-done.24.move_far_ref
  157.3 7.4 %shard_map.148 = (bf16[8,4,128,384]{3,2,1,0:T(8,128)(2,1)}, bf16[8,128,768]{2,1,0:T(8,128)(2,1)}) custom-call(s32[4]{0:T(128)S(1)} %pad_add_fusion.place_ref, bf16[4,256,384]{2,1,0:T(8,128)(2,1)S(1)} %all-to-all-done.rows_ref, bf16[8,400,256]{2,1,0:T(8,128)(2,1)} %bitcast.121, bf16[4,4,16,1152]{3,2,1,0:T(8,128)(2,1)S(1)} %pad_maximum_fusion.2.act_near_ref, ...), custom_call_target="tpu_custom_call" | custom-call | flops 1610612736 | bytes 9371648 | tf_op jit(solution)/shard_map/pallas_call | solution.py:75
  164.7 8.4 %all-to-all-start.4 = ((bf16[32,128,384]{2,1,0:T(8,128)(2,1)}), bf16[32,128,384]{2,1,0:T(8,128)(2,1)S(1)}, u32[]{:S(2)}, u32[]{:S(2)}) async-start(bf16[32,128,384]{2,1,0:T(8,128)(2,1)} %bitcast.125), calls=%async_computation.4 | async-start | bytes 6291456 | tf_op jit(solution)/shard_map/all_to_all | solution.py:452
  173.1 32.4 %reduce-scatter.2.cloned.1.call-done = bf16[1,128,768]{2,1,0:T(8,128)(2,1)} async-done(((bf16[8,128,768]{2,1,0:T(8,128)(2,1)}), bf16[1,128,768]{2,1,0:T(8,128)(2,1)}) %reduce-scatter.2.cloned.1.call-update) | async-done | bytes 196624 | tf_op jit(solution)/shard_map/reduce_scatter | solution.py:450
  205.5 1.9 collective-permute-start.25
  209.2 2.4 all-to-all-done.4
  211.7 13.7 %all-to-all-start.5 = ((f32[256,1,128]{2,1,0:T(1,128)}), f32[256,1,128]{2,1,0:T(1,128)S(1)}, u32[]{:S(2)}, u32[]{:S(2)}) async-start(f32[256,1,128]{2,1,0:T(1,128)} %bitcast.45), calls=%async_computation.6 | async-start | bytes 262144 | tf_op jit(solution)/shard_map/all_to_all | solution.py:466
  225.4 3.0 %collective-permute-start.26 = (bf16[128,768]{1,0:T(8,128)(2,1)}, bf16[128,768]{1,0:T(8,128)(2,1)}, u32[]{:S(2)}, u32[]{:S(2)}) collective-permute-start(bf16[128,768]{1,0:T(8,128)(2,1)} %collective-permute-done.25), channel_id=1, source_target_pairs={{0,0},{1,1},{2,2},{3,3},{4,4},{5,5},{6,6},{7,7},{32,39},{33,32},{3... | collective-permute-start | bytes 589832 | tf_op jit(solution)/shard_map/ppermute | solution.py:468
  228.4 2.4 shard_map.149
  230.8 6.6 %all-to-all-done.5 = f32[256,1,128]{2,1,0:T(1,128)S(1)} async-done(((f32[256,1,128]{2,1,0:T(1,128)}), f32[256,1,128]{2,1,0:T(1,128)S(1)}, u32[]{:S(2)}, u32[]{:S(2)}) %all-to-all-start.5) | async-done | bytes 131104 | tf_op jit(solution)/shard_map/all_to_all | solution.py:466
  239.9 2.0 fusion.11
  (93 shorter events, 26.9 us)
Async XLA Ops:
  10.3 21.7 %all-to-all-start = ((bf16[4,256,384]{2,1,0:T(8,128)(2,1)}), bf16[4,256,384]{2,1,0:T(8,128)(2,1)S(1)}, u32[]{:S(2)}, u32[]{:S(2)}) async-start(bf16[4,256,384]{2,1,0:T(8,128)(2,1)} %maximum_maximum_fusion), calls=%async_computation | async-start | bytes 1572864 | tf_op jit(solution)/shard_map/all_to_all | solution.py:368
  14.7 70.6 %all-gather.3.cloned.1.call-start = ((), (), s32[]{:S(2)}) async-start(), calls=%async_computation.8 | async-start | bytes 1843200 | tf_op jit(solution)/shard_map/all_gather | solution.py:376
  14.9 11.6 %collective-permute-start.3 = (bf16[400,256]{1,0:T(8,128)(2,1)S(1)}, bf16[400,256]{1,0:T(8,128)(2,1)S(1)}, u32[]{:S(2)}, u32[]{:S(2)}) collective-permute-start(bf16[400,256]{1,0:T(8,128)(2,1)S(1)} %shard_map.144.own_ref), channel_id=1, source_target_pairs={{0,128},{64,192},{128,0},{192,64},{1,129},{65,193},{129,1},{193,65... | collective-permute-start | bytes 614408 | tf_op jit(solution)/shard_map/ppermute | solution.py:88
  17.1 14.7 %collective-permute-start.2 = (bf16[400,256]{1,0:T(8,128)(2,1)S(1)}, bf16[400,256]{1,0:T(8,128)(2,1)S(1)}, u32[]{:S(2)}, u32[]{:S(2)}) collective-permute-start(bf16[400,256]{1,0:T(8,128)(2,1)S(1)} %shard_map.144.own_ref), channel_id=1, source_target_pairs={{0,192},{64,0},{128,64},{192,128},{1,193},{65,1},{129,65},{193,129... | collective-permute-start | bytes 614408 | tf_op jit(solution)/shard_map/ppermute | solution.py:88
  18.6 13.3 %collective-permute-start.1 = (bf16[400,256]{1,0:T(8,128)(2,1)S(1)}, bf16[400,256]{1,0:T(8,128)(2,1)S(1)}, u32[]{:S(2)}, u32[]{:S(2)}) collective-permute-start(bf16[400,256]{1,0:T(8,128)(2,1)S(1)} %shard_map.144.own_ref), channel_id=1, source_target_pairs={{0,64},{64,128},{128,192},{192,0},{1,65},{65,129},{129,193},{193,1... | collective-permute-start | bytes 614408 | tf_op jit(solution)/shard_map/ppermute | solution.py:88
  19.2 12.8 %collective-permute-start = (bf16[400,256]{1,0:T(8,128)(2,1)S(1)}, bf16[400,256]{1,0:T(8,128)(2,1)S(1)}, u32[]{:S(2)}, u32[]{:S(2)}) collective-permute-start(bf16[400,256]{1,0:T(8,128)(2,1)S(1)} %shard_map.144.own_ref), channel_id=1, source_target_pairs={{0,0},{1,33},{2,66},{3,99},{4,132},{5,165},{6,198},{7,231},{32,4},... | collective-permute-start | bytes 614408 | tf_op jit(solution)/shard_map/ppermute | solution.py:372
  32.6 2.4 collective-permute-start.4
  83.3 6.4 %collective-permute-start.6 = (bf16[32,16,256]{2,1,0:T(8,128)(2,1)S(1)}, bf16[32,16,256]{2,1,0:T(8,128)(2,1)S(1)}, u32[]{:S(2)}, u32[]{:S(2)}) collective-permute-start(bf16[32,16,256]{2,1,0:T(8,128)(2,1)S(1)} %all_to_all.38), channel_id=1, source_target_pairs={{0,192},{64,0},{128,64},{192,128},{1,193},{65,1},{129,65},{193,129... | collective-permute-start | bytes 786440 | tf_op jit(solution)/shard_map/ppermute | solution.py:88
  84.7 6.4 %collective-permute-start.5 = (bf16[32,16,256]{2,1,0:T(8,128)(2,1)S(1)}, bf16[32,16,256]{2,1,0:T(8,128)(2,1)S(1)}, u32[]{:S(2)}, u32[]{:S(2)}) collective-permute-start(bf16[32,16,256]{2,1,0:T(8,128)(2,1)S(1)} %all_to_all.38), channel_id=1, source_target_pairs={{0,64},{64,128},{128,192},{192,0},{1,65},{65,129},{129,193},{193,1... | collective-permute-start | bytes 786440 | tf_op jit(solution)/shard_map/ppermute | solution.py:88
  91.1 3.4 %collective-permute-start.7 = (bf16[4,4,16,3072]{3,2,1,0:T(8,128)(2,1)S(1)}, bf16[4,4,16,3072]{3,2,1,0:T(8,128)(2,1)S(1)}, u32[]{:S(2)}, u32[]{:S(2)}) collective-permute-start(bf16[4,4,16,3072]{3,2,1,0:T(8,128)(2,1)S(1)} %get-tuple-element.30), channel_id=1, source_target_pairs={{0,32},{32,0},{1,33},{33,1},{2,34},{34,2},{3,35},{35,3},{4,36},{36... | collective-permute-start | bytes 4718600 | tf_op jit(solution)/shard_map/ppermute | solution.py:404
  96.2 31.4 %all-to-all-start.3 = ((bf16[16,16,3072]{2,1,0:T(8,128)(2,1)}), bf16[16,16,3072]{2,1,0:T(8,128)(2,1)S(1)}, u32[]{:S(2)}, u32[]{:S(2)}) async-start(bf16[16,16,3072]{2,1,0:T(8,128)(2,1)} %bitcast.123), calls=%async_computation.3 | async-start | bytes 3145728 | tf_op jit(solution)/shard_map/all_to_all | solution.py:411
  101.6 103.9 %reduce-scatter.2.cloned.1.call-start = ((), (), s32[]{:S(2)}) async-start(), calls=%async_computation.7 | async-start | bytes 1769472 | tf_op jit(solution)/shard_map/reduce_scatter | solution.py:450
  101.7 21.7 %collective-permute-start.9 = (bf16[16,16,256]{2,1,0:T(8,128)(2,1)S(1)}, bf16[16,16,256]{2,1,0:T(8,128)(2,1)S(1)}, u32[]{:S(2)}, u32[]{:S(2)}) collective-permute-start(bf16[16,16,256]{2,1,0:T(8,128)(2,1)S(1)} %slice.10), channel_id=1, source_target_pairs={{0,192},{64,0},{128,64},{192,128},{1,193},{65,1},{129,65},{193,129... | collective-permute-start | bytes 393224 | tf_op jit(solution)/shard_map/ppermute | solution.py:88
  101.8 21.5 %collective-permute-start.8 = (bf16[16,16,256]{2,1,0:T(8,128)(2,1)S(1)}, bf16[16,16,256]{2,1,0:T(8,128)(2,1)S(1)}, u32[]{:S(2)}, u32[]{:S(2)}) collective-permute-start(bf16[16,16,256]{2,1,0:T(8,128)(2,1)S(1)} %slice.9), channel_id=1, source_target_pairs={{0,64},{64,128},{128,192},{192,0},{1,65},{65,129},{129,193},{193,1... | collective-permute-start | bytes 393224 | tf_op jit(solution)/shard_map/ppermute | solution.py:88
  124.6 3.1 %collective-permute-start.10 = (bf16[4,32,16,256]{3,2,1,0:T(8,128)(2,1)S(1)}, bf16[4,32,16,256]{3,2,1,0:T(8,128)(2,1)}, u32[]{:S(2)}, u32[]{:S(2)}) collective-permute-start(bf16[4,32,16,256]{3,2,1,0:T(8,128)(2,1)S(1)} %pad_maximum_fusion.near_ref), channel_id=1, source_target_pairs={{0,32},{32,0},{1,33},{33,1},{2,34},{34,2},{3,35},{35,3},{4,36},{36... | collective-permute-start | bytes 3145736 | tf_op jit(solution)/shard_map/ppermute | solution.py:410
  132.6 7.8 %collective-permute-start.13 = (bf16[16,1152]{1,0:T(8,128)(2,1)S(1)}, bf16[16,1152]{1,0:T(8,128)(2,1)S(1)}, u32[]{:S(2)}, u32[]{:S(2)}) collective-permute-start(bf16[16,1152]{1,0:T(8,128)(2,1)S(1)} %get-tuple-element.33), channel_id=1, source_target_pairs={{0,128},{64,192},{128,0},{192,64},{1,129},{65,193},{129,1},{193,65... | collective-permute-start | bytes 110600 | tf_op jit(solution)/shard_map/ppermute | solution.py:88
  134.3 6.9 %collective-permute-start.12 = (bf16[16,1152]{1,0:T(8,128)(2,1)S(1)}, bf16[16,1152]{1,0:T(8,128)(2,1)S(1)}, u32[]{:S(2)}, u32[]{:S(2)}) collective-permute-start(bf16[16,1152]{1,0:T(8,128)(2,1)S(1)} %get-tuple-element.33), channel_id=1, source_target_pairs={{0,192},{64,0},{128,64},{192,128},{1,193},{65,1},{129,65},{193,129... | collective-permute-start | bytes 110600 | tf_op jit(solution)/shard_map/ppermute | solution.py:88
  136.2 5.0 %collective-permute-start.11 = (bf16[16,1152]{1,0:T(8,128)(2,1)S(1)}, bf16[16,1152]{1,0:T(8,128)(2,1)S(1)}, u32[]{:S(2)}, u32[]{:S(2)}) collective-permute-start(bf16[16,1152]{1,0:T(8,128)(2,1)S(1)} %get-tuple-element.33), channel_id=1, source_target_pairs={{0,64},{64,128},{128,192},{192,0},{1,65},{65,129},{129,193},{193,1... | collective-permute-start | bytes 110600 | tf_op jit(solution)/shard_map/ppermute | solution.py:88
  136.4 7.5 %collective-permute-start.20 = (bf16[16,1024]{1,0:T(8,128)(2,1)S(1)}, bf16[16,1024]{1,0:T(8,128)(2,1)S(1)}, u32[]{:S(2)}, u32[]{:S(2)}) collective-permute-start(bf16[16,1024]{1,0:T(8,128)(2,1)S(1)} %get-tuple-element.34), channel_id=1, source_target_pairs={{0,16},{8,24},{16,0},{24,8},{1,17},{9,25},{17,1},{25,9},{2,18},{10... | collective-permute-start | bytes 98312 | tf_op jit(solution)/shard_map/ppermute | solution.py:88
  139.1 6.2 %collective-permute-start.19 = (bf16[16,1024]{1,0:T(8,128)(2,1)S(1)}, bf16[16,1024]{1,0:T(8,128)(2,1)S(1)}, u32[]{:S(2)}, u32[]{:S(2)}) collective-permute-start(bf16[16,1024]{1,0:T(8,128)(2,1)S(1)} %get-tuple-element.34), channel_id=1, source_target_pairs={{0,24},{8,0},{16,8},{24,16},{1,25},{9,1},{17,9},{25,17},{2,26},{10... | collective-permute-start | bytes 98312 | tf_op jit(solution)/shard_map/ppermute | solution.py:88
  140.4 5.1 %collective-permute-start.18 = (bf16[16,1024]{1,0:T(8,128)(2,1)S(1)}, bf16[16,1024]{1,0:T(8,128)(2,1)S(1)}, u32[]{:S(2)}, u32[]{:S(2)}) collective-permute-start(bf16[16,1024]{1,0:T(8,128)(2,1)S(1)} %get-tuple-element.34), channel_id=1, source_target_pairs={{0,8},{8,16},{16,24},{24,0},{1,9},{9,17},{17,25},{25,1},{2,10},{10... | collective-permute-start | bytes 98312 | tf_op jit(solution)/shard_map/ppermute | solution.py:88
  141.2 6.9 %collective-permute-start.15 = (bf16[4,16,1152]{2,1,0:T(8,128)(2,1)S(1)}, bf16[4,16,1152]{2,1,0:T(8,128)(2,1)S(1)}, u32[]{:S(2)}, u32[]{:S(2)}) collective-permute-start(bf16[4,16,1152]{2,1,0:T(8,128)(2,1)S(1)} %get-tuple-element.54), channel_id=1, source_target_pairs={{0,24},{8,0},{16,8},{24,16},{1,25},{9,1},{17,9},{25,17},{2,26},{10... | collective-permute-start | bytes 442376 | tf_op jit(solution)/shard_map/ppermute | solution.py:88
  143.8 8.3 %collective-permute-start.14 = (bf16[4,16,1152]{2,1,0:T(8,128)(2,1)S(1)}, bf16[4,16,1152]{2,1,0:T(8,128)(2,1)S(1)}, u32[]{:S(2)}, u32[]{:S(2)}) collective-permute-start(bf16[4,16,1152]{2,1,0:T(8,128)(2,1)S(1)} %get-tuple-element.54), channel_id=1, source_target_pairs={{0,8},{8,16},{16,24},{24,0},{1,9},{9,17},{17,25},{25,1},{2,10},{10... | collective-permute-start | bytes 442376 | tf_op jit(solution)/shard_map/ppermute | solution.py:88
  143.8 8.3 %collective-permute-start.16 = (bf16[4,16,1152]{2,1,0:T(8,128)(2,1)S(1)}, bf16[4,16,1152]{2,1,0:T(8,128)(2,1)S(1)}, u32[]{:S(2)}, u32[]{:S(2)}) collective-permute-start(bf16[4,16,1152]{2,1,0:T(8,128)(2,1)S(1)} %get-tuple-element.54), channel_id=1, source_target_pairs={{0,16},{8,24},{16,0},{24,8},{1,17},{9,25},{17,1},{25,9},{2,18},{10... | collective-permute-start | bytes 442376 | tf_op jit(solution)/shard_map/ppermute | solution.py:88
  145.6 6.7 %collective-permute-start.22 = (bf16[4,16,1024]{2,1,0:T(8,128)(2,1)S(1)}, bf16[4,16,1024]{2,1,0:T(8,128)(2,1)S(1)}, u32[]{:S(2)}, u32[]{:S(2)}) collective-permute-start(bf16[4,16,1024]{2,1,0:T(8,128)(2,1)S(1)} %get-tuple-element.56), channel_id=1, source_target_pairs={{0,192},{64,0},{128,64},{192,128},{1,193},{65,1},{129,65},{193,129... | collective-permute-start | bytes 393224 | tf_op jit(solution)/shard_map/ppermute | solution.py:88
  147.7 5.2 %collective-permute-start.21 = (bf16[4,16,1024]{2,1,0:T(8,128)(2,1)S(1)}, bf16[4,16,1024]{2,1,0:T(8,128)(2,1)S(1)}, u32[]{:S(2)}, u32[]{:S(2)}) collective-permute-start(bf16[4,16,1024]{2,1,0:T(8,128)(2,1)S(1)} %get-tuple-element.56), channel_id=1, source_target_pairs={{0,64},{64,128},{128,192},{192,0},{1,65},{65,129},{129,193},{193,1... | collective-permute-start | bytes 393224 | tf_op jit(solution)/shard_map/ppermute | solution.py:88
  148.1 6.9 %collective-permute-start.23 = (bf16[4,16,1024]{2,1,0:T(8,128)(2,1)S(1)}, bf16[4,16,1024]{2,1,0:T(8,128)(2,1)S(1)}, u32[]{:S(2)}, u32[]{:S(2)}) collective-permute-start(bf16[4,16,1024]{2,1,0:T(8,128)(2,1)S(1)} %get-tuple-element.56), channel_id=1, source_target_pairs={{0,128},{64,192},{128,0},{192,64},{1,129},{65,193},{129,1},{193,65... | collective-permute-start | bytes 393224 | tf_op jit(solution)/shard_map/ppermute | solution.py:88
  152.2 5.1 %collective-permute-start.17 = (bf16[4,4,16,1152]{3,2,1,0:T(8,128)(2,1)S(1)}, bf16[4,4,16,1152]{3,2,1,0:T(8,128)(2,1)S(1)}, u32[]{:S(2)}, u32[]{:S(2)}) collective-permute-start(bf16[4,4,16,1152]{3,2,1,0:T(8,128)(2,1)S(1)} %pad_maximum_fusion.2.act_near_ref), channel_id=1, source_target_pairs={{0,32},{32,0},{1,33},{33,1},{2,34},{34,2},{3,35},{35,3},{4,36},{36... | collective-permute-start | bytes 1769480 | tf_op jit(solution)/shard_map/ppermute | solution.py:430
  164.7 47.0 %all-to-all-start.4 = ((bf16[32,128,384]{2,1,0:T(8,128)(2,1)}), bf16[32,128,384]{2,1,0:T(8,128)(2,1)S(1)}, u32[]{:S(2)}, u32[]{:S(2)}) async-start(bf16[32,128,384]{2,1,0:T(8,128)(2,1)} %bitcast.125), calls=%async_computation.4 | async-start | bytes 6291456 | tf_op jit(solution)/shard_map/all_to_all | solution.py:452
  205.5 19.9 %collective-permute-start.25 = (bf16[128,768]{1,0:T(8,128)(2,1)}, bf16[128,768]{1,0:T(8,128)(2,1)}, u32[]{:S(2)}, u32[]{:S(2)}) collective-permute-start(bf16[128,768]{1,0:T(8,128)(2,1)} %bitcast.117), channel_id=1, source_target_pairs={{0,0},{33,1},{66,2},{99,3},{132,4},{165,5},{198,6},{231,7},{4,33},... | collective-permute-start | bytes 589832 | tf_op jit(solution)/shard_map/ppermute | solution.py:468
  211.7 25.8 %all-to-all-start.5 = ((f32[256,1,128]{2,1,0:T(1,128)}), f32[256,1,128]{2,1,0:T(1,128)S(1)}, u32[]{:S(2)}, u32[]{:S(2)}) async-start(f32[256,1,128]{2,1,0:T(1,128)} %bitcast.45), calls=%async_computation.6 | async-start | bytes 262144 | tf_op jit(solution)/shard_map/all_to_all | solution.py:466
  225.4 13.4 %collective-permute-start.26 = (bf16[128,768]{1,0:T(8,128)(2,1)}, bf16[128,768]{1,0:T(8,128)(2,1)}, u32[]{:S(2)}, u32[]{:S(2)}) collective-permute-start(bf16[128,768]{1,0:T(8,128)(2,1)} %collective-permute-done.25), channel_id=1, source_target_pairs={{0,0},{1,1},{2,2},{3,3},{4,4},{5,5},{6,6},{7,7},{32,39},{33,32},{3... | collective-permute-start | bytes 589832 | tf_op jit(solution)/shard_map/ppermute | solution.py:468
  (14 other events, 90.3 us)
Sparse Core Ops, SparseCore 0:
  32.8 49.0 all-gather.2
  164.8 40.6 reduce-scatter.1
